TPU v7x, 32 devices: a whole 2x2x4 slice. The times are simulated.
32 devices in a mesh: dp: 4 (over x, core), ctx: 2 (over y), tp: 4 (over z).
Axes of the slice: x: 2, y: 2, z: 4, core: 2. Of those that a mesh axis runs over, the one named last changes fastest.
Arguments:
- block_in: bfloat16 [8, 1024, 2048], P('dp', 'ctx', 'tp'), may hold values from -6 to 6
- doc_starts: int32 [8, 3], P('dp'), may hold values from 0 to 1023, as said below
- query_weight: bfloat16 [2048, 2048], P('dp', 'tp'), may hold values from -0.125 to 0.125
- key_weight: bfloat16 [2048, 2048], P('dp', 'tp'), may hold values from -0.125 to 0.125
- value_weight: bfloat16 [2048, 2048], P('dp', 'tp'), may hold values from -0.125 to 0.125
- output_weight: bfloat16 [2048, 2048], P('tp', 'dp'), may hold values from -0.5 to 0.5
- up_weight: bfloat16 [2048, 8192], P('dp', 'tp'), may hold values from -0.125 to 0.125
- down_weight: bfloat16 [8192, 2048], P('tp', 'dp'), may hold values from -0.0625 to 0.0625
- query_bias: bfloat16 [2048], P(('tp', 'dp')), may hold values from -3 to 3
- key_bias: bfloat16 [2048], P(('tp', 'dp')), may hold values from -3 to 3
- value_bias: bfloat16 [2048], P(('tp', 'dp')), may hold values from -3 to 3
- up_bias: bfloat16 [8192], P(('tp', 'dp')), may hold values from -3 to 3
- output_bias: bfloat16 [2048], P(('tp', 'dp')), may hold values from -3 to 3
- norm_gain: bfloat16 [2048], P(('tp', 'dp')), may hold values from 0.2 to 4.2
- norm_shift: bfloat16 [2048], P(('tp', 'dp')), may hold values from -3 to 3
- cotangent: bfloat16 [8, 1024, 2048], P('dp', 'ctx', 'tp'), may hold values from -6 to 6
Outputs:
- block_out: bfloat16 [8, 1024, 2048], P('dp', 'ctx', 'tp')
- in_grad: float32 [8, 1024, 2048], P('dp', 'ctx', 'tp')
- query_weight_grad: float32 [2048, 2048], P('dp', 'tp')
- key_weight_grad: float32 [2048, 2048], P('dp', 'tp')
- value_weight_grad: float32 [2048, 2048], P('dp', 'tp')
- output_weight_grad: float32 [2048, 2048], P('tp', 'dp')
- up_weight_grad: float32 [2048, 8192], P('dp', 'tp')
- down_weight_grad: float32 [8192, 2048], P('tp', 'dp')
- query_bias_grad: float32 [2048], P(('tp', 'dp'))
- key_bias_grad: float32 [2048], P(('tp', 'dp'))
- value_bias_grad: float32 [2048], P(('tp', 'dp'))
- up_bias_grad: float32 [8192], P(('tp', 'dp'))
- output_bias_grad: float32 [2048], P(('tp', 'dp'))
- gain_grad: float32 [2048], P(('tp', 'dp'))
- shift_grad: float32 [2048], P(('tp', 'dp'))
Inputs may be any that keep to these rules, and one draw needn't show every extreme that they name: `doc_starts`: each sequence has 3 ascending starts: the first is 0, the second lies among the first 512 tokens, the third among the last 512 tokens, so the middle document reaches from the first index of ctx to the last.
All inputs are finite; a program needn't handle non-finite values.
Results may differ from a plain program's by a relative error of at most 0.025.
Values may be sent and summed in bfloat16 or wider, within the bound.
No kernel may reach another device: no remote copies, remote signals or barrier semaphores. Data moves between devices by JAX's collectives and lax.ppermute only.
A program may use at most 256 MiB of HBM per device.

v0:
```python
import math

import jax
import jax.numpy as jnp
from jax import lax
from jax.sharding import PartitionSpec as P

HEAD_DIM = 64
ROT = 32
D = 2048


epsilon = 1e-05
masked_score = -1e30


def gelu_tanh(values):
    inner = math.sqrt(2.0 / math.pi) * (values + 0.044715 * values * values * values)
    return 0.5 * values * (1.0 + jnp.tanh(inner))


def document_index(starts, positions):
    before = starts[:, None, :] <= positions[None, :, None]
    return jnp.sum(before.astype(jnp.int32), axis=2)


def rotary_tables(starts, positions):
    before = starts[:, None, :] <= positions[None, :, None]
    document_ids = jnp.sum(before.astype(jnp.int32), axis=2)
    opening = jnp.max(jnp.where(before, starts[:, None, :], 0), axis=2)
    relative = (positions[None, :] - opening).astype(jnp.float32)
    halfway = ROT // 2
    frequency = jnp.exp(jnp.arange(halfway, dtype=jnp.float32) * (-math.log(10000.0) / halfway))
    angles = relative[:, :, None] * frequency
    return (document_ids, jnp.cos(angles), jnp.sin(angles))


def rotate(values, cosine_table, sine_table):
    halfway = ROT // 2
    first_half = values[..., :halfway]
    second_half = values[..., halfway:ROT]
    cosine_part = cosine_table[:, :, None, :]
    sine_part = sine_table[:, :, None, :]
    return jnp.concatenate(
        [
            first_half * cosine_part - second_half * sine_part,
            second_half * cosine_part + first_half * sine_part,
            values[..., ROT:],
        ],
        axis=-1,
    )


def unrotate(grads, cosine_table, sine_table):
    halfway = ROT // 2
    first_half = grads[..., :halfway]
    second_half = grads[..., halfway:ROT]
    cosine_part = cosine_table[:, :, None, :]
    sine_part = sine_table[:, :, None, :]
    return jnp.concatenate(
        [
            first_half * cosine_part + second_half * sine_part,
            second_half * cosine_part - first_half * sine_part,
            grads[..., ROT:],
        ],
        axis=-1,
    )


def row_total(values):
    return lax.psum(jnp.sum(values, axis=2), "tp")


def body(
    block_in,
    doc_starts,
    query_weight,
    key_weight,
    value_weight,
    output_weight,
    up_weight,
    down_weight,
    query_bias,
    key_bias,
    value_bias,
    up_bias,
    output_bias,
    norm_gain,
    norm_shift,
    cotangent,
):
    (
        query_full,
        key_full,
        value_full,
        output_full,
        up_full,
        down_full,
        query_shift,
        key_shift,
        value_shift,
        up_shift,
        output_shift,
        gain_part,
        shift_part,
    ) = (
        lax.all_gather(query_weight, "dp", axis=0, tiled=True),
        lax.all_gather(key_weight, "dp", axis=0, tiled=True),
        lax.all_gather(value_weight, "dp", axis=0, tiled=True),
        lax.all_gather(output_weight, "dp", axis=1, tiled=True),
        lax.all_gather(up_weight, "dp", axis=0, tiled=True),
        lax.all_gather(down_weight, "dp", axis=1, tiled=True),
        lax.all_gather(query_bias, "dp", axis=0, tiled=True),
        lax.all_gather(key_bias, "dp", axis=0, tiled=True),
        lax.all_gather(value_bias, "dp", axis=0, tiled=True),
        lax.all_gather(up_bias, "dp", axis=0, tiled=True),
        lax.all_gather(output_bias, "dp", axis=0, tiled=True),
        lax.all_gather(norm_gain, "dp", axis=0, tiled=True),
        lax.all_gather(norm_shift, "dp", axis=0, tiled=True),
    )
    sequences_here, tokens_here, width_here = block_in.shape
    heads_here = width_here // HEAD_DIM
    context_size = lax.axis_size("ctx")
    length = context_size * tokens_here
    score_scale = HEAD_DIM ** (-0.5)
    positions = lax.axis_index("ctx") * tokens_here + jnp.arange(tokens_here, dtype=jnp.int32)
    query_documents, cosine_table, sine_table = rotary_tables(doc_starts, positions)
    inputs = block_in.astype(jnp.float32)
    average = row_total(inputs) / D
    centred = inputs - average[:, :, None]
    variance = row_total(centred * centred) / D
    inverse_root = lax.rsqrt(variance + epsilon)
    standard = centred * inverse_root[:, :, None]
    gain_local = gain_part.astype(jnp.float32)
    normed_local = (standard * gain_local + shift_part.astype(jnp.float32)).astype(jnp.bfloat16)
    normed = lax.all_gather(normed_local, "tp", axis=2, tiled=True)

    def project(weight, bias):
        return jnp.einsum(
            "std,de->ste", normed, weight, preferred_element_type=jnp.float32
        ) + bias.astype(jnp.float32)

    def heads_of(values):
        return values.reshape(sequences_here, tokens_here, heads_here, HEAD_DIM)

    queries = rotate(heads_of(project(query_full, query_shift)), cosine_table, sine_table).astype(
        jnp.bfloat16
    )
    keys_rot = rotate(heads_of(project(key_full, key_shift)), cosine_table, sine_table).astype(
        jnp.bfloat16
    )
    values_heads = heads_of(project(value_full, value_shift)).astype(jnp.bfloat16)
    keys_send = keys_rot.reshape(sequences_here, tokens_here, width_here)
    values_send = values_heads.reshape(sequences_here, tokens_here, width_here)

    def allowed_for(key_positions):
        key_documents = document_index(doc_starts, key_positions)
        same_document = query_documents[:, :, None] == key_documents[:, None, :]
        causal = key_positions[None, None, :] <= positions[None, :, None]
        return (same_document & causal)[:, None]

    def attend_block(running, key_block, value_block, key_positions):
        run_peak, run_total, run_values = running
        allowed = allowed_for(key_positions)
        scores = (
            jnp.einsum("sqhd,skhd->shqk", queries, key_block, preferred_element_type=jnp.float32)
            * score_scale
        )
        scores = jnp.where(allowed, scores, masked_score)
        new_peak = jnp.maximum(run_peak, jnp.max(scores, axis=3))
        expo_terms = jnp.where(allowed, jnp.exp(scores - new_peak[..., None]), 0.0)
        rescale = jnp.exp(run_peak - new_peak)
        run_total = run_total * rescale + jnp.sum(expo_terms, axis=3)
        run_values = run_values * rescale[..., None] + jnp.einsum(
            "shqk,skhd->shqd",
            expo_terms.astype(jnp.bfloat16),
            value_block,
            preferred_element_type=jnp.float32,
        )
        return (new_peak, run_total, run_values)

    empty_peak = jnp.full((sequences_here, heads_here, tokens_here), masked_score, jnp.float32)
    empty_total = jnp.zeros((sequences_here, heads_here, tokens_here), jnp.float32)
    empty_values = jnp.zeros((sequences_here, heads_here, tokens_here, HEAD_DIM), jnp.float32)
    key_piece = lax.all_gather(keys_send, "ctx", axis=1, tiled=True)
    value_piece = lax.all_gather(values_send, "ctx", axis=1, tiled=True)
    piece_rows = key_piece.shape[1]
    fold_block_rows = math.gcd(piece_rows, 512)

    def advance(block_index, state_now):
        offset = block_index * fold_block_rows
        key_block = lax.dynamic_slice_in_dim(key_piece, offset, fold_block_rows, 1).reshape(
            sequences_here, fold_block_rows, heads_here, HEAD_DIM
        )
        value_block = lax.dynamic_slice_in_dim(value_piece, offset, fold_block_rows, 1).reshape(
            sequences_here, fold_block_rows, heads_here, HEAD_DIM
        )
        key_positions = offset + jnp.arange(fold_block_rows, dtype=jnp.int32)
        return attend_block(state_now, key_block, value_block, key_positions)

    run_peak, run_total, run_values = lax.fori_loop(
        0, piece_rows // fold_block_rows, advance, (empty_peak, empty_total, empty_values)
    )
    attention = run_values / run_total[..., None]
    log_total = run_peak + jnp.log(run_total)
    attention_b = (
        attention.transpose(0, 2, 1, 3)
        .reshape(sequences_here, tokens_here, width_here)
        .astype(jnp.bfloat16)
    )
    upward = project(up_full, up_shift)
    gelu_value, gelu_pull = jax.vjp(gelu_tanh, upward)
    hidden = gelu_value.astype(jnp.bfloat16)
    partial_value = jnp.einsum(
        "ste,ed->std", attention_b, output_full, preferred_element_type=jnp.float32
    ) + jnp.einsum("stf,fd->std", hidden, down_full, preferred_element_type=jnp.float32)
    summed = lax.psum_scatter(
        partial_value.astype(jnp.bfloat16), "tp", scatter_dimension=2, tiled=True
    ).astype(jnp.float32)
    block_out = (inputs + summed + output_shift.astype(jnp.float32)).astype(jnp.bfloat16)
    grad_rows = lax.all_gather(cotangent, "tp", axis=2, tiled=True)
    output_weight_grad = jnp.einsum(
        "ste,std->ed", attention_b, grad_rows, preferred_element_type=jnp.float32
    )
    down_weight_grad = jnp.einsum(
        "stf,std->fd", hidden, grad_rows, preferred_element_type=jnp.float32
    )
    output_bias_grad = jnp.sum(cotangent.astype(jnp.float32), axis=(0, 1))
    attention_grad = jnp.einsum(
        "std,ed->ste", grad_rows, output_full, preferred_element_type=jnp.float32
    ).astype(jnp.bfloat16)
    hidden_grad = jnp.einsum(
        "std,fd->stf", grad_rows, down_full, preferred_element_type=jnp.float32
    )
    up_grad = gelu_pull(hidden_grad)[0].astype(jnp.bfloat16)
    grad_heads = attention_grad.reshape(sequences_here, tokens_here, heads_here, HEAD_DIM)
    row_delta = jnp.sum(grad_heads.astype(jnp.float32).transpose(0, 2, 1, 3) * attention, axis=3)
    keys_all, values_all = (
        lax.all_gather(keys_send, "ctx", axis=1, tiled=True),
        lax.all_gather(values_send, "ctx", axis=1, tiled=True),
    )
    block_rows = math.gcd(length, 512)
    query_start = jnp.zeros((sequences_here, tokens_here, heads_here, HEAD_DIM), jnp.float32)

    def back_step(query_acc, block_index):
        offset = block_index * block_rows
        key_block = lax.dynamic_slice_in_dim(keys_all, offset, block_rows, 1).reshape(
            sequences_here, block_rows, heads_here, HEAD_DIM
        )
        value_block = lax.dynamic_slice_in_dim(values_all, offset, block_rows, 1).reshape(
            sequences_here, block_rows, heads_here, HEAD_DIM
        )
        key_positions = offset + jnp.arange(block_rows, dtype=jnp.int32)
        allowed = allowed_for(key_positions)
        scores = (
            jnp.einsum("sqhd,skhd->shqk", queries, key_block, preferred_element_type=jnp.float32)
            * score_scale
        )
        soft_weights = jnp.exp(jnp.where(allowed, scores - log_total[..., None], masked_score))
        weight_grad = jnp.einsum(
            "sqhd,skhd->shqk", grad_heads, value_block, preferred_element_type=jnp.float32
        )
        score_grad = (soft_weights * (weight_grad - row_delta[..., None])).astype(jnp.bfloat16)
        query_acc = (
            query_acc
            + jnp.einsum(
                "shqk,skhd->sqhd", score_grad, key_block, preferred_element_type=jnp.float32
            )
            * score_scale
        )
        key_part = (
            jnp.einsum("shqk,sqhd->skhd", score_grad, queries, preferred_element_type=jnp.float32)
            * score_scale
        )
        value_part = jnp.einsum(
            "shqk,sqhd->skhd",
            soft_weights.astype(jnp.bfloat16),
            grad_heads,
            preferred_element_type=jnp.float32,
        )
        return (query_acc, (key_part, value_part))

    query_acc, (key_parts, value_parts) = lax.scan(
        back_step, query_start, jnp.arange(length // block_rows, dtype=jnp.int32)
    )
    key_grads_all = key_parts.transpose(1, 0, 2, 3, 4).reshape(sequences_here, length, width_here)
    value_grads_all = value_parts.transpose(1, 0, 2, 3, 4).reshape(
        sequences_here, length, width_here
    )
    key_grad_here, value_grad_here = (
        lax.psum_scatter(
            key_grads_all.astype(jnp.bfloat16), "ctx", scatter_dimension=1, tiled=True
        ).astype(jnp.float32),
        lax.psum_scatter(
            value_grads_all.astype(jnp.bfloat16), "ctx", scatter_dimension=1, tiled=True
        ).astype(jnp.float32),
    )
    query_grad = (
        unrotate(query_acc, cosine_table, sine_table)
        .astype(jnp.bfloat16)
        .reshape(sequences_here, tokens_here, width_here)
    )
    key_grad = (
        unrotate(heads_of(key_grad_here), cosine_table, sine_table)
        .astype(jnp.bfloat16)
        .reshape(sequences_here, tokens_here, width_here)
    )
    value_grad = value_grad_here.astype(jnp.bfloat16)

    def weight_grad_of(grads_b):
        return jnp.einsum("std,ste->de", normed, grads_b, preferred_element_type=jnp.float32)

    def bias_grad_of(grads_b):
        return jnp.sum(grads_b.astype(jnp.float32), axis=(0, 1))

    query_weight_grad = weight_grad_of(query_grad)
    key_weight_grad = weight_grad_of(key_grad)
    value_weight_grad = weight_grad_of(value_grad)
    up_weight_grad = weight_grad_of(up_grad)
    query_bias_grad = bias_grad_of(query_grad)
    key_bias_grad = bias_grad_of(key_grad)
    value_bias_grad = bias_grad_of(value_grad)
    up_bias_grad = bias_grad_of(up_grad)
    normed_grad = jnp.einsum(
        "ste,de->std", query_grad, query_full, preferred_element_type=jnp.float32
    )
    normed_grad = normed_grad + jnp.einsum(
        "ste,de->std", key_grad, key_full, preferred_element_type=jnp.float32
    )
    normed_grad = normed_grad + jnp.einsum(
        "ste,de->std", value_grad, value_full, preferred_element_type=jnp.float32
    )
    normed_grad = normed_grad + jnp.einsum(
        "stf,df->std", up_grad, up_full, preferred_element_type=jnp.float32
    )
    normed_grad_here = lax.psum_scatter(
        normed_grad.astype(jnp.bfloat16), "tp", scatter_dimension=2, tiled=True
    ).astype(jnp.float32)
    scaled = normed_grad_here * gain_local
    total_plain, total_cross = lax.psum(
        (jnp.sum(scaled, axis=2), jnp.sum(scaled * standard, axis=2)), "tp"
    )
    in_grad = cotangent.astype(jnp.float32) + inverse_root[:, :, None] * (
        scaled - total_plain[:, :, None] / D - standard * total_cross[:, :, None] / D
    )
    gain_grad = jnp.sum(normed_grad_here * standard, axis=(0, 1))
    shift_grad = jnp.sum(normed_grad_here, axis=(0, 1))
    (
        query_wg,
        key_wg,
        value_wg,
        output_wg,
        up_wg,
        down_wg,
        query_bg,
        key_bg,
        value_bg,
        up_bg,
        output_bg,
        gain_g,
        shift_g,
    ) = (
        lax.psum_scatter(
            query_weight_grad.astype(jnp.bfloat16), "dp", scatter_dimension=0, tiled=True
        ).astype(jnp.float32),
        lax.psum_scatter(
            key_weight_grad.astype(jnp.bfloat16), "dp", scatter_dimension=0, tiled=True
        ).astype(jnp.float32),
        lax.psum_scatter(
            value_weight_grad.astype(jnp.bfloat16), "dp", scatter_dimension=0, tiled=True
        ).astype(jnp.float32),
        lax.psum_scatter(
            output_weight_grad.astype(jnp.bfloat16), "dp", scatter_dimension=1, tiled=True
        ).astype(jnp.float32),
        lax.psum_scatter(
            up_weight_grad.astype(jnp.bfloat16), "dp", scatter_dimension=0, tiled=True
        ).astype(jnp.float32),
        lax.psum_scatter(
            down_weight_grad.astype(jnp.bfloat16), "dp", scatter_dimension=1, tiled=True
        ).astype(jnp.float32),
        lax.psum_scatter(
            query_bias_grad.astype(jnp.bfloat16), "dp", scatter_dimension=0, tiled=True
        ).astype(jnp.float32),
        lax.psum_scatter(
            key_bias_grad.astype(jnp.bfloat16), "dp", scatter_dimension=0, tiled=True
        ).astype(jnp.float32),
        lax.psum_scatter(
            value_bias_grad.astype(jnp.bfloat16), "dp", scatter_dimension=0, tiled=True
        ).astype(jnp.float32),
        lax.psum_scatter(
            up_bias_grad.astype(jnp.bfloat16), "dp", scatter_dimension=0, tiled=True
        ).astype(jnp.float32),
        lax.psum_scatter(
            output_bias_grad.astype(jnp.bfloat16), "dp", scatter_dimension=0, tiled=True
        ).astype(jnp.float32),
        lax.psum_scatter(
            gain_grad.astype(jnp.bfloat16), "dp", scatter_dimension=0, tiled=True
        ).astype(jnp.float32),
        lax.psum_scatter(
            shift_grad.astype(jnp.bfloat16), "dp", scatter_dimension=0, tiled=True
        ).astype(jnp.float32),
    )
    (
        query_wg,
        key_wg,
        value_wg,
        output_wg,
        up_wg,
        down_wg,
        query_bg,
        key_bg,
        value_bg,
        up_bg,
        output_bg,
        gain_g,
        shift_g,
    ) = (
        lax.psum(query_wg.astype(jnp.bfloat16), "ctx").astype(jnp.float32),
        lax.psum(key_wg.astype(jnp.bfloat16), "ctx").astype(jnp.float32),
        lax.psum(value_wg.astype(jnp.bfloat16), "ctx").astype(jnp.float32),
        lax.psum(output_wg.astype(jnp.bfloat16), "ctx").astype(jnp.float32),
        lax.psum(up_wg.astype(jnp.bfloat16), "ctx").astype(jnp.float32),
        lax.psum(down_wg.astype(jnp.bfloat16), "ctx").astype(jnp.float32),
        lax.psum(query_bg.astype(jnp.bfloat16), "ctx").astype(jnp.float32),
        lax.psum(key_bg.astype(jnp.bfloat16), "ctx").astype(jnp.float32),
        lax.psum(value_bg.astype(jnp.bfloat16), "ctx").astype(jnp.float32),
        lax.psum(up_bg.astype(jnp.bfloat16), "ctx").astype(jnp.float32),
        lax.psum(output_bg.astype(jnp.bfloat16), "ctx").astype(jnp.float32),
        lax.psum(gain_g.astype(jnp.bfloat16), "ctx").astype(jnp.float32),
        lax.psum(shift_g.astype(jnp.bfloat16), "ctx").astype(jnp.float32),
    )
    return (
        block_out,
        in_grad,
        query_wg,
        key_wg,
        value_wg,
        output_wg,
        up_wg,
        down_wg,
        query_bg,
        key_bg,
        value_bg,
        up_bg,
        output_bg,
        gain_g,
        shift_g,
    )


def solution(mesh):
    return jax.shard_map(
        body,
        mesh=mesh,
        in_specs=(
            P("dp", "ctx", "tp"),
            P("dp", None),
            P("dp", "tp"),
            P("dp", "tp"),
            P("dp", "tp"),
            P("tp", "dp"),
            P("dp", "tp"),
            P("tp", "dp"),
            P(("tp", "dp")),
            P(("tp", "dp")),
            P(("tp", "dp")),
            P(("tp", "dp")),
            P(("tp", "dp")),
            P(("tp", "dp")),
            P(("tp", "dp")),
            P("dp", "ctx", "tp"),
        ),
        out_specs=(
            P("dp", "ctx", "tp"),
            P("dp", "ctx", "tp"),
            P("dp", "tp"),
            P("dp", "tp"),
            P("dp", "tp"),
            P("tp", "dp"),
            P("dp", "tp"),
            P("tp", "dp"),
            P(("tp", "dp")),
            P(("tp", "dp")),
            P(("tp", "dp")),
            P(("tp", "dp")),
            P(("tp", "dp")),
            P(("tp", "dp")),
            P(("tp", "dp")),
        ),
        check_vma=False,
    )
```

profile of v0, /device:TPU:0, one launch (start us, length us, event | category | flops | bytes accessed | tf_op | source)
XLA Modules:
  0.0 1308.9 jit_solution(6358507401931292821)
XLA Ops:
  65.6 61.7 %all-gather.18.cloned.1.call-done = bf16[2,512,2048]{2,1,0:T(8,128)(2,1)} async-done(((bf16[2,512,512]{2,1,0:T(8,128)(2,1)}), bf16[2,512,2048]{2,1,0:T(8,128)(2,1)}) %all-gather.18.cloned.1.call-update) | async-done | bytes 4194320 | tf_op jit(solution)/shard_map/all_gather | solution.py:136
  133.9 16.7 %all-gather.20.cloned.1.call-done = bf16[2048,512]{0,1:T(8,128)(2,1)} async-done(((bf16[512,512]{0,1:T(8,128)(2,1)}), bf16[2048,512]{0,1:T(8,128)(2,1)}) %all-gather.20.cloned.1.call-update) | async-done | bytes 2097168 | tf_op jit(solution)/shard_map/all_gather | solution.py:108
  155.9 19.3 %all-gather.24.cloned.1.call-done = bf16[2048,512]{0,1:T(8,128)(2,1)} async-done(((bf16[512,512]{0,1:T(8,128)(2,1)}), bf16[2048,512]{0,1:T(8,128)(2,1)}) %all-gather.24.cloned.1.call-update) | async-done | bytes 2097168 | tf_op jit(solution)/shard_map/all_gather | solution.py:107
  184.2 15.1 %all-gather.30.cloned.1.call-done = bf16[512,2048]{1,0:T(8,128)(2,1)} async-done(((bf16[512,512]{1,0:T(8,128)(2,1)}), bf16[512,2048]{1,0:T(8,128)(2,1)}) %all-gather.30.cloned.1.call-update) | async-done | bytes 2097168 | tf_op jit(solution)/shard_map/all_gather | solution.py:110
  199.2 82.2 %all-gather.36.cloned.1.call-done = bf16[2,512,2048]{2,1,0:T(8,128)(2,1)} async-done(((bf16[2,512,512]{2,1,0:T(8,128)(2,1)}), bf16[2,512,2048]{2,1,0:T(8,128)(2,1)}) %all-gather.36.cloned.1.call-update) | async-done | bytes 4194320 | tf_op jit(solution)/shard_map/all_gather | solution.py:221
  287.7 27.6 %all-gather.28.cloned.1.call-done = bf16[2,1024,512]{2,1,0:T(8,128)(2,1)} async-done(((bf16[2,512,512]{2,1,0:T(8,128)(2,1)}), bf16[2,1024,512]{2,1,0:T(8,128)(2,1)}) %all-gather.28.cloned.1.call-update) | async-done | bytes 2097168 | tf_op jit(solution)/shard_map/all_gather | solution.py:186
  319.3 31.3 %all-gather.22.cloned.1.call-done = bf16[2,1024,512]{1,2,0:T(8,128)(2,1)} async-done(((bf16[2,512,512]{1,2,0:T(8,128)(2,1)}), bf16[2,1024,512]{1,2,0:T(8,128)(2,1)}) %all-gather.22.cloned.1.call-update) | async-done | bytes 2097168 | tf_op jit(solution)/shard_map/all_gather | solution.py:185
  350.5 53.1 %while.33 = (s32[]{:T(128)}, f32[2,8,512]{2,1,0:T(8,128)S(1)}, f32[2,8,512]{2,1,0:T(8,128)S(1)}, f32[2,8,512,64]{2,3,1,0:T(8,128)}, s32[2,512]{1,0:T(2,128)S(1)}...) while((s32[]{:T(128)}, f32[2,8,512]{2,1,0:T(8,128)S(1)}, ...), condition=%wide.region_10.11_spmd.clone, body=%wide.region_6.10_spmd.clone.sunk | while | flops 1131201536 | bytes 132143360 | solution.py:201
  407.0 86.9 %while.34 = (s32[]{:T(128)}, f32[2,512,8,64]{1,3,2,0:T(8,128)}, bf16[2,2,512,8,64]{2,4,3,1,0:T(8,128)(2,1)}, bf16[2,2,512,8,64]{2,4,3,1,0:T(8,128)(2,1)}, s32[2]...) while((s32[]{:T(128)}, f32[2,512,8,64]{1,3,2,0:T(8,128)}, ...), condition=%wide.region_15.16_spmd.clone, body=%wide.region_13.15_spmd.clone.sunk | while | flops 2729714688 | bytes 156359584 | solution.py:283
  514.5 17.8 %reduce-scatter.13.cloned.1.call-done = bf16[2,512,512]{1,2,0:T(8,128)(2,1)} async-done(((bf16[2,1024,512]{1,2,0:T(8,128)(2,1)}), bf16[2,512,512]{1,2,0:T(8,128)(2,1)}) %reduce-scatter.13.cloned.1.call-update) | async-done | bytes 1048592 | tf_op jit(solution)/shard_map/reduce_scatter | solution.py:291
  552.3 14.7 %reduce-scatter.15.cloned.1.call-done = bf16[2,512,512]{1,2,0:T(8,128)(2,1)} async-done(((bf16[2,1024,512]{1,2,0:T(8,128)(2,1)}), bf16[2,512,512]{1,2,0:T(8,128)(2,1)}) %reduce-scatter.15.cloned.1.call-update) | async-done | bytes 1048592 | tf_op jit(solution)/shard_map/reduce_scatter | solution.py:294
  573.3 53.6 %all-gather.32.cloned.1.call-done = bf16[2048,2048]{1,0:T(8,128)(2,1)} async-done(((bf16[512,2048]{1,0:T(8,128)(2,1)}), bf16[2048,2048]{1,0:T(8,128)(2,1)}) %all-gather.32.cloned.1.call-update) | async-done | bytes 8388624 | tf_op jit(solution)/shard_map/all_gather | solution.py:111
  626.8 14.4 %fusion.42 = f32[2,512,2048]{2,1,0:T(8,128)} fusion(bf16[2,512,2048]{2,1,0:T(8,128)(2,1)} %all-gather.18.cloned.1.call-done, bf16[2048,2048]{1,0:T(8,128)(2,1)} %all-gather.32.cloned.1.call-done), kind=kOutput, calls=%fused_computation.64 | convolution fusion | flops 8589934592 | bytes 20971520 | tf_op jit(solution)/shard_map/std,de->ste/dot_general | solution.py:139
  641.3 45.3 %all-gather.34.cloned.1.call-done = bf16[2048,2048]{1,0:T(8,128)(2,1)} async-done(((bf16[2048,512]{1,0:T(8,128)(2,1)}), bf16[2048,2048]{1,0:T(8,128)(2,1)}) %all-gather.34.cloned.1.call-update) | async-done | bytes 8388624 | tf_op jit(solution)/shard_map/all_gather | solution.py:112
  686.6 20.1 %fusion.104 = (bf16[2048]{0:T(1024)(128)(2,1)S(1)}, bf16[2,512,2048]{2,1,0:T(8,128)(2,1)S(1)}) fusion(f32[2,512,2048]{2,1,0:T(8,128)} %fusion.42, f32[2048]{0:T(1024)S(1)} %bitcast.254, bf16[2,512,2048]{2,1,0:T(8,128)(2,1)} %all-gather.36.cloned.1.call-done, bf16[2048,2048]{1,0:T(8,128)(2,1)} %all-gather.34.cloned.1.call-done), kind=kOutput, calls=%fused_computation.152 | convolution fusion | flops 8644458496 | bytes 25178112 | tf_op jit(solution)/shard_map/std,fd->stf/dot_general | solution.py:232
  720.4 15.9 %bitcast_convert_fusion = bf16[2048,2048]{1,0:T(8,128)(2,1)} fusion(bf16[2,512,2048]{2,1,0:T(8,128)(2,1)} %all-gather.36.cloned.1.call-done, f32[2,512,2048]{2,1,0:T(8,128)} %fusion.42, f32[2048]{0:T(1024)S(1)} %bitcast.255), kind=kOutput, calls=%fused_computation.46 | convolution fusion | flops 8615100416 | bytes 20979712 | tf_op jit(solution)/shard_map/stf,std->fd/dot_general | solution.py:225
  755.2 19.1 %add_convert_fusion = bf16[2,512,2048]{2,1,0:T(8,128)(2,1)} fusion(f32[2,512,2048]{2,1,0:T(8,128)} %fusion.74, f32[2,512,2048]{2,1,0:T(8,128)} %fusion.78, f32[2,512,2048]{2,1,0:T(8,128)} %fusion.82, bf16[2,512,2048]{2,1,0:T(8,128)(2,1)} %copy-done.43, bf16[2048,2048]{1,0:T(8,128)(2,1)} %all-gather.32.cloned.1.call-done), kind=kOutput, calls=%fused_computation.66 | convolution fusion | flops 8598323200 | bytes 41943040 | tf_op jit(solution)/shard_map/stf,df->std/dot_general | solution.py:333
  779.7 16.1 %add_convert_fusion.1 = bf16[2,512,2048]{2,1,0:T(8,128)(2,1)} fusion(f32[2,512,2048]{2,1,0:T(8,128)S(1)} %fusion.72, bf16[2048,2048]{1,0:T(8,128)(2,1)} %all-gather.34.cloned.1.call-done, f32[2,512,2048]{2,1,0:T(8,128)} %fusion.42, f32[2048]{0:T(1024)S(1)} %bitcast.256), kind=kOutput, calls=%fused_computation.69 | convolution fusion | flops 8615100416 | bytes 29368320 | tf_op jit(solution)/shard_map/stf,fd->std/dot_general | solution.py:216
  796.0 27.1 %reduce-scatter.23.cloned.1.call-done = bf16[512,512]{1,0:T(8,128)(2,1)} async-done(((bf16[2048,512]{1,0:T(8,128)(2,1)}), bf16[512,512]{1,0:T(8,128)(2,1)}) %reduce-scatter.23.cloned.1.call-update) | async-done | bytes 524304 | tf_op jit(solution)/shard_map/reduce_scatter | solution.py:369
  823.0 74.2 %reduce-scatter.27.cloned.1.call-done = bf16[512,2048]{1,0:T(8,128)(2,1)} async-done(((bf16[2048,2048]{1,0:T(8,128)(2,1)}), bf16[512,2048]{1,0:T(8,128)(2,1)}) %reduce-scatter.27.cloned.1.call-update) | async-done | bytes 2097168 | tf_op jit(solution)/shard_map/reduce_scatter | solution.py:375
  897.2 74.3 %reduce-scatter.29.cloned.1.call-done = bf16[2048,512]{1,0:T(8,128)(2,1)} async-done(((bf16[2048,2048]{1,0:T(8,128)(2,1)}), bf16[2048,512]{1,0:T(8,128)(2,1)}) %reduce-scatter.29.cloned.1.call-update) | async-done | bytes 2097168 | tf_op jit(solution)/shard_map/reduce_scatter | solution.py:378
  979.2 72.1 %reduce-scatter.17.cloned.1.call-done = bf16[2,512,512]{2,1,0:T(8,128)(2,1)} async-done(((bf16[2,512,2048]{2,1,0:T(8,128)(2,1)}), bf16[2,512,512]{2,1,0:T(8,128)(2,1)}) %reduce-scatter.17.cloned.1.call-update) | async-done | bytes 1048592 | tf_op jit(solution)/shard_map/reduce_scatter | solution.py:336
  1087.9 44.0 %reduce-scatter.11.cloned.1.call-done = bf16[2,512,512]{2,1,0:T(8,128)(2,1)} async-done(((bf16[2,512,2048]{2,1,0:T(8,128)(2,1)}), bf16[2,512,512]{2,1,0:T(8,128)(2,1)}) %reduce-scatter.11.cloned.1.call-update) | async-done | bytes 1048592 | tf_op jit(solution)/shard_map/reduce_scatter | solution.py:217
  1135.5 154.8 %all-reduce.13.cloned.1.call-done = (bf16[512,512]{1,0:T(8,128)(2,1)}, bf16[512,512]{1,0:T(8,128)(2,1)}, bf16[512,512]{1,0:T(8,128)(2,1)}, bf16[512,512]{1,0:T(8...) async-done(((bf16[512,512]{1,0:T(8,128)(2,1)}, bf16[512,512]{1,0:T(8,128)(2,1)}, bf16[512,512]{1,0:T(8,128)(2,1)}, bf16[512,512]{1,0:T(8,128)(2,1)}, ...) | async-done | bytes 6291472 | tf_op jit(solution)/shard_map/psum | solution.py:418
  (289 shorter events, 372.9 us)
Async XLA Ops:
  7.2 58.4 %all-gather.26.cloned.1.call-start = ((), (), s32[]{:S(2)}) async-start(), calls=%async_computation.14 | async-start | bytes 2621440 | tf_op jit(solution)/shard_map/all_gather | solution.py:109
  7.9 119.4 %all-gather.18.cloned.1.call-start = ((), (), s32[]{:S(2)}) async-start(), calls=%async_computation.10 | async-start | bytes 5242880 | tf_op jit(solution)/shard_map/all_gather | solution.py:136
  46.8 103.8 %all-gather.20.cloned.1.call-start = ((), (), s32[]{:S(2)}) async-start(), calls=%async_computation.11 | async-start | bytes 2621440 | tf_op jit(solution)/shard_map/all_gather | solution.py:108
  47.9 127.3 %all-gather.24.cloned.1.call-start = ((), (), s32[]{:S(2)}) async-start(), calls=%async_computation.13 | async-start | bytes 2621440 | tf_op jit(solution)/shard_map/all_gather | solution.py:107
  49.0 150.3 %all-gather.30.cloned.1.call-start = ((), (), s32[]{:S(2)}) async-start(), calls=%async_computation.16 | async-start | bytes 2621440 | tf_op jit(solution)/shard_map/all_gather | solution.py:110
  49.6 231.9 %all-gather.36.cloned.1.call-start = ((), (), s32[]{:S(2)}) async-start(), calls=%async_computation.20 | async-start | bytes 5242880 | tf_op jit(solution)/shard_map/all_gather | solution.py:221
  50.2 265.1 %all-gather.28.cloned.1.call-start = ((), (), s32[]{:S(2)}) async-start(), calls=%async_computation.15 | async-start | bytes 3145728 | tf_op jit(solution)/shard_map/all_gather | solution.py:186
  133.5 217.0 %all-gather.22.cloned.1.call-start = ((), (), s32[]{:S(2)}) async-start(), calls=%async_computation.12 | async-start | bytes 3145728 | tf_op jit(solution)/shard_map/all_gather | solution.py:185
  182.1 350.2 %reduce-scatter.13.cloned.1.call-start = ((), (), s32[]{:S(2)}) async-start(), calls=%async_computation.21 | async-start | bytes 3145728 | tf_op jit(solution)/shard_map/reduce_scatter | solution.py:291
  500.4 66.6 %reduce-scatter.15.cloned.1.call-start = ((), (), s32[]{:S(2)}) async-start(), calls=%async_computation.22 | async-start | bytes 3145728 | tf_op jit(solution)/shard_map/reduce_scatter | solution.py:294
  506.9 119.9 %all-gather.32.cloned.1.call-start = ((), (), s32[]{:S(2)}) async-start(), calls=%async_computation.17 | async-start | bytes 10485760 | tf_op jit(solution)/shard_map/all_gather | solution.py:111
  507.6 179.0 %all-gather.34.cloned.1.call-start = ((), (), s32[]{:S(2)}) async-start(), calls=%async_computation.18 | async-start | bytes 10485760 | tf_op jit(solution)/shard_map/all_gather | solution.py:112
  508.2 287.7 %reduce-scatter.25.cloned.1.call-start = ((), (), s32[]{:S(2)}) async-start(), calls=%async_computation.27 | async-start | bytes 2621440 | tf_op jit(solution)/shard_map/reduce_scatter | solution.py:372
  514.3 281.6 %reduce-scatter.19.cloned.1.call-start = ((), (), s32[]{:S(2)}) async-start(), calls=%async_computation.24 | async-start | bytes 2621440 | tf_op jit(solution)/shard_map/reduce_scatter | solution.py:363
  540.2 255.7 %reduce-scatter.21.cloned.1.call-start = ((), (), s32[]{:S(2)}) async-start(), calls=%async_computation.25 | async-start | bytes 2621440 | tf_op jit(solution)/shard_map/reduce_scatter | solution.py:366
  547.0 276.0 %reduce-scatter.23.cloned.1.call-start = ((), (), s32[]{:S(2)}) async-start(), calls=%async_computation.26 | async-start | bytes 2621440 | tf_op jit(solution)/shard_map/reduce_scatter | solution.py:369
  573.2 324.0 %reduce-scatter.27.cloned.1.call-start = ((), (), s32[]{:S(2)}) async-start(), calls=%async_computation.28 | async-start | bytes 10485760 | tf_op jit(solution)/shard_map/reduce_scatter | solution.py:375
  720.3 251.2 %reduce-scatter.29.cloned.1.call-start = ((), (), s32[]{:S(2)}) async-start(), calls=%async_computation.29 | async-start | bytes 10485760 | tf_op jit(solution)/shard_map/reduce_scatter | solution.py:378
  736.4 314.9 %reduce-scatter.17.cloned.1.call-start = ((), (), s32[]{:S(2)}) async-start(), calls=%async_computation.23 | async-start | bytes 5242880 | tf_op jit(solution)/shard_map/reduce_scatter | solution.py:336
  774.4 357.6 %reduce-scatter.11.cloned.1.call-start = ((), (), s32[]{:S(2)}) async-start(), calls=%async_computation.19 | async-start | bytes 5242880 | tf_op jit(solution)/shard_map/reduce_scatter | solution.py:217
  795.8 177.9 %copy-start.37 = (bf16[128]{0:T(256)(128)(2,1)S(1)}, bf16[128]{0:T(256)(128)(2,1)}, u32[]{:S(2)}) copy-start(bf16[128]{0:T(256)(128)(2,1)} %param.32) | copy-start | bytes 772
  795.8 183.0 %copy-start.31 = (bf16[8,64]{1,0:T(8,128)(2,1)S(1)}, bf16[8,64]{1,0:T(8,128)(2,1)}, u32[]{:S(2)}) copy-start(bf16[8,64]{1,0:T(8,128)(2,1)} %get-tuple-element.557) | copy-start | bytes 3076
  795.8 183.0 %copy-start.30 = (bf16[8,64]{1,0:T(8,128)(2,1)S(1)}, bf16[8,64]{1,0:T(8,128)(2,1)}, u32[]{:S(2)}) copy-start(bf16[8,64]{1,0:T(8,128)(2,1)} %get-tuple-element.523) | copy-start | bytes 3076
  795.8 494.5 %all-reduce.13.cloned.1.call-start = ((), (), s32[]{:S(2)}) async-start(), calls=%async_computation.30 | async-start | bytes 12582912 | tf_op jit(solution)/shard_map/psum | solution.py:418
  (47 other events, 1189.1 us)
Sparse Core Ops, SparseCore 0:
  9.6 25.2 all-gather.25
  46.9 80.3 all-gather.17
  129.4 21.1 all-gather.19
  152.6 22.5 all-gather.23
  176.6 22.5 all-gather.29
  200.7 80.7 all-gather.35
  283.6 31.6 all-gather.27
  317.4 33.1 all-gather.21
  500.5 31.8 reduce-scatter.12
  535.1 31.8 reduce-scatter.14
  568.5 58.2 all-gather.31
  628.3 58.2 all-gather.33
  689.1 31.4 reduce-scatter.24
  723.7 31.4 reduce-scatter.18
  757.5 31.4 reduce-scatter.20
  791.6 31.4 reduce-scatter.22
  825.5 71.7 reduce-scatter.26
  899.8 71.6 reduce-scatter.28
  974.4 76.7 reduce-scatter.16
  1054.1 77.7 reduce-scatter.10
  1134.9 155.3 all-reduce.12
where the time goes:
time: 1320 us; the launch traced here: 1310 us
  waiting for transfers between devices  835 us (63%)
  matrix products  267 us (20%)
  blocking collectives  85.8 us (6%)
  other arithmetic  56.6 us (4%)
  local copies, waits for them, and re-layouts  43.9 us (3%)
  between operations  16.7 us (1%)
    psum x1, waiting for transfers between devices, body(): lax.psum(query_wg.astype(jnp.bfloat16), 'ctx').astype(jnp.float32)  155 us
    all_gather x1, waiting for transfers between devices, body(): grad_rows = lax.all_gather(cotangent, 'tp', axis=2, tiled=True)  82.2 us
    reduce_scatter x1, waiting for transfers between devices, body(): lax.psum_scatter(down_weight_grad.astype(jnp.bfloat16), 'dp', scatter_dim...  74.3 us
    reduce_scatter x1, waiting for transfers between devices, body(): lax.psum_scatter(up_weight_grad.astype(jnp.bfloat16), 'dp', scatter_dimen...  74.2 us
    reduce_scatter x1, waiting for transfers between devices, body(): lax.psum_scatter(normed_grad.astype(jnp.bfloat16), 'tp', scatter_dimensio...  72.1 us
    all_gather x1, waiting for transfers between devices, body(): normed = lax.all_gather(normed_local, 'tp', axis=2, tiled=True)  61.7 us
    all_gather x1, waiting for transfers between devices, body(): lax.all_gather(up_weight, 'dp', axis=0, tiled=True)  53.6 us
    all_gather x1, waiting for transfers between devices, body(): lax.all_gather(down_weight, 'dp', axis=1, tiled=True)  45.3 us
  transfers between devices with their start and end apart: 21, of which 17 were waited for; matrix products, arithmetic and copies ran while one was open for 16% of the time, Pallas kernels for 0%

commit v1 on v0

v1 whole, which is shorter than its diff:
```python
import functools
import math

import jax
import jax.numpy as jnp
from jax import lax
from jax.experimental import pallas as pl
from jax.experimental.pallas import tpu as pltpu
from jax.sharding import PartitionSpec as P

HEAD_DIM = 64
ROT = 32
D = 2048
N_DP = 4
N_TP = 4
CH = D // N_TP
EPS = 1e-05
NEG = -1e30
VMEM = 56 * 2**20

bf16 = jnp.bfloat16
f32 = jnp.float32


def dot_nn(a, b):
    return lax.dot_general(a, b, (((1,), (0,)), ((), ())), preferred_element_type=f32)


def dot_nt(a, b):
    return lax.dot_general(a, b, (((1,), (1,)), ((), ())), preferred_element_type=f32)


def dot_tn(a, b):
    return lax.dot_general(a, b, (((0,), (0,)), ((), ())), preferred_element_type=f32)


def spec(block, index):
    return pl.BlockSpec(block, index)


def whole(*block):
    zeros = (0,) * len(block)
    return pl.BlockSpec(block, lambda g, *_: zeros)


def shaped(shape, dtype=bf16):
    return jax.ShapeDtypeStruct(tuple(shape), dtype)


def call(body, name, grid, info, ins, in_specs, outs, out_specs, flops, scratch=()):
    moved = sum(math.prod(a.shape) * a.dtype.itemsize for a in (*ins, *outs))
    return pl.pallas_call(
        body,
        grid_spec=pltpu.PrefetchScalarGridSpec(
            num_scalar_prefetch=1,
            grid=(grid,),
            in_specs=in_specs,
            out_specs=out_specs,
            scratch_shapes=list(scratch),
        ),
        out_shape=outs,
        compiler_params=pltpu.CompilerParams(vmem_limit_bytes=VMEM),
        cost_estimate=pl.CostEstimate(
            flops=int(flops), bytes_accessed=int(moved), transcendentals=0
        ),
        name=name,
    )(info, *ins)


def columns(index, width=CH):
    return pl.ds(pl.multiple_of(index * width, width), width)


def place(pieces, axis, shape, name):
    starts = jnp.stack([jnp.asarray(at, jnp.int32) for _, at in pieces])
    arrays = [a for a, _ in pieces]

    def body(at_ref, *refs):
        *sources, out, sems = refs
        copies = []
        for n, source in enumerate(sources):
            size = arrays[n].shape[axis]
            window = pl.ds(pl.multiple_of(at_ref[n], 256), size)
            target = out.at[window, :] if axis == 0 else out.at[:, window]
            copies.append(pltpu.make_async_copy(source, target, sems.at[n]))
        for copy in copies:
            copy.start()
        for copy in copies:
            copy.wait()

    anywhere = pl.BlockSpec(memory_space=pl.ANY)
    return pl.pallas_call(
        body,
        grid_spec=pltpu.PrefetchScalarGridSpec(
            num_scalar_prefetch=1,
            grid=(1,),
            in_specs=[anywhere] * len(arrays),
            out_specs=anywhere,
            scratch_shapes=[pltpu.SemaphoreType.DMA((len(arrays),))],
        ),
        out_shape=shaped(shape),
        compiler_params=pltpu.CompilerParams(vmem_limit_bytes=VMEM),
        cost_estimate=pl.CostEstimate(
            flops=0, bytes_accessed=4 * math.prod(shape), transcendentals=0
        ),
        name=name,
    )(starts, *arrays)


def swap(array, axis, bit, size):
    return lax.ppermute(array, axis, [(i, i ^ bit) for i in range(size)])


def gather_shards(own, axis, d, c, two, name):
    size = own.shape[axis]
    shape = list(own.shape)
    shape[axis] = size * N_DP
    if two:
        half = size // 2
        mine = lax.dynamic_slice_in_dim(own, c * half, half, axis)
        first = swap(mine, "dp", 2, N_DP)
        second = swap(first, "ctx", 1, 2)
        near = swap(own, "dp", 1, N_DP)
        far = [(first, c * half), (second, (1 - c) * half)]
        pieces = [(own, d * size), (near, (d ^ 1) * size)]
        pieces += [(a, (d ^ 2) * size + at) for a, at in far]
        pieces += [(swap(a, "dp", 1, N_DP), (d ^ 3) * size + at) for a, at in far]
    else:
        near = swap(own, "dp", 1, N_DP)
        across = swap(own, "dp", 2, N_DP)
        pieces = [
            (own, d * size),
            (near, (d ^ 1) * size),
            (across, (d ^ 2) * size),
            (swap(across, "dp", 1, N_DP), (d ^ 3) * size),
        ]
    return place(pieces, axis, shape, name)


def rotary_tables(starts, positions):
    before = starts[:, None, :] <= positions[None, :, None]
    opening = jnp.max(jnp.where(before, starts[:, None, :], 0), axis=2)
    relative = (positions[None, :] - opening).astype(f32)
    half = ROT // 2
    frequency = jnp.exp(jnp.arange(half, dtype=f32) * (-math.log(10000.0) / half))
    angles = relative[:, :, None] * frequency
    cosine, sine = jnp.cos(angles), jnp.sin(angles)
    ones = jnp.ones(cosine.shape[:2] + (HEAD_DIM - ROT,), f32)
    none = jnp.zeros_like(ones)
    gap = jnp.zeros_like(sine)

    def lanes(*parts):
        return jnp.concatenate(parts * 2, axis=2)

    return (
        lanes(cosine, cosine, ones),
        lanes(-sine, gap, none),
        lanes(gap, sine, none),
    ), opening


def turn(x, own, up, down):
    return x * own + pltpu.roll(x, 112, 1) * up + pltpu.roll(x, 16, 1) * down


def turn_back(x, own, up, down):
    return x * own - pltpu.roll(x, 112, 1) * up - pltpu.roll(x, 16, 1) * down


def norm_qkv_body(
    info, x0, xa, xc, xb, gain, shift, w, bias, own, up, down, xf, normed, avg, inv, q, kv
):
    j = pl.program_id(0)
    t = info[0]
    rows = x0.shape[0]

    @pl.when(j == 0)
    def _():
        for part, step in ((x0, 0), (xa, 3), (xc, 1), (xb, 2)):
            xf[:, columns((t + step) % N_TP)] = part[...]

        tile = 128

        def rows_of(i, carry):
            window = pl.ds(pl.multiple_of(i * tile, tile), tile)
            x = xf[window, :].astype(f32)
            average = jnp.sum(x, axis=1, keepdims=True) * (1.0 / D)
            centred = x - average
            variance = jnp.sum(centred * centred, axis=1, keepdims=True) * (1.0 / D)
            root = lax.rsqrt(variance + EPS)
            avg[window, :] = average
            inv[window, :] = root
            normed[window, :] = (
                centred * root * gain[...].astype(f32) + shift[...].astype(f32)
            ).astype(bf16)
            return carry

        lax.fori_loop(0, rows // tile, rows_of, 0)

    y = dot_nn(normed[...], w[...]) + bias[...].astype(f32)

    def rotated():
        parts = [
            turn(y[:, 128 * n : 128 * n + 128], own[...], up[...], down[...])
            for n in range(CH // 128)
        ]
        return jnp.concatenate(parts, axis=1).astype(bf16)

    @pl.when(j == 0)
    def _():
        q[...] = rotated()

    @pl.when(j == 1)
    def _():
        kv[0] = rotated()

    @pl.when(j == 2)
    def _():
        kv[0] = y.astype(bf16)


def norm_qkv(info, parts, gain, shift, w, bias, tables):
    rows = parts[0].shape[0]
    outs = (
        shaped((rows, D)),
        shaped((rows, D)),
        shaped((rows, 1), f32),
        shaped((rows, 1), f32),
        shaped((rows, CH)),
        shaped((2, rows, CH)),
    )
    return call(
        norm_qkv_body,
        "norm_qkv",
        3,
        info,
        (*parts, gain, shift, w, bias, *tables),
        [whole(rows, CH)] * 4
        + [whole(1, D)] * 2
        + [spec((D, CH), lambda j, *_: (0, j)), spec((1, CH), lambda j, *_: (0, j))]
        + [whole(rows, 128)] * 3,
        outs,
        [
            whole(rows, D),
            whole(rows, D),
            whole(rows, 1),
            whole(rows, 1),
            whole(rows, CH),
            spec((1, rows, CH), lambda j, *_: (jnp.maximum(j - 1, 0), 0, 0)),
        ],
        2 * rows * D * 3 * CH,
    )


def mlp_up_body(info, n0, n1, w, bias, h0, h1, g0, g1):
    root = math.sqrt(2.0 / math.pi)
    for n, h, g in ((n0, h0, g0), (n1, h1, g1)):
        u = dot_nn(n[...], w[...]) + bias[...].astype(f32)
        square = u * u
        t = jnp.tanh(root * u * (1.0 + 0.044715 * square))
        h[...] = (0.5 * u * (1.0 + t)).astype(bf16)
        slope = root * (1.0 + 3 * 0.044715 * square)
        g[...] = (0.5 * (1.0 + t) + 0.5 * u * (1.0 - t * t) * slope).astype(bf16)


def mlp_up(info, normed, w, bias):
    rows, units = normed[0].shape[0], w.shape[1]
    block = spec((rows, CH), lambda j, *_: (0, j))
    return call(
        mlp_up_body,
        "mlp_up",
        units // CH,
        info,
        (*normed, w, bias),
        [whole(rows, D)] * 2
        + [spec((D, CH), lambda j, *_: (0, j)), spec((1, CH), lambda j, *_: (0, j))],
        (shaped((rows, units)),) * 4,
        [block] * 4,
        4 * rows * D * units,
    )


def back_out_body(info, c0, ca, cc, cb, w, slope, cf, bias_grad, datt, dup):
    j = pl.program_id(0)
    t = info[0]

    @pl.when(j == 0)
    def _():
        for part, step in ((c0, 0), (ca, 3), (cc, 1), (cb, 2)):
            cf[:, columns((t + step) % N_TP)] = part[...]
        bias_grad[...] = jnp.sum(c0[...].astype(f32), axis=0, keepdims=True)

    y = dot_nt(cf[...], w[...])

    @pl.when(j == 0)
    def _():
        datt[...] = y.astype(bf16)

    @pl.when(j > 0)
    def _():
        dup[...] = (y * slope[...].astype(f32)).astype(bf16)


def back_out(info, parts, w, slope):
    rows, units = slope.shape
    later = spec((rows, CH), lambda j, *_: (0, jnp.maximum(j - 1, 0)))
    return call(
        back_out_body,
        "back_out",
        w.shape[0] // CH,
        info,
        (*parts, w, slope),
        [whole(rows, CH)] * 4 + [spec((CH, D), lambda j, *_: (j, 0)), later],
        (
            shaped((rows, D)),
            shaped((1, CH), f32),
            shaped((rows, CH)),
            shaped((rows, units)),
        ),
        [whole(rows, D), whole(1, CH), whole(rows, CH), later],
        2 * rows * D * w.shape[0],
    )


def attention_body(
    blocks, info, low, q, kv, kvp, do, own, up, down, ownp, upp, downp,
    att, dq, dkv, dkvp, scores, probs,
):
    rows = q.shape[0]
    before, start = info[1], info[1] * rows
    lane = lax.broadcasted_iota(jnp.int32, (rows, 128), 1)
    key_row = lax.broadcasted_iota(jnp.int32, (rows, 1), 0)
    query_at = start + lax.broadcasted_iota(jnp.int32, (1, rows), 1)
    first = low[0]
    do_t = do[...].astype(f32).T
    nothing = jnp.zeros((), bf16)
    outputs = []
    for head in range(2):
        mine = (lane < HEAD_DIM) if head == 0 else (lane >= HEAD_DIM)
        half = slice(HEAD_DIM * head, HEAD_DIM * (head + 1))
        qh = jnp.where(mine, q[...] * jnp.asarray(HEAD_DIM**-0.5, bf16), nothing)
        dh = jnp.where(mine, do[...], nothing)

        key_at = start + key_row
        s = dot_nt(kv[0], qh)
        s = jnp.where((key_at >= first) & (key_at <= query_at), s, NEG)
        scores[blocks] = s
        peak = jnp.max(s, axis=0, keepdims=True)

        def score(n, peak):
            s = dot_nt(kvp[n, 0], qh)
            s = jnp.where(n * rows + key_row >= first, s, NEG)
            scores[n] = s
            return jnp.maximum(peak, jnp.max(s, axis=0, keepdims=True))

        peak = lax.fori_loop(0, before, score, peak)

        def expo(n, total):
            e = jnp.exp(scores[n] - peak)
            scores[n] = e
            return total + jnp.sum(e, axis=0, keepdims=True)

        total = expo(blocks, jnp.zeros((1, rows), f32))
        total = lax.fori_loop(0, before, expo, total)
        scale = 1.0 / total

        def weigh(n, values):
            p = (scores[n] * scale).astype(bf16)
            probs[n] = p
            return dot_tn(values, p)

        out_t = weigh(blocks, kv[1])
        out_t = lax.fori_loop(0, before, lambda n, acc: acc + weigh(n, kvp[n, 1]), out_t)
        delta = jnp.sum(out_t[half] * do_t[half], axis=0, keepdims=True)

        def back(n, keys, values):
            dp = dot_nt(values, dh)
            ds = ((scores[n] * scale) * (dp - delta)).astype(bf16)
            return dot_nn(ds, qh), dot_nn(probs[n], dh), dot_tn(keys, ds)

        dk, dv, dq_t = back(blocks, kv[0], kv[1])
        if head == 0:
            dk_sum, dv_sum = dk, dv
        else:
            dk_sum, dv_sum = dk_sum + dk, dv_sum + dv

        def back_before(n, acc):
            dk, dv, more = back(n, kvp[n, 0], kvp[n, 1])
            dk = turn_back(dk, ownp[n], upp[n], downp[n])
            if head == 0:
                dkvp[n, 0] = dk.astype(bf16)
                dkvp[n, 1] = dv.astype(bf16)
            else:
                dkvp[n, 0] = (dkvp[n, 0].astype(f32) + dk).astype(bf16)
                dkvp[n, 1] = (dkvp[n, 1].astype(f32) + dv).astype(bf16)
            return acc + more

        dq_t = lax.fori_loop(0, before, back_before, dq_t)
        outputs.append((out_t[half], dq_t[half]))

    def clear(n, carry):
        dkvp[n] = jnp.zeros(dkvp.shape[1:], bf16)
        return carry

    lax.fori_loop(before, blocks, clear, 0)
    att[...] = jnp.concatenate([outputs[0][0], outputs[1][0]], axis=0).T.astype(bf16)
    grad = jnp.concatenate([outputs[0][1], outputs[1][1]], axis=0).T * HEAD_DIM**-0.5
    dq[...] = turn_back(grad, own[...], up[...], down[...]).astype(bf16)
    dkv[0] = turn_back(dk_sum, own[...], up[...], down[...]).astype(bf16)
    dkv[1] = dv_sum.astype(bf16)


def attention(info, low, q, kv, kvp, do, tables, tables_before):
    rows, width = q.shape
    blocks = kvp.shape[0]
    token = spec((rows, 128), lambda g, *_: (0, g))
    pair = spec((2, rows, 128), lambda g, *_: (0, 0, g))
    pairs = spec((blocks, 2, rows, 128), lambda g, *_: (0, 0, 0, g))
    return call(
        functools.partial(attention_body, blocks),
        "attention",
        width // 128,
        info,
        (low, q, kv, kvp, do, *tables, *tables_before),
        [whole(1, rows), token, pair, pairs, token]
        + [whole(rows, 128)] * 3
        + [whole(blocks, rows, 128)] * 3,
        (
            shaped((rows, width)),
            shaped((rows, width)),
            shaped((2, rows, width)),
            shaped((blocks, 2, rows, width)),
        ),
        [token, token, pair, pairs],
        48 * rows * rows * width,
        [
            pltpu.VMEM((blocks + 1, rows, rows), f32),
            pltpu.VMEM((blocks + 1, rows, rows), bf16),
        ],
    )


ORDER = (2, 3, 1, 0)


def relative(step):
    return jnp.where(step < 2, step + 2, 3 - step)


def out_body(info, att, hidden, w, *outs):
    j = pl.program_id(0)
    y = dot_nn(att[...], w[:CH, :]) + dot_nn(hidden[...], w[CH:, :])
    y = y.astype(bf16)
    for step, r in enumerate(ORDER):

        @pl.when(j == step)
        def _(r=r):
            outs[r][...] = y


def project_out(info, att, hidden, w):
    rows, units = hidden.shape
    return call(
        out_body,
        "project_out",
        N_TP,
        info,
        (att, hidden, w),
        [
            whole(rows, CH),
            whole(rows, units),
            spec((CH + units, CH), lambda j, info: (0, (info[0] + relative(j)) % N_TP)),
        ],
        (shaped((rows, CH)),) * N_TP,
        [whole(rows, CH)] * N_TP,
        2 * rows * D * (CH + units),
    )


def back_in_body(info, dq, dkv, dup, wq, wu, xf, gain, avg, inv, *outs):
    j = pl.program_id(0)
    *chunks, row_sums, column_sums = outs
    y = dot_nt(dup[...], wu[...])
    y = y + dot_nt(dq[...], wq[:, :CH])
    y = y + dot_nt(dkv[0], wq[:, CH : 2 * CH])
    y = y + dot_nt(dkv[1], wq[:, 2 * CH :])
    yb = y.astype(bf16)
    for step, r in enumerate(ORDER):

        @pl.when(j == step)
        def _(r=r):
            chunks[r][...] = yb

    standard = (xf[...].astype(f32) - avg[...]) * inv[...]
    cross = y * standard
    weight = gain[...].astype(f32)
    column_sums[0, 0:1, :] = jnp.sum(cross, axis=0, keepdims=True)
    column_sums[0, 1:2, :] = jnp.sum(y, axis=0, keepdims=True)
    plain_row = jnp.sum(y * weight, axis=1, keepdims=True)
    cross_row = jnp.sum(cross * weight, axis=1, keepdims=True)

    @pl.when(j == 0)
    def _():
        row_sums[:, 0:1] = plain_row
        row_sums[:, 1:2] = cross_row

    @pl.when(j > 0)
    def _():
        row_sums[:, 0:1] += plain_row
        row_sums[:, 1:2] += cross_row


def back_in(info, dq, dkv, dup, wq, wu, xf, gain, avg, inv):
    rows, units = dup.shape

    def chunk(j, info):
        return (info[0] + relative(j)) % N_TP

    return call(
        back_in_body,
        "back_in",
        N_TP,
        info,
        (dq, dkv, dup, wq, wu, xf, gain, avg, inv),
        [
            whole(rows, CH),
            whole(2, rows, CH),
            whole(rows, units),
            spec((CH, 3 * CH), lambda j, info: (chunk(j, info), 0)),
            spec((CH, units), lambda j, info: (chunk(j, info), 0)),
            spec((rows, CH), lambda j, info: (0, chunk(j, info))),
            spec((1, CH), lambda j, info: (0, chunk(j, info))),
            whole(rows, 1),
            whole(rows, 1),
        ],
        (shaped((rows, CH)),) * N_TP + (shaped((rows, 2), f32), shaped((N_TP, 2, CH), f32)),
        [whole(rows, CH)] * N_TP
        + [
            whole(rows, 2),
            spec((1, 2, CH), lambda j, info: (chunk(j, info), 0, 0)),
        ],
        2 * rows * D * (3 * CH + units),
    )


KEPT = ((0, 0), (2, 1))
GIVEN = ((1, 0), (3, 1))


def grad_up_body(info, n0, n1, g0, g1, kept, given, sums):
    d = info[2]
    left, right = g0[...], g1[...]
    for target, which in ((given, GIVEN), (kept, KEPT)):
        for r, at in which:
            rows = columns(d ^ r)
            target[at, 0] = (dot_tn(n0[:, rows], left) + dot_tn(n1[:, rows], right)).astype(bf16)
    sums[...] = jnp.sum(left.astype(f32), axis=0, keepdims=True) + jnp.sum(
        right.astype(f32), axis=0, keepdims=True
    )


def grad_up(info, normed, dup):
    rows, units = dup[0].shape
    count = units // CH
    block = spec((rows, CH), lambda j, *_: (0, j))
    message = spec((2, 1, CH, CH), lambda j, *_: (0, j, 0, 0))
    return call(
        grad_up_body,
        "grad_up",
        count,
        info,
        (*normed, *dup),
        [whole(rows, D)] * 2 + [block] * 2,
        (shaped((2, count, CH, CH)),) * 2 + (shaped((1, units), f32),),
        [message, message, spec((1, CH), lambda j, *_: (0, j))],
        4 * rows * D * units,
    )


def grad_down_body(info, h0, h1, c0, c1, kept, given):
    j = pl.program_id(0)
    y = (dot_tn(h0[...], c0[...]) + dot_tn(h1[...], c1[...])).astype(bf16)

    def store(target):
        for n in range(target.shape[1]):
            target[0, n] = y[CH * n : CH * (n + 1), :]

    @pl.when(j < 2)
    def _():
        store(given)

    @pl.when(j >= 2)
    def _():
        store(kept)


def grad_down(info, hidden, ct):
    rows, units = hidden[0].shape
    count = units // CH
    block = spec(
        (rows, CH),
        lambda j, info: (0, info[2] ^ jnp.where(j < 2, 2 * j + 1, 2 * j - 4)),
    )
    return call(
        grad_down_body,
        "grad_down",
        N_DP,
        info,
        (*hidden, *ct),
        [whole(rows, units)] * 2 + [block] * 2,
        (shaped((2, count, CH, CH)),) * 2,
        [
            spec((1, count, CH, CH), lambda j, *_: (jnp.maximum(j - 2, 0), 0, 0, 0)),
            spec((1, count, CH, CH), lambda j, *_: (jnp.minimum(j, 1), 0, 0, 0)),
        ],
        4 * rows * D * units,
    )


def grad_heads_body(
    info, n0, n1, c0, c1, a0, a1, q0, q1, kv0, kv1, kept, given, sums
):
    j = pl.program_id(0)
    d = info[2]

    def store(lefts, rights, of_rows):
        for target, which in ((given, GIVEN), (kept, KEPT)):
            for r, at in which:
                window = columns(d ^ r)
                if of_rows:
                    y = sum(dot_tn(a[:, window], b) for a, b in zip(lefts, rights))
                else:
                    y = sum(dot_tn(b, a[:, window]) for a, b in zip(lefts, rights))
                target[at, 0] = y.astype(bf16)

    def add_up(rights):
        sums[0] = sum(jnp.sum(b.astype(f32), axis=0, keepdims=True) for b in rights)

    @pl.when(j == 0)
    def _():
        rights = (a0[...], a1[...])
        store((c0, c1), rights, False)
        add_up(rights)

    @pl.when(j == 1)
    def _():
        rights = (q0[...], q1[...])
        store((n0, n1), rights, True)
        add_up(rights)

    @pl.when(j > 1)
    def _():
        rights = (kv0[0], kv1[0])
        store((n0, n1), rights, True)
        add_up(rights)


def grad_heads(info, normed, ct, att, dq, dkv):
    rows = normed[0].shape[0]
    message = spec((2, 1, CH, CH), lambda j, *_: (0, j, 0, 0))
    pair = spec((1, rows, CH), lambda j, *_: (jnp.maximum(j - 2, 0), 0, 0))
    return call(
        grad_heads_body,
        "grad_heads",
        4,
        info,
        (*normed, *ct, *att, *dq, *dkv),
        [whole(rows, D)] * 4 + [whole(rows, CH)] * 4 + [pair] * 2,
        (shaped((2, 4, CH, CH)),) * 2 + (shaped((4, 1, CH), f32),),
        [message, message, spec((1, 1, CH), lambda j, *_: (j, 0, 0))],
        4 * rows * D * 4 * CH,
    )


def ring(array, step):
    return lax.ppermute(array, "tp", [(i, (i + step) % N_TP) for i in range(N_TP)])


def gather_tp(own):
    behind = ring(own, 1)
    ahead = ring(own, -1)
    return own, behind, ahead, ring(behind, 1)


def scatter_tp(chunks):
    far = ring(chunks[2], 1)
    back = ring(chunks[3], -1)
    both = (chunks[1].astype(f32) + far.astype(f32)).astype(bf16)
    near = ring(both, 1)
    return chunks[0].astype(f32) + back.astype(f32) + near.astype(f32)


def reduce_grads(kept, given, c, two):
    got = swap(given, "dp", 1, N_DP)
    across = (kept[1].astype(f32) + got[1].astype(f32)).astype(bf16)
    moved = swap(across, "dp", 2, N_DP)
    total = (kept[0].astype(f32) + got[0].astype(f32) + moved.astype(f32)).astype(bf16)
    if not two:
        return lax.psum(total, "ctx").astype(f32)
    half = total.shape[0] // 2
    mine = lax.dynamic_slice_in_dim(total, c * half, half, 0)
    theirs = lax.dynamic_slice_in_dim(total, (1 - c) * half, half, 0)
    received = swap(theirs, "ctx", 1, 2)
    mine = (mine.astype(f32) + received.astype(f32)).astype(bf16)
    other = swap(mine, "ctx", 1, 2)
    low = jnp.where(c == 0, mine, other)
    high = jnp.where(c == 0, other, mine)
    return jnp.concatenate([low, high], axis=0).astype(f32)


def body(
    block_in,
    doc_starts,
    query_weight,
    key_weight,
    value_weight,
    output_weight,
    up_weight,
    down_weight,
    query_bias,
    key_bias,
    value_bias,
    up_bias,
    output_bias,
    norm_gain,
    norm_shift,
    cotangent,
):
    seqs, rows, _ = block_in.shape
    d, c, t = lax.axis_index("dp"), lax.axis_index("ctx"), lax.axis_index("tp")
    n_ctx = lax.axis_size("ctx")
    two = n_ctx == 2
    info = jnp.stack([t, c, d]).astype(jnp.int32)

    x_parts = [gather_tp(block_in[s]) for s in range(seqs)]

    small = jnp.concatenate(
        [query_bias, key_bias, value_bias, up_bias, output_bias, norm_gain, norm_shift]
    )
    small_all = lax.all_gather(small, ("tp", "dp"), axis=0, tiled=False)
    small_all = small_all.reshape(N_TP, N_DP, -1)
    small_here = lax.dynamic_index_in_dim(small_all, t, 0, keepdims=False)
    sizes = [query_bias.size] * 3 + [up_bias.size] + [output_bias.size] * 3
    offsets = [sum(sizes[:n]) for n in range(len(sizes) + 1)]

    def small_of(table, n):
        return table[..., offsets[n] : offsets[n + 1]].reshape(1, -1)

    qkv_bias = jnp.concatenate([small_of(small_here, n) for n in range(3)], axis=1)
    up_shift = small_of(small_here, 3)
    output_shift = small_of(small_here, 4)
    gain, shift = small_of(small_all, 5), small_of(small_all, 6)
    gain_here = small_of(small_here, 5).astype(f32)

    wq = gather_shards(
        jnp.concatenate([query_weight, key_weight, value_weight], axis=1), 0, d, c, two, "place_qkv"
    )
    wu = gather_shards(up_weight, 0, d, c, two, "place_up")
    wo = gather_shards(
        jnp.concatenate([output_weight, down_weight], axis=0), 1, d, c, two, "place_out"
    )

    ct_parts = [gather_tp(cotangent[s]) for s in range(seqs)]

    here = c * rows + jnp.arange(rows, dtype=jnp.int32)
    tables, opening = rotary_tables(doc_starts, here)
    blocks = 1 if two else n_ctx
    before, _ = rotary_tables(doc_starts, jnp.arange(blocks * rows, dtype=jnp.int32))
    before = [a.reshape(seqs, blocks, rows, 128) for a in before]

    xf, normed, avg, inv, q, kv, kvp = [], [], [], [], [], [], []
    for s in range(seqs):
        one = norm_qkv(info, x_parts[s], gain, shift, wq, qkv_bias, [a[s] for a in tables])
        for target, value in zip((xf, normed, avg, inv, q, kv), one):
            target.append(value)
        if two:
            kvp.append(lax.ppermute(kv[s], "ctx", [(0, 1)])[None])
        else:
            kvp.append(lax.all_gather(kv[s], "ctx", axis=0, tiled=False))
    h0, h1, g0, g1 = mlp_up(info, normed, wu, up_shift)
    hidden, slope = (h0, h1), (g0, g1)

    cf, out_bias_sum, datt, dup = [], [], [], []
    att, dq, dkv = [], [], []
    out_sum = []
    for s in range(seqs):
        one = back_out(info, ct_parts[s], wo, slope[s])
        for target, value in zip((cf, out_bias_sum, datt, dup), one):
            target.append(value)
    up_kept, up_given, up_sum = grad_up(info, normed, dup)
    down_kept, down_given = grad_down(info, hidden, cf)
    for s in range(seqs):
        a, b, own, sent = attention(
            info,
            opening[s][None],
            q[s],
            kv[s],
            kvp[s],
            datt[s],
            [x[s] for x in tables],
            [x[s] for x in before],
        )
        att.append(a)
        dq.append(b)
        if two:
            back = lax.ppermute(sent[0], "ctx", [(1, 0)])
        else:
            back = lax.psum_scatter(sent, "ctx", scatter_dimension=0, tiled=False)
        dkv.append((own.astype(f32) + back.astype(f32)).astype(bf16))
        out_sum.append(scatter_tp(project_out(info, att[s], hidden[s], wo)))
    block_out = jnp.stack(out_sum)
    block_out = (block_in.astype(f32) + block_out + output_shift.astype(f32)).astype(bf16)

    normed_grad, row_sums, column_sums = [], [], []
    for s in range(seqs):
        *chunks, row_sum, column_sum = back_in(
            info, dq[s], dkv[s], dup[s], wq, wu, xf[s], gain, avg[s], inv[s]
        )
        normed_grad.append(scatter_tp(chunks))
        row_sums.append(row_sum)
        column_sums.append(column_sum)
    head_kept, head_given, head_sum = grad_heads(info, normed, cf, att, dq, dkv)

    up_wg = reduce_grads(up_kept, up_given, c, two)
    down_wg = reduce_grads(down_kept, down_given, c, two)
    head_wg = reduce_grads(head_kept, head_given, c, two)
    up_wg = up_wg.transpose(1, 0, 2).reshape(CH, -1)
    down_wg = down_wg.reshape(-1, CH)

    row_sums = lax.psum(jnp.stack(row_sums), "tp")
    total_plain, total_cross = row_sums[..., 0:1], row_sums[..., 1:2]
    root = jnp.stack(inv)
    standard = (block_in.astype(f32) - jnp.stack(avg)) * root
    scaled = jnp.stack(normed_grad) * gain_here
    in_grad = cotangent.astype(f32) + root * (
        scaled - total_plain / D - standard * total_cross / D
    )

    local = jnp.concatenate(
        [head_sum[1:].reshape(-1), up_sum.reshape(-1), sum(out_bias_sum).reshape(-1)]
    )
    both = sum(column_sums)
    both = lax.psum_scatter(both, "tp", scatter_dimension=0, tiled=False).reshape(-1)
    summed = lax.psum(jnp.concatenate([local, both]), ("dp", "ctx"))
    at = 0
    small_grads = []
    for size in (CH, CH, CH, up_sum.size, CH, CH, CH):
        part = summed[at : at + size]
        at += size
        share = size // N_DP
        small_grads.append(lax.dynamic_slice_in_dim(part, d * share, share, 0))
    query_bg, key_bg, value_bg, up_bg, output_bg, gain_g, shift_g = small_grads
    return (
        block_out,
        in_grad,
        head_wg[1],
        head_wg[2],
        head_wg[3],
        head_wg[0],
        up_wg,
        down_wg,
        query_bg,
        key_bg,
        value_bg,
        up_bg,
        output_bg,
        gain_g,
        shift_g,
    )


def solution(mesh):
    return jax.shard_map(
        body,
        mesh=mesh,
        in_specs=(
            P("dp", "ctx", "tp"),
            P("dp", None),
            P("dp", "tp"),
            P("dp", "tp"),
            P("dp", "tp"),
            P("tp", "dp"),
            P("dp", "tp"),
            P("tp", "dp"),
        )
        + (P(("tp", "dp")),) * 7
        + (P("dp", "ctx", "tp"),),
        out_specs=(
            P("dp", "ctx", "tp"),
            P("dp", "ctx", "tp"),
            P("dp", "tp"),
            P("dp", "tp"),
            P("dp", "tp"),
            P("tp", "dp"),
            P("dp", "tp"),
            P("tp", "dp"),
        )
        + (P(("tp", "dp")),) * 7,
        check_vma=False,
    )
```

time: 1320 us -> 1560 us (1.18)
  Pallas kernels: 0 us -> 975 us
  waiting for transfers between devices: 835 us -> 196 us
  matrix products: 267 us -> 0 us
  blocking collectives: 85.8 us -> 209 us
  starting transfers between devices: 2.19 us -> 65.5 us
    pallas_call x0 -> x17, Pallas kernels: none -> 975 us  [the longest x3 768 us: place(): pl.pallas_call(body, grid_spec=pltpu.PrefetchScalarGridSpec(num_scalar_pr...]
    all_gather x10 -> x0, waiting for transfers between devices: 353 us -> none  [the longest x1 82.2 us: body(): grad_rows = lax.all_gather(cotangent, 'tp', axis=2, tiled=True)]
    reduce_scatter x10 -> x0, waiting for transfers between devices: 324 us -> none  [the longest x1 74.3 us: body(): lax.psum_scatter(down_weight_grad.astype(jnp.bfloat16), 'dp', scatter_dim...]
    dot_general x32 -> x0, matrix products: 267 us -> none  [the longest x4 31.1 us: project(): jnp.einsum('std,de->ste', normed, weight, preferred_element_type=jnp.floa...]
    ppermute x0 -> x55, waiting for transfers between devices: none -> 196 us  [the longest x27 163 us: swap(): return lax.ppermute(array, axis, [(i, i ^ bit) for i in range(size)])]
    psum x1 -> x0, waiting for transfers between devices: 155 us -> none  [body(): lax.psum(query_wg.astype(jnp.bfloat16), 'ctx').astype(jnp.float32)]
    psum x4 -> x2, blocking collectives: 37.4 us -> 162 us  [the longest x1 147 us: body(): summed = lax.psum(jnp.concatenate([local, both]), ('dp', 'ctx'))]
    ppermute x0 -> x55, starting transfers between devices: none -> 65.5 us  [the longest x24 32.4 us: ring(): lax.ppermute(array, 'tp', [(i, (i + step) % N_TP) for i in range(N_TP)])]
  transfers between devices with their start and end apart: 21 -> 55, of which waited for: 17 -> 13; matrix products, arithmetic and copies ran while one was open for 16% -> 6% of each run, Pallas kernels for 0% -> 63%
where the time goes in v1:
time: 1560 us; the launch traced here: 1550 us
  Pallas kernels  975 us (62%)
  blocking collectives  209 us (13%)
  waiting for transfers between devices  196 us (13%)
  starting transfers between devices  65.5 us (4%)
  other arithmetic  55 us (4%)
  local copies, waits for them, and re-layouts  52.6 us (3%)
    pallas_call x3, Pallas kernels, place(): pl.pallas_call(body, grid_spec=pltpu.PrefetchScalarGridSpec(num_scalar_pr...  768 us
    pallas_call x14, Pallas kernels, call(): pl.pallas_call(body, grid_spec=pltpu.PrefetchScalarGridSpec(num_scalar_pr...  207 us
    ppermute x27, waiting for transfers between devices, swap(): return lax.ppermute(array, axis, [(i, i ^ bit) for i in range(size)])  163 us
    psum x1, blocking collectives, body(): summed = lax.psum(jnp.concatenate([local, both]), ('dp', 'ctx'))  147 us
    all_gather x1, blocking collectives, body(): small_all = lax.all_gather(small, ('tp', 'dp'), axis=0, tiled=False)  46.1 us
    ppermute x24, waiting for transfers between devices, ring(): lax.ppermute(array, 'tp', [(i, (i + step) % N_TP) for i in range(N_TP)])  33.1 us
    ppermute x24, starting transfers between devices, ring(): lax.ppermute(array, 'tp', [(i, (i + step) % N_TP) for i in range(N_TP)])  32.4 us
  transfers between devices with their start and end apart: 55, of which 13 were waited for; matrix products, arithmetic and copies ran while one was open for 6% of the time, Pallas kernels for 63%

profile of v1, /device:TPU:0, one launch (start us, length us, event | category | flops | bytes accessed | tf_op | source)
XLA Modules:
  0.0 1554.6 jit_solution(15026110623869253679)
XLA Ops:
  19.7 46.1 %all-gather.1 = bf16[16,1,1280]{2,1,0:T(2,128)(2,1)S(1)} all-gather(bf16[1,1,1280]{2,1,0:T(2,128)(2,1)S(1)} %reshape.187), channel_id=2, replica_groups=mesh['dp'=4,'ctx'=2,'tp'=4] {'tp','dp'}, dimensions={0}, use_global_device_ids=true | all-gather | bytes 43520 | tf_op jit(solution)/shard_map/all_gather | solution.py:740
  101.8 35.1 %collective-permute-done.21.refs_2_ = bf16[256,2048]{1,0:T(8,128)(2,1)} collective-permute-done((bf16[256,2048]{1,0:T(8,128)(2,1)}, bf16[256,2048]{1,0:T(8,128)(2,1)}, u32[]{:S(2)}, u32[]{:S(2)}) %collective-permute-start.21) | collective-permute-done | bytes 1048608 | tf_op jit(solution)/shard_map/ppermute | solution.py:111
  145.1 18.0 %collective-permute-done.22.refs_3_ = bf16[256,2048]{1,0:T(8,128)(2,1)} collective-permute-done((bf16[256,2048]{1,0:T(8,128)(2,1)}, bf16[256,2048]{1,0:T(8,128)(2,1)}, u32[]{:S(2)}, u32[]{:S(2)}) %collective-permute-start.22) | collective-permute-done | bytes 1048608 | tf_op jit(solution)/shard_map/ppermute | solution.py:111
  173.4 192.4 %place_qkv.1.w.wq = bf16[2048,1536]{1,0:T(8,128)(2,1)} custom-call(s32[6]{0:T(128)} %stack.102.at_ref, bf16[512,1536]{1,0:T(8,128)(2,1)} %copy-done.1, bf16[512,1536]{1,0:T(8,128)(2,1)} %collective-permute-done.3.refs_1_, bf16[256,1536]{1,0:T(8,128)(2,1)} %collective-permute-done.4.refs_2_, bf16[256,1536]{1,0:T(8,128)(2,1)} %collective-permute-done.5.refs_3_, ...), custom_call_target="tpu_custom_call" | custom-call | bytes 12582912 | tf_op jit(solution)/shard_map/place_qkv/pallas_call | solution.py:92
  366.8 12.8 norm_qkv.3
  379.6 12.8 norm_qkv.2
  392.4 256.1 %place_up.1.w.wu = bf16[2048,2048]{1,0:T(8,128)(2,1)} custom-call(s32[6]{0:T(128)} %stack.102.at_ref, bf16[512,2048]{1,0:T(8,128)(2,1)} %refs_0_.1, bf16[512,2048]{1,0:T(8,128)(2,1)} %collective-permute-done.20.refs_1_, bf16[256,2048]{1,0:T(8,128)(2,1)} %collective-permute-done.21.refs_2_, bf16[256,2048]{1,0:T(8,128)(2,1)} %collective-permute-done.22.refs_3_, ...), custom_call_target="tpu_custom_call" | custom-call | bytes 16777216 | tf_op jit(solution)/shard_map/place_up/pallas_call | solution.py:92
  656.7 18.8 %mlp_up.1 = (bf16[512,2048]{1,0:T(8,128)(2,1)}, bf16[512,2048]{1,0:T(8,128)(2,1)}, bf16[512,2048]{1,0:T(8,128)(2,1)}, bf16[512,2048]{1,0:T(8,128)(2,1)}) custom-call(s32[3]{0:T(128)} %pad_add_fusion.info, bf16[512,2048]{1,0:T(8,128)(2,1)} %get-tuple-element.77.n0, bf16[512,2048]{1,0:T(8,128)(2,1)} %get-tuple-element.78.n1, bf16[2048,2048]{1,0:T(8,128)(2,1)} %place_up.1.w.wu, ...), custom_call_target="tpu_custom_call" | custom-call | flops 8589934592 | bytes 20975616 | tf_op jit(solution)/shard_map/mlp_up/pallas_call | solution.py:52
  680.5 319.5 %place_out.1.w = bf16[2560,2048]{1,0:T(8,128)(2,1)} custom-call(s32[6]{0:T(128)} %stack.102.at_ref, bf16[2560,512]{1,0:T(8,128)(2,1)} %copy-done, bf16[2560,512]{1,0:T(8,128)(2,1)} %collective-permute-done.12.refs_1_, bf16[2560,256]{1,0:T(8,128)(2,1)} %collective-permute-done.13.refs_2_, bf16[2560,256]{1,0:T(8,128)(2,1)} %collective-permute-done.14.refs_3_, ...), custom_call_target="tpu_custom_call" | custom-call | bytes 20971520 | tf_op jit(solution)/shard_map/place_out/pallas_call | solution.py:92
  1015.1 17.1 %attention.3 = (bf16[512,512]{1,0:T(8,128)(2,1)}, bf16[512,512]{1,0:T(8,128)(2,1)}, bf16[2,512,512]{2,1,0:T(8,128)(2,1)}, bf16[1,2,512,512]{3,2,1,0:T(8,128)(2,1)}) custom-call(s32[3]{0:T(128)} %pad_add_fusion.info, s32[1,512]{1,0:T(1,128)} %get-tuple-element.249.low, bf16[512,512]{1,0:T(8,128)(2,1)} %get-tuple-element.87.q, ...), custom_call_target="tpu_custom_call" | custom-call | flops 6442450944 | bytes 7866368 | tf_op jit(solution)/shard_map/attention/pallas_call | solution.py:52
  1047.6 17.1 %attention.2 = (bf16[512,512]{1,0:T(8,128)(2,1)}, bf16[512,512]{1,0:T(8,128)(2,1)}, bf16[2,512,512]{2,1,0:T(8,128)(2,1)}, bf16[1,2,512,512]{3,2,1,0:T(8,128)(2,1)}) custom-call(s32[3]{0:T(128)} %pad_add_fusion.info, s32[1,512]{1,0:T(1,128)} %get-tuple-element.248.low, bf16[512,512]{1,0:T(8,128)(2,1)} %get-tuple-element.75.q, ...), custom_call_target="tpu_custom_call" | custom-call | flops 6442450944 | bytes 7866368 | tf_op jit(solution)/shard_map/attention/pallas_call | solution.py:52
  1092.0 14.3 grad_up.1
  1106.3 15.9 %grad_down.1 = (bf16[2,4,512,512]{3,2,1,0:T(8,128)(2,1)}, bf16[2,4,512,512]{3,2,1,0:T(8,128)(2,1)}) custom-call(s32[3]{0:T(128)} %pad_add_fusion.info, bf16[512,2048]{1,0:T(8,128)(2,1)} %get-tuple-element.82.hidden.h0, bf16[512,2048]{1,0:T(8,128)(2,1)} %get-tuple-element.92.hidden.h1, bf16[512,2048]{1,0:T(8,128)(2,1)} %get-tuple-element.121.c0, ...), custom_call_target="tpu_custom_call" | custom-call | flops 8589934592 | bytes 16777216 | tf_op jit(solution)/shard_map/grad_down/pallas_call | solution.py:52
  1126.0 16.2 %grad_heads.1 = (bf16[2,4,512,512]{3,2,1,0:T(8,128)(2,1)}, bf16[2,4,512,512]{3,2,1,0:T(8,128)(2,1)}, f32[4,1,512]{2,1,0:T(1,128)}) custom-call(s32[3]{0:T(128)} %pad_add_fusion.info, bf16[512,2048]{1,0:T(8,128)(2,1)} %get-tuple-element.77.n0, bf16[512,2048]{1,0:T(8,128)(2,1)} %get-tuple-element.78.n1, bf16[512,2048]{1,0:T(8,128)(2,1)} %get-tuple-element.121.c0, ...), custom_call_target="tpu_custom_call" | custom-call | flops 8589934592 | bytes 20979712 | tf_op jit(solution)/shard_map/grad_heads/pallas_call | solution.py:52
  1159.7 13.2 collective-permute-done.27
  1174.5 17.1 %back_in.3 = (bf16[512,512]{1,0:T(8,128)(2,1)}, bf16[512,512]{1,0:T(8,128)(2,1)}, bf16[512,512]{1,0:T(8,128)(2,1)}, bf16[512,512]{1,0:T(8,128)(2,1)}, f32[512,2]{1,0:T(8,128)}, /*index=5*/f32[4,2,512]{2,1,0:T(2,128)}) custom-call(s32[3]{0:T(128)} %pad_add_fusion.info, bf16[512,512]{1,0:T(8,128)(2,1)} %get-tuple-element.109.dq.q1, ...), custom_call_target="tpu_custom_call" | custom-call | flops 7516192768 | bytes 22573056 | tf_op jit(solution)/shard_map/back_in/pallas_call | solution.py:52
  1196.5 17.2 %back_in.2 = (bf16[512,512]{1,0:T(8,128)(2,1)}, bf16[512,512]{1,0:T(8,128)(2,1)}, bf16[512,512]{1,0:T(8,128)(2,1)}, bf16[512,512]{1,0:T(8,128)(2,1)}, f32[512,2]{1,0:T(8,128)}, /*index=5*/f32[4,2,512]{2,1,0:T(2,128)}) custom-call(s32[3]{0:T(128)} %pad_add_fusion.info, bf16[512,512]{1,0:T(8,128)(2,1)} %get-tuple-element.99.dq.q0, ...), custom_call_target="tpu_custom_call" | custom-call | flops 7516192768 | bytes 22573056 | tf_op jit(solution)/shard_map/back_in/pallas_call | solution.py:52
  1215.5 15.9 %all-reduce.1 = (f32[2,512,2]{1,2,0:T(2,128)S(1)}, f32[4,2,512]{2,1,0:T(2,128)S(1)}) all-reduce(f32[2,512,2]{1,2,0:T(2,128)S(1)} %pad_maximum_fusion.2, f32[4,2,512]{2,1,0:T(2,128)S(1)} %add.224), channel_id=1, replica_groups=mesh['dp'=4,'ctx'=2,'tp'=4] {'tp'}, use_global_device_ids=true, to_apply=%region_2.3 | all-reduce | flops 6144 | bytes 49152 | tf_op jit(solution)/shard_map/psum | solution.py:830
  1255.0 146.6 %psum.15 = f32[5120]{0:T(1024)S(1)} all-reduce(f32[5120]{0:T(1024)S(1)} %pad_maximum_fusion.1), channel_id=1, replica_groups=mesh['dp'=4,'ctx'=2,'tp'=4] {'dp','ctx'}, use_global_device_ids=true, to_apply=%region_4.5 | all-reduce | flops 5120 | bytes 40960 | tf_op jit(solution)/shard_map/psum | solution.py:844
  1425.5 15.3 collective-permute-done.49
  1443.5 19.8 %collective-permute-done.53 = bf16[2,512,512]{2,1,0:T(8,128)(2,1)S(1)} collective-permute-done((bf16[2,512,512]{2,1,0:T(8,128)(2,1)S(1)}, bf16[2,512,512]{2,1,0:T(8,128)(2,1)S(1)}, u32[]{:S(2)}, u32[]{:S(2)}) %collective-permute-start.53) | collective-permute-done | bytes 1048608 | tf_op jit(solution)/shard_map/ppermute | solution.py:111
  1468.9 16.9 %collective-permute-done.45 = bf16[2,512,512]{2,1,0:T(8,128)(2,1)S(1)} collective-permute-done((bf16[2,512,512]{2,1,0:T(8,128)(2,1)S(1)}, bf16[2,512,512]{2,1,0:T(8,128)(2,1)S(1)}, u32[]{:S(2)}, u32[]{:S(2)}) %collective-permute-start.45) | collective-permute-done | bytes 1048608 | tf_op jit(solution)/shard_map/ppermute | solution.py:111
  1488.2 20.1 %collective-permute-done.50 = bf16[2,512,512]{2,1,0:T(8,128)(2,1)S(1)} collective-permute-done((bf16[2,512,512]{2,1,0:T(8,128)(2,1)S(1)}, bf16[2,512,512]{2,1,0:T(8,128)(2,1)S(1)}, u32[]{:S(2)}, u32[]{:S(2)}) %collective-permute-start.50) | collective-permute-done | bytes 1048608 | tf_op jit(solution)/shard_map/ppermute | solution.py:111
  1535.5 16.2 %collective-permute-done.46 = bf16[2,512,512]{2,1,0:T(8,128)(2,1)S(1)} collective-permute-done((bf16[2,512,512]{2,1,0:T(8,128)(2,1)S(1)}, bf16[2,512,512]{2,1,0:T(8,128)(2,1)S(1)}, u32[]{:S(2)}, u32[]{:S(2)}) %collective-permute-start.46) | collective-permute-done | bytes 1048608 | tf_op jit(solution)/shard_map/ppermute | solution.py:111
  (335 shorter events, 262.0 us)
Async XLA Ops:
  11.3 127.1 %collective-permute-start.3 = (bf16[512,1536]{1,0:T(8,128)(2,1)S(1)}, bf16[512,1536]{1,0:T(8,128)(2,1)}, u32[]{:S(2)}, u32[]{:S(2)}) collective-permute-start(bf16[512,1536]{1,0:T(8,128)(2,1)S(1)} %constant_dynamic-update-slice_fusion.refs_0_), channel_id=1, source_target_pairs={{0,8},{8,0},{16,24},{24,16},{1,9},{9,1},{17,25},{25,17},{2,10},{10... | collective-permute-start | bytes 4718600 | tf_op jit(solution)/shard_map/ppermute | solution.py:111
  101.8 264.0 %collective-permute-start.20 = (bf16[512,2048]{1,0:T(8,128)(2,1)}, bf16[512,2048]{1,0:T(8,128)(2,1)}, u32[]{:S(2)}, u32[]{:S(2)}) collective-permute-start(bf16[512,2048]{1,0:T(8,128)(2,1)} %refs_0_.1), channel_id=1, source_target_pairs={{0,8},{8,0},{16,24},{24,16},{1,9},{9,1},{17,25},{25,17},{2,10},{10... | collective-permute-start | bytes 6291464 | tf_op jit(solution)/shard_map/ppermute | solution.py:111
  138.4 513.9 %collective-permute-start.12 = (bf16[2560,512]{1,0:T(8,128)(2,1)}, bf16[2560,512]{1,0:T(8,128)(2,1)}, u32[]{:S(2)}, u32[]{:S(2)}) collective-permute-start(bf16[2560,512]{1,0:T(8,128)(2,1)} %copy-done), channel_id=1, source_target_pairs={{0,8},{8,0},{16,24},{24,16},{1,9},{9,1},{17,25},{25,17},{2,10},{10... | collective-permute-start | bytes 7864328 | tf_op jit(solution)/shard_map/ppermute | solution.py:111
  144.6 221.6 %collective-permute-start.14 = (bf16[2560,256]{1,0:T(8,128)(2,1)}, bf16[2560,256]{1,0:T(8,128)(2,1)}, u32[]{:S(2)}, u32[]{:S(2)}) collective-permute-start(bf16[2560,256]{1,0:T(8,128)(2,1)} %collective-permute-done.13.refs_2_), channel_id=1, source_target_pairs={{0,4},{4,0},{1,5},{5,1},{2,6},{6,2},{3,7},{7,3},{8,12},{12,8},{9,1... | collective-permute-start | bytes 3932168 | tf_op jit(solution)/shard_map/ppermute | solution.py:111
  163.1 202.7 %collective-permute-start.23 = (bf16[256,2048]{1,0:T(8,128)(2,1)}, bf16[256,2048]{1,0:T(8,128)(2,1)}, u32[]{:S(2)}, u32[]{:S(2)}) collective-permute-start(bf16[256,2048]{1,0:T(8,128)(2,1)} %collective-permute-done.21.refs_2_), channel_id=1, source_target_pairs={{0,8},{8,0},{16,24},{24,16},{1,9},{9,1},{17,25},{25,17},{2,10},{10... | collective-permute-start | bytes 3145736 | tf_op jit(solution)/shard_map/ppermute | solution.py:111
  163.2 203.1 %collective-permute-start.24 = (bf16[256,2048]{1,0:T(8,128)(2,1)}, bf16[256,2048]{1,0:T(8,128)(2,1)}, u32[]{:S(2)}, u32[]{:S(2)}) collective-permute-start(bf16[256,2048]{1,0:T(8,128)(2,1)} %collective-permute-done.22.refs_3_), channel_id=1, source_target_pairs={{0,8},{8,0},{16,24},{24,16},{1,9},{9,1},{17,25},{25,17},{2,10},{10... | collective-permute-start | bytes 3145736 | tf_op jit(solution)/shard_map/ppermute | solution.py:111
  365.8 282.6 %collective-permute-start.29 = (bf16[512,512]{1,0:T(8,128)(2,1)S(1)}, bf16[512,512]{1,0:T(8,128)(2,1)}, u32[]{:S(2)}, u32[]{:S(2)}) collective-permute-start(bf16[512,512]{1,0:T(8,128)(2,1)S(1)} %get-tuple-element.212.c0), channel_id=1, source_target_pairs={{0,1},{1,2},{2,3},{3,0},{4,5},{5,6},{6,7},{7,4},{8,9},{9,10},{10,1... | collective-permute-start | bytes 1572872 | tf_op jit(solution)/shard_map/ppermute | solution.py:676
  365.9 286.4 %collective-permute-start.9 = (bf16[512,512]{1,0:T(8,128)(2,1)S(1)}, bf16[512,512]{1,0:T(8,128)(2,1)}, u32[]{:S(2)}, u32[]{:S(2)}) collective-permute-start(bf16[512,512]{1,0:T(8,128)(2,1)S(1)} %get-tuple-element.211.c0), channel_id=1, source_target_pairs={{0,1},{1,2},{2,3},{3,0},{4,5},{5,6},{6,7},{7,4},{8,9},{9,10},{10,1... | collective-permute-start | bytes 1572872 | tf_op jit(solution)/shard_map/ppermute | solution.py:676
  366.2 309.3 %collective-permute-start.15 = (bf16[2560,256]{1,0:T(8,128)(2,1)}, bf16[2560,256]{1,0:T(8,128)(2,1)S(1)}, u32[]{:S(2)}, u32[]{:S(2)}) collective-permute-start(bf16[2560,256]{1,0:T(8,128)(2,1)} %collective-permute-done.13.refs_2_), channel_id=1, source_target_pairs={{0,8},{8,0},{16,24},{24,16},{1,9},{9,1},{17,25},{25,17},{2,10},{10... | collective-permute-start | bytes 3932168 | tf_op jit(solution)/shard_map/ppermute | solution.py:111
  366.3 313.1 %collective-permute-start.16 = (bf16[2560,256]{1,0:T(8,128)(2,1)}, bf16[2560,256]{1,0:T(8,128)(2,1)S(1)}, u32[]{:S(2)}, u32[]{:S(2)}) collective-permute-start(bf16[2560,256]{1,0:T(8,128)(2,1)} %collective-permute-done.14.refs_3_), channel_id=1, source_target_pairs={{0,8},{8,0},{16,24},{24,16},{1,9},{9,1},{17,25},{25,17},{2,10},{10... | collective-permute-start | bytes 3932168 | tf_op jit(solution)/shard_map/ppermute | solution.py:111
  648.4 351.5 %collective-permute-start.30 = (bf16[512,512]{1,0:T(8,128)(2,1)S(1)}, bf16[512,512]{1,0:T(8,128)(2,1)S(1)}, u32[]{:S(2)}, u32[]{:S(2)}) collective-permute-start(bf16[512,512]{1,0:T(8,128)(2,1)S(1)} %get-tuple-element.212.c0), channel_id=1, source_target_pairs={{0,3},{1,0},{2,1},{3,2},{4,7},{5,4},{6,5},{7,6},{8,11},{9,8},{10,9... | collective-permute-start | bytes 1572872 | tf_op jit(solution)/shard_map/ppermute | solution.py:676
  652.2 350.1 %collective-permute-start.31 = (bf16[512,512]{1,0:T(8,128)(2,1)}, bf16[512,512]{1,0:T(8,128)(2,1)}, u32[]{:S(2)}, u32[]{:S(2)}) collective-permute-start(bf16[512,512]{1,0:T(8,128)(2,1)} %collective-permute-done.29.ca), channel_id=1, source_target_pairs={{0,1},{1,2},{2,3},{3,0},{4,5},{5,6},{6,7},{7,4},{8,9},{9,10},{10,1... | collective-permute-start | bytes 1572872 | tf_op jit(solution)/shard_map/ppermute | solution.py:676
  652.3 362.8 %collective-permute-start.28 = (bf16[2,512,512]{2,1,0:T(8,128)(2,1)S(1)}, bf16[2,512,512]{2,1,0:T(8,128)(2,1)}, u32[]{:S(2)}, u32[]{:S(2)}) collective-permute-start(bf16[2,512,512]{2,1,0:T(8,128)(2,1)S(1)} %copy-done.49), channel_id=1, source_target_pairs={{0,4},{1,5},{2,6},{3,7},{8,12},{9,13},{10,14},{11,15},{16,20},{17,... | collective-permute-start | bytes 3145736 | tf_op jit(solution)/shard_map/ppermute | solution.py:777
  675.5 358.4 %collective-permute-start.10 = (bf16[512,512]{1,0:T(8,128)(2,1)S(1)}, bf16[512,512]{1,0:T(8,128)(2,1)}, u32[]{:S(2)}, u32[]{:S(2)}) collective-permute-start(bf16[512,512]{1,0:T(8,128)(2,1)S(1)} %get-tuple-element.211.c0), channel_id=1, source_target_pairs={{0,3},{1,0},{2,1},{3,2},{4,7},{5,4},{6,5},{7,6},{8,11},{9,8},{10,9... | collective-permute-start | bytes 1572872 | tf_op jit(solution)/shard_map/ppermute | solution.py:676
  679.4 354.5 %collective-permute-start.11 = (bf16[512,512]{1,0:T(8,128)(2,1)}, bf16[512,512]{1,0:T(8,128)(2,1)}, u32[]{:S(2)}, u32[]{:S(2)}) collective-permute-start(bf16[512,512]{1,0:T(8,128)(2,1)} %collective-permute-done.9.ca), channel_id=1, source_target_pairs={{0,1},{1,2},{2,3},{3,0},{4,5},{5,6},{6,7},{7,4},{8,9},{9,10},{10,1... | collective-permute-start | bytes 1572872 | tf_op jit(solution)/shard_map/ppermute | solution.py:676
  1032.1 90.3 %collective-permute-start.39 = (bf16[2,512,512]{2,1,0:T(8,128)(2,1)}, bf16[2,512,512]{2,1,0:T(8,128)(2,1)S(1)}, u32[]{:S(2)}, u32[]{:S(2)}) collective-permute-start(bf16[2,512,512]{2,1,0:T(8,128)(2,1)} %bitcast.143), channel_id=1, source_target_pairs={{4,0},{5,1},{6,2},{7,3},{12,8},{13,9},{14,10},{15,11},{20,16},{21,... | collective-permute-start | bytes 3145736 | tf_op jit(solution)/shard_map/ppermute | solution.py:806
  1122.2 109.8 %collective-permute-start.47 = (bf16[2,4,512,512]{3,2,1,0:T(8,128)(2,1)}, bf16[2,4,512,512]{3,2,1,0:T(8,128)(2,1)}, u32[]{:S(2)}, u32[]{:S(2)}) collective-permute-start(bf16[2,4,512,512]{3,2,1,0:T(8,128)(2,1)} %get-tuple-element.126), channel_id=1, source_target_pairs={{0,8},{8,0},{16,24},{24,16},{1,9},{9,1},{17,25},{25,17},{2,10},{10... | collective-permute-start | bytes 12582920 | tf_op jit(solution)/shard_map/ppermute | solution.py:111
  1122.5 114.5 %collective-permute-start.51 = (bf16[2,4,512,512]{3,2,1,0:T(8,128)(2,1)}, bf16[2,4,512,512]{3,2,1,0:T(8,128)(2,1)}, u32[]{:S(2)}, u32[]{:S(2)}) collective-permute-start(bf16[2,4,512,512]{3,2,1,0:T(8,128)(2,1)} %get-tuple-element.128), channel_id=1, source_target_pairs={{0,8},{8,0},{16,24},{24,16},{1,9},{9,1},{17,25},{25,17},{2,10},{10... | collective-permute-start | bytes 12582920 | tf_op jit(solution)/shard_map/ppermute | solution.py:111
  1142.2 102.1 %collective-permute-start.43 = (bf16[2,4,512,512]{3,2,1,0:T(8,128)(2,1)}, bf16[2,4,512,512]{3,2,1,0:T(8,128)(2,1)}, u32[]{:S(2)}, u32[]{:S(2)}) collective-permute-start(bf16[2,4,512,512]{3,2,1,0:T(8,128)(2,1)} %get-tuple-element.124), channel_id=1, source_target_pairs={{0,8},{8,0},{16,24},{24,16},{1,9},{9,1},{17,25},{25,17},{2,10},{10... | collective-permute-start | bytes 12582920 | tf_op jit(solution)/shard_map/ppermute | solution.py:111
  1191.7 215.5 %collective-permute-start.40 = (bf16[512,512]{1,0:T(8,128)(2,1)}, bf16[512,512]{1,0:T(8,128)(2,1)}, u32[]{:S(2)}, u32[]{:S(2)}) collective-permute-start(bf16[512,512]{1,0:T(8,128)(2,1)} %get-tuple-element.116), channel_id=1, source_target_pairs={{0,3},{1,0},{2,1},{3,2},{4,7},{5,4},{6,5},{7,6},{8,11},{9,8},{10,9... | collective-permute-start | bytes 1572872 | tf_op jit(solution)/shard_map/ppermute | solution.py:676
  1236.5 174.6 %collective-permute-start.48 = (bf16[4,512,512]{2,1,0:T(8,128)(2,1)}, bf16[4,512,512]{2,1,0:T(8,128)(2,1)}, u32[]{:S(2)}, u32[]{:S(2)}) collective-permute-start(bf16[4,512,512]{2,1,0:T(8,128)(2,1)} %fusion.12), channel_id=1, source_target_pairs={{0,16},{8,24},{16,0},{24,8},{1,17},{9,25},{17,1},{25,9},{2,18},{10... | collective-permute-start | bytes 6291464 | tf_op jit(solution)/shard_map/ppermute | solution.py:111
  1240.7 176.0 %collective-permute-start.52 = (bf16[4,512,512]{2,1,0:T(8,128)(2,1)}, bf16[4,512,512]{2,1,0:T(8,128)(2,1)}, u32[]{:S(2)}, u32[]{:S(2)}) collective-permute-start(bf16[4,512,512]{2,1,0:T(8,128)(2,1)} %fusion.13), channel_id=1, source_target_pairs={{0,16},{8,24},{16,0},{24,8},{1,17},{9,25},{17,1},{25,9},{2,18},{10... | collective-permute-start | bytes 6291464 | tf_op jit(solution)/shard_map/ppermute | solution.py:111
  1244.3 164.9 %collective-permute-start.42 = (bf16[512,512]{1,0:T(8,128)(2,1)}, bf16[512,512]{1,0:T(8,128)(2,1)}, u32[]{:S(2)}, u32[]{:S(2)}) collective-permute-start(bf16[512,512]{1,0:T(8,128)(2,1)} %add_convert_fusion.8), channel_id=1, source_target_pairs={{0,1},{1,2},{2,3},{3,0},{4,5},{5,6},{6,7},{7,4},{8,9},{9,10},{10,1... | collective-permute-start | bytes 1572872 | tf_op jit(solution)/shard_map/ppermute | solution.py:676
  1252.1 168.1 %collective-permute-start.44 = (bf16[4,512,512]{2,1,0:T(8,128)(2,1)}, bf16[4,512,512]{2,1,0:T(8,128)(2,1)}, u32[]{:S(2)}, u32[]{:S(2)}) collective-permute-start(bf16[4,512,512]{2,1,0:T(8,128)(2,1)} %fusion.11), channel_id=1, source_target_pairs={{0,16},{8,24},{16,0},{24,8},{1,17},{9,25},{17,1},{25,9},{2,18},{10... | collective-permute-start | bytes 6291464 | tf_op jit(solution)/shard_map/ppermute | solution.py:111
  (86 other events, 3384.0 us)

commit v2 on v1

--- a/solution.py
+++ b/solution.py
@@ -17,6 +17,7 @@
 EPS = 1e-05
 NEG = -1e30
 VMEM = 56 * 2**20
+COST = 0.3
 
 bf16 = jnp.bfloat16
 f32 = jnp.float32
@@ -48,7 +49,7 @@
 
 
 def call(body, name, grid, info, ins, in_specs, outs, out_specs, flops, scratch=()):
-    moved = sum(math.prod(a.shape) * a.dtype.itemsize for a in (*ins, *outs))
+    moved = sum(math.prod(a.shape) * a.dtype.itemsize for a in (*ins, *jax.tree.leaves(outs)))
     return pl.pallas_call(
         body,
         grid_spec=pltpu.PrefetchScalarGridSpec(
@@ -61,7 +62,7 @@
         out_shape=outs,
         compiler_params=pltpu.CompilerParams(vmem_limit_bytes=VMEM),
         cost_estimate=pl.CostEstimate(
-            flops=int(flops), bytes_accessed=int(moved), transcendentals=0
+            flops=int(flops * COST), bytes_accessed=int(moved * COST), transcendentals=0
         ),
         name=name,
     )(info, *ins)
@@ -72,49 +73,54 @@
 
 
 def place(pieces, axis, shape, name):
-    starts = jnp.stack([jnp.asarray(at, jnp.int32) for _, at in pieces])
-    arrays = [a for a, _ in pieces]
-
-    def body(at_ref, *refs):
-        *sources, out, sems = refs
-        copies = []
-        for n, source in enumerate(sources):
-            size = arrays[n].shape[axis]
-            window = pl.ds(pl.multiple_of(at_ref[n], 256), size)
-            target = out.at[window, :] if axis == 0 else out.at[:, window]
-            copies.append(pltpu.make_async_copy(source, target, sems.at[n]))
-        for copy in copies:
-            copy.start()
-        for copy in copies:
-            copy.wait()
-
-    anywhere = pl.BlockSpec(memory_space=pl.ANY)
-    return pl.pallas_call(
+    step = 256
+    places, steps = [], []
+    for array, at in pieces:
+        count = array.shape[axis] // step
+        steps.append((len(places), count))
+        places += [at // step + n for n in range(count)]
+    where = jnp.stack([jnp.asarray(at, jnp.int32) for at in places])
+
+    def body(where_ref, *refs):
+        *sources, out = refs
+        g = pl.program_id(0)
+        for source, (first, count) in zip(sources, steps):
+
+            @pl.when((g >= first) & (g < first + count))
+            def _(source=source):
+                out[...] = source[...]
+
+    block = (step, shape[1]) if axis == 0 else (shape[0], step)
+
+    def at(index):
+        return (index, 0) if axis == 0 else (0, index)
+
+    def source_spec(first, count):
+        return spec(block, lambda g, _: at(jnp.clip(g - first, 0, count - 1)))
+
+    return call(
         body,
-        grid_spec=pltpu.PrefetchScalarGridSpec(
-            num_scalar_prefetch=1,
-            grid=(1,),
-            in_specs=[anywhere] * len(arrays),
-            out_specs=anywhere,
-            scratch_shapes=[pltpu.SemaphoreType.DMA((len(arrays),))],
-        ),
-        out_shape=shaped(shape),
-        compiler_params=pltpu.CompilerParams(vmem_limit_bytes=VMEM),
-        cost_estimate=pl.CostEstimate(
-            flops=0, bytes_accessed=4 * math.prod(shape), transcendentals=0
-        ),
-        name=name,
-    )(starts, *arrays)
+        name,
+        len(places),
+        where,
+        [a for a, _ in pieces],
+        [source_spec(*pair) for pair in steps],
+        shaped(shape),
+        spec(block, lambda g, where_ref: at(where_ref[g])),
+        0,
+    )
+
+
+def after(value, *others):
+    return lax.optimization_barrier((value, others))[0]
 
 
 def swap(array, axis, bit, size):
     return lax.ppermute(array, axis, [(i, i ^ bit) for i in range(size)])
 
 
-def gather_shards(own, axis, d, c, two, name):
+def gather_shards(own, axis, d, c, two):
     size = own.shape[axis]
-    shape = list(own.shape)
-    shape[axis] = size * N_DP
     if two:
         half = size // 2
         mine = lax.dynamic_slice_in_dim(own, c * half, half, axis)
@@ -134,7 +140,7 @@
             (across, (d ^ 2) * size),
             (swap(across, "dp", 1, N_DP), (d ^ 3) * size),
         ]
-    return place(pieces, axis, shape, name)
+    return pieces
 
 
 def rotary_tables(starts, positions):
@@ -440,6 +446,7 @@
     )
 
 
+TAIL = 16
 ORDER = (2, 3, 1, 0)
 
 
@@ -479,7 +486,8 @@
 
 def back_in_body(info, dq, dkv, dup, wq, wu, xf, gain, avg, inv, *outs):
     j = pl.program_id(0)
-    *chunks, row_sums, column_sums = outs
+    *chunks, column_sums, row_sums = outs
+    rows = dq.shape[0]
     y = dot_nt(dup[...], wu[...])
     y = y + dot_nt(dq[...], wq[:, :CH])
     y = y + dot_nt(dkv[0], wq[:, CH : 2 * CH])
@@ -489,25 +497,26 @@
 
         @pl.when(j == step)
         def _(r=r):
-            chunks[r][...] = yb
+            chunks[r][:rows, :] = yb
 
     standard = (xf[...].astype(f32) - avg[...]) * inv[...]
     cross = y * standard
     weight = gain[...].astype(f32)
     column_sums[0, 0:1, :] = jnp.sum(cross, axis=0, keepdims=True)
     column_sums[0, 1:2, :] = jnp.sum(y, axis=0, keepdims=True)
-    plain_row = jnp.sum(y * weight, axis=1, keepdims=True)
-    cross_row = jnp.sum(cross * weight, axis=1, keepdims=True)
 
     @pl.when(j == 0)
     def _():
-        row_sums[:, 0:1] = plain_row
-        row_sums[:, 1:2] = cross_row
-
-    @pl.when(j > 0)
-    def _():
-        row_sums[:, 0:1] += plain_row
-        row_sums[:, 1:2] += cross_row
+        row_sums[...] = jnp.zeros(row_sums.shape, f32)
+
+    row_sums[:, 0:1] += jnp.sum(y * weight, axis=1, keepdims=True)
+    row_sums[:, 1:2] += jnp.sum(cross * weight, axis=1, keepdims=True)
+
+    @pl.when(j == N_TP - 1)
+    def _():
+        turned = row_sums[...].T[:TAIL].astype(bf16)
+        for chunk in chunks:
+            chunk[rows:, :] = turned
 
 
 def back_in(info, dq, dkv, dup, wq, wu, xf, gain, avg, inv):
@@ -533,13 +542,11 @@
             whole(rows, 1),
             whole(rows, 1),
         ],
-        (shaped((rows, CH)),) * N_TP + (shaped((rows, 2), f32), shaped((N_TP, 2, CH), f32)),
-        [whole(rows, CH)] * N_TP
-        + [
-            whole(rows, 2),
-            spec((1, 2, CH), lambda j, info: (chunk(j, info), 0, 0)),
-        ],
+        (shaped((rows + TAIL, CH)),) * N_TP + (shaped((N_TP, 2, CH), f32),),
+        [whole(rows + TAIL, CH)] * N_TP
+        + [spec((1, 2, CH), lambda j, _: (relative(j), 0, 0))],
         2 * rows * D * (3 * CH + units),
+        [pltpu.VMEM((rows, 128), f32)],
     )
 
 
@@ -690,22 +697,41 @@
     return chunks[0].astype(f32) + back.astype(f32) + near.astype(f32)
 
 
-def reduce_grads(kept, given, c, two):
-    got = swap(given, "dp", 1, N_DP)
-    across = (kept[1].astype(f32) + got[1].astype(f32)).astype(bf16)
-    moved = swap(across, "dp", 2, N_DP)
-    total = (kept[0].astype(f32) + got[0].astype(f32) + moved.astype(f32)).astype(bf16)
-    if not two:
-        return lax.psum(total, "ctx").astype(f32)
-    half = total.shape[0] // 2
-    mine = lax.dynamic_slice_in_dim(total, c * half, half, 0)
-    theirs = lax.dynamic_slice_in_dim(total, (1 - c) * half, half, 0)
-    received = swap(theirs, "ctx", 1, 2)
-    mine = (mine.astype(f32) + received.astype(f32)).astype(bf16)
-    other = swap(mine, "ctx", 1, 2)
-    low = jnp.where(c == 0, mine, other)
-    high = jnp.where(c == 0, other, mine)
-    return jnp.concatenate([low, high], axis=0).astype(f32)
+class Reduction:
+    def __init__(self, kept, given, c, two):
+        self.kept, self.c, self.two = kept, c, two
+        self.got = swap(given, "dp", 1, N_DP)
+
+    def over_x(self):
+        self.across = (self.kept[1].astype(f32) + self.got[1].astype(f32)).astype(bf16)
+        self.moved = swap(self.across, "dp", 2, N_DP)
+        return self.across
+
+    def over_y(self):
+        parts = (self.kept[0], self.got[0], self.moved)
+        total = sum(a.astype(f32) for a in parts).astype(bf16)
+        if not self.two:
+            self.total = lax.psum(total, "ctx")
+            return total
+        half = total.shape[0] // 2
+        self.mine = lax.dynamic_slice_in_dim(total, self.c * half, half, 0)
+        theirs = lax.dynamic_slice_in_dim(total, (1 - self.c) * half, half, 0)
+        self.received = swap(theirs, "ctx", 1, 2)
+        return theirs
+
+    def back_y(self):
+        if self.two:
+            self.mine = (self.mine.astype(f32) + self.received.astype(f32)).astype(bf16)
+            self.other = swap(self.mine, "ctx", 1, 2)
+            return self.mine
+        return self.total
+
+    def result(self):
+        if not self.two:
+            return [a.astype(f32) for a in self.total]
+        low = jnp.where(self.c == 0, self.mine, self.other).astype(f32)
+        high = jnp.where(self.c == 0, self.other, self.mine).astype(f32)
+        return [*low, *high]
 
 
 def body(
@@ -732,12 +758,26 @@
     two = n_ctx == 2
     info = jnp.stack([t, c, d]).astype(jnp.int32)
 
-    x_parts = [gather_tp(block_in[s]) for s in range(seqs)]
-
     small = jnp.concatenate(
         [query_bias, key_bias, value_bias, up_bias, output_bias, norm_gain, norm_shift]
     )
     small_all = lax.all_gather(small, ("tp", "dp"), axis=0, tiled=False)
+    big = (block_in, query_weight, key_weight, value_weight, output_weight, up_weight, down_weight)
+    big, small_all = lax.optimization_barrier((big, small_all))
+    block_in, query_weight, key_weight, value_weight, output_weight, up_weight, down_weight = big
+
+    x_parts = [gather_tp(block_in[0])]
+    x_parts.append(gather_tp(after(block_in[1], x_parts[0][1])))
+
+    wq_shard = jnp.concatenate([query_weight, key_weight, value_weight], axis=1)
+    wo_shard = jnp.concatenate([output_weight, down_weight], axis=0)
+    wq_pieces = gather_shards(wq_shard, 0, d, c, two)
+    wu_pieces = gather_shards(after(up_weight, wq_pieces[2][0]), 0, d, c, two)
+    wo_pieces = gather_shards(after(wo_shard, wu_pieces[2][0]), 1, d, c, two)
+
+    ct_parts = [gather_tp(after(cotangent[0], x_parts[1][1]))]
+    ct_parts.append(gather_tp(after(cotangent[1], ct_parts[0][1])))
+
     small_all = small_all.reshape(N_TP, N_DP, -1)
     small_here = lax.dynamic_index_in_dim(small_all, t, 0, keepdims=False)
     sizes = [query_bias.size] * 3 + [up_bias.size] + [output_bias.size] * 3
@@ -752,16 +792,6 @@
     gain, shift = small_of(small_all, 5), small_of(small_all, 6)
     gain_here = small_of(small_here, 5).astype(f32)
 
-    wq = gather_shards(
-        jnp.concatenate([query_weight, key_weight, value_weight], axis=1), 0, d, c, two, "place_qkv"
-    )
-    wu = gather_shards(up_weight, 0, d, c, two, "place_up")
-    wo = gather_shards(
-        jnp.concatenate([output_weight, down_weight], axis=0), 1, d, c, two, "place_out"
-    )
-
-    ct_parts = [gather_tp(cotangent[s]) for s in range(seqs)]
-
     here = c * rows + jnp.arange(rows, dtype=jnp.int32)
     tables, opening = rotary_tables(doc_starts, here)
     blocks = 1 if two else n_ctx
@@ -769,7 +799,12 @@
     before = [a.reshape(seqs, blocks, rows, 128) for a in before]
 
     xf, normed, avg, inv, q, kv, kvp = [], [], [], [], [], [], []
-    for s in range(seqs):
+    hidden, slope = [], []
+    cf, out_bias_sum, datt, dup = [], [], [], []
+    att, dq, dkv_own, dkv_sent, dkv = [], [], [], [], []
+    out_sum, normed_grad, column_sums = [], [], []
+
+    def norm_step(s, info):
         one = norm_qkv(info, x_parts[s], gain, shift, wq, qkv_bias, [a[s] for a in tables])
         for target, value in zip((xf, normed, avg, inv, q, kv), one):
             target.append(value)
@@ -777,20 +812,14 @@
             kvp.append(lax.ppermute(kv[s], "ctx", [(0, 1)])[None])
         else:
             kvp.append(lax.all_gather(kv[s], "ctx", axis=0, tiled=False))
-    h0, h1, g0, g1 = mlp_up(info, normed, wu, up_shift)
-    hidden, slope = (h0, h1), (g0, g1)
-
-    cf, out_bias_sum, datt, dup = [], [], [], []
-    att, dq, dkv = [], [], []
-    out_sum = []
-    for s in range(seqs):
+
+    def back_out_step(s, info):
         one = back_out(info, ct_parts[s], wo, slope[s])
         for target, value in zip((cf, out_bias_sum, datt, dup), one):
             target.append(value)
-    up_kept, up_given, up_sum = grad_up(info, normed, dup)
-    down_kept, down_given = grad_down(info, hidden, cf)
-    for s in range(seqs):
-        a, b, own, sent = attention(
+
+    def attention_step(s, info):
+        one = attention(
             info,
             opening[s][None],
             q[s],
@@ -800,48 +829,81 @@
             [x[s] for x in tables],
             [x[s] for x in before],
         )
-        att.append(a)
-        dq.append(b)
+        for target, value in zip((att, dq, dkv_own, dkv_sent), one):
+            target.append(value)
         if two:
-            back = lax.ppermute(sent[0], "ctx", [(1, 0)])
+            back = lax.ppermute(dkv_sent[s][0], "ctx", [(1, 0)])
         else:
-            back = lax.psum_scatter(sent, "ctx", scatter_dimension=0, tiled=False)
-        dkv.append((own.astype(f32) + back.astype(f32)).astype(bf16))
-        out_sum.append(scatter_tp(project_out(info, att[s], hidden[s], wo)))
+            back = lax.psum_scatter(dkv_sent[s], "ctx", scatter_dimension=0, tiled=False)
+        dkv.append((dkv_own[s].astype(f32) + back.astype(f32)).astype(bf16))
+
+    def out_step(s, info):
+        chunks = project_out(info, att[s], hidden[s], wo)
+        out_sum.append(scatter_tp(chunks))
+        return chunks
+
+    def back_in_step(s, info):
+        *chunks, sums = back_in(info, dq[s], dkv[s], dup[s], wq, wu, xf[s], gain, avg[s], inv[s])
+        normed_grad.append(scatter_tp(chunks))
+        column_sums.append(sums)
+        return chunks
+
+    wq = place(wq_pieces, 0, (D, 3 * CH), "place_qkv")
+    norm_step(0, info)
+    norm_step(1, after(info, kv[0]))
+    wu = place(wu_pieces, 0, (D, up_weight.shape[1]), "place_up")
+    h0, h1, g0, g1 = mlp_up(after(info, kv[1]), normed, wu, up_shift)
+    hidden, slope = (h0, h1), (g0, g1)
+    wo = place(wo_pieces, 1, (wo_shard.shape[0], D), "place_out")
+    back_out_step(0, after(info, h1))
+    attention_step(0, after(info, dup[0]))
+    chunks = out_step(0, after(info, att[0]))
+    back_out_step(1, after(info, chunks))
+    up_kept, up_given, up_sum = grad_up(after(info, dup[1]), normed, dup)
+    up = Reduction(up_kept, up_given, c, two)
+    down_kept, down_given = grad_down(after(info, up_kept), hidden, cf)
+    down = Reduction(down_kept, down_given, c, two)
+    attention_step(1, after(info, down_kept, up.over_x()))
+    head_kept, head_given, head_sum = grad_heads(
+        after(info, att[1], down.over_x()), normed, cf, att, dq, dkv
+    )
+    head = Reduction(head_kept, head_given, c, two)
+    chunks = back_in_step(0, after(info, head_kept))
+    chunks = out_step(1, after(info, chunks, head.over_x(), up.over_y()))
+    chunks = back_in_step(1, after(info, chunks, up.back_y()))
+    down.over_y()
+    down.back_y()
+    head.over_y()
+    head.back_y()
+
     block_out = jnp.stack(out_sum)
     block_out = (block_in.astype(f32) + block_out + output_shift.astype(f32)).astype(bf16)
-
-    normed_grad, row_sums, column_sums = [], [], []
-    for s in range(seqs):
-        *chunks, row_sum, column_sum = back_in(
-            info, dq[s], dkv[s], dup[s], wq, wu, xf[s], gain, avg[s], inv[s]
-        )
-        normed_grad.append(scatter_tp(chunks))
-        row_sums.append(row_sum)
-        column_sums.append(column_sum)
-    head_kept, head_given, head_sum = grad_heads(info, normed, cf, att, dq, dkv)
-
-    up_wg = reduce_grads(up_kept, up_given, c, two)
-    down_wg = reduce_grads(down_kept, down_given, c, two)
-    head_wg = reduce_grads(head_kept, head_given, c, two)
-    up_wg = up_wg.transpose(1, 0, 2).reshape(CH, -1)
-    down_wg = down_wg.reshape(-1, CH)
-
-    row_sums = lax.psum(jnp.stack(row_sums), "tp")
-    total_plain, total_cross = row_sums[..., 0:1], row_sums[..., 1:2]
-    root = jnp.stack(inv)
-    standard = (block_in.astype(f32) - jnp.stack(avg)) * root
-    scaled = jnp.stack(normed_grad) * gain_here
-    in_grad = cotangent.astype(f32) + root * (
-        scaled - total_plain / D - standard * total_cross / D
-    )
-
-    local = jnp.concatenate(
-        [head_sum[1:].reshape(-1), up_sum.reshape(-1), sum(out_bias_sum).reshape(-1)]
-    )
-    both = sum(column_sums)
-    both = lax.psum_scatter(both, "tp", scatter_dimension=0, tiled=False).reshape(-1)
-    summed = lax.psum(jnp.concatenate([local, both]), ("dp", "ctx"))
+    up_wg = jnp.concatenate(up.result(), axis=1)
+    down_wg = jnp.concatenate(down.result(), axis=0)
+    output_wg, query_wg, key_wg, value_wg = head.result()
+
+    def input_gradient(s):
+        total = normed_grad[s]
+        plain, cross = total[rows][:, None], total[rows + 1][:, None]
+        standard = (block_in[s].astype(f32) - avg[s]) * inv[s]
+        scaled = total[:rows] * gain_here
+        return cotangent[s].astype(f32) + inv[s] * (scaled - plain / D - standard * cross / D)
+
+    in_grad = jnp.stack([input_gradient(s) for s in range(seqs)])
+
+    sums = sum(column_sums)
+    both = sums[0] + sum(ring(sums[r], r) for r in range(1, N_TP))
+    summed = jnp.concatenate(
+        [
+            head_sum[1:].reshape(-1),
+            up_sum.reshape(-1),
+            sum(out_bias_sum).reshape(-1),
+            both.reshape(-1),
+        ]
+    )
+    summed = summed + swap(summed, "dp", 1, N_DP)
+    summed = summed + swap(summed, "dp", 2, N_DP)
+    summed = summed + swap(summed, "ctx", 1, 2) if two else lax.psum(summed, "ctx")
     at = 0
     small_grads = []
     for size in (CH, CH, CH, up_sum.size, CH, CH, CH):
@@ -853,10 +915,10 @@
     return (
         block_out,
         in_grad,
-        head_wg[1],
-        head_wg[2],
-        head_wg[3],
-        head_wg[0],
+        query_wg,
+        key_wg,
+        value_wg,
+        output_wg,
         up_wg,
         down_wg,
         query_bg,

time: 1560 us -> 742 us (0.48)
  the two profiles are of different devices: /device:TPU:0 before, /device:TPU:16 now
where the time goes in v2:
time: 742 us; the launch traced here: 733 us
  waiting for transfers between devices  274 us (37%)
  Pallas kernels  237 us (32%)
  starting transfers between devices  91 us (12%)
  local copies, waits for them, and re-layouts  58.5 us (8%)
  other arithmetic  54.5 us (7%)
  blocking collectives  16.2 us (2%)
    pallas_call x17, Pallas kernels, call(): pl.pallas_call(body, grid_spec=pltpu.PrefetchScalarGridSpec(num_scalar_pr...  237 us
    ppermute x27, waiting for transfers between devices, ring(): lax.ppermute(array, 'tp', [(i, (i + step) % N_TP) for i in range(N_TP)])  143 us
    ppermute x30, waiting for transfers between devices, swap(): return lax.ppermute(array, axis, [(i, i ^ bit) for i in range(size)])  94.1 us
    ppermute x27, starting transfers between devices, ring(): lax.ppermute(array, 'tp', [(i, (i + step) % N_TP) for i in range(N_TP)])  52.7 us
    ppermute x2, waiting for transfers between devices, attention_step(): back = lax.ppermute(dkv_sent[s][0], 'ctx', [(1, 0)])  27.4 us
    ppermute x30, starting transfers between devices, swap(): return lax.ppermute(array, axis, [(i, i ^ bit) for i in range(size)])  19.7 us
    all_gather x1, blocking collectives, body(): small_all = lax.all_gather(small, ('tp', 'dp'), axis=0, tiled=False)  16.2 us
    ppermute x2, starting transfers between devices, norm_step(): kvp.append(lax.ppermute(kv[s], 'ctx', [(0, 1)])[None])  15.7 us
  transfers between devices with their start and end apart: 61, of which 20 were waited for; matrix products, arithmetic and copies ran while one was open for 12% of the time, Pallas kernels for 26%

profile of v2, /device:TPU:16, one launch (start us, length us, event | category | flops | bytes accessed | tf_op | source)
XLA Modules:
  0.0 732.6 jit_solution(2073112686516613257)
XLA Ops:
  6.6 16.2 %all-gather.1 = bf16[16,1,1280]{2,1,0:T(2,128)(2,1)S(1)} all-gather(bf16[1,1,1280]{2,1,0:T(2,128)(2,1)S(1)} %reshape.193), channel_id=2, replica_groups=mesh['dp'=4,'ctx'=2,'tp'=4] {'tp','dp'}, dimensions={0}, use_global_device_ids=true | all-gather | bytes 43520 | tf_op jit(solution)/shard_map/all_gather | solution.py:764
  33.4 15.3 %collective-permute-done.4.refs_2_ = bf16[256,1536]{1,0:T(8,128)(2,1)} collective-permute-done((bf16[256,1536]{1,0:T(8,128)(2,1)S(1)}, bf16[256,1536]{1,0:T(8,128)(2,1)}, u32[]{:S(2)}, u32[]{:S(2)}) %collective-permute-start.4) | collective-permute-done | bytes 786464 | tf_op jit(solution)/shard_map/ppermute | solution.py:119
  62.0 19.7 %collective-permute-done.8.xa = bf16[512,512]{1,0:T(8,128)(2,1)} collective-permute-done((bf16[512,512]{1,0:T(8,128)(2,1)}, bf16[512,512]{1,0:T(8,128)(2,1)}, u32[]{:S(2)}, u32[]{:S(2)}) %collective-permute-start.8) | collective-permute-done | bytes 524320 | tf_op jit(solution)/shard_map/ppermute | solution.py:683
  83.8 19.2 %collective-permute-done.2.xb = bf16[512,512]{1,0:T(8,128)(2,1)} collective-permute-done((bf16[512,512]{1,0:T(8,128)(2,1)}, bf16[512,512]{1,0:T(8,128)(2,1)}, u32[]{:S(2)}, u32[]{:S(2)}) %collective-permute-start.2) | collective-permute-done | bytes 524320 | tf_op jit(solution)/shard_map/ppermute | solution.py:683
  104.5 17.4 %collective-permute-done.9.xc = bf16[512,512]{1,0:T(8,128)(2,1)} collective-permute-done((bf16[512,512]{1,0:T(8,128)(2,1)}, bf16[512,512]{1,0:T(8,128)(2,1)}, u32[]{:S(2)}, u32[]{:S(2)}) %collective-permute-start.9) | collective-permute-done | bytes 524320 | tf_op jit(solution)/shard_map/ppermute | solution.py:683
  159.4 34.8 %collective-permute-done.13.refs_3_ = bf16[256,2048]{1,0:T(8,128)(2,1)} collective-permute-done((bf16[256,2048]{1,0:T(8,128)(2,1)}, bf16[256,2048]{1,0:T(8,128)(2,1)}, u32[]{:S(2)}, u32[]{:S(2)}) %collective-permute-start.13) | collective-permute-done | bytes 1048608 | tf_op jit(solution)/shard_map/ppermute | solution.py:119
  207.6 12.8 %norm_qkv.2 = (bf16[512,2048]{1,0:T(8,128)(2,1)}, bf16[512,2048]{1,0:T(8,128)(2,1)}, f32[512,1]{1,0:T(8,128)}, f32[512,1]{1,0:T(8,128)}, bf16[512,512]{1,0:T(8,128)(2,1)}, /*index=5*/bf16[2,512,512]{2,1,0:T(8,128)(2,1)}) custom-call(s32[3]{0:T(128)} %pad_add_fusion.info, bf16[512,512]{1,0:T(8,128)(2,1)} %get-tuple-element.212.x0, ...), custom_call_target="tpu_custom_call" | custom-call | flops 966367616 | bytes 4487270 | tf_op jit(solution)/shard_map/norm_qkv/pallas_call | solution.py:53
  227.4 11.8 %collective-permute-start.17 = (bf16[512,512]{1,0:T(8,128)(2,1)S(1)}, bf16[512,512]{1,0:T(8,128)(2,1)S(1)}, u32[]{:S(2)}, u32[]{:S(2)}) collective-permute-start(bf16[512,512]{1,0:T(8,128)(2,1)S(1)} %copy-done.13), channel_id=1, source_target_pairs={{0,3},{1,0},{2,1},{3,2},{4,7},{5,4},{6,5},{7,6},{8,11},{9,8},{10,9... | collective-permute-start | bytes 1572872 | tf_op jit(solution)/shard_map/ppermute | solution.py:683
  240.3 12.8 %norm_qkv.3 = (bf16[512,2048]{1,0:T(8,128)(2,1)}, bf16[512,2048]{1,0:T(8,128)(2,1)}, f32[512,1]{1,0:T(8,128)}, f32[512,1]{1,0:T(8,128)}, bf16[512,512]{1,0:T(8,128)(2,1)}, /*index=5*/bf16[2,512,512]{2,1,0:T(8,128)(2,1)}) custom-call(s32[3]{0:T(128)} %pad_add_fusion.info, bf16[512,512]{1,0:T(8,128)(2,1)} %get-tuple-element.106.x0, ...), custom_call_target="tpu_custom_call" | custom-call | flops 966367616 | bytes 4487270 | tf_op jit(solution)/shard_map/norm_qkv/pallas_call | solution.py:53
  266.3 18.7 %mlp_up.1 = (bf16[512,2048]{1,0:T(8,128)(2,1)}, bf16[512,2048]{1,0:T(8,128)(2,1)}, bf16[512,2048]{1,0:T(8,128)(2,1)}, bf16[512,2048]{1,0:T(8,128)(2,1)}) custom-call(s32[3]{0:T(128)} %pad_add_fusion.info, bf16[512,2048]{1,0:T(8,128)(2,1)} %get-tuple-element.109.n0, bf16[512,2048]{1,0:T(8,128)(2,1)} %get-tuple-element.110.n1, ...), custom_call_target="tpu_custom_call" | custom-call | flops 2576980480 | bytes 6292684 | tf_op jit(solution)/shard_map/mlp_up/pallas_call | solution.py:53
  296.8 12.7 %back_out.2 = (bf16[512,2048]{1,0:T(8,128)(2,1)}, f32[1,512]{1,0:T(1,128)}, bf16[512,512]{1,0:T(8,128)(2,1)}, bf16[512,2048]{1,0:T(8,128)(2,1)}) custom-call(s32[3]{0:T(128)} %pad_add_fusion.info, bf16[512,512]{1,0:T(8,128)(2,1)} %copy-done.12, bf16[512,512]{1,0:T(8,128)(2,1)} %copy-done.24, bf16[512,512]{1,0:T(8,128)(2,1)} %copy-done.31, ...), custom_call_target="tpu_custom_call" | custom-call | flops 1610612736 | bytes 5820211 | tf_op jit(solution)/shard_map/back_out/pallas_call | solution.py:53
  309.5 17.1 %attention.2 = (bf16[512,512]{1,0:T(8,128)(2,1)}, bf16[512,512]{1,0:T(8,128)(2,1)}, bf16[2,512,512]{2,1,0:T(8,128)(2,1)}, bf16[1,2,512,512]{3,2,1,0:T(8,128)(2,1)}) custom-call(s32[3]{0:T(128)} %pad_add_fusion.info, s32[1,512]{1,0:T(1,128)} %get-tuple-element.248.low, bf16[512,512]{1,0:T(8,128)(2,1)} %get-tuple-element.122.q, ...), custom_call_target="tpu_custom_call" | custom-call | flops 1932735232 | bytes 2359910 | tf_op jit(solution)/shard_map/attention/pallas_call | solution.py:53
  338.5 12.7 %back_out.3 = (bf16[512,2048]{1,0:T(8,128)(2,1)}, f32[1,512]{1,0:T(1,128)}, bf16[512,512]{1,0:T(8,128)(2,1)}, bf16[512,2048]{1,0:T(8,128)(2,1)}) custom-call(s32[3]{0:T(128)} %pad_add_fusion.info, bf16[512,512]{1,0:T(8,128)(2,1)} %get-tuple-element.132.c0, bf16[512,512]{1,0:T(8,128)(2,1)} %collective-permute-done.28.ca, bf16[512,512]{1,0:T(8,128)(2,1)} %copy-done.30, ...), custom_call_target="tpu_custom_call" | custom-call | flops 1610612736 | bytes 5820211 | tf_op jit(solution)/shard_map/back_out/pallas_call | solution.py:53
  351.3 14.5 %grad_up.1 = (bf16[2,4,512,512]{3,2,1,0:T(8,128)(2,1)}, bf16[2,4,512,512]{3,2,1,0:T(8,128)(2,1)}, f32[1,2048]{1,0:T(1,128)}) custom-call(s32[3]{0:T(128)} %pad_add_fusion.info, bf16[512,2048]{1,0:T(8,128)(2,1)} %get-tuple-element.109.n0, bf16[512,2048]{1,0:T(8,128)(2,1)} %get-tuple-element.110.n1, bf16[512,2048]{1,0:T(8,128)(2,1)} %get-tuple-element.120.g0.dup, ...), custom_call_target="tpu_custom_call" | custom-call | flops 2576980480 | bytes 5035622 | tf_op jit(solution)/shard_map/grad_up/pallas_call | solution.py:53
  365.7 16.3 %grad_down.1 = (bf16[2,4,512,512]{3,2,1,0:T(8,128)(2,1)}, bf16[2,4,512,512]{3,2,1,0:T(8,128)(2,1)}) custom-call(s32[3]{0:T(128)} %pad_add_fusion.info, bf16[512,2048]{1,0:T(8,128)(2,1)} %get-tuple-element.126.hidden.h0, bf16[512,2048]{1,0:T(8,128)(2,1)} %get-tuple-element.113.h1.hidden, bf16[512,2048]{1,0:T(8,128)(2,1)} %get-tuple-element.138.c0, ...), custom_call_target="tpu_custom_call" | custom-call | flops 2576980480 | bytes 5033164 | tf_op jit(solution)/shard_map/grad_down/pallas_call | solution.py:53
  417.4 17.2 %attention.3 = (bf16[512,512]{1,0:T(8,128)(2,1)}, bf16[512,512]{1,0:T(8,128)(2,1)}, bf16[2,512,512]{2,1,0:T(8,128)(2,1)}, bf16[1,2,512,512]{3,2,1,0:T(8,128)(2,1)}) custom-call(s32[3]{0:T(128)} %pad_add_fusion.info, s32[1,512]{1,0:T(1,128)} %get-tuple-element.247.low, bf16[512,512]{1,0:T(8,128)(2,1)} %get-tuple-element.143.q, ...), custom_call_target="tpu_custom_call" | custom-call | flops 1932735232 | bytes 2359910 | tf_op jit(solution)/shard_map/attention/pallas_call | solution.py:53
  445.1 27.4 %collective-permute-done.35 = bf16[2,512,512]{2,1,0:T(8,128)(2,1)} collective-permute-done((bf16[2,512,512]{2,1,0:T(8,128)(2,1)}, bf16[2,512,512]{2,1,0:T(8,128)(2,1)}, u32[]{:S(2)}, u32[]{:S(2)}) %collective-permute-start.35) | collective-permute-done | bytes 1048608 | tf_op jit(solution)/shard_map/ppermute | solution.py:835
  475.0 16.6 %grad_heads.1 = (bf16[2,4,512,512]{3,2,1,0:T(8,128)(2,1)}, bf16[2,4,512,512]{3,2,1,0:T(8,128)(2,1)}, f32[4,1,512]{2,1,0:T(1,128)}) custom-call(s32[3]{0:T(128)} %pad_add_fusion.info, bf16[512,2048]{1,0:T(8,128)(2,1)} %get-tuple-element.109.n0, bf16[512,2048]{1,0:T(8,128)(2,1)} %get-tuple-element.110.n1, bf16[512,2048]{1,0:T(8,128)(2,1)} %get-tuple-element.138.c0, ...), custom_call_target="tpu_custom_call" | custom-call | flops 2576980480 | bytes 6293913 | tf_op jit(solution)/shard_map/grad_heads/pallas_call | solution.py:53
  494.9 17.4 %back_in.2 = (bf16[528,512]{1,0:T(8,128)(2,1)}, bf16[528,512]{1,0:T(8,128)(2,1)}, bf16[528,512]{1,0:T(8,128)(2,1)}, bf16[528,512]{1,0:T(8,128)(2,1)}, f32[4,2,512]{2,1,0:T(2,128)}) custom-call(s32[3]{0:T(128)} %pad_add_fusion.info, bf16[512,512]{1,0:T(8,128)(2,1)} %get-tuple-element.148.q0.dq, bf16[2,512,512]{2,1,0:T(8,128)(2,1)} %add_convert_fusion.7.kv0.dkv, ...), custom_call_target="tpu_custom_call" | custom-call | flops 2254857728 | bytes 6790348 | tf_op jit(solution)/shard_map/back_in/pallas_call | solution.py:53
  562.3 15.2 %collective-permute-done.54 = bf16[2,512,512]{2,1,0:T(8,128)(2,1)} collective-permute-done((bf16[2,512,512]{2,1,0:T(8,128)(2,1)}, bf16[2,512,512]{2,1,0:T(8,128)(2,1)}, u32[]{:S(2)}, u32[]{:S(2)}) %collective-permute-start.54) | collective-permute-done | bytes 1048608 | tf_op jit(solution)/shard_map/ppermute | solution.py:119
  581.9 16.6 %collective-permute-done.51 = bf16[2,512,512]{2,1,0:T(8,128)(2,1)S(1)} collective-permute-done((bf16[2,512,512]{2,1,0:T(8,128)(2,1)S(1)}, bf16[2,512,512]{2,1,0:T(8,128)(2,1)S(1)}, u32[]{:S(2)}, u32[]{:S(2)}) %collective-permute-start.51) | collective-permute-done | bytes 1048608 | tf_op jit(solution)/shard_map/ppermute | solution.py:119
  614.3 17.5 %back_in.3 = (bf16[528,512]{1,0:T(8,128)(2,1)}, bf16[528,512]{1,0:T(8,128)(2,1)}, bf16[528,512]{1,0:T(8,128)(2,1)}, bf16[528,512]{1,0:T(8,128)(2,1)}, f32[4,2,512]{2,1,0:T(2,128)}) custom-call(s32[3]{0:T(128)} %pad_add_fusion.info, bf16[512,512]{1,0:T(8,128)(2,1)} %get-tuple-element.149.q1.dq, bf16[2,512,512]{2,1,0:T(8,128)(2,1)} %add_convert_fusion.6.kv1.dkv, ...), custom_call_target="tpu_custom_call" | custom-call | flops 2254857728 | bytes 6790348 | tf_op jit(solution)/shard_map/back_in/pallas_call | solution.py:53
  650.5 19.6 %collective-permute-done.39 = bf16[512,512]{1,0:T(8,128)(2,1)S(1)} collective-permute-done((bf16[512,512]{1,0:T(8,128)(2,1)S(1)}, bf16[512,512]{1,0:T(8,128)(2,1)S(1)}, u32[]{:S(2)}, u32[]{:S(2)}) %collective-permute-start.39) | collective-permute-done | bytes 524320 | tf_op jit(solution)/shard_map/ppermute | solution.py:683
  684.1 20.4 %collective-permute-done.40 = bf16[512,512]{1,0:T(8,128)(2,1)S(1)} collective-permute-done((bf16[512,512]{1,0:T(8,128)(2,1)S(1)}, bf16[512,512]{1,0:T(8,128)(2,1)S(1)}, u32[]{:S(2)}, u32[]{:S(2)}) %collective-permute-start.40) | collective-permute-done | bytes 524320 | tf_op jit(solution)/shard_map/ppermute | solution.py:683
  (330 shorter events, 310.8 us)
Async XLA Ops:
  57.6 64.3 %collective-permute-start.9 = (bf16[512,512]{1,0:T(8,128)(2,1)}, bf16[512,512]{1,0:T(8,128)(2,1)}, u32[]{:S(2)}, u32[]{:S(2)}) collective-permute-start(bf16[512,512]{1,0:T(8,128)(2,1)} %get-tuple-element.106.x0), channel_id=1, source_target_pairs={{0,3},{1,0},{2,1},{3,2},{4,7},{5,4},{6,5},{7,6},{8,11},{9,8},{10,9... | collective-permute-start | bytes 1572872 | tf_op jit(solution)/shard_map/ppermute | solution.py:683
  60.9 42.1 %collective-permute-start.2 = (bf16[512,512]{1,0:T(8,128)(2,1)}, bf16[512,512]{1,0:T(8,128)(2,1)}, u32[]{:S(2)}, u32[]{:S(2)}) collective-permute-start(bf16[512,512]{1,0:T(8,128)(2,1)} %collective-permute-done.xa), channel_id=1, source_target_pairs={{0,1},{1,2},{2,3},{3,0},{4,5},{5,6},{6,7},{7,4},{8,9},{9,10},{10,1... | collective-permute-start | bytes 1572872 | tf_op jit(solution)/shard_map/ppermute | solution.py:683
  81.6 43.6 %collective-permute-start.16 = (bf16[512,512]{1,0:T(8,128)(2,1)S(1)}, bf16[512,512]{1,0:T(8,128)(2,1)S(1)}, u32[]{:S(2)}, u32[]{:S(2)}) collective-permute-start(bf16[512,512]{1,0:T(8,128)(2,1)S(1)} %get-tuple-element.115.c0), channel_id=1, source_target_pairs={{0,1},{1,2},{2,3},{3,0},{4,5},{5,6},{6,7},{7,4},{8,9},{9,10},{10,1... | collective-permute-start | bytes 1572872 | tf_op jit(solution)/shard_map/ppermute | solution.py:683
  81.6 43.6 %collective-permute-start.10 = (bf16[512,512]{1,0:T(8,128)(2,1)}, bf16[512,512]{1,0:T(8,128)(2,1)S(1)}, u32[]{:S(2)}, u32[]{:S(2)}) collective-permute-start(bf16[512,512]{1,0:T(8,128)(2,1)} %collective-permute-done.8.xa), channel_id=1, source_target_pairs={{0,1},{1,2},{2,3},{3,0},{4,5},{5,6},{6,7},{7,4},{8,9},{9,10},{10,1... | collective-permute-start | bytes 1572872 | tf_op jit(solution)/shard_map/ppermute | solution.py:683
  83.8 58.4 %collective-permute-start.3 = (bf16[512,1536]{1,0:T(8,128)(2,1)}, bf16[512,1536]{1,0:T(8,128)(2,1)}, u32[]{:S(2)}, u32[]{:S(2)}) collective-permute-start(bf16[512,1536]{1,0:T(8,128)(2,1)} %constant_dynamic-update-slice_fusion.refs_0_), channel_id=1, source_target_pairs={{0,8},{8,0},{16,24},{24,16},{1,9},{9,1},{17,25},{25,17},{2,10},{10... | collective-permute-start | bytes 4718600 | tf_op jit(solution)/shard_map/ppermute | solution.py:119
  140.6 57.3 %collective-permute-start.21 = (bf16[2560,256]{1,0:T(8,128)(2,1)}, bf16[2560,256]{1,0:T(8,128)(2,1)}, u32[]{:S(2)}, u32[]{:S(2)}) collective-permute-start(bf16[2560,256]{1,0:T(8,128)(2,1)} %collective-permute-done.20.refs_2_), channel_id=1, source_target_pairs={{0,4},{4,0},{1,5},{5,1},{2,6},{6,2},{3,7},{7,3},{8,12},{12,8},{9,1... | collective-permute-start | bytes 3932168 | tf_op jit(solution)/shard_map/ppermute | solution.py:119
  142.1 120.6 %collective-permute-start.19 = (bf16[2560,512]{1,0:T(8,128)(2,1)}, bf16[2560,512]{1,0:T(8,128)(2,1)}, u32[]{:S(2)}, u32[]{:S(2)}) collective-permute-start(bf16[2560,512]{1,0:T(8,128)(2,1)} %copy-done), channel_id=1, source_target_pairs={{0,8},{8,0},{16,24},{24,16},{1,9},{9,1},{17,25},{25,17},{2,10},{10... | collective-permute-start | bytes 7864328 | tf_op jit(solution)/shard_map/ppermute | solution.py:119
  150.1 44.1 %collective-permute-start.13 = (bf16[256,2048]{1,0:T(8,128)(2,1)}, bf16[256,2048]{1,0:T(8,128)(2,1)}, u32[]{:S(2)}, u32[]{:S(2)}) collective-permute-start(bf16[256,2048]{1,0:T(8,128)(2,1)} %collective-permute-done.12.refs_2_), channel_id=1, source_target_pairs={{0,4},{4,0},{1,5},{5,1},{2,6},{6,2},{3,7},{7,3},{8,12},{12,8},{9,1... | collective-permute-start | bytes 3145736 | tf_op jit(solution)/shard_map/ppermute | solution.py:119
  158.9 61.5 %collective-permute-start.14 = (bf16[256,2048]{1,0:T(8,128)(2,1)}, bf16[256,2048]{1,0:T(8,128)(2,1)}, u32[]{:S(2)}, u32[]{:S(2)}) collective-permute-start(bf16[256,2048]{1,0:T(8,128)(2,1)} %collective-permute-done.12.refs_2_), channel_id=1, source_target_pairs={{0,8},{8,0},{16,24},{24,16},{1,9},{9,1},{17,25},{25,17},{2,10},{10... | collective-permute-start | bytes 3145736 | tf_op jit(solution)/shard_map/ppermute | solution.py:119
  158.9 80.3 %collective-permute-start.22 = (bf16[2560,256]{1,0:T(8,128)(2,1)}, bf16[2560,256]{1,0:T(8,128)(2,1)}, u32[]{:S(2)}, u32[]{:S(2)}) collective-permute-start(bf16[2560,256]{1,0:T(8,128)(2,1)} %collective-permute-done.20.refs_2_), channel_id=1, source_target_pairs={{0,8},{8,0},{16,24},{24,16},{1,9},{9,1},{17,25},{25,17},{2,10},{10... | collective-permute-start | bytes 3932168 | tf_op jit(solution)/shard_map/ppermute | solution.py:119
  197.9 67.4 %collective-permute-start.23 = (bf16[2560,256]{1,0:T(8,128)(2,1)}, bf16[2560,256]{1,0:T(8,128)(2,1)}, u32[]{:S(2)}, u32[]{:S(2)}) collective-permute-start(bf16[2560,256]{1,0:T(8,128)(2,1)} %collective-permute-done.21.refs_3_), channel_id=1, source_target_pairs={{0,8},{8,0},{16,24},{24,16},{1,9},{9,1},{17,25},{25,17},{2,10},{10... | collective-permute-start | bytes 3932168 | tf_op jit(solution)/shard_map/ppermute | solution.py:119
  220.4 89.0 %collective-permute-start.24 = (bf16[2,512,512]{2,1,0:T(8,128)(2,1)}, bf16[2,512,512]{2,1,0:T(8,128)(2,1)}, u32[]{:S(2)}, u32[]{:S(2)}) collective-permute-start(bf16[2,512,512]{2,1,0:T(8,128)(2,1)} %get-tuple-element.104.kv), channel_id=1, source_target_pairs={{0,4},{1,5},{2,6},{3,7},{8,12},{9,13},{10,14},{11,15},{16,20},{17,... | collective-permute-start | bytes 3145736 | tf_op jit(solution)/shard_map/ppermute | solution.py:812
  227.4 68.4 %collective-permute-start.17 = (bf16[512,512]{1,0:T(8,128)(2,1)S(1)}, bf16[512,512]{1,0:T(8,128)(2,1)S(1)}, u32[]{:S(2)}, u32[]{:S(2)}) collective-permute-start(bf16[512,512]{1,0:T(8,128)(2,1)S(1)} %copy-done.13), channel_id=1, source_target_pairs={{0,3},{1,0},{2,1},{3,2},{4,7},{5,4},{6,5},{7,6},{8,11},{9,8},{10,9... | collective-permute-start | bytes 1572872 | tf_op jit(solution)/shard_map/ppermute | solution.py:683
  239.2 56.6 %collective-permute-start.18 = (bf16[512,512]{1,0:T(8,128)(2,1)S(1)}, bf16[512,512]{1,0:T(8,128)(2,1)S(1)}, u32[]{:S(2)}, u32[]{:S(2)}) collective-permute-start(bf16[512,512]{1,0:T(8,128)(2,1)S(1)} %copy-done.25), channel_id=1, source_target_pairs={{0,1},{1,2},{2,3},{3,0},{4,5},{5,6},{6,7},{7,4},{8,9},{9,10},{10,1... | collective-permute-start | bytes 1572872 | tf_op jit(solution)/shard_map/ppermute | solution.py:683
  262.7 74.9 %collective-permute-start.29 = (bf16[512,512]{1,0:T(8,128)(2,1)S(1)}, bf16[512,512]{1,0:T(8,128)(2,1)S(1)}, u32[]{:S(2)}, u32[]{:S(2)}) collective-permute-start(bf16[512,512]{1,0:T(8,128)(2,1)S(1)} %copy-done.11), channel_id=1, source_target_pairs={{0,3},{1,0},{2,1},{3,2},{4,7},{5,4},{6,5},{7,6},{8,11},{9,8},{10,9... | collective-permute-start | bytes 1572872 | tf_op jit(solution)/shard_map/ppermute | solution.py:683
  265.2 72.4 %collective-permute-start.30 = (bf16[512,512]{1,0:T(8,128)(2,1)}, bf16[512,512]{1,0:T(8,128)(2,1)S(1)}, u32[]{:S(2)}, u32[]{:S(2)}) collective-permute-start(bf16[512,512]{1,0:T(8,128)(2,1)} %collective-permute-done.28.ca), channel_id=1, source_target_pairs={{0,1},{1,2},{2,3},{3,0},{4,5},{5,6},{6,7},{7,4},{8,9},{9,10},{10,1... | collective-permute-start | bytes 1572872 | tf_op jit(solution)/shard_map/ppermute | solution.py:683
  393.8 43.9 %collective-permute-start.26 = (bf16[512,512]{1,0:T(8,128)(2,1)}, bf16[512,512]{1,0:T(8,128)(2,1)}, u32[]{:S(2)}, u32[]{:S(2)}) collective-permute-start(bf16[512,512]{1,0:T(8,128)(2,1)} %get-tuple-element.130), channel_id=1, source_target_pairs={{0,1},{1,2},{2,3},{3,0},{4,5},{5,6},{6,7},{7,4},{8,9},{9,10},{10,1... | collective-permute-start | bytes 1572872 | tf_op jit(solution)/shard_map/ppermute | solution.py:683
  397.6 43.3 %collective-permute-start.34 = (bf16[2,512,512]{2,1,0:T(8,128)(2,1)}, bf16[2,512,512]{2,1,0:T(8,128)(2,1)S(1)}, u32[]{:S(2)}, u32[]{:S(2)}) collective-permute-start(bf16[2,512,512]{2,1,0:T(8,128)(2,1)} %bitcast.27), channel_id=1, source_target_pairs={{4,0},{5,1},{6,2},{7,3},{12,8},{13,9},{14,10},{15,11},{20,16},{21,... | collective-permute-start | bytes 3145736 | tf_op jit(solution)/shard_map/ppermute | solution.py:835
  404.0 87.6 %collective-permute-start.52 = (bf16[4,512,512]{2,1,0:T(8,128)(2,1)}, bf16[4,512,512]{2,1,0:T(8,128)(2,1)}, u32[]{:S(2)}, u32[]{:S(2)}) collective-permute-start(bf16[4,512,512]{2,1,0:T(8,128)(2,1)} %fusion.4), channel_id=1, source_target_pairs={{0,16},{8,24},{16,0},{24,8},{1,17},{9,25},{17,1},{25,9},{2,18},{10... | collective-permute-start | bytes 6291464 | tf_op jit(solution)/shard_map/ppermute | solution.py:119
  436.3 76.1 %collective-permute-start.37 = (bf16[4,512,512]{2,1,0:T(8,128)(2,1)}, bf16[4,512,512]{2,1,0:T(8,128)(2,1)}, u32[]{:S(2)}, u32[]{:S(2)}) collective-permute-start(bf16[4,512,512]{2,1,0:T(8,128)(2,1)} %fusion.3), channel_id=1, source_target_pairs={{0,16},{8,24},{16,0},{24,8},{1,17},{9,25},{17,1},{25,9},{2,18},{10... | collective-permute-start | bytes 6291464 | tf_op jit(solution)/shard_map/ppermute | solution.py:119
  437.8 93.5 %collective-permute-start.25 = (bf16[512,512]{1,0:T(8,128)(2,1)}, bf16[512,512]{1,0:T(8,128)(2,1)}, u32[]{:S(2)}, u32[]{:S(2)}) collective-permute-start(bf16[512,512]{1,0:T(8,128)(2,1)} %get-tuple-element.128), channel_id=1, source_target_pairs={{0,3},{1,0},{2,1},{3,2},{4,7},{5,4},{6,5},{7,6},{8,11},{9,8},{10,9... | collective-permute-start | bytes 1572872 | tf_op jit(solution)/shard_map/ppermute | solution.py:683
  440.9 94.5 %collective-permute-start.27 = (bf16[512,512]{1,0:T(8,128)(2,1)}, bf16[512,512]{1,0:T(8,128)(2,1)}, u32[]{:S(2)}, u32[]{:S(2)}) collective-permute-start(bf16[512,512]{1,0:T(8,128)(2,1)} %add_convert_fusion.11), channel_id=1, source_target_pairs={{0,1},{1,2},{2,3},{3,0},{4,5},{5,6},{6,7},{7,4},{8,9},{9,10},{10,1... | collective-permute-start | bytes 1572872 | tf_op jit(solution)/shard_map/ppermute | solution.py:683
  491.6 107.3 %collective-permute-start.36 = (bf16[2,4,512,512]{3,2,1,0:T(8,128)(2,1)}, bf16[2,4,512,512]{3,2,1,0:T(8,128)(2,1)}, u32[]{:S(2)}, u32[]{:S(2)}) collective-permute-start(bf16[2,4,512,512]{3,2,1,0:T(8,128)(2,1)} %get-tuple-element.163), channel_id=1, source_target_pairs={{0,8},{8,0},{16,24},{24,16},{1,9},{9,1},{17,25},{25,17},{2,10},{10... | collective-permute-start | bytes 12582920 | tf_op jit(solution)/shard_map/ppermute | solution.py:119
  602.4 67.9 %collective-permute-start.48 = (bf16[4,512,512]{2,1,0:T(8,128)(2,1)}, bf16[4,512,512]{2,1,0:T(8,128)(2,1)}, u32[]{:S(2)}, u32[]{:S(2)}) collective-permute-start(bf16[4,512,512]{2,1,0:T(8,128)(2,1)} %fusion.5), channel_id=1, source_target_pairs={{0,16},{8,24},{16,0},{24,8},{1,17},{9,25},{17,1},{25,9},{2,18},{10... | collective-permute-start | bytes 6291464 | tf_op jit(solution)/shard_map/ppermute | solution.py:119
  (86 other events, 1559.0 us)

commit v3 on v2

v3 whole, which is shorter than its diff:
```python
import functools
import math

import jax
import jax.numpy as jnp
from jax import lax
from jax.experimental import pallas as pl
from jax.experimental.pallas import tpu as pltpu
from jax.sharding import PartitionSpec as P

HEAD_DIM = 64
ROT = 32
D = 2048
N_DP = 4
N_TP = 4
CH = D // N_TP
EPS = 1e-05
NEG = -1e30
VMEM = 56 * 2**20
COST = 0.02

bf16 = jnp.bfloat16
f32 = jnp.float32


def dot_nn(a, b):
    return lax.dot_general(a, b, (((1,), (0,)), ((), ())), preferred_element_type=f32)


def dot_nt(a, b):
    return lax.dot_general(a, b, (((1,), (1,)), ((), ())), preferred_element_type=f32)


def dot_tn(a, b):
    return lax.dot_general(a, b, (((0,), (0,)), ((), ())), preferred_element_type=f32)


def spec(block, index):
    return pl.BlockSpec(block, index)


def whole(*block):
    zeros = (0,) * len(block)
    return pl.BlockSpec(block, lambda g, *_: zeros)


def one_of(s, *block):
    zeros = (0,) * len(block)
    return pl.BlockSpec((None, *block), lambda g, *_: (s, *zeros))


def shaped(shape, dtype=bf16):
    return jax.ShapeDtypeStruct(tuple(shape), dtype)


HBM = pl.BlockSpec(memory_space=pltpu.HBM)


def call(body, name, grid, info, ins, in_specs, outs, out_specs, flops, scratch=(), deps=()):
    moved = sum(math.prod(a.shape) * a.dtype.itemsize for a in (*ins, *jax.tree.leaves(outs)))
    first, last = 1 + len(ins), 1 + len(ins) + len(deps)

    def without_deps(*refs):
        body(*refs[:first], *refs[last:])

    return pl.pallas_call(
        without_deps,
        grid_spec=pltpu.PrefetchScalarGridSpec(
            num_scalar_prefetch=1,
            grid=(grid,),
            in_specs=[*in_specs, *[HBM] * len(deps)],
            out_specs=out_specs,
            scratch_shapes=list(scratch),
        ),
        out_shape=outs,
        compiler_params=pltpu.CompilerParams(vmem_limit_bytes=VMEM),
        cost_estimate=pl.CostEstimate(
            flops=int(flops * COST), bytes_accessed=int(moved * COST), transcendentals=0
        ),
        name=name,
    )(info, *ins, *deps)


def tie(value, *deps):
    def nothing(*refs):
        del refs

    return pl.pallas_call(
        nothing,
        in_specs=[HBM] * (1 + len(deps)),
        out_specs=HBM,
        out_shape=shaped(value.shape, value.dtype),
        input_output_aliases={0: 0},
        cost_estimate=pl.CostEstimate(flops=0, bytes_accessed=0, transcendentals=0),
        name="tie",
    )(value, *deps)


def columns(index, width=CH):
    return pl.ds(pl.multiple_of(index * width, width), width)


def layout_of(two):
    if two:
        halves = [("c", CH // 2), ("other", CH // 2)]
    else:
        halves = [("", CH)]
    return [(0, "", CH), (1, "", CH)] + [(r, *half) for r in (2, 3) for half in halves]


def piece_offset(info, half):
    return {"": 0, "c": info[1], "other": 1 - info[1]}[half] * (CH // 2)


def piece_window(info, piece):
    r, half, size = piece
    start = (info[2] ^ r) * CH + piece_offset(info, half)
    return pl.ds(pl.multiple_of(start, size), size)


class Clock:
    def __init__(self):
        self.marks = ()

    def go(self, value):
        return tie(value, *self.marks) if self.marks else value

    def sync(self, *arrays):
        def nothing(*refs):
            del refs

        self.marks = (
            pl.pallas_call(
                nothing,
                in_specs=[HBM] * (len(arrays) + len(self.marks)),
                out_specs=HBM,
                out_shape=shaped((8, 128), f32),
                cost_estimate=pl.CostEstimate(flops=0, bytes_accessed=0, transcendentals=0),
                name="sync",
            )(*arrays, *self.marks),
        )


def swap(array, axis, bit, size):
    return lax.ppermute(array, axis, [(i, i ^ bit) for i in range(size)])


class Shards:
    def __init__(self, own, axis, d, c, two, made=True):
        self.own, self.two, self.made = own, two, made
        size = own.shape[axis] // 2
        self.part = lax.dynamic_slice_in_dim(own, c * size, size, axis) if two else own

    def near_core(self, clock):
        self.own = clock.go(self.own) if self.made else self.own
        self.near = swap(self.own, "dp", 1, N_DP)

    def over_x(self, clock):
        self.first = swap(clock.go(self.part), "dp", 2, N_DP)

    def over_y(self, clock):
        self.first = clock.go(self.first)
        self.second = swap(self.first, "ctx", 1, 2) if self.two else self.first

    def far_core(self, clock):
        self.first = clock.go(self.first)
        far = [self.first]
        if self.two:
            self.second = clock.go(self.second)
            far.append(self.second)
        self.far_near = [swap(a, "dp", 1, N_DP) for a in far]
        self.pieces = [self.own, self.near, *far, *self.far_near]


def rotary_tables(starts, positions):
    before = starts[:, None, :] <= positions[None, :, None]
    opening = jnp.max(jnp.where(before, starts[:, None, :], 0), axis=2)
    relative = (positions[None, :] - opening).astype(f32)
    half = ROT // 2
    lane = jnp.arange(128, dtype=jnp.int32) % HEAD_DIM
    frequency = jnp.exp((lane % half).astype(f32) * (-math.log(10000.0) / half))
    angles = relative[:, :, None] * jnp.where(lane < ROT, frequency, 0.0)
    sine = jnp.sin(angles)
    return (
        jnp.cos(angles),
        jnp.where(lane < half, -sine, 0.0),
        jnp.where(lane >= half, sine, 0.0),
    ), opening


def turn(x, own, up, down):
    return x * own + pltpu.roll(x, 112, 1) * up + pltpu.roll(x, 16, 1) * down


def turn_back(x, own, up, down):
    return x * own - pltpu.roll(x, 112, 1) * up - pltpu.roll(x, 16, 1) * down


def stream_pieces(layout, info, sources, held, sems, axis, blocks):
    j = pl.program_id(0)

    def copies(block):
        cut = pl.ds(pl.multiple_of(block * CH, CH), CH)
        for n, (piece, source) in enumerate(zip(layout, sources)):
            window = piece_window(info, piece)
            if axis == 0:
                pair = source.at[:, cut], held.at[window, cut]
            else:
                pair = source.at[cut, :], held.at[cut, window]
            yield pltpu.make_async_copy(*pair, sems.at[block, n])

    @pl.when(j == 0)
    def _():
        for block in range(blocks):
            for copy in copies(block):
                copy.start()

    for copy in copies(j):
        copy.wait()


def norm_qkv_body(layout, info, x0, xa, xc, xb, gain, shift, bias, own, up, down, *refs):
    *w, normed, avg, inv, q, kv0, kv1, held, sems = refs
    j = pl.program_id(0)
    t = info[0]
    seqs, rows, _ = x0.shape
    stream_pieces(layout, info, w, held, sems, 0, 3)

    @pl.when(j == 0)
    def _():
        parts = [(x0, t), (xa, (t + 3) % N_TP), (xc, (t + 1) % N_TP), (xb, (t + 2) % N_TP)]
        tile = 128

        def rows_of(i, carry):
            s = i // (rows // tile)
            window = pl.ds(pl.multiple_of((i % (rows // tile)) * tile, tile), tile)
            x = [part[s, window, :].astype(f32) for part, _ in parts]
            average = sum(jnp.sum(a, axis=1, keepdims=True) for a in x) * (1.0 / D)
            x = [a - average for a in x]
            variance = sum(jnp.sum(a * a, axis=1, keepdims=True) for a in x) * (1.0 / D)
            root = lax.rsqrt(variance + EPS)
            avg[s, window, :] = average
            inv[s, window, :] = root
            for a, (_, index) in zip(x, parts):
                at = columns(index)
                y = a * root * gain[:, at].astype(f32) + shift[:, at].astype(f32)
                normed[s, window, at] = y.astype(bf16)
            return carry

        lax.fori_loop(0, seqs * rows // tile, rows_of, 0)

    for s, kv in ((0, kv0), (1, kv1)):
        y = dot_nn(normed[s], held[:, columns(j)]) + bias[...].astype(f32)

        def rotated(s=s, y=y):
            parts = [
                turn(y[:, 128 * n : 128 * n + 128], own[s], up[s], down[s])
                for n in range(CH // 128)
            ]
            return jnp.concatenate(parts, axis=1).astype(bf16)

        @pl.when(j == 0)
        def _(s=s, rotated=rotated):
            q[s] = rotated()

        @pl.when(j == 1)
        def _(kv=kv, rotated=rotated):
            kv[0] = rotated()

        @pl.when(j == 2)
        def _(kv=kv, y=y):
            kv[0] = y.astype(bf16)


def norm_qkv(layout, info, parts, gain, shift, w, bias, tables, deps=()):
    seqs, rows, _ = parts[0].shape
    outs = (
        shaped((seqs, rows, D)),
        shaped((seqs, rows, 1), f32),
        shaped((seqs, rows, 1), f32),
        shaped((seqs, rows, CH)),
        shaped((2, rows, CH)),
        shaped((2, rows, CH)),
    )
    pair = spec((1, rows, CH), lambda j, *_: (jnp.maximum(j - 1, 0), 0, 0))
    return call(
        functools.partial(norm_qkv_body, layout),
        "norm_qkv",
        3,
        info,
        (*parts, gain, shift, bias, *tables, *w),
        [whole(seqs, rows, CH)] * 4
        + [whole(1, D)] * 2
        + [spec((1, CH), lambda j, *_: (0, j))]
        + [whole(seqs, rows, 128)] * 3
        + [HBM] * len(w),
        outs,
        [
            whole(seqs, rows, D),
            whole(seqs, rows, 1),
            whole(seqs, rows, 1),
            whole(seqs, rows, CH),
            pair,
            pair,
        ],
        2 * seqs * rows * D * 3 * CH,
        [pltpu.VMEM((D, 3 * CH), bf16), pltpu.SemaphoreType.DMA((3, len(w)))],
        deps=deps,
    )


def mlp_up_body(layout, info, normed, bias, *refs):
    *w, hidden, grad, held, sems = refs
    j = pl.program_id(0)
    stream_pieces(layout, info, w, held, sems, 0, held.shape[1] // CH)
    root = math.sqrt(2.0 / math.pi)
    for s in range(normed.shape[0]):
        u = dot_nn(normed[s], held[:, columns(j)]) + bias[...].astype(f32)
        square = u * u
        t = jnp.tanh(u * (root + (root * 0.044715) * square))
        half = 0.5 + 0.5 * t
        hidden[s] = (u * half).astype(bf16)
        slope = root + (3 * 0.044715 * root) * square
        grad[s] = (half + (0.5 * u) * (1.0 - t * t) * slope).astype(bf16)


def mlp_up(layout, info, normed, w, bias, deps=()):
    seqs, rows, _ = normed.shape
    units = w[0].shape[1]
    block = spec((seqs, rows, CH), lambda j, *_: (0, 0, j))
    return call(
        functools.partial(mlp_up_body, layout),
        "mlp_up",
        units // CH,
        info,
        (normed, bias, *w),
        [whole(seqs, rows, D), spec((1, CH), lambda j, *_: (0, j))] + [HBM] * len(w),
        (shaped((seqs, rows, units)),) * 2,
        [block] * 2,
        2 * seqs * rows * D * units,
        [pltpu.VMEM((D, units), bf16), pltpu.SemaphoreType.DMA((units // CH, len(w)))],
        deps=deps,
    )


def back_out_body(layout, info, c0, ca, cc, cb, slope, *refs):
    *w, cf, bias_grad, datt, dup, held, sems = refs
    j = pl.program_id(0)
    t = info[0]
    stream_pieces(layout, info, w, held, sems, 1, held.shape[0] // CH)

    @pl.when(j == 0)
    def _():
        for part, step in ((c0, 0), (ca, 3), (cc, 1), (cb, 2)):
            cf[:, columns((t + step) % N_TP)] = part[...]
        bias_grad[...] = jnp.sum(c0[...].astype(f32), axis=0, keepdims=True)

    y = dot_nt(cf[...], held[columns(j), :])

    @pl.when(j == 0)
    def _():
        datt[...] = y.astype(bf16)

    @pl.when(j > 0)
    def _():
        dup[...] = (y * slope[...].astype(f32)).astype(bf16)


def back_out(layout, info, s, parts, w, slope, deps=()):
    _, rows, units = slope.shape
    later = spec((rows, CH), lambda j, *_: (0, jnp.maximum(j - 1, 0)))
    slopes = spec((None, rows, CH), lambda j, *_: (s, 0, jnp.maximum(j - 1, 0)))
    return call(
        functools.partial(back_out_body, layout),
        "back_out",
        1 + units // CH,
        info,
        (*parts, slope, *w),
        [whole(rows, CH)] * 4 + [slopes] + [HBM] * len(w),
        (
            shaped((rows, D)),
            shaped((1, CH), f32),
            shaped((rows, CH)),
            shaped((rows, units)),
        ),
        [whole(rows, D), whole(1, CH), whole(rows, CH), later],
        2 * rows * D * (CH + units),
        [
            pltpu.VMEM((CH + units, D), bf16),
            pltpu.SemaphoreType.DMA((1 + units // CH, len(w))),
        ],
        deps=deps,
    )


def attention_body(
    blocks, info, low, q, kv, kvp, do, own, up, down, ownp, upp, downp,
    att, dq, dkv, dkvp, scores, probs,
):
    rows = q.shape[0]
    before, start = info[1], info[1] * rows
    lane = lax.broadcasted_iota(jnp.int32, (rows, 128), 1)
    key_row = lax.broadcasted_iota(jnp.int32, (rows, 1), 0)
    query_at = start + lax.broadcasted_iota(jnp.int32, (1, rows), 1)
    first = low[0]
    do_t = do[...].astype(f32).T
    nothing = jnp.zeros((), bf16)
    outputs = []
    for head in range(2):
        mine = (lane < HEAD_DIM) if head == 0 else (lane >= HEAD_DIM)
        half = slice(HEAD_DIM * head, HEAD_DIM * (head + 1))
        qh = jnp.where(mine, q[...] * jnp.asarray(HEAD_DIM**-0.5, bf16), nothing)
        dh = jnp.where(mine, do[...], nothing)

        key_at = start + key_row
        s = dot_nt(kv[0], qh)
        s = jnp.where((key_at >= first) & (key_at <= query_at), s, NEG)
        scores[blocks] = s
        peak = jnp.max(s, axis=0, keepdims=True)

        def score(n, peak):
            s = dot_nt(kvp[n, 0], qh)
            s = jnp.where(n * rows + key_row >= first, s, NEG)
            scores[n] = s
            return jnp.maximum(peak, jnp.max(s, axis=0, keepdims=True))

        peak = lax.fori_loop(0, before, score, peak)

        def expo(n, total):
            e = jnp.exp(scores[n] - peak)
            scores[n] = e
            return total + jnp.sum(e, axis=0, keepdims=True)

        total = expo(blocks, jnp.zeros((1, rows), f32))
        total = lax.fori_loop(0, before, expo, total)
        scale = 1.0 / total

        def weigh(n, values):
            p = (scores[n] * scale).astype(bf16)
            probs[n] = p
            return dot_tn(values, p)

        out_t = weigh(blocks, kv[1])
        out_t = lax.fori_loop(0, before, lambda n, acc: acc + weigh(n, kvp[n, 1]), out_t)
        delta = jnp.sum(out_t[half] * do_t[half], axis=0, keepdims=True)

        def back(n, keys, values):
            dp = dot_nt(values, dh)
            ds = ((scores[n] * scale) * (dp - delta)).astype(bf16)
            return dot_nn(ds, qh), dot_nn(probs[n], dh), dot_tn(keys, ds)

        dk, dv, dq_t = back(blocks, kv[0], kv[1])
        if head == 0:
            dk_sum, dv_sum = dk, dv
        else:
            dk_sum, dv_sum = dk_sum + dk, dv_sum + dv

        def back_before(n, acc):
            dk, dv, more = back(n, kvp[n, 0], kvp[n, 1])
            dk = turn_back(dk, ownp[n], upp[n], downp[n])
            if head == 0:
                dkvp[n, 0] = dk.astype(bf16)
                dkvp[n, 1] = dv.astype(bf16)
            else:
                dkvp[n, 0] = (dkvp[n, 0].astype(f32) + dk).astype(bf16)
                dkvp[n, 1] = (dkvp[n, 1].astype(f32) + dv).astype(bf16)
            return acc + more

        dq_t = lax.fori_loop(0, before, back_before, dq_t)
        outputs.append((out_t[half], dq_t[half]))

    def clear(n, carry):
        dkvp[n] = jnp.zeros(dkvp.shape[1:], bf16)
        return carry

    lax.fori_loop(before, blocks, clear, 0)
    att[...] = jnp.concatenate([outputs[0][0], outputs[1][0]], axis=0).T.astype(bf16)
    grad = jnp.concatenate([outputs[0][1], outputs[1][1]], axis=0).T * HEAD_DIM**-0.5
    dq[...] = turn_back(grad, own[...], up[...], down[...]).astype(bf16)
    dkv[0] = turn_back(dk_sum, own[...], up[...], down[...]).astype(bf16)
    dkv[1] = dv_sum.astype(bf16)


def attention_two_body(
    info, low, q, kv, kvp, do, own, up, down, ownp, upp, downp, att, dq, dkv, dkvp
):
    rows = q.shape[0]
    part = rows // 2
    before, start = info[1], info[1] * rows

    def tail(x, skipped):
        return x[:, skipped:] if skipped else x

    def merge(acc, x, skipped, op):
        if acc is None:
            return x
        if not skipped:
            return op(acc, x)
        return jnp.concatenate([acc[:, :skipped], op(acc[:, skipped:], x)], axis=1)

    def run(with_before):
        lane = lax.broadcasted_iota(jnp.int32, (rows, 128), 1)
        key_row = lax.broadcasted_iota(jnp.int32, (part, 1), 0)
        query_at = start + lax.broadcasted_iota(jnp.int32, (1, rows), 1)
        first = low[...]
        do_t = do[...].astype(f32).T
        nothing = jnp.zeros((), bf16)
        blocks = []
        for n in range(2):
            if with_before:
                blocks.append((kvp.at[0], n * part, 0, False))
        for n in range(2):
            blocks.append((kv, n * part, n * part, True))
        outputs = []
        dk_sum, dv_sum = [0.0] * len(blocks), [0.0] * len(blocks)
        for head in range(2):
            mine = (lane < HEAD_DIM) if head == 0 else (lane >= HEAD_DIM)
            half = slice(HEAD_DIM * head, HEAD_DIM * (head + 1))
            qh = jnp.where(mine, q[...] * jnp.asarray(HEAD_DIM**-0.5, bf16), nothing)
            dh = jnp.where(mine, do[...], nothing)
            scores, peak = [], None
            for ref, row, skip, here in blocks:
                s = dot_nt(ref[0, row : row + part], qh[skip:])
                key_at = (start if here else start - rows) + row + key_row
                allowed = key_at >= tail(first, skip)
                if here:
                    allowed = allowed & (key_at <= tail(query_at, skip))
                s = jnp.where(allowed, s, NEG)
                scores.append(s)
                peak = merge(peak, jnp.max(s, axis=0, keepdims=True), skip, jnp.maximum)
            terms, total = [], None
            for s, (_, _, skip, _) in zip(scores, blocks):
                e = jnp.exp(s - tail(peak, skip))
                terms.append(e)
                total = merge(total, jnp.sum(e, axis=0, keepdims=True), skip, jnp.add)
            scale = 1.0 / total
            probs, rounded, out_t = [], [], None
            for e, (ref, row, skip, _) in zip(terms, blocks):
                p = e * tail(scale, skip)
                pb = p.astype(bf16)
                probs.append(p)
                rounded.append(pb)
                out_t = merge(out_t, dot_tn(ref[1, row : row + part], pb), skip, jnp.add)
            delta = jnp.sum(out_t[half] * do_t[half], axis=0, keepdims=True)
            dq_t = None
            for n, (ref, row, skip, _) in enumerate(blocks):
                dp = dot_nt(ref[1, row : row + part], dh[skip:])
                ds = (probs[n] * (dp - tail(delta, skip))).astype(bf16)
                dv_sum[n] = dv_sum[n] + dot_nn(rounded[n], dh[skip:])
                dk_sum[n] = dk_sum[n] + dot_nn(ds, qh[skip:])
                dq_t = merge(dq_t, dot_tn(ref[0, row : row + part], ds), skip, jnp.add)
            outputs.append((out_t[half], dq_t[half]))
        att[...] = jnp.concatenate([outputs[0][0], outputs[1][0]], axis=0).T.astype(bf16)
        grad = jnp.concatenate([outputs[0][1], outputs[1][1]], axis=0).T * HEAD_DIM**-0.5
        dq[...] = turn_back(grad, own[...], up[...], down[...]).astype(bf16)
        dk = jnp.concatenate(dk_sum[-2:], axis=0)
        dkv[0] = turn_back(dk, own[...], up[...], down[...]).astype(bf16)
        dkv[1] = jnp.concatenate(dv_sum[-2:], axis=0).astype(bf16)
        if with_before:
            dk = jnp.concatenate(dk_sum[:2], axis=0)
            dkvp[0, 0] = turn_back(dk, ownp[0], upp[0], downp[0]).astype(bf16)
            dkvp[0, 1] = jnp.concatenate(dv_sum[:2], axis=0).astype(bf16)
        else:
            dkvp[...] = jnp.zeros(dkvp.shape, bf16)

    @pl.when(before == 0)
    def _():
        run(False)

    @pl.when(before > 0)
    def _():
        run(True)


def attention(info, s, low, q, kv, kvp, do, tables, tables_before, deps=()):
    _, rows, width = q.shape
    blocks = kvp.shape[0]
    token = spec((rows, 128), lambda g, *_: (0, g))
    query = spec((None, rows, 128), lambda g, *_: (s, 0, g))
    pair = spec((2, rows, 128), lambda g, *_: (0, 0, g))
    pairs = spec((blocks, 2, rows, 128), lambda g, *_: (0, 0, 0, g))
    return call(
        attention_two_body if blocks == 1 else functools.partial(attention_body, blocks),
        "attention",
        width // 128,
        info,
        (low, q, kv, kvp, do, *tables, *tables_before),
        [one_of(s, 1, rows), query, pair, pairs, token]
        + [one_of(s, rows, 128)] * 3
        + [one_of(s, blocks, rows, 128)] * 3,
        (
            shaped((rows, width)),
            shaped((rows, width)),
            shaped((2, rows, width)),
            shaped((blocks, 2, rows, width)),
        ),
        [token, token, pair, pairs],
        48 * rows * rows * width,
        []
        if blocks == 1
        else [
            pltpu.VMEM((blocks + 1, rows, rows), f32),
            pltpu.VMEM((blocks + 1, rows, rows), bf16),
        ],
        deps=deps,
    )


TAIL = 16


def fetch_pieces(layout, sources, targets, sems, axis):
    copies = [[] for _ in range(N_DP)]
    at = [r * CH for r in range(N_DP)]
    n = 0
    for group, target in zip(sources, targets):
        at = [r * CH for r in range(N_DP)]
        for (r, _, size), source in zip(layout, group):
            window = pl.ds(at[r], size)
            place = target.at[window, :] if axis == 0 else target.at[:, window]
            copies[r].append(pltpu.make_async_copy(source, place, sems.at[n]))
            at[r] += size
            n += 1
    return copies


def with_chunk(layout, info, copies, work):
    j = pl.program_id(0)

    @pl.when(j == 0)
    def _():
        for group in copies:
            for copy in group:
                copy.start()

    for r in range(N_DP):

        @pl.when(j == r)
        def _(r=r):
            for copy in copies[r]:
                copy.wait()
            at = r * CH
            for s, half, size in layout:
                if s == r:
                    offset = pl.multiple_of(piece_offset(info, half), size)
                    work(pl.ds(at, size), pl.ds(offset, size))
                    at += size


def chunk_now(info):
    return ((info[2] ^ pl.program_id(0)) + N_TP - info[0]) % N_TP


def out_body(layout, info, att, hidden, *refs):
    count = len(layout)
    w, outs = refs[:count], refs[count : count + N_TP]
    held, y, sems = refs[count + N_TP :]

    def work(place, window):
        part = dot_nn(att[...], held[:CH, place]) + dot_nn(hidden[...], held[CH:, place])
        y[:, window] = part.astype(bf16)

    with_chunk(layout, info, fetch_pieces(layout, [w], [held], sems, 1), work)
    for r in range(N_TP):

        @pl.when(chunk_now(info) == r)
        def _(r=r):
            outs[r][...] = y[...]


def project_out(layout, info, s, att, hidden, w, deps=()):
    _, rows, units = hidden.shape
    return call(
        functools.partial(out_body, layout),
        "project_out",
        N_TP,
        info,
        (att, hidden, *w),
        [whole(rows, CH), one_of(s, rows, units)] + [HBM] * len(w),
        (shaped((rows, CH)),) * N_TP,
        [whole(rows, CH)] * N_TP,
        2 * rows * D * (CH + units),
        [
            pltpu.VMEM((CH + units, D), bf16),
            pltpu.VMEM((rows, CH), bf16),
            pltpu.SemaphoreType.DMA((len(w),)),
        ],
        deps=deps,
    )


def back_in_body(layout, info, x0, xa, xc, xb, dq, dkv, dup, gain, avg, inv, *refs):
    count = len(layout)
    wq, wu = refs[:count], refs[count : 2 * count]
    *chunks, held_q, held_u, y, xs, row_sums, column_sums, sems = refs[2 * count :]
    j = pl.program_id(0)
    rows = dq.shape[0]

    def work(place, window):
        part = dot_nt(dup[...], held_u[place, :])
        part = part + dot_nt(dq[...], held_q[place, :CH])
        part = part + dot_nt(dkv[0], held_q[place, CH : 2 * CH])
        y[:, window] = part + dot_nt(dkv[1], held_q[place, 2 * CH :])

    copies = fetch_pieces(layout, [wq, wu], [held_q, held_u], sems, 0)
    with_chunk(layout, info, copies, work)
    for r, part in enumerate((x0, xc, xb, xa)):

        @pl.when(chunk_now(info) == r)
        def _(r=r, part=part):
            chunks[r][:rows, :] = y[...].astype(bf16)
            xs[...] = part[...]

    total = y[...]
    standard = (xs[...].astype(f32) - avg[...]) * inv[...]
    cross = total * standard
    weight = gain[...].astype(f32)

    @pl.when(j == 0)
    def _():
        row_sums[...] = jnp.zeros(row_sums.shape, f32)
        column_sums[...] = jnp.zeros(column_sums.shape, f32)

    both = jnp.concatenate(
        [jnp.sum(cross, axis=0, keepdims=True), jnp.sum(total, axis=0, keepdims=True)], axis=0
    )
    column_sums[chunk_now(info), 0:2, :] = both
    row_sums[:, 0:1] += jnp.sum(total * weight, axis=1, keepdims=True)
    row_sums[:, 1:2] += jnp.sum(cross * weight, axis=1, keepdims=True)

    @pl.when(j == N_TP - 1)
    def _():
        turned = row_sums[...].T[: TAIL // 2]
        for r, chunk in enumerate(chunks):
            chunk[rows:, :] = jnp.concatenate([turned, column_sums[r]], axis=0).astype(bf16)


def back_in(layout, info, s, parts, dq, dkv, dup, wq, wu, gain, avg, inv, deps=()):
    rows, units = dup.shape
    return call(
        functools.partial(back_in_body, layout),
        "back_in",
        N_TP,
        info,
        (*parts, dq, dkv, dup, gain, avg, inv, *wq, *wu),
        [one_of(s, rows, CH)] * 4
        + [
            whole(rows, CH),
            whole(2, rows, CH),
            whole(rows, units),
            spec((1, CH), lambda j, info: (0, info[2] ^ j)),
            one_of(s, rows, 1),
            one_of(s, rows, 1),
        ]
        + [HBM] * (2 * len(wq)),
        (shaped((rows + TAIL, CH)),) * N_TP,
        [whole(rows + TAIL, CH)] * N_TP,
        2 * rows * D * (3 * CH + units),
        [
            pltpu.VMEM((D, 3 * CH), bf16),
            pltpu.VMEM((D, units), bf16),
            pltpu.VMEM((rows, CH), f32),
            pltpu.VMEM((rows, CH), bf16),
            pltpu.VMEM((rows, 128), f32),
            pltpu.VMEM((N_TP, TAIL // 2, CH), f32),
            pltpu.SemaphoreType.DMA((2 * len(wq),)),
        ],
        deps=deps,
    )


KEPT = ((0, 0), (2, 1))
GIVEN = ((1, 0), (3, 1))


def grad_up_body(info, normed, g0, g1, kept, given, sums):
    d = info[2]
    rights = (g0[...], g1[...])
    store_by_rows(d, normed, rights, kept, given)
    sums[...] = sum(jnp.sum(b.astype(f32), axis=0, keepdims=True) for b in rights)


def grad_up(info, normed, dup, n, deps=()):
    rows = dup[0].shape[0]
    block = spec((rows, CH), lambda j, *_: (0, 2 * n + j))
    message = spec((2, 1, CH, CH), lambda j, *_: (0, j, 0, 0))
    return call(
        grad_up_body,
        "grad_up",
        2,
        info,
        (normed, *dup),
        [whole(2, rows, D)] + [block] * 2,
        (shaped((2, 2, CH, CH)),) * 2 + (shaped((1, 2 * CH), f32),),
        [message, message, spec((1, CH), lambda j, *_: (0, j))],
        8 * rows * D * CH,
        deps=deps,
    )


def grad_down_body(info, hidden, c0, c1, kept, given):
    j = pl.program_id(0)
    y = (dot_tn(hidden[0], c0[...]) + dot_tn(hidden[1], c1[...])).astype(bf16)

    def store(target):
        for n in range(target.shape[1]):
            target[0, n] = y[CH * n : CH * (n + 1), :]

    @pl.when(j < 2)
    def _():
        store(given)

    @pl.when(j >= 2)
    def _():
        store(kept)


def grad_down(info, hidden, ct, deps=()):
    _, rows, units = hidden.shape
    count = units // CH
    block = spec(
        (rows, CH),
        lambda j, info: (0, info[2] ^ jnp.where(j < 2, 2 * j + 1, 2 * j - 4)),
    )
    return call(
        grad_down_body,
        "grad_down",
        N_DP,
        info,
        (hidden, *ct),
        [whole(2, rows, units)] + [block] * 2,
        (shaped((2, count, CH, CH)),) * 2,
        [
            spec((1, count, CH, CH), lambda j, *_: (jnp.maximum(j - 2, 0), 0, 0, 0)),
            spec((1, count, CH, CH), lambda j, *_: (jnp.minimum(j, 1), 0, 0, 0)),
        ],
        4 * rows * D * units,
        deps=deps,
    )


def store_by_rows(d, lefts, rights, kept, given):
    for target, which in ((given, GIVEN), (kept, KEPT)):
        for r, at in which:
            window = columns(d ^ r)
            y = sum(dot_tn(lefts[s, :, window], b) for s, b in enumerate(rights))
            target[at, 0] = y.astype(bf16)


def grad_out_query_body(info, normed, c0, c1, a0, a1, q0, q1, kept, given, sums):
    j = pl.program_id(0)
    d = info[2]

    @pl.when(j == 0)
    def _():
        lefts = (a0[...], a1[...])
        for target, which in ((given, GIVEN), (kept, KEPT)):
            for r, at in which:
                window = columns(d ^ r)
                y = sum(dot_tn(a, b[:, window]) for a, b in zip(lefts, (c0, c1)))
                target[at, 0] = y.astype(bf16)

    @pl.when(j == 1)
    def _():
        rights = (q0[...], q1[...])
        store_by_rows(d, normed, rights, kept, given)
        sums[...] = sum(jnp.sum(b.astype(f32), axis=0, keepdims=True) for b in rights)


def grad_out_query(info, normed, ct, att, dq, deps=()):
    rows = normed.shape[1]
    message = spec((2, 1, CH, CH), lambda j, *_: (0, j, 0, 0))
    return call(
        grad_out_query_body,
        "grad_out_query",
        2,
        info,
        (normed, *ct, *att, *dq),
        [whole(2, rows, D)] + [whole(rows, D)] * 2 + [whole(rows, CH)] * 4,
        (shaped((2, 2, CH, CH)),) * 2 + (shaped((1, CH), f32),),
        [message, message, whole(1, CH)],
        4 * rows * D * 2 * CH,
        deps=deps,
    )


def grad_key_value_body(info, normed, kv0, kv1, kept, given, sums):
    rights = (kv0[0], kv1[0])
    store_by_rows(info[2], normed, rights, kept, given)
    sums[0] = sum(jnp.sum(b.astype(f32), axis=0, keepdims=True) for b in rights)


def grad_key_value(info, normed, dkv, deps=()):
    rows = normed.shape[1]
    message = spec((2, 1, CH, CH), lambda j, *_: (0, j, 0, 0))
    pair = spec((1, rows, CH), lambda j, *_: (j, 0, 0))
    return call(
        grad_key_value_body,
        "grad_key_value",
        2,
        info,
        (normed, *dkv),
        [whole(2, rows, D)] + [pair] * 2,
        (shaped((2, 2, CH, CH)),) * 2 + (shaped((2, 1, CH), f32),),
        [message, message, spec((1, 1, CH), lambda j, *_: (j, 0, 0))],
        4 * rows * D * 2 * CH,
        deps=deps,
    )


def ring(array, step):
    return lax.ppermute(array, "tp", [(i, (i + step) % N_TP) for i in range(N_TP)])


class Gather:
    def __init__(self, own):
        self.own = own

    def forth(self, clock):
        self.own = clock.go(self.own)
        self.behind = ring(self.own, 1)

    def back(self):
        self.ahead = ring(self.own, -1)

    def sides(self, clock):
        self.forth(clock)
        self.ahead = ring(self.own, -1)

    def onward(self, clock):
        self.behind = clock.go(self.behind)
        self.far = ring(self.behind, 1)
        self.parts = (self.own, self.behind, self.ahead, self.far)


class Scatter:
    def __init__(self, chunks, clock):
        self.own, self.share, far, self.given = chunks
        self.far = ring(clock.go(far), 1)

    def backward(self, clock):
        self.back = ring(clock.go(self.given), -1)

    def onward(self, clock):
        both = (self.share.astype(f32) + self.far.astype(f32)).astype(bf16)
        self.near = ring(clock.go(both), 1)

    def total(self, clock):
        return self.own.astype(f32) + self.back.astype(f32) + clock.go(self.near).astype(f32)


class Reduction:
    def __init__(self, kept, given, clock, two):
        self.kept, self.two = kept, two
        self.got = swap(clock.go(given), "dp", 1, N_DP)
        self.moved, self.here, self.there = {}, {}, {}

    def add(self):
        total = (self.kept[1].astype(f32) + self.got[1].astype(f32)).astype(bf16)
        self.across = [total[n : n + 2] for n in range(0, total.shape[0], 2)]

    def over_x(self, n, clock):
        self.moved[n] = swap(clock.go(self.across[n]), "dp", 2, N_DP)

    def over_y(self, n, clock):
        at = slice(2 * n, 2 * n + 2)
        parts = (self.kept[0, at], self.got[0, at], clock.go(self.moved[n]))
        here = sum(a.astype(f32) for a in parts).astype(bf16)
        self.here[n] = here
        self.there[n] = swap(here, "ctx", 1, 2) if self.two else lax.psum(here, "ctx")

    def result(self, clock):
        blocks = []
        for n in sorted(self.here):
            total = clock.go(self.there[n]).astype(f32)
            if self.two:
                total = total + self.here[n].astype(f32)
            blocks += [*total]
        return blocks


def body(
    block_in,
    doc_starts,
    query_weight,
    key_weight,
    value_weight,
    output_weight,
    up_weight,
    down_weight,
    query_bias,
    key_bias,
    value_bias,
    up_bias,
    output_bias,
    norm_gain,
    norm_shift,
    cotangent,
):
    seqs, rows, _ = block_in.shape
    d, c, t = lax.axis_index("dp"), lax.axis_index("ctx"), lax.axis_index("tp")
    n_ctx = lax.axis_size("ctx")
    two = n_ctx == 2
    info = jnp.stack([t, c, d]).astype(jnp.int32)

    clock = Clock()

    x = Gather(block_in)
    x.forth(clock)
    small = jnp.concatenate(
        [query_bias, key_bias, value_bias, up_bias, output_bias, norm_gain, norm_shift]
    )
    size = small.size
    near = swap(small, "dp", 1, N_DP)
    flip = (d & 1) == 1
    pair = jnp.concatenate([jnp.where(flip, near, small), jnp.where(flip, small, near)])
    across = swap(pair, "dp", 2, N_DP)
    flip = (d & 2) == 2
    small_here = jnp.concatenate([jnp.where(flip, across, pair), jnp.where(flip, pair, across)])
    small_here = small_here.reshape(N_DP, size)

    def small_of(first, length):
        return small_here[:, first : first + length].reshape(1, -1)

    share = query_bias.size
    share_units = up_bias.size
    qkv_bias = jnp.concatenate([small_of(n * share, share) for n in range(3)], axis=1)
    up_shift = small_of(3 * share, share_units)
    output_shift = small_of(3 * share + share_units, share)
    gain_here = small_of(4 * share + share_units, share)
    shift_here = small_of(5 * share + share_units, share)
    both = jnp.concatenate([gain_here, shift_here], axis=0)
    others = [ring(both, -r) for r in range(1, N_TP)]
    wq_shard = jnp.concatenate([query_weight, key_weight, value_weight], axis=1)
    shards_q = Shards(tie(wq_shard, across), 0, d, c, two)
    shards_q.over_x(clock)
    shards_u = Shards(up_weight, 0, d, c, two, made=False)
    wo_shard = jnp.concatenate([output_weight, down_weight], axis=0)
    shards_o = Shards(wo_shard, 1, d, c, two)
    clock.sync(x.behind, shards_q.first, *others)

    x.back()
    x.onward(clock)
    shards_q.over_y(clock)
    shards_u.over_x(clock)
    gain_here = gain_here.astype(f32)
    circle = jnp.concatenate([both, *others] * 2, axis=1)
    gain_shift = lax.dynamic_slice_in_dim(circle, (N_TP - t) % N_TP * CH, D, 1)
    gain, shift = gain_shift[0:1], gain_shift[1:2]

    here = c * rows + jnp.arange(rows, dtype=jnp.int32)
    tables, opening = rotary_tables(doc_starts, here)
    blocks = 1 if two else n_ctx
    before, _ = rotary_tables(doc_starts, jnp.arange(blocks * rows, dtype=jnp.int32))
    before = [a.reshape(seqs, blocks, rows, 128) for a in before]

    clock.sync(shards_q.second, shards_u.first, x.ahead)

    shards_q.near_core(clock)
    shards_q.far_core(clock)
    shards_u.near_core(clock)
    clock.sync(shards_q.near, *shards_q.far_near, shards_u.near)

    shards_u.over_y(clock)
    shards_o.over_x(clock)
    ct = [Gather(cotangent[s]) for s in range(seqs)]
    clock.sync(x.far, shards_u.second, shards_o.first, *before, *(g.own for g in ct))

    def send_keys(s):
        kv[s] = clock.go(kv[s])
        if two:
            kvp[s] = lax.ppermute(kv[s], "ctx", [(0, 1)])[None]
        else:
            kvp[s] = lax.all_gather(kv[s], "ctx", axis=0, tiled=False)

    def back_out_step(s):
        return back_out(layout, info, s, ct[s].parts, shards_o.pieces, slope, deps=clock.marks)

    def attention_step(s):
        return attention(
            info,
            s,
            opening[:, None],
            q,
            kv[s],
            kvp[s],
            datt[s],
            tables,
            before,
            deps=clock.marks,
        )

    def returned(sent):
        if two:
            return lax.ppermute(clock.go(sent[0]), "ctx", [(1, 0)])
        return lax.psum_scatter(clock.go(sent), "ctx", scatter_dimension=0, tiled=False)

    def out_step(s):
        return project_out(
            layout, info, s, att[s], hidden, shards_o.pieces, deps=clock.marks
        )

    def back_in_step(s):
        return back_in(
            layout,
            info,
            s,
            x.parts,
            dq[s],
            dkv[s],
            dup[s],
            shards_q.pieces,
            shards_u.pieces,
            gain,
            avg,
            inv,
            deps=clock.marks,
        )

    layout = layout_of(two)
    kvp, datt, att, dq, dkv, dup, cf, out_bias_sum = ([None] * seqs for _ in range(8))

    shards_o.over_y(clock)
    shards_u.far_core(clock)
    ct[0].sides(clock)
    normed, avg, inv, q, *kv = norm_qkv(
        layout, info, x.parts, gain, shift, shards_q.pieces, qkv_bias, tables, deps=clock.marks
    )
    clock.sync(normed, *shards_u.far_near, ct[0].behind, ct[0].ahead)

    ct[0].onward(clock)
    ct[1].sides(clock)
    send_keys(0)
    hidden, slope = mlp_up(layout, info, normed, shards_u.pieces, up_shift, deps=clock.marks)
    clock.sync(hidden, ct[0].far, ct[1].behind, shards_o.second)

    shards_o.near_core(clock)
    shards_o.far_core(clock)
    clock.sync(shards_o.near, *shards_o.far_near)
    ct[1].onward(clock)
    send_keys(1)
    cf[0], out_bias_sum[0], datt[0], dup[0] = back_out_step(0)
    clock.sync(datt[0], kvp[0])

    att[0], dq[0], dkv_0, sent_0 = attention_step(0)
    clock.sync(att[0], ct[1].ahead, ct[1].far)

    sent_0 = returned(sent_0)
    cf[1], out_bias_sum[1], datt[1], dup[1] = back_out_step(1)
    clock.sync(datt[1], kvp[1])

    def grad_up_step(n):
        kept, given, sums = grad_up(info, normed, dup, n, deps=clock.marks)
        up_sums.append(sums)
        clock.sync(kept)
        return Reduction(kept, given, clock, two)

    up, up_sums = [], []
    up.append(grad_up_step(0))
    clock.sync(sent_0)
    dkv[0] = (dkv_0.astype(f32) + sent_0.astype(f32)).astype(bf16)
    up.append(grad_up_step(1))
    clock.sync(up[0].got)

    up[0].add()
    up[0].over_x(0, clock)
    down_kept, down_given = grad_down(info, hidden, cf, deps=clock.marks)
    clock.sync(down_kept, up[1].got)

    down = Reduction(down_kept, down_given, clock, two)
    up[1].add()
    up[1].over_x(0, clock)
    chunks_0 = out_step(0)
    clock.sync(chunks_0[0], up[0].moved[0], down.got)

    up[0].over_y(0, clock)
    down.add()
    down.over_x(0, clock)
    out_0 = Scatter(chunks_0, clock)
    out_0.backward(clock)
    att[1], dq[1], dkv_1, sent_1 = attention_step(1)
    clock.sync(att[1], up[1].moved[0], out_0.far, out_0.back)

    sent_1 = returned(sent_1)
    up[1].over_y(0, clock)
    out_0.onward(clock)
    head_kept, head_given, query_sum = grad_out_query(
        info, normed, cf, att, dq, deps=clock.marks
    )
    clock.sync(head_kept, out_0.near, up[0].there[0])

    head = Reduction(head_kept, head_given, clock, two)
    down.over_x(1, clock)
    chunks_0 = back_in_step(0)
    clock.sync(chunks_0[0], head.got, sent_1, down.moved[0])

    head.add()
    head.over_x(0, clock)
    down.over_y(0, clock)
    in_0 = Scatter(chunks_0, clock)
    in_0.backward(clock)
    dkv[1] = (dkv_1.astype(f32) + sent_1.astype(f32)).astype(bf16)
    pair_kept, pair_given, pair_sum = grad_key_value(info, normed, dkv, deps=clock.marks)
    clock.sync(pair_kept, up[1].there[0], down.moved[1])

    pair = Reduction(pair_kept, pair_given, clock, two)
    chunks_1 = out_step(1)
    clock.sync(chunks_1[0], pair.got, in_0.far, in_0.back, head.moved[0])

    pair.add()
    pair.over_x(0, clock)
    down.over_y(1, clock)
    in_0.onward(clock)
    out_1 = Scatter(chunks_1, clock)
    chunks_1 = back_in_step(1)
    clock.sync(chunks_1[0], in_0.near, down.there[0], pair.moved[0], out_1.far)

    in_1 = Scatter(chunks_1, clock)
    in_1.backward(clock)
    head.over_y(0, clock)
    out_1.backward(clock)
    clock.sync(in_1.far, in_1.back, down.there[1])

    in_1.onward(clock)
    out_1.onward(clock)
    pair.over_y(0, clock)
    clock.sync(in_1.near, out_1.near)

    block_out = jnp.stack([out_0.total(clock), out_1.total(clock)])
    normed_grad = [in_0.total(clock), in_1.total(clock)]
    block_out = (block_in.astype(f32) + block_out + output_shift.astype(f32)).astype(bf16)
    up_wg = jnp.concatenate(up[0].result(clock) + up[1].result(clock), axis=1)
    down_wg = jnp.concatenate(down.result(clock), axis=0)
    output_wg, query_wg = head.result(clock)
    key_wg, value_wg = pair.result(clock)

    def input_gradient(s):
        total = normed_grad[s]
        plain, cross = total[rows][:, None], total[rows + 1][:, None]
        standard = (block_in[s].astype(f32) - avg[s]) * inv[s]
        scaled = total[:rows] * gain_here
        return cotangent[s].astype(f32) + inv[s] * (scaled - plain / D - standard * cross / D)

    in_grad = jnp.stack([input_gradient(s) for s in range(seqs)])

    summed = jnp.concatenate(
        [
            query_sum.reshape(-1),
            pair_sum.reshape(-1),
            *(a.reshape(-1) for a in up_sums),
            sum(out_bias_sum).reshape(-1),
            sum(a[rows + 8 : rows + 10] for a in normed_grad).reshape(-1),
        ]
    )
    summed = summed + swap(summed, "dp", 1, N_DP)
    summed = summed + swap(summed, "dp", 2, N_DP)
    summed = summed + swap(summed, "ctx", 1, 2) if two else lax.psum(summed, "ctx")
    at = 0
    small_grads = []
    for size in (CH, CH, CH, N_DP * share_units, CH, CH, CH):
        part = summed[at : at + size]
        at += size
        share = size // N_DP
        small_grads.append(lax.dynamic_slice_in_dim(part, d * share, share, 0))
    query_bg, key_bg, value_bg, up_bg, output_bg, gain_g, shift_g = small_grads
    return (
        block_out,
        in_grad,
        query_wg,
        key_wg,
        value_wg,
        output_wg,
        up_wg,
        down_wg,
        query_bg,
        key_bg,
        value_bg,
        up_bg,
        output_bg,
        gain_g,
        shift_g,
    )


def solution(mesh):
    return jax.shard_map(
        body,
        mesh=mesh,
        in_specs=(
            P("dp", "ctx", "tp"),
            P("dp", None),
            P("dp", "tp"),
            P("dp", "tp"),
            P("dp", "tp"),
            P("tp", "dp"),
            P("dp", "tp"),
            P("tp", "dp"),
        )
        + (P(("tp", "dp")),) * 7
        + (P("dp", "ctx", "tp"),),
        out_specs=(
            P("dp", "ctx", "tp"),
            P("dp", "ctx", "tp"),
            P("dp", "tp"),
            P("dp", "tp"),
            P("dp", "tp"),
            P("tp", "dp"),
            P("dp", "tp"),
            P("tp", "dp"),
        )
        + (P(("tp", "dp")),) * 7,
        check_vma=False,
    )
```

time: 742 us -> 573 us (0.77)
  the two profiles are of different devices: /device:TPU:16 before, /device:TPU:0 now
where the time goes in v3:
time: 573 us; the launch traced here: 564 us
  Pallas kernels  212 us (37%)
  waiting for transfers between devices  132 us (23%)
  other arithmetic  79 us (14%)
  starting transfers between devices  77.7 us (14%)
  local copies, waits for them, and re-layouts  61.2 us (11%)
    pallas_call x15, Pallas kernels, call(): pl.pallas_call(without_deps, grid_spec=pltpu.PrefetchScalarGridSpec(num_s...  212 us
    ppermute x24, waiting for transfers between devices, ring(): lax.ppermute(array, 'tp', [(i, (i + step) % N_TP) for i in range(N_TP)])  93.7 us
    ppermute x24, starting transfers between devices, ring(): lax.ppermute(array, 'tp', [(i, (i + step) % N_TP) for i in range(N_TP)])  34.5 us
    ppermute x37, starting transfers between devices, swap(): return lax.ppermute(array, axis, [(i, i ^ bit) for i in range(size)])  34.4 us
    unnamed x202, local copies, waits for them, and re-layouts  34.4 us
    ppermute x37, waiting for transfers between devices, swap(): return lax.ppermute(array, axis, [(i, i ^ bit) for i in range(size)])  30.2 us
    convert_element_type x5, other arithmetic, over_y(): here = sum((a.astype(f32) for a in parts)).astype(bf16)  15.9 us
    convert_element_type x5, other arithmetic, add(): total = (self.kept[1].astype(f32) + self.got[1].astype(f32)).astype(bf16)  13.2 us
  transfers between devices with their start and end apart: 65, of which 22 were waited for; matrix products, arithmetic and copies ran while one was open for 18% of the time, Pallas kernels for 38%

profile of v3, /device:TPU:0, one launch (start us, length us, event | category | flops | bytes accessed | tf_op | source)
XLA Modules:
  0.0 563.6 jit_solution(7909101550771449284)
XLA Ops:
  25.9 7.1 %collective-permute-done.4.refs_2_ = bf16[2,512]{1,0:T(2,128)(2,1)S(1)} collective-permute-done((bf16[2,512]{1,0:T(2,128)(2,1)S(1)}, bf16[2,512]{1,0:T(2,128)(2,1)S(1)}, u32[]{:S(2)}, u32[]{:S(2)}) %collective-permute-start.4) | collective-permute-done | bytes 2080 | tf_op jit(solution)/shard_map/ppermute | solution.py:912
  42.3 16.9 %collective-permute-done.7.refs_2_.refs_3_ = bf16[2,512,512]{2,1,0:T(8,128)(2,1)} collective-permute-done((bf16[2,512,512]{2,1,0:T(8,128)(2,1)S(1)}, bf16[2,512,512]{2,1,0:T(8,128)(2,1)}, u32[]{:S(2)}, u32[]{:S(2)}) %collective-permute-start.7) | collective-permute-done | bytes 1048608 | tf_op jit(solution)/shard_map/ppermute | solution.py:912
  83.6 16.1 %collective-permute-done.8.refs_0_.refs_4_ = bf16[2,512,512]{2,1,0:T(8,128)(2,1)S(1)} collective-permute-done((bf16[2,512,512]{2,1,0:T(8,128)(2,1)}, bf16[2,512,512]{2,1,0:T(8,128)(2,1)S(1)}, u32[]{:S(2)}, u32[]{:S(2)}) %collective-permute-start.8) | collective-permute-done | bytes 1048608 | tf_op jit(solution)/shard_map/ppermute | solution.py:912
  111.4 22.6 %norm_qkv.1 = (bf16[2,512,2048]{2,1,0:T(8,128)(2,1)}, f32[2,512,1]{2,1,0:T(8,128)}, f32[2,512,1]{2,1,0:T(8,128)}, bf16[2,512,512]{2,1,0:T(8,128)(2,1)}, bf16[2,5...) custom-call(s32[3]{0:T(128)} %pad_add_fusion.refs_0_, bf16[2,512,512]{2,1,0:T(8,128)(2,1)} %refs_1_.5, ...), custom_call_target="tpu_custom_call" | custom-call | flops 128849016 | bytes 388362 | tf_op jit(solution)/shard_map/norm_qkv/pallas_call | solution.py:66
  137.3 19.5 %mlp_up.1 = (bf16[2,512,2048]{2,1,0:T(8,128)(2,1)}, bf16[2,512,2048]{2,1,0:T(8,128)(2,1)}) custom-call(s32[3]{0:T(128)} %pad_add_fusion.refs_0_, bf16[2,512,2048]{2,1,0:T(8,128)(2,1)} %get-tuple-element.71.refs_0_.refs_1_, bf16[1,2048]{1,0:T(2,128)(2,1)} %bitcast.142, bf16[512,2048]{1,0:T(8,128)(2,1)} %refs_17_.3, ...), custom_call_target="tpu_custom_call" | custom-call | flops 171798688 | bytes 419512 | tf_op jit(solution)/shard_map/mlp_up/pallas_call | solution.py:66
  176.6 13.2 %back_out.2 = (bf16[512,2048]{1,0:T(8,128)(2,1)}, f32[1,512]{1,0:T(1,128)}, bf16[512,512]{1,0:T(8,128)(2,1)}, bf16[512,2048]{1,0:T(8,128)(2,1)}) custom-call(s32[3]{0:T(128)} %pad_add_fusion.refs_0_, bf16[512,512]{1,0:T(8,128)(2,1)} %tie.73.refs_1_, bf16[512,512]{1,0:T(8,128)(2,1)} %tie.75.refs_2_, bf16[512,512]{1,0:T(8,128)(2,1)} %copy-done.67, ...), custom_call_target="tpu_custom_call" | custom-call | flops 107374184 | bytes 429957 | tf_op jit(solution)/shard_map/back_out/pallas_call | solution.py:66
  189.9 12.9 %attention.2 = (bf16[512,512]{1,0:T(8,128)(2,1)}, bf16[512,512]{1,0:T(8,128)(2,1)}, bf16[2,512,512]{2,1,0:T(8,128)(2,1)}, bf16[1,2,512,512]{3,2,1,0:T(8,128)(2,1)}) custom-call(s32[3]{0:T(128)} %pad_add_fusion.refs_0_, s32[2,1,512]{2,1,0:T(1,128)} %broadcast_in_dim.65.refs_1_, bf16[2,512,512]{2,1,0:T(8,128)(2,1)} %get-tuple-element.69.refs_2_, ...), custom_call_target="tpu_custom_call" | custom-call | flops 128849016 | bytes 199311 | tf_op jit(solution)/shard_map/attention/pallas_call | solution.py:66
  205.3 13.2 %back_out.3 = (bf16[512,2048]{1,0:T(8,128)(2,1)}, f32[1,512]{1,0:T(1,128)}, bf16[512,512]{1,0:T(8,128)(2,1)}, bf16[512,2048]{1,0:T(8,128)(2,1)}) custom-call(s32[3]{0:T(128)} %pad_add_fusion.refs_0_, bf16[512,512]{1,0:T(8,128)(2,1)} %tie.76.refs_1_, bf16[512,512]{1,0:T(8,128)(2,1)} %tie.81.refs_2_, bf16[512,512]{1,0:T(8,128)(2,1)} %collective-permute-done.28.refs_1_.refs_3_, ...), custom_call_target="tpu_custom_call" | custom-call | flops 107374184 | bytes 429957 | tf_op jit(solution)/shard_map/back_out/pallas_call | solution.py:66
  219.6 9.5 %grad_up.2 = (bf16[2,2,512,512]{3,2,1,0:T(8,128)(2,1)}, bf16[2,2,512,512]{3,2,1,0:T(8,128)(2,1)}, f32[1,1024]{1,0:T(1,128)}) custom-call(s32[3]{0:T(128)} %pad_add_fusion.refs_0_, bf16[2,512,2048]{2,1,0:T(8,128)(2,1)} %get-tuple-element.71.refs_0_.refs_1_, bf16[512,2048]{1,0:T(8,128)(2,1)} %get-tuple-element.78.refs_2_.refs_7_, ...), custom_call_target="tpu_custom_call" | custom-call | flops 85899344 | bytes 251740 | tf_op jit(solution)/shard_map/grad_up/pallas_call | solution.py:66
  229.1 8.0 %collective-permute-done.32.refs_0_ = bf16[2,512,512]{2,1,0:T(8,128)(2,1)S(1)} collective-permute-done((bf16[2,512,512]{2,1,0:T(8,128)(2,1)}, bf16[2,512,512]{2,1,0:T(8,128)(2,1)S(1)}, u32[]{:S(2)}, u32[]{:S(2)}) %collective-permute-start.32) | collective-permute-done | bytes 1048608 | tf_op jit(solution)/shard_map/ppermute | solution.py:1095
  238.1 9.4 %grad_up.3 = (bf16[2,2,512,512]{3,2,1,0:T(8,128)(2,1)}, bf16[2,2,512,512]{3,2,1,0:T(8,128)(2,1)}, f32[1,1024]{1,0:T(1,128)}) custom-call(s32[3]{0:T(128)} %pad_add_fusion.refs_0_, bf16[2,512,2048]{2,1,0:T(8,128)(2,1)} %get-tuple-element.71.refs_0_.refs_1_, bf16[512,2048]{1,0:T(8,128)(2,1)} %get-tuple-element.78.refs_2_.refs_7_, ...), custom_call_target="tpu_custom_call" | custom-call | flops 85899344 | bytes 251740 | tf_op jit(solution)/shard_map/grad_up/pallas_call | solution.py:66
  247.5 15.7 %grad_down.1 = (bf16[2,4,512,512]{3,2,1,0:T(8,128)(2,1)}, bf16[2,4,512,512]{3,2,1,0:T(8,128)(2,1)}) custom-call(s32[3]{0:T(128)} %pad_add_fusion.refs_0_, bf16[2,512,2048]{2,1,0:T(8,128)(2,1)} %get-tuple-element.73.refs_0_.refs_1_.refs_2_, bf16[512,2048]{1,0:T(8,128)(2,1)} %get-tuple-element.76.refs_2_, bf16[512,2048]{1,0:T(8,128)(2,1)} %get-tuple-element.77.refs_3_, ...), custom_call_target="tpu_custom_call" | custom-call | flops 171798688 | bytes 335544 | tf_op jit(solution)/shard_map/grad_down/pallas_call | solution.py:66
  272.5 12.4 %project_out.2 = (bf16[512,512]{1,0:T(8,128)(2,1)}, bf16[512,512]{1,0:T(8,128)(2,1)}, bf16[512,512]{1,0:T(8,128)(2,1)}, bf16[512,512]{1,0:T(8,128)(2,1)}) custom-call(s32[3]{0:T(128)} %pad_add_fusion.refs_0_, bf16[512,512]{1,0:T(8,128)(2,1)} %get-tuple-element.75.refs_0_.refs_1_.refs_4_, bf16[2,512,2048]{2,1,0:T(8,128)(2,1)} %get-tuple-element.73.refs_0_.refs_1_.refs_2_, ...), custom_call_target="tpu_custom_call" | custom-call | flops 107374184 | bytes 346030 | tf_op jit(solution)/shard_map/project_out/pallas_call | solution.py:66
  284.8 9.3 %collective-permute-done.34.refs_1_.refs_0_ = bf16[2,512,512]{2,1,0:T(8,128)(2,1)S(1)} collective-permute-done((bf16[2,512,512]{2,1,0:T(8,128)(2,1)}, bf16[2,512,512]{2,1,0:T(8,128)(2,1)S(1)}, u32[]{:S(2)}, u32[]{:S(2)}) %collective-permute-start.34) | collective-permute-done | bytes 1048608 | tf_op jit(solution)/shard_map/ppermute | solution.py:145
  302.8 13.0 %attention.3 = (bf16[512,512]{1,0:T(8,128)(2,1)}, bf16[512,512]{1,0:T(8,128)(2,1)}, bf16[2,512,512]{2,1,0:T(8,128)(2,1)}, bf16[1,2,512,512]{3,2,1,0:T(8,128)(2,1)}) custom-call(s32[3]{0:T(128)} %pad_add_fusion.refs_0_, s32[2,1,512]{2,1,0:T(1,128)} %broadcast_in_dim.65.refs_1_, bf16[2,512,512]{2,1,0:T(8,128)(2,1)} %get-tuple-element.69.refs_2_, ...), custom_call_target="tpu_custom_call" | custom-call | flops 128849016 | bytes 199311 | tf_op jit(solution)/shard_map/attention/pallas_call | solution.py:66
  321.5 11.2 %grad_out_query.1 = (bf16[2,2,512,512]{3,2,1,0:T(8,128)(2,1)}, bf16[2,2,512,512]{3,2,1,0:T(8,128)(2,1)}, f32[1,512]{1,0:T(1,128)}) custom-call(s32[3]{0:T(128)} %pad_add_fusion.refs_0_, bf16[2,512,2048]{2,1,0:T(8,128)(2,1)} %get-tuple-element.71.refs_0_.refs_1_, bf16[512,2048]{1,0:T(8,128)(2,1)} %get-tuple-element.76.refs_2_, ...), custom_call_target="tpu_custom_call" | custom-call | flops 85899344 | bytes 293642 | tf_op jit(solution)/shard_map/grad_out_query/pallas_call | solution.py:66
  356.2 18.7 %back_in.2 = (bf16[528,512]{1,0:T(8,128)(2,1)}, bf16[528,512]{1,0:T(8,128)(2,1)}, bf16[528,512]{1,0:T(8,128)(2,1)}, bf16[528,512]{1,0:T(8,128)(2,1)}) custom-call(s32[3]{0:T(128)} %pad_add_fusion.refs_0_, bf16[2,512,512]{2,1,0:T(8,128)(2,1)} %refs_1_.5, bf16[2,512,512]{2,1,0:T(8,128)(2,1)} %tie.63.refs_2_, ...), custom_call_target="tpu_custom_call" | custom-call | flops 150323856 | bytes 494387 | tf_op jit(solution)/shard_map/back_in/pallas_call | solution.py:66
  378.4 9.4 %grad_key_value.1 = (bf16[2,2,512,512]{3,2,1,0:T(8,128)(2,1)}, bf16[2,2,512,512]{3,2,1,0:T(8,128)(2,1)}, f32[2,1,512]{2,1,0:T(1,128)}) custom-call(s32[3]{0:T(128)} %pad_add_fusion.refs_0_, bf16[2,512,2048]{2,1,0:T(8,128)(2,1)} %get-tuple-element.71.refs_0_.refs_1_, bf16[2,512,512]{2,1,0:T(8,128)(2,1)} %add_convert_fusion.3.refs_6_.refs_2_, ...), custom_call_target="tpu_custom_call" | custom-call | flops 85899344 | bytes 209797 | tf_op jit(solution)/shard_map/grad_key_value/pallas_call | solution.py:66
  387.7 7.0 %collective-permute-done.44.refs_1_.refs_0_ = bf16[2,512,512]{2,1,0:T(8,128)(2,1)S(1)} collective-permute-done((bf16[2,512,512]{2,1,0:T(8,128)(2,1)}, bf16[2,512,512]{2,1,0:T(8,128)(2,1)S(1)}, u32[]{:S(2)}, u32[]{:S(2)}) %collective-permute-start.44) | collective-permute-done | bytes 1048608 | tf_op jit(solution)/shard_map/ppermute | solution.py:145
  402.7 12.3 %project_out.3 = (bf16[512,512]{1,0:T(8,128)(2,1)}, bf16[512,512]{1,0:T(8,128)(2,1)}, bf16[512,512]{1,0:T(8,128)(2,1)}, bf16[512,512]{1,0:T(8,128)(2,1)}) custom-call(s32[3]{0:T(128)} %pad_add_fusion.refs_0_, bf16[512,512]{1,0:T(8,128)(2,1)} %get-tuple-element.93.refs_0_.refs_5_.refs_1_, bf16[2,512,2048]{2,1,0:T(8,128)(2,1)} %get-tuple-element.73.refs_0_.refs_1_.refs_2_, ...), custom_call_target="tpu_custom_call" | custom-call | flops 107374184 | bytes 346030 | tf_op jit(solution)/shard_map/project_out/pallas_call | solution.py:66
  417.6 8.6 %collective-permute-done.48.refs_3_ = bf16[528,512]{1,0:T(8,128)(2,1)S(1)} collective-permute-done((bf16[528,512]{1,0:T(8,128)(2,1)}, bf16[528,512]{1,0:T(8,128)(2,1)S(1)}, u32[]{:S(2)}, u32[]{:S(2)}) %collective-permute-start.48) | collective-permute-done | bytes 540704 | tf_op jit(solution)/shard_map/ppermute | solution.py:912
  439.2 18.6 %back_in.3 = (bf16[528,512]{1,0:T(8,128)(2,1)}, bf16[528,512]{1,0:T(8,128)(2,1)}, bf16[528,512]{1,0:T(8,128)(2,1)}, bf16[528,512]{1,0:T(8,128)(2,1)}) custom-call(s32[3]{0:T(128)} %pad_add_fusion.refs_0_, bf16[2,512,512]{2,1,0:T(8,128)(2,1)} %refs_1_.5, bf16[2,512,512]{2,1,0:T(8,128)(2,1)} %tie.63.refs_2_, ...), custom_call_target="tpu_custom_call" | custom-call | flops 150323856 | bytes 494387 | tf_op jit(solution)/shard_map/back_in/pallas_call | solution.py:66
  467.8 11.2 %collective-permute-done.54.refs_0_ = bf16[528,512]{1,0:T(8,128)(2,1)S(1)} collective-permute-done((bf16[528,512]{1,0:T(8,128)(2,1)}, bf16[528,512]{1,0:T(8,128)(2,1)S(1)}, u32[]{:S(2)}, u32[]{:S(2)}) %collective-permute-start.54) | collective-permute-done | bytes 540704 | tf_op jit(solution)/shard_map/ppermute | solution.py:912
  498.3 15.7 %collective-permute-done.58.refs_1_.refs_0_ = bf16[512,512]{1,0:T(8,128)(2,1)} collective-permute-done((bf16[512,512]{1,0:T(8,128)(2,1)}, bf16[512,512]{1,0:T(8,128)(2,1)}, u32[]{:S(2)}, u32[]{:S(2)}) %collective-permute-start.58) | collective-permute-done | bytes 524320 | tf_op jit(solution)/shard_map/ppermute | solution.py:912
  (497 shorter events, 250.1 us)
Async XLA Ops:
  7.0 30.4 %collective-permute-start = (bf16[2,512,512]{2,1,0:T(8,128)(2,1)}, bf16[2,512,512]{2,1,0:T(8,128)(2,1)S(1)}, u32[]{:S(2)}, u32[]{:S(2)}) collective-permute-start(bf16[2,512,512]{2,1,0:T(8,128)(2,1)} %refs_1_.5), channel_id=1, source_target_pairs={{0,1},{1,2},{2,3},{3,0},{4,5},{5,6},{6,7},{7,4},{8,9},{9,10},{10,1... | collective-permute-start | bytes 3145736 | tf_op jit(solution)/shard_map/ppermute | solution.py:912
  71.2 31.0 %collective-permute-start.16 = (bf16[2560,256]{1,0:T(8,128)(2,1)}, bf16[2560,256]{1,0:T(8,128)(2,1)S(1)}, u32[]{:S(2)}, u32[]{:S(2)}) collective-permute-start(bf16[2560,256]{1,0:T(8,128)(2,1)} %tie.70), channel_id=1, source_target_pairs={{0,16},{8,24},{16,0},{24,8},{1,17},{9,25},{17,1},{25,9},{2,18},{10... | collective-permute-start | bytes 3932168 | tf_op jit(solution)/shard_map/ppermute | solution.py:145
  103.3 30.8 %collective-permute-start.18 = (bf16[256,2048]{1,0:T(8,128)(2,1)}, bf16[256,2048]{1,0:T(8,128)(2,1)S(1)}, u32[]{:S(2)}, u32[]{:S(2)}) collective-permute-start(bf16[256,2048]{1,0:T(8,128)(2,1)} %tie.72.refs_6_.refs_20_), channel_id=1, source_target_pairs={{0,8},{8,0},{16,24},{24,16},{1,9},{9,1},{17,25},{25,17},{2,10},{10... | collective-permute-start | bytes 3145736 | tf_op jit(solution)/shard_map/ppermute | solution.py:145
  104.5 29.6 %collective-permute-start.17 = (bf16[256,2048]{1,0:T(8,128)(2,1)S(1)}, bf16[256,2048]{1,0:T(8,128)(2,1)}, u32[]{:S(2)}, u32[]{:S(2)}) collective-permute-start(bf16[256,2048]{1,0:T(8,128)(2,1)S(1)} %copy-done.5), channel_id=1, source_target_pairs={{0,8},{8,0},{16,24},{24,16},{1,9},{9,1},{17,25},{25,17},{2,10},{10... | collective-permute-start | bytes 3145736 | tf_op jit(solution)/shard_map/ppermute | solution.py:145
  105.2 51.6 %collective-permute-start.24 = (bf16[2560,256]{1,0:T(8,128)(2,1)}, bf16[2560,256]{1,0:T(8,128)(2,1)S(1)}, u32[]{:S(2)}, u32[]{:S(2)}) collective-permute-start(bf16[2560,256]{1,0:T(8,128)(2,1)} %tie.77.refs_0_), channel_id=1, source_target_pairs={{0,4},{4,0},{1,5},{5,1},{2,6},{6,2},{3,7},{7,3},{8,12},{12,8},{9,1... | collective-permute-start | bytes 3932168 | tf_op jit(solution)/shard_map/ppermute | solution.py:145
  166.9 35.9 %collective-permute-start.28 = (bf16[512,512]{1,0:T(8,128)(2,1)S(1)}, bf16[512,512]{1,0:T(8,128)(2,1)}, u32[]{:S(2)}, u32[]{:S(2)}) collective-permute-start(bf16[512,512]{1,0:T(8,128)(2,1)S(1)} %copy-done.30), channel_id=1, source_target_pairs={{0,3},{1,0},{2,1},{3,2},{4,7},{5,4},{6,5},{7,6},{8,11},{9,8},{10,9... | collective-permute-start | bytes 1572872 | tf_op jit(solution)/shard_map/ppermute | solution.py:912
  173.5 29.3 %collective-permute-start.29 = (bf16[512,512]{1,0:T(8,128)(2,1)}, bf16[512,512]{1,0:T(8,128)(2,1)S(1)}, u32[]{:S(2)}, u32[]{:S(2)}) collective-permute-start(bf16[512,512]{1,0:T(8,128)(2,1)} %tie.81.refs_2_), channel_id=1, source_target_pairs={{0,1},{1,2},{2,3},{3,0},{4,5},{5,6},{6,7},{7,4},{8,9},{9,10},{10,1... | collective-permute-start | bytes 1572872 | tf_op jit(solution)/shard_map/ppermute | solution.py:912
  174.1 44.4 %collective-permute-start.30 = (bf16[2,512,512]{2,1,0:T(8,128)(2,1)}, bf16[2,512,512]{2,1,0:T(8,128)(2,1)S(1)}, u32[]{:S(2)}, u32[]{:S(2)}) collective-permute-start(bf16[2,512,512]{2,1,0:T(8,128)(2,1)} %tie.82.refs_3_), channel_id=1, source_target_pairs={{0,4},{1,5},{2,6},{3,7},{8,12},{9,13},{10,14},{11,15},{16,20},{17,... | collective-permute-start | bytes 3145736 | tf_op jit(solution)/shard_map/ppermute | solution.py:1072
  203.6 33.5 %collective-permute-start.32 = (bf16[2,512,512]{2,1,0:T(8,128)(2,1)}, bf16[2,512,512]{2,1,0:T(8,128)(2,1)S(1)}, u32[]{:S(2)}, u32[]{:S(2)}) collective-permute-start(bf16[2,512,512]{2,1,0:T(8,128)(2,1)} %tie.84), channel_id=1, source_target_pairs={{4,0},{5,1},{6,2},{7,3},{12,8},{13,9},{14,10},{15,11},{20,16},{21,... | collective-permute-start | bytes 3145736 | tf_op jit(solution)/shard_map/ppermute | solution.py:1095
  264.5 29.7 %collective-permute-start.35 = (bf16[2,4,512,512]{3,2,1,0:T(8,128)(2,1)}, bf16[2,4,512,512]{3,2,1,0:T(8,128)(2,1)}, u32[]{:S(2)}, u32[]{:S(2)}) collective-permute-start(bf16[2,4,512,512]{3,2,1,0:T(8,128)(2,1)} %tie.87), channel_id=1, source_target_pairs={{0,8},{8,0},{16,24},{24,16},{1,9},{9,1},{17,25},{25,17},{2,10},{10... | collective-permute-start | bytes 12582920 | tf_op jit(solution)/shard_map/ppermute | solution.py:145
  271.9 43.9 %collective-permute-start.38 = (bf16[2,512,512]{2,1,0:T(8,128)(2,1)}, bf16[2,512,512]{2,1,0:T(8,128)(2,1)S(1)}, u32[]{:S(2)}, u32[]{:S(2)}) collective-permute-start(bf16[2,512,512]{2,1,0:T(8,128)(2,1)} %tie.90), channel_id=1, source_target_pairs={{0,16},{8,24},{16,0},{24,8},{1,17},{9,25},{17,1},{25,9},{2,18},{10... | collective-permute-start | bytes 3145736 | tf_op jit(solution)/shard_map/ppermute | solution.py:145
  301.3 31.4 %collective-permute-start.41 = (bf16[2,512,512]{2,1,0:T(8,128)(2,1)S(1)}, bf16[2,512,512]{2,1,0:T(8,128)(2,1)S(1)}, u32[]{:S(2)}, u32[]{:S(2)}) collective-permute-start(bf16[2,512,512]{2,1,0:T(8,128)(2,1)S(1)} %fusion.7), channel_id=1, source_target_pairs={{0,4},{4,0},{1,5},{5,1},{2,6},{6,2},{3,7},{7,3},{8,12},{12,8},{9,1... | collective-permute-start | bytes 3145736 | tf_op jit(solution)/shard_map/ppermute | solution.py:145
  335.6 41.8 %collective-permute-start.42 = (bf16[2,2,512,512]{3,2,1,0:T(8,128)(2,1)}, bf16[2,2,512,512]{3,2,1,0:T(8,128)(2,1)}, u32[]{:S(2)}, u32[]{:S(2)}) collective-permute-start(bf16[2,2,512,512]{3,2,1,0:T(8,128)(2,1)} %tie.94), channel_id=1, source_target_pairs={{0,8},{8,0},{16,24},{24,16},{1,9},{9,1},{17,25},{25,17},{2,10},{10... | collective-permute-start | bytes 6291464 | tf_op jit(solution)/shard_map/ppermute | solution.py:145
  339.9 37.5 %collective-permute-start.43 = (bf16[2,512,512]{2,1,0:T(8,128)(2,1)}, bf16[2,512,512]{2,1,0:T(8,128)(2,1)S(1)}, u32[]{:S(2)}, u32[]{:S(2)}) collective-permute-start(bf16[2,512,512]{2,1,0:T(8,128)(2,1)} %tie.95), channel_id=1, source_target_pairs={{0,16},{8,24},{16,0},{24,8},{1,17},{9,25},{17,1},{25,9},{2,18},{10... | collective-permute-start | bytes 3145736 | tf_op jit(solution)/shard_map/ppermute | solution.py:145
  341.4 33.4 %collective-permute-start.40 = (bf16[2,512,512]{2,1,0:T(8,128)(2,1)}, bf16[2,512,512]{2,1,0:T(8,128)(2,1)}, u32[]{:S(2)}, u32[]{:S(2)}) collective-permute-start(bf16[2,512,512]{2,1,0:T(8,128)(2,1)} %tie.92), channel_id=1, source_target_pairs={{4,0},{5,1},{6,2},{7,3},{12,8},{13,9},{14,10},{15,11},{20,16},{21,... | collective-permute-start | bytes 3145736 | tf_op jit(solution)/shard_map/ppermute | solution.py:1095
  346.0 48.8 %collective-permute-start.44 = (bf16[2,512,512]{2,1,0:T(8,128)(2,1)}, bf16[2,512,512]{2,1,0:T(8,128)(2,1)S(1)}, u32[]{:S(2)}, u32[]{:S(2)}) collective-permute-start(bf16[2,512,512]{2,1,0:T(8,128)(2,1)} %fusion.6), channel_id=1, source_target_pairs={{0,4},{4,0},{1,5},{5,1},{2,6},{6,2},{3,7},{7,3},{8,12},{12,8},{9,1... | collective-permute-start | bytes 3145736 | tf_op jit(solution)/shard_map/ppermute | solution.py:145
  352.9 41.9 %collective-permute-start.45 = (bf16[2,512,512]{2,1,0:T(8,128)(2,1)}, bf16[2,512,512]{2,1,0:T(8,128)(2,1)S(1)}, u32[]{:S(2)}, u32[]{:S(2)}) collective-permute-start(bf16[2,512,512]{2,1,0:T(8,128)(2,1)} %tie.97), channel_id=1, source_target_pairs={{0,16},{8,24},{16,0},{24,8},{1,17},{9,25},{17,1},{25,9},{2,18},{10... | collective-permute-start | bytes 3145736 | tf_op jit(solution)/shard_map/ppermute | solution.py:145
  427.5 32.7 %collective-permute-start.52 = (bf16[2,512,512]{2,1,0:T(8,128)(2,1)}, bf16[2,512,512]{2,1,0:T(8,128)(2,1)S(1)}, u32[]{:S(2)}, u32[]{:S(2)}) collective-permute-start(bf16[2,512,512]{2,1,0:T(8,128)(2,1)} %tie.104), channel_id=1, source_target_pairs={{0,16},{8,24},{16,0},{24,8},{1,17},{9,25},{17,1},{25,9},{2,18},{10... | collective-permute-start | bytes 3145736 | tf_op jit(solution)/shard_map/ppermute | solution.py:145
  437.1 42.9 %collective-permute-start.56 = (bf16[2,512,512]{2,1,0:T(8,128)(2,1)}, bf16[2,512,512]{2,1,0:T(8,128)(2,1)S(1)}, u32[]{:S(2)}, u32[]{:S(2)}) collective-permute-start(bf16[2,512,512]{2,1,0:T(8,128)(2,1)} %get-tuple-element.133), channel_id=1, source_target_pairs={{0,4},{4,0},{1,5},{5,1},{2,6},{6,2},{3,7},{7,3},{8,12},{12,8},{9,1... | collective-permute-start | bytes 3145736 | tf_op jit(solution)/shard_map/ppermute | solution.py:145
  485.4 28.7 %collective-permute-start.57 = (bf16[528,512]{1,0:T(8,128)(2,1)}, bf16[528,512]{1,0:T(8,128)(2,1)}, u32[]{:S(2)}, u32[]{:S(2)}) collective-permute-start(bf16[528,512]{1,0:T(8,128)(2,1)} %tie.109), channel_id=1, source_target_pairs={{0,1},{1,2},{2,3},{3,0},{4,5},{5,6},{6,7},{7,4},{8,9},{9,10},{10,1... | collective-permute-start | bytes 1622024 | tf_op jit(solution)/shard_map/ppermute | solution.py:912
  491.6 40.2 %collective-permute-start.60 = (bf16[2,512,512]{2,1,0:T(8,128)(2,1)}, bf16[2,512,512]{2,1,0:T(8,128)(2,1)}, u32[]{:S(2)}, u32[]{:S(2)}) collective-permute-start(bf16[2,512,512]{2,1,0:T(8,128)(2,1)} %fusion.3), channel_id=1, source_target_pairs={{0,4},{4,0},{1,5},{5,1},{2,6},{6,2},{3,7},{7,3},{8,12},{12,8},{9,1... | collective-permute-start | bytes 3145736 | tf_op jit(solution)/shard_map/ppermute | solution.py:145
  493.0 53.7 %collective-permute-start.59 = (bf16[512,512]{1,0:T(8,128)(2,1)}, bf16[512,512]{1,0:T(8,128)(2,1)}, u32[]{:S(2)}, u32[]{:S(2)}) collective-permute-start(bf16[512,512]{1,0:T(8,128)(2,1)} %tie.112), channel_id=1, source_target_pairs={{0,3},{1,0},{2,1},{3,2},{4,7},{5,4},{6,5},{7,6},{8,11},{9,8},{10,9... | collective-permute-start | bytes 1572872 | tf_op jit(solution)/shard_map/ppermute | solution.py:912
  497.8 62.3 %collective-permute-start.61 = (bf16[2,512,512]{2,1,0:T(8,128)(2,1)}, bf16[2,512,512]{2,1,0:T(8,128)(2,1)}, u32[]{:S(2)}, u32[]{:S(2)}) collective-permute-start(bf16[2,512,512]{2,1,0:T(8,128)(2,1)} %fusion.2), channel_id=1, source_target_pairs={{0,4},{4,0},{1,5},{5,1},{2,6},{6,2},{3,7},{7,3},{8,12},{12,8},{9,1... | collective-permute-start | bytes 3145736 | tf_op jit(solution)/shard_map/ppermute | solution.py:145
  517.4 30.8 %collective-permute-start.62 = (f32[5120]{0:T(1024)S(1)}, f32[5120]{0:T(1024)S(1)}, u32[]{:S(2)}, u32[]{:S(2)}) collective-permute-start(f32[5120]{0:T(1024)S(1)} %constant_dynamic-update-slice_fusion.15), channel_id=1, source_target_pairs={{0,8},{8,0},{16,24},{24,16},{1,9},{9,1},{17,25},{25,17},{2,10},{10... | collective-permute-start | bytes 61448 | tf_op jit(solution)/shard_map/ppermute | solution.py:145
  (131 other events, 1062.8 us)

commit v4 on v3

--- a/solution.py
+++ b/solution.py
@@ -53,7 +53,7 @@
     return jax.ShapeDtypeStruct(tuple(shape), dtype)
 
 
-HBM = pl.BlockSpec(memory_space=pltpu.HBM)
+ANYWHERE = pl.BlockSpec(memory_space=pl.ANY)
 
 
 def call(body, name, grid, info, ins, in_specs, outs, out_specs, flops, scratch=(), deps=()):
@@ -68,7 +68,7 @@
         grid_spec=pltpu.PrefetchScalarGridSpec(
             num_scalar_prefetch=1,
             grid=(grid,),
-            in_specs=[*in_specs, *[HBM] * len(deps)],
+            in_specs=[*in_specs, *[ANYWHERE] * len(deps)],
             out_specs=out_specs,
             scratch_shapes=list(scratch),
         ),
@@ -87,8 +87,8 @@
 
     return pl.pallas_call(
         nothing,
-        in_specs=[HBM] * (1 + len(deps)),
-        out_specs=HBM,
+        in_specs=[ANYWHERE] * (1 + len(deps)),
+        out_specs=ANYWHERE,
         out_shape=shaped(value.shape, value.dtype),
         input_output_aliases={0: 0},
         cost_estimate=pl.CostEstimate(flops=0, bytes_accessed=0, transcendentals=0),
@@ -132,8 +132,8 @@
         self.marks = (
             pl.pallas_call(
                 nothing,
-                in_specs=[HBM] * (len(arrays) + len(self.marks)),
-                out_specs=HBM,
+                in_specs=[ANYWHERE] * (len(arrays) + len(self.marks)),
+                out_specs=ANYWHERE,
                 out_shape=shaped((8, 128), f32),
                 cost_estimate=pl.CostEstimate(flops=0, bytes_accessed=0, transcendentals=0),
                 name="sync",
@@ -188,6 +188,10 @@
     ), opening
 
 
+def add_rounded(a, b):
+    return (a.astype(f32) + b.astype(f32)).astype(bf16)
+
+
 def turn(x, own, up, down):
     return x * own + pltpu.roll(x, 112, 1) * up + pltpu.roll(x, 16, 1) * down
 
@@ -220,7 +224,7 @@
 
 
 def norm_qkv_body(layout, info, x0, xa, xc, xb, gain, shift, bias, own, up, down, *refs):
-    *w, normed, avg, inv, q, kv0, kv1, held, sems = refs
+    *w, normed, stats, q, kv0, kv1, columns_held, held, sems = refs
     j = pl.program_id(0)
     t = info[0]
     seqs, rows, _ = x0.shape
@@ -239,15 +243,18 @@
             x = [a - average for a in x]
             variance = sum(jnp.sum(a * a, axis=1, keepdims=True) for a in x) * (1.0 / D)
             root = lax.rsqrt(variance + EPS)
-            avg[s, window, :] = average
-            inv[s, window, :] = root
+            columns_held[s, window, 0:1] = average
+            columns_held[s, window, 1:2] = root
             for a, (_, index) in zip(x, parts):
                 at = columns(index)
                 y = a * root * gain[:, at].astype(f32) + shift[:, at].astype(f32)
                 normed[s, window, at] = y.astype(bf16)
             return carry
 
+        columns_held[...] = jnp.zeros(columns_held.shape, f32)
         lax.fori_loop(0, seqs * rows // tile, rows_of, 0)
+        for s in range(seqs):
+            stats[s] = columns_held[s].T[: stats.shape[1]]
 
     for s, kv in ((0, kv0), (1, kv1)):
         y = dot_nn(normed[s], held[:, columns(j)]) + bias[...].astype(f32)
@@ -276,8 +283,7 @@
     seqs, rows, _ = parts[0].shape
     outs = (
         shaped((seqs, rows, D)),
-        shaped((seqs, rows, 1), f32),
-        shaped((seqs, rows, 1), f32),
+        shaped((seqs, 8, rows), f32),
         shaped((seqs, rows, CH)),
         shaped((2, rows, CH)),
         shaped((2, rows, CH)),
@@ -293,18 +299,21 @@
         + [whole(1, D)] * 2
         + [spec((1, CH), lambda j, *_: (0, j))]
         + [whole(seqs, rows, 128)] * 3
-        + [HBM] * len(w),
+        + [ANYWHERE] * len(w),
         outs,
         [
             whole(seqs, rows, D),
-            whole(seqs, rows, 1),
-            whole(seqs, rows, 1),
+            whole(seqs, 8, rows),
             whole(seqs, rows, CH),
             pair,
             pair,
         ],
         2 * seqs * rows * D * 3 * CH,
-        [pltpu.VMEM((D, 3 * CH), bf16), pltpu.SemaphoreType.DMA((3, len(w)))],
+        [
+            pltpu.VMEM((seqs, rows, 128), f32),
+            pltpu.VMEM((D, 3 * CH), bf16),
+            pltpu.SemaphoreType.DMA((3, len(w))),
+        ],
         deps=deps,
     )
 
@@ -334,7 +343,7 @@
         units // CH,
         info,
         (normed, bias, *w),
-        [whole(seqs, rows, D), spec((1, CH), lambda j, *_: (0, j))] + [HBM] * len(w),
+        [whole(seqs, rows, D), spec((1, CH), lambda j, *_: (0, j))] + [ANYWHERE] * len(w),
         (shaped((seqs, rows, units)),) * 2,
         [block] * 2,
         2 * seqs * rows * D * units,
@@ -347,44 +356,47 @@
     *w, cf, bias_grad, datt, dup, held, sems = refs
     j = pl.program_id(0)
     t = info[0]
+    seqs = c0.shape[0]
     stream_pieces(layout, info, w, held, sems, 1, held.shape[0] // CH)
 
     @pl.when(j == 0)
     def _():
         for part, step in ((c0, 0), (ca, 3), (cc, 1), (cb, 2)):
-            cf[:, columns((t + step) % N_TP)] = part[...]
-        bias_grad[...] = jnp.sum(c0[...].astype(f32), axis=0, keepdims=True)
-
-    y = dot_nt(cf[...], held[columns(j), :])
-
-    @pl.when(j == 0)
-    def _():
-        datt[...] = y.astype(bf16)
-
-    @pl.when(j > 0)
-    def _():
-        dup[...] = (y * slope[...].astype(f32)).astype(bf16)
-
-
-def back_out(layout, info, s, parts, w, slope, deps=()):
-    _, rows, units = slope.shape
-    later = spec((rows, CH), lambda j, *_: (0, jnp.maximum(j - 1, 0)))
-    slopes = spec((None, rows, CH), lambda j, *_: (s, 0, jnp.maximum(j - 1, 0)))
+            cf[:, :, columns((t + step) % N_TP)] = part[...]
+        bias_grad[...] = sum(
+            jnp.sum(c0[s].astype(f32), axis=0, keepdims=True) for s in range(seqs)
+        )
+
+    for s in range(seqs):
+        y = dot_nt(cf[s], held[columns(j), :])
+
+        @pl.when(j == 0)
+        def _(s=s, y=y):
+            datt[s] = y.astype(bf16)
+
+        @pl.when(j > 0)
+        def _(s=s, y=y):
+            dup[s] = (y * slope[s].astype(f32)).astype(bf16)
+
+
+def back_out(layout, info, parts, w, slope, deps=()):
+    seqs, rows, units = slope.shape
+    later = spec((seqs, rows, CH), lambda j, *_: (0, 0, jnp.maximum(j - 1, 0)))
     return call(
         functools.partial(back_out_body, layout),
         "back_out",
         1 + units // CH,
         info,
         (*parts, slope, *w),
-        [whole(rows, CH)] * 4 + [slopes] + [HBM] * len(w),
+        [whole(seqs, rows, CH)] * 4 + [later] + [ANYWHERE] * len(w),
         (
-            shaped((rows, D)),
+            shaped((seqs, rows, D)),
             shaped((1, CH), f32),
-            shaped((rows, CH)),
-            shaped((rows, units)),
+            shaped((seqs, rows, CH)),
+            shaped((seqs, rows, units)),
         ),
-        [whole(rows, D), whole(1, CH), whole(rows, CH), later],
-        2 * rows * D * (CH + units),
+        [whole(seqs, rows, D), whole(1, CH), whole(seqs, rows, CH), later],
+        2 * seqs * rows * D * (CH + units),
         [
             pltpu.VMEM((CH + units, D), bf16),
             pltpu.SemaphoreType.DMA((1 + units // CH, len(w))),
@@ -585,7 +597,7 @@
         width // 128,
         info,
         (low, q, kv, kvp, do, *tables, *tables_before),
-        [one_of(s, 1, rows), query, pair, pairs, token]
+        [one_of(s, 1, rows), query, pair, pairs, query]
         + [one_of(s, rows, 128)] * 3
         + [one_of(s, blocks, rows, 128)] * 3,
         (
@@ -676,7 +688,7 @@
         N_TP,
         info,
         (att, hidden, *w),
-        [whole(rows, CH), one_of(s, rows, units)] + [HBM] * len(w),
+        [whole(rows, CH), one_of(s, rows, units)] + [ANYWHERE] * len(w),
         (shaped((rows, CH)),) * N_TP,
         [whole(rows, CH)] * N_TP,
         2 * rows * D * (CH + units),
@@ -689,18 +701,23 @@
     )
 
 
-def back_in_body(layout, info, x0, xa, xc, xb, dq, dkv, dup, gain, avg, inv, *refs):
+def back_in_body(layout, info, x0, xa, xc, xb, dq, dkv, back, dup, gain, stats, *refs):
     count = len(layout)
     wq, wu = refs[:count], refs[count : 2 * count]
-    *chunks, held_q, held_u, y, xs, row_sums, column_sums, sems = refs[2 * count :]
+    *chunks, held_q, held_u, y, xs, row_sums, column_sums, both, sems = refs[2 * count :]
     j = pl.program_id(0)
     rows = dq.shape[0]
+
+    @pl.when(j == 0)
+    def _():
+        both[...] = add_rounded(dkv[...], back[...])
+
 
     def work(place, window):
         part = dot_nt(dup[...], held_u[place, :])
         part = part + dot_nt(dq[...], held_q[place, :CH])
-        part = part + dot_nt(dkv[0], held_q[place, CH : 2 * CH])
-        y[:, window] = part + dot_nt(dkv[1], held_q[place, 2 * CH :])
+        part = part + dot_nt(both[0], held_q[place, CH : 2 * CH])
+        y[:, window] = part + dot_nt(both[1], held_q[place, 2 * CH :])
 
     copies = fetch_pieces(layout, [wq, wu], [held_q, held_u], sems, 0)
     with_chunk(layout, info, copies, work)
@@ -712,7 +729,8 @@
             xs[...] = part[...]
 
     total = y[...]
-    standard = (xs[...].astype(f32) - avg[...]) * inv[...]
+    turned = stats[...].T
+    standard = (xs[...].astype(f32) - turned[:, 0:1]) * turned[:, 1:2]
     cross = total * standard
     weight = gain[...].astype(f32)
 
@@ -735,24 +753,24 @@
             chunk[rows:, :] = jnp.concatenate([turned, column_sums[r]], axis=0).astype(bf16)
 
 
-def back_in(layout, info, s, parts, dq, dkv, dup, wq, wu, gain, avg, inv, deps=()):
-    rows, units = dup.shape
+def back_in(layout, info, s, parts, dq, dkv, back, dup, wq, wu, gain, stats, deps=()):
+    _, rows, units = dup.shape
     return call(
         functools.partial(back_in_body, layout),
         "back_in",
         N_TP,
         info,
-        (*parts, dq, dkv, dup, gain, avg, inv, *wq, *wu),
+        (*parts, dq, dkv, back, dup, gain, stats, *wq, *wu),
         [one_of(s, rows, CH)] * 4
         + [
             whole(rows, CH),
             whole(2, rows, CH),
-            whole(rows, units),
+            whole(2, rows, CH),
+            one_of(s, rows, units),
             spec((1, CH), lambda j, info: (0, info[2] ^ j)),
-            one_of(s, rows, 1),
-            one_of(s, rows, 1),
+            one_of(s, 8, rows),
         ]
-        + [HBM] * (2 * len(wq)),
+        + [ANYWHERE] * (2 * len(wq)),
         (shaped((rows + TAIL, CH)),) * N_TP,
         [whole(rows + TAIL, CH)] * N_TP,
         2 * rows * D * (3 * CH + units),
@@ -763,6 +781,7 @@
             pltpu.VMEM((rows, CH), bf16),
             pltpu.VMEM((rows, 128), f32),
             pltpu.VMEM((N_TP, TAIL // 2, CH), f32),
+            pltpu.VMEM((2, rows, CH), bf16),
             pltpu.SemaphoreType.DMA((2 * len(wq),)),
         ],
         deps=deps,
@@ -773,24 +792,24 @@
 GIVEN = ((1, 0), (3, 1))
 
 
-def grad_up_body(info, normed, g0, g1, kept, given, sums):
+def grad_up_body(info, normed, dup, kept, given, sums):
     d = info[2]
-    rights = (g0[...], g1[...])
+    rights = (dup[0], dup[1])
     store_by_rows(d, normed, rights, kept, given)
     sums[...] = sum(jnp.sum(b.astype(f32), axis=0, keepdims=True) for b in rights)
 
 
 def grad_up(info, normed, dup, n, deps=()):
-    rows = dup[0].shape[0]
-    block = spec((rows, CH), lambda j, *_: (0, 2 * n + j))
+    rows = dup.shape[1]
+    block = spec((2, rows, CH), lambda j, *_: (0, 0, 2 * n + j))
     message = spec((2, 1, CH, CH), lambda j, *_: (0, j, 0, 0))
     return call(
         grad_up_body,
         "grad_up",
         2,
         info,
-        (normed, *dup),
-        [whole(2, rows, D)] + [block] * 2,
+        (normed, dup),
+        [whole(2, rows, D), block],
         (shaped((2, 2, CH, CH)),) * 2 + (shaped((1, 2 * CH), f32),),
         [message, message, spec((1, CH), lambda j, *_: (0, j))],
         8 * rows * D * CH,
@@ -798,9 +817,9 @@
     )
 
 
-def grad_down_body(info, hidden, c0, c1, kept, given):
+def grad_down_body(info, hidden, ct, kept, given):
     j = pl.program_id(0)
-    y = (dot_tn(hidden[0], c0[...]) + dot_tn(hidden[1], c1[...])).astype(bf16)
+    y = (dot_tn(hidden[0], ct[0]) + dot_tn(hidden[1], ct[1])).astype(bf16)
 
     def store(target):
         for n in range(target.shape[1]):
@@ -819,16 +838,16 @@
     _, rows, units = hidden.shape
     count = units // CH
     block = spec(
-        (rows, CH),
-        lambda j, info: (0, info[2] ^ jnp.where(j < 2, 2 * j + 1, 2 * j - 4)),
+        (2, rows, CH),
+        lambda j, info: (0, 0, info[2] ^ jnp.where(j < 2, 2 * j + 1, 2 * j - 4)),
     )
     return call(
         grad_down_body,
         "grad_down",
         N_DP,
         info,
-        (hidden, *ct),
-        [whole(2, rows, units)] + [block] * 2,
+        (hidden, ct),
+        [whole(2, rows, units), block],
         (shaped((2, count, CH, CH)),) * 2,
         [
             spec((1, count, CH, CH), lambda j, *_: (jnp.maximum(j - 2, 0), 0, 0, 0)),
@@ -847,7 +866,7 @@
             target[at, 0] = y.astype(bf16)
 
 
-def grad_out_query_body(info, normed, c0, c1, a0, a1, q0, q1, kept, given, sums):
+def grad_out_query_body(info, normed, ct, a0, a1, q0, q1, kept, given, sums):
     j = pl.program_id(0)
     d = info[2]
 
@@ -857,7 +876,7 @@
         for target, which in ((given, GIVEN), (kept, KEPT)):
             for r, at in which:
                 window = columns(d ^ r)
-                y = sum(dot_tn(a, b[:, window]) for a, b in zip(lefts, (c0, c1)))
+                y = sum(dot_tn(a, ct[s, :, window]) for s, a in enumerate(lefts))
                 target[at, 0] = y.astype(bf16)
 
     @pl.when(j == 1)
@@ -875,8 +894,8 @@
         "grad_out_query",
         2,
         info,
-        (normed, *ct, *att, *dq),
-        [whole(2, rows, D)] + [whole(rows, D)] * 2 + [whole(rows, CH)] * 4,
+        (normed, ct, *att, *dq),
+        [whole(2, rows, D)] * 2 + [whole(rows, CH)] * 4,
         (shaped((2, 2, CH, CH)),) * 2 + (shaped((1, CH), f32),),
         [message, message, whole(1, CH)],
         4 * rows * D * 2 * CH,
@@ -884,13 +903,13 @@
     )
 
 
-def grad_key_value_body(info, normed, kv0, kv1, kept, given, sums):
-    rights = (kv0[0], kv1[0])
+def grad_key_value_body(info, normed, kv0, back0, kv1, back1, kept, given, sums):
+    rights = (add_rounded(kv0[0], back0[0]), add_rounded(kv1[0], back1[0]))
     store_by_rows(info[2], normed, rights, kept, given)
     sums[0] = sum(jnp.sum(b.astype(f32), axis=0, keepdims=True) for b in rights)
 
 
-def grad_key_value(info, normed, dkv, deps=()):
+def grad_key_value(info, normed, dkv, sent, deps=()):
     rows = normed.shape[1]
     message = spec((2, 1, CH, CH), lambda j, *_: (0, j, 0, 0))
     pair = spec((1, rows, CH), lambda j, *_: (j, 0, 0))
@@ -899,8 +918,8 @@
         "grad_key_value",
         2,
         info,
-        (normed, *dkv),
-        [whole(2, rows, D)] + [pair] * 2,
+        (normed, dkv[0], sent[0], dkv[1], sent[1]),
+        [whole(2, rows, D)] + [pair] * 4,
         (shaped((2, 2, CH, CH)),) * 2 + (shaped((2, 1, CH), f32),),
         [message, message, spec((1, 1, CH), lambda j, *_: (j, 0, 0))],
         4 * rows * D * 2 * CH,
@@ -908,6 +927,157 @@
     )
 
 
+def finish_blocks_body(info, *refs):
+    *sums, out = refs
+    j = pl.program_id(0)
+    for n in range(len(sums) // 2):
+        here, there = sums[2 * n : 2 * n + 2]
+
+        @pl.when((j >= 2 * n) & (j < 2 * n + 2))
+        def _(here=here, there=there):
+            out[...] = here[0].astype(f32) + there[0].astype(f32)
+
+
+def finish_blocks(info, sums, axis, deps=()):
+    count = len(sums)
+    arrays = [a for pair in sums for a in pair]
+    blocks = [
+        spec((1, CH, CH), lambda j, _, n=n: (jnp.clip(j - 2 * n, 0, 1), 0, 0))
+        for n in range(count)
+        for _ in range(2)
+    ]
+    return call(
+        finish_blocks_body,
+        "finish_blocks",
+        2 * count,
+        info,
+        arrays,
+        blocks,
+        shaped((2 * count * CH, CH) if axis == 0 else (CH, 2 * count * CH), f32),
+        spec((CH, CH), lambda j, _: (j, 0) if axis == 0 else (0, j)),
+        0,
+        deps=deps,
+    )
+
+
+def finish_pair_body(info, here, there, *outs):
+    for n, out in enumerate(outs):
+        out[...] = here[n].astype(f32) + there[n].astype(f32)
+
+
+def finish_pair(info, here, there, deps=()):
+    part = CH // 2
+    return call(
+        finish_pair_body,
+        "finish_pair",
+        2,
+        info,
+        (here, there),
+        [spec((2, part, CH), lambda j, _: (0, j, 0))] * 2,
+        (shaped((CH, CH), f32),) * 2,
+        [spec((part, CH), lambda j, _: (j, 0))] * 2,
+        0,
+        deps=deps,
+    )
+
+
+def finish_out_body(info, *refs):
+    *shares, x, shift, out = refs
+    for s in range(2):
+        own, back, near = shares[3 * s : 3 * s + 3]
+        total = own[...].astype(f32) + back[...].astype(f32) + near[...].astype(f32)
+        out[s] = (x[s].astype(f32) + total + shift[...].astype(f32)).astype(bf16)
+
+
+def finish_out(info, shares, x, shift, deps=()):
+    seqs, rows, _ = x.shape
+    part = rows // 2
+    both = spec((seqs, part, CH), lambda j, _: (0, j, 0))
+    return call(
+        finish_out_body,
+        "finish_out",
+        2,
+        info,
+        (*shares, x, shift),
+        [spec((part, CH), lambda j, _: (j, 0))] * 6 + [both, whole(1, CH)],
+        shaped(x.shape),
+        both,
+        0,
+        deps=deps,
+    )
+
+
+def finish_in_body(info, *refs):
+    shares, tails, wide = refs[:6], refs[6:12], refs[12:18]
+    x, ct, stats, gain, out, sums = refs[18:]
+    weight = gain[...].astype(f32)
+    for s in range(2):
+        at = slice(3 * s, 3 * s + 3)
+        total = sum(a[...].astype(f32) for a in shares[at])
+        tail = sum(a[...].astype(f32) for a in tails[at])
+        column = jnp.concatenate([tail[:8], stats[s]], axis=0).T
+        plain, cross = column[:, 0:1], column[:, 1:2]
+        average, root = column[:, 8:9], column[:, 9:10]
+        standard = (x[s].astype(f32) - average) * root
+        scaled = total * weight - plain * (1.0 / D) - standard * (cross * (1.0 / D))
+        out[s] = ct[s].astype(f32) + root * scaled
+
+    @pl.when(pl.program_id(0) == 0)
+    def _():
+        sums[...] = sum(a[...].astype(f32)[8:] for a in wide)
+
+
+def finish_in(info, shares, x, ct, stats, gain, deps=()):
+    seqs, rows, _ = x.shape
+    part = rows // 2
+    both = spec((seqs, part, CH), lambda j, _: (0, j, 0))
+    last = rows // TAIL
+    return call(
+        finish_in_body,
+        "finish_in",
+        2,
+        info,
+        (*shares, *shares, *shares, x, ct, stats, gain),
+        [spec((part, CH), lambda j, _: (j, 0))] * 6
+        + [spec((TAIL, part), lambda j, _: (last, j))] * 6
+        + [spec((TAIL, CH), lambda j, _: (last, 0))] * 6
+        + [both, both, spec((seqs, 8, part), lambda j, _: (0, 0, j)), whole(1, CH)],
+        (shaped(x.shape, f32), shaped((TAIL // 2, CH), f32)),
+        [both, whole(TAIL // 2, CH)],
+        0,
+        deps=deps,
+    )
+
+
+SMALL = 16
+
+
+def small_table_body(info, query, pair, up0, up1, out, last, table):
+    table[...] = jnp.zeros(table.shape, f32)
+    table[0:1, :] = query[...]
+    table[1:2, :] = pair[0]
+    table[2:3, :] = pair[1]
+    for n in range(2):
+        table[3 + n : 4 + n, :] = up0[:, CH * n : CH * (n + 1)]
+        table[5 + n : 6 + n, :] = up1[:, CH * n : CH * (n + 1)]
+    table[7:8, :] = out[...]
+    table[8:10, :] = last[0:2, :]
+
+
+def small_table(info, arrays):
+    return call(
+        small_table_body,
+        "small_table",
+        1,
+        info,
+        arrays,
+        [whole(*a.shape) for a in arrays],
+        shaped((SMALL, CH), f32),
+        whole(SMALL, CH),
+        0,
+    )
+
+
 def ring(array, step):
     return lax.ppermute(array, "tp", [(i, (i + step) % N_TP) for i in range(N_TP)])
 
@@ -945,8 +1115,8 @@
         both = (self.share.astype(f32) + self.far.astype(f32)).astype(bf16)
         self.near = ring(clock.go(both), 1)
 
-    def total(self, clock):
-        return self.own.astype(f32) + self.back.astype(f32) + clock.go(self.near).astype(f32)
+    def shares(self):
+        return self.own, self.back, self.near
 
 
 class Reduction:
@@ -969,14 +1139,10 @@
         self.here[n] = here
         self.there[n] = swap(here, "ctx", 1, 2) if self.two else lax.psum(here, "ctx")
 
-    def result(self, clock):
-        blocks = []
-        for n in sorted(self.here):
-            total = clock.go(self.there[n]).astype(f32)
-            if self.two:
-                total = total + self.here[n].astype(f32)
-            blocks += [*total]
-        return blocks
+    def sums(self, n):
+        if self.two:
+            return self.here[n], self.there[n]
+        return self.there[n], jnp.zeros_like(self.there[n])
 
 
 def body(
@@ -1037,13 +1203,12 @@
     shards_u = Shards(up_weight, 0, d, c, two, made=False)
     wo_shard = jnp.concatenate([output_weight, down_weight], axis=0)
     shards_o = Shards(wo_shard, 1, d, c, two)
-    clock.sync(x.behind, shards_q.first, *others)
+    clock.sync(x.behind, shards_q.first, *others, shards_u.part)
 
     x.back()
-    x.onward(clock)
     shards_q.over_y(clock)
     shards_u.over_x(clock)
-    gain_here = gain_here.astype(f32)
+    shards_q.near_core(clock)
     circle = jnp.concatenate([both, *others] * 2, axis=1)
     gain_shift = lax.dynamic_slice_in_dim(circle, (N_TP - t) % N_TP * CH, D, 1)
     gain, shift = gain_shift[0:1], gain_shift[1:2]
@@ -1054,17 +1219,20 @@
     before, _ = rotary_tables(doc_starts, jnp.arange(blocks * rows, dtype=jnp.int32))
     before = [a.reshape(seqs, blocks, rows, 128) for a in before]
 
-    clock.sync(shards_q.second, shards_u.first, x.ahead)
-
-    shards_q.near_core(clock)
-    shards_q.far_core(clock)
+    clock.sync(shards_q.second, shards_u.first, x.ahead, shards_q.near, shards_o.part)
     shards_u.near_core(clock)
-    clock.sync(shards_q.near, *shards_q.far_near, shards_u.near)
-
+
+    x.onward(clock)
     shards_u.over_y(clock)
     shards_o.over_x(clock)
-    ct = [Gather(cotangent[s]) for s in range(seqs)]
-    clock.sync(x.far, shards_u.second, shards_o.first, *before, *(g.own for g in ct))
+    shards_q.far_core(clock)
+    clock.sync(
+        x.far,
+        *shards_q.far_near,
+        shards_u.second,
+        shards_o.first,
+        *before,
+    )
 
     def send_keys(s):
         kv[s] = clock.go(kv[s])
@@ -1072,9 +1240,6 @@
             kvp[s] = lax.ppermute(kv[s], "ctx", [(0, 1)])[None]
         else:
             kvp[s] = lax.all_gather(kv[s], "ctx", axis=0, tiled=False)
-
-    def back_out_step(s):
-        return back_out(layout, info, s, ct[s].parts, shards_o.pieces, slope, deps=clock.marks)
 
     def attention_step(s):
         return attention(
@@ -1084,7 +1249,7 @@
             q,
             kv[s],
             kvp[s],
-            datt[s],
+            datt,
             tables,
             before,
             deps=clock.marks,
@@ -1108,46 +1273,41 @@
             x.parts,
             dq[s],
             dkv[s],
-            dup[s],
+            sent[s],
+            dup,
             shards_q.pieces,
             shards_u.pieces,
             gain,
-            avg,
-            inv,
+            stats,
             deps=clock.marks,
         )
 
     layout = layout_of(two)
-    kvp, datt, att, dq, dkv, dup, cf, out_bias_sum = ([None] * seqs for _ in range(8))
+    kvp, att, dq, dkv, sent = ([None] * seqs for _ in range(5))
 
     shards_o.over_y(clock)
     shards_u.far_core(clock)
-    ct[0].sides(clock)
-    normed, avg, inv, q, *kv = norm_qkv(
+    ct = Gather(cotangent)
+    ct.behind, ct.ahead = ring(ct.own, 1), ring(ct.own, -1)
+    normed, stats, q, *kv = norm_qkv(
         layout, info, x.parts, gain, shift, shards_q.pieces, qkv_bias, tables, deps=clock.marks
     )
-    clock.sync(normed, *shards_u.far_near, ct[0].behind, ct[0].ahead)
-
-    ct[0].onward(clock)
-    ct[1].sides(clock)
+    clock.sync(normed, *shards_u.far_near, shards_u.near, ct.behind)
+
+    shards_o.near_core(clock)
+    ct.onward(clock)
+    hidden, slope = mlp_up(layout, info, normed, shards_u.pieces, up_shift, deps=clock.marks)
+    clock.sync(hidden, shards_o.second, ct.ahead, ct.far, shards_o.near)
+
+    shards_o.far_core(clock)
     send_keys(0)
-    hidden, slope = mlp_up(layout, info, normed, shards_u.pieces, up_shift, deps=clock.marks)
-    clock.sync(hidden, ct[0].far, ct[1].behind, shards_o.second)
-
-    shards_o.near_core(clock)
-    shards_o.far_core(clock)
-    clock.sync(shards_o.near, *shards_o.far_near)
-    ct[1].onward(clock)
     send_keys(1)
-    cf[0], out_bias_sum[0], datt[0], dup[0] = back_out_step(0)
-    clock.sync(datt[0], kvp[0])
-
-    att[0], dq[0], dkv_0, sent_0 = attention_step(0)
-    clock.sync(att[0], ct[1].ahead, ct[1].far)
-
-    sent_0 = returned(sent_0)
-    cf[1], out_bias_sum[1], datt[1], dup[1] = back_out_step(1)
-    clock.sync(datt[1], kvp[1])
+    clock.sync(*shards_o.far_near)
+
+    cf, out_bias_sum, datt, dup = back_out(
+        layout, info, ct.parts, shards_o.pieces, slope, deps=clock.marks
+    )
+    clock.sync(datt, kvp[0])
 
     def grad_up_step(n):
         kept, given, sums = grad_up(info, normed, dup, n, deps=clock.marks)
@@ -1157,112 +1317,98 @@
 
     up, up_sums = [], []
     up.append(grad_up_step(0))
-    clock.sync(sent_0)
-    dkv[0] = (dkv_0.astype(f32) + sent_0.astype(f32)).astype(bf16)
     up.append(grad_up_step(1))
     clock.sync(up[0].got)
 
     up[0].add()
     up[0].over_x(0, clock)
-    down_kept, down_given = grad_down(info, hidden, cf, deps=clock.marks)
-    clock.sync(down_kept, up[1].got)
-
-    down = Reduction(down_kept, down_given, clock, two)
+    att[0], dq[0], dkv[0], sent[0] = attention_step(0)
+    clock.sync(att[0], up[0].moved[0], up[1].got, kvp[1])
+
+    sent[0] = returned(sent[0])
     up[1].add()
     up[1].over_x(0, clock)
+    att[1], dq[1], dkv[1], sent[1] = attention_step(1)
+    clock.sync(att[1], sent[0], up[1].moved[0])
+
+    sent[1] = returned(sent[1])
     chunks_0 = out_step(0)
-    clock.sync(chunks_0[0], up[0].moved[0], down.got)
+    clock.sync(chunks_0[0], *clock.marks)
+    down_kept, down_given = grad_down(info, hidden, cf, deps=clock.marks)
+    clock.sync(down_kept, sent[1])
 
     up[0].over_y(0, clock)
+    down = Reduction(down_kept, down_given, clock, two)
+    out_0 = Scatter(chunks_0, clock)
+    out_0.backward(clock)
+    chunks_0 = back_in_step(0)
+    clock.sync(chunks_0[0], up[0].there[0], down.got, out_0.far, out_0.back)
+
+    up[1].over_y(0, clock)
     down.add()
     down.over_x(0, clock)
-    out_0 = Scatter(chunks_0, clock)
-    out_0.backward(clock)
-    att[1], dq[1], dkv_1, sent_1 = attention_step(1)
-    clock.sync(att[1], up[1].moved[0], out_0.far, out_0.back)
-
-    sent_1 = returned(sent_1)
-    up[1].over_y(0, clock)
-    out_0.onward(clock)
+    in_0 = Scatter(chunks_0, clock)
+    in_0.backward(clock)
     head_kept, head_given, query_sum = grad_out_query(
         info, normed, cf, att, dq, deps=clock.marks
     )
-    clock.sync(head_kept, out_0.near, up[0].there[0])
-
+    clock.sync(head_kept, *clock.marks)
+    pair_kept, pair_given, pair_sum = grad_key_value(info, normed, dkv, sent, deps=clock.marks)
+    clock.sync(pair_kept, up[1].there[0], down.moved[0], in_0.far, in_0.back)
+
+    down.over_y(0, clock)
+    down.over_x(1, clock)
     head = Reduction(head_kept, head_given, clock, two)
-    down.over_x(1, clock)
-    chunks_0 = back_in_step(0)
-    clock.sync(chunks_0[0], head.got, sent_1, down.moved[0])
-
+    out_0.onward(clock)
+    in_0.onward(clock)
+    chunks_1 = out_step(1)
+    clock.sync(chunks_1[0], down.there[0], down.moved[1], head.got, out_0.near, in_0.near)
+
+    down.over_y(1, clock)
     head.add()
     head.over_x(0, clock)
-    down.over_y(0, clock)
-    in_0 = Scatter(chunks_0, clock)
-    in_0.backward(clock)
-    dkv[1] = (dkv_1.astype(f32) + sent_1.astype(f32)).astype(bf16)
-    pair_kept, pair_given, pair_sum = grad_key_value(info, normed, dkv, deps=clock.marks)
-    clock.sync(pair_kept, up[1].there[0], down.moved[1])
-
     pair = Reduction(pair_kept, pair_given, clock, two)
-    chunks_1 = out_step(1)
-    clock.sync(chunks_1[0], pair.got, in_0.far, in_0.back, head.moved[0])
-
-    pair.add()
-    pair.over_x(0, clock)
-    down.over_y(1, clock)
-    in_0.onward(clock)
     out_1 = Scatter(chunks_1, clock)
+    out_1.backward(clock)
     chunks_1 = back_in_step(1)
-    clock.sync(chunks_1[0], in_0.near, down.there[0], pair.moved[0], out_1.far)
+    clock.sync(chunks_1[0], down.there[1], head.moved[0], pair.got, out_1.far, out_1.back)
 
     in_1 = Scatter(chunks_1, clock)
     in_1.backward(clock)
     head.over_y(0, clock)
-    out_1.backward(clock)
-    clock.sync(in_1.far, in_1.back, down.there[1])
+    pair.add()
+    pair.over_x(0, clock)
+    up_wg = finish_blocks(info, [up[0].sums(0), up[1].sums(0)], 1, deps=clock.marks)
+    down_wg = finish_blocks(info, [down.sums(0), down.sums(1)], 0, deps=clock.marks)
+    clock.sync(in_1.far, in_1.back, head.there[0], pair.moved[0], up_wg, down_wg)
 
     in_1.onward(clock)
+    pair.over_y(0, clock)
+    output_wg, query_wg = finish_pair(info, *head.sums(0), deps=clock.marks)
+    clock.sync(in_1.near, output_wg)
+
     out_1.onward(clock)
-    pair.over_y(0, clock)
-    clock.sync(in_1.near, out_1.near)
-
-    block_out = jnp.stack([out_0.total(clock), out_1.total(clock)])
-    normed_grad = [in_0.total(clock), in_1.total(clock)]
-    block_out = (block_in.astype(f32) + block_out + output_shift.astype(f32)).astype(bf16)
-    up_wg = jnp.concatenate(up[0].result(clock) + up[1].result(clock), axis=1)
-    down_wg = jnp.concatenate(down.result(clock), axis=0)
-    output_wg, query_wg = head.result(clock)
-    key_wg, value_wg = pair.result(clock)
-
-    def input_gradient(s):
-        total = normed_grad[s]
-        plain, cross = total[rows][:, None], total[rows + 1][:, None]
-        standard = (block_in[s].astype(f32) - avg[s]) * inv[s]
-        scaled = total[:rows] * gain_here
-        return cotangent[s].astype(f32) + inv[s] * (scaled - plain / D - standard * cross / D)
-
-    in_grad = jnp.stack([input_gradient(s) for s in range(seqs)])
-
-    summed = jnp.concatenate(
-        [
-            query_sum.reshape(-1),
-            pair_sum.reshape(-1),
-            *(a.reshape(-1) for a in up_sums),
-            sum(out_bias_sum).reshape(-1),
-            sum(a[rows + 8 : rows + 10] for a in normed_grad).reshape(-1),
-        ]
-    )
-    summed = summed + swap(summed, "dp", 1, N_DP)
-    summed = summed + swap(summed, "dp", 2, N_DP)
-    summed = summed + swap(summed, "ctx", 1, 2) if two else lax.psum(summed, "ctx")
-    at = 0
-    small_grads = []
-    for size in (CH, CH, CH, N_DP * share_units, CH, CH, CH):
-        part = summed[at : at + size]
-        at += size
-        share = size // N_DP
-        small_grads.append(lax.dynamic_slice_in_dim(part, d * share, share, 0))
-    query_bg, key_bg, value_bg, up_bg, output_bg, gain_g, shift_g = small_grads
+    in_grad, last = finish_in(
+        info,
+        (*in_0.shares(), *in_1.shares()),
+        block_in,
+        cotangent,
+        stats,
+        gain_here,
+        deps=clock.marks,
+    )
+    table = small_table(info, (query_sum, pair_sum, *up_sums, out_bias_sum, last))
+    table = table + swap(table, "dp", 1, N_DP)
+    table = table + swap(table, "dp", 2, N_DP)
+    table = table + swap(table, "ctx", 1, 2) if two else lax.psum(table, "ctx")
+    block_out = finish_out(info, (*out_0.shares(), *out_1.shares()), block_in, output_shift)
+    key_wg, value_wg = finish_pair(info, *pair.sums(0))
+
+    share = CH // N_DP
+    mine = lax.dynamic_slice_in_dim(table, d * share, share, 1)
+    query_bg, key_bg, value_bg = mine[0], mine[1], mine[2]
+    output_bg, gain_g, shift_g = mine[7], mine[8], mine[9]
+    up_bg = lax.dynamic_slice_in_dim(table, 3 + d, 1, 0).reshape(-1)
     return (
         block_out,
         in_grad,

time: 573 us -> 542 us (0.946)
  other arithmetic: 79 us -> 45.3 us
  Pallas kernels: 212 us -> 237 us
  local copies, waits for them, and re-layouts: 61.2 us -> 44.3 us
  starting transfers between devices: 77.7 us -> 68.6 us
    pallas_call x15 -> x21, Pallas kernels: 212 us -> 237 us  [call(): pl.pallas_call(without_deps, grid_spec=pltpu.PrefetchScalarGridSpec(num_s...]
    add x12 -> x3, other arithmetic: 14.1 us -> 0.78 us  [the longest x1 0.77 us: body(): table = table + swap(table, 'dp', 1, N_DP)]
    another operation x6 -> x0, local copies, waits for them, and re-layouts: 8.91 us -> none  [result(): blocks += [*total]]
    ppermute x37, waiting for transfers between devices: 30.2 us -> 21.9 us  [swap(): return lax.ppermute(array, axis, [(i, i ^ bit) for i in range(size)])]
    ppermute x37, starting transfers between devices: 34.4 us -> 26.3 us  [swap(): return lax.ppermute(array, axis, [(i, i ^ bit) for i in range(size)])]
    ppermute x24 -> x21, waiting for transfers between devices: 93.7 us -> 101 us  [ring(): lax.ppermute(array, 'tp', [(i, (i + step) % N_TP) for i in range(N_TP)])]
    convert_element_type x4 -> x0, other arithmetic: 7.23 us -> none  [the longest x1 2.8 us: body(): dkv[0] = (dkv_0.astype(f32) + sent_0.astype(f32)).astype(bf16)]
    another operation x4 -> x0, other arithmetic: 6.15 us -> none  [the longest x2 3.47 us: body(): in_grad = jnp.stack([input_gradient(s) for s in range(seqs)])]
  transfers between devices with their start and end apart: 65 -> 62, of which waited for: 22 -> 23; matrix products, arithmetic and copies ran while one was open for 18% -> 10% of each run, Pallas kernels for 38% -> 42%
where the time goes in v4:
time: 542 us; the launch traced here: 534 us
  Pallas kernels  237 us (44%)
  waiting for transfers between devices  137 us (25%)
  starting transfers between devices  68.6 us (13%)
  other arithmetic  45.3 us (8%)
  local copies, waits for them, and re-layouts  44.3 us (8%)
    pallas_call x21, Pallas kernels, call(): pl.pallas_call(without_deps, grid_spec=pltpu.PrefetchScalarGridSpec(num_s...  237 us
    ppermute x21, waiting for transfers between devices, ring(): lax.ppermute(array, 'tp', [(i, (i + step) % N_TP) for i in range(N_TP)])  101 us
    unnamed x135, local copies, waits for them, and re-layouts  33.1 us
    ppermute x21, starting transfers between devices, ring(): lax.ppermute(array, 'tp', [(i, (i + step) % N_TP) for i in range(N_TP)])  32 us
    ppermute x37, starting transfers between devices, swap(): return lax.ppermute(array, axis, [(i, i ^ bit) for i in range(size)])  26.3 us
    ppermute x37, waiting for transfers between devices, swap(): return lax.ppermute(array, axis, [(i, i ^ bit) for i in range(size)])  21.9 us
    convert_element_type x6, other arithmetic, over_y(): here = sum((a.astype(f32) for a in parts)).astype(bf16)  16.9 us
    convert_element_type x5, other arithmetic, add(): total = (self.kept[1].astype(f32) + self.got[1].astype(f32)).astype(bf16)  11.5 us
  transfers between devices with their start and end apart: 62, of which 23 were waited for; matrix products, arithmetic and copies ran while one was open for 10% of the time, Pallas kernels for 42%

profile of v4, /device:TPU:0, one launch (start us, length us, event | category | flops | bytes accessed | tf_op | source)
XLA Modules:
  0.0 533.9 jit_solution(3956914976265765368)
XLA Ops:
  24.5 8.6 %collective-permute-done.4.refs_2_ = bf16[2,512]{1,0:T(2,128)(2,1)S(1)} collective-permute-done((bf16[2,512]{1,0:T(2,128)(2,1)S(1)}, bf16[2,512]{1,0:T(2,128)(2,1)S(1)}, u32[]{:S(2)}, u32[]{:S(2)}) %collective-permute-start.4) | collective-permute-done | bytes 2080 | tf_op jit(solution)/shard_map/ppermute | solution.py:1082
  46.5 17.1 %collective-permute-done.9.refs_2_.refs_3_ = bf16[2,512,512]{2,1,0:T(8,128)(2,1)} collective-permute-done((bf16[2,512,512]{2,1,0:T(8,128)(2,1)}, bf16[2,512,512]{2,1,0:T(8,128)(2,1)}, u32[]{:S(2)}, u32[]{:S(2)}) %collective-permute-start.9) | collective-permute-done | bytes 1048608 | tf_op jit(solution)/shard_map/ppermute | solution.py:1082
  77.1 18.4 %collective-permute-done.11.refs_0_.refs_4_ = bf16[2,512,512]{2,1,0:T(8,128)(2,1)} collective-permute-done((bf16[2,512,512]{2,1,0:T(8,128)(2,1)}, bf16[2,512,512]{2,1,0:T(8,128)(2,1)}, u32[]{:S(2)}, u32[]{:S(2)}) %collective-permute-start.11) | collective-permute-done | bytes 1048608 | tf_op jit(solution)/shard_map/ppermute | solution.py:1082
  100.4 22.5 %norm_qkv.1 = (bf16[2,512,2048]{2,1,0:T(8,128)(2,1)}, f32[2,8,512]{2,1,0:T(8,128)}, bf16[2,512,512]{2,1,0:T(8,128)(2,1)}, bf16[2,512,512]{2,1,0:T(8,128)(2,1)}, bf16[2,512,512]{2,1,0:T(8,128)(2,1)}) custom-call(s32[3]{0:T(128)} %pad_add_fusion.refs_0_, bf16[2,512,512]{2,1,0:T(8,128)(2,1)} %refs_19_.1, bf16[2,512,512]{2,1,0:T(8,128)(2,1)} %tie.53.refs_2_, ...), custom_call_target="tpu_custom_call" | custom-call | flops 128849016 | bytes 388853 | tf_op jit(solution)/shard_map/norm_qkv/pallas_call | solution.py:66
  129.9 19.5 %mlp_up.1 = (bf16[2,512,2048]{2,1,0:T(8,128)(2,1)}, bf16[2,512,2048]{2,1,0:T(8,128)(2,1)}) custom-call(s32[3]{0:T(128)} %pad_add_fusion.refs_0_, bf16[2,512,2048]{2,1,0:T(8,128)(2,1)} %get-tuple-element.72.refs_0_.refs_1_, bf16[1,2048]{1,0:T(2,128)(2,1)} %bitcast.96, bf16[512,2048]{1,0:T(8,128)(2,1)} %refs_17_.3, bf16[512,2048]{1,0:T(8,128)(2,1)} %copy-done.3, ...), custom_call_target="tpu_custom_call" | custom-call | flops 171798688 | bytes 419512 | tf_op jit(solution)/shard_map/mlp_up/pallas_call | solution.py:66
  156.1 19.1 %collective-permute-done.22.refs_3_.refs_4_ = bf16[2,512,512]{2,1,0:T(8,128)(2,1)S(1)} collective-permute-done((bf16[2,512,512]{2,1,0:T(8,128)(2,1)}, bf16[2,512,512]{2,1,0:T(8,128)(2,1)S(1)}, u32[]{:S(2)}, u32[]{:S(2)}) %collective-permute-start.22) | collective-permute-done | bytes 1048608 | tf_op jit(solution)/shard_map/ppermute | solution.py:1082
  184.1 22.1 %back_out.1 = (bf16[2,512,2048]{2,1,0:T(8,128)(2,1)}, f32[1,512]{1,0:T(1,128)}, bf16[2,512,512]{2,1,0:T(8,128)(2,1)}, bf16[2,512,2048]{2,1,0:T(8,128)(2,1)}) custom-call(s32[3]{0:T(128)} %pad_add_fusion.refs_0_, bf16[2,512,512]{2,1,0:T(8,128)(2,1)} %refs_20_.1, bf16[2,512,512]{2,1,0:T(8,128)(2,1)} %tie.61.refs_2_, ...), custom_call_target="tpu_custom_call" | custom-call | flops 214748368 | bytes 566272 | tf_op jit(solution)/shard_map/back_out/pallas_call | solution.py:66
  206.2 9.3 %grad_up.2 = (bf16[2,2,512,512]{3,2,1,0:T(8,128)(2,1)}, bf16[2,2,512,512]{3,2,1,0:T(8,128)(2,1)}, f32[1,1024]{1,0:T(1,128)}) custom-call(s32[3]{0:T(128)} %pad_add_fusion.refs_0_, bf16[2,512,2048]{2,1,0:T(8,128)(2,1)} %get-tuple-element.72.refs_0_.refs_1_, bf16[2,512,2048]{2,1,0:T(8,128)(2,1)} %get-tuple-element.76.refs_2_.refs_8_, ...), custom_call_target="tpu_custom_call" | custom-call | flops 85899344 | bytes 251740 | tf_op jit(solution)/shard_map/grad_up/pallas_call | solution.py:66
  215.7 9.4 %grad_up.3 = (bf16[2,2,512,512]{3,2,1,0:T(8,128)(2,1)}, bf16[2,2,512,512]{3,2,1,0:T(8,128)(2,1)}, f32[1,1024]{1,0:T(1,128)}) custom-call(s32[3]{0:T(128)} %pad_add_fusion.refs_0_, bf16[2,512,2048]{2,1,0:T(8,128)(2,1)} %get-tuple-element.72.refs_0_.refs_1_, bf16[2,512,2048]{2,1,0:T(8,128)(2,1)} %get-tuple-element.76.refs_2_.refs_8_, ...), custom_call_target="tpu_custom_call" | custom-call | flops 85899344 | bytes 251740 | tf_op jit(solution)/shard_map/grad_up/pallas_call | solution.py:66
  233.4 13.1 %attention.2 = (bf16[512,512]{1,0:T(8,128)(2,1)}, bf16[512,512]{1,0:T(8,128)(2,1)}, bf16[2,512,512]{2,1,0:T(8,128)(2,1)}, bf16[1,2,512,512]{3,2,1,0:T(8,128)(2,1)}) custom-call(s32[3]{0:T(128)} %pad_add_fusion.refs_0_, s32[2,1,512]{2,1,0:T(1,128)} %broadcast_in_dim.64.refs_1_, bf16[2,512,512]{2,1,0:T(8,128)(2,1)} %get-tuple-element.70.refs_2_, ...), custom_call_target="tpu_custom_call" | custom-call | flops 128849016 | bytes 209797 | tf_op jit(solution)/shard_map/attention/pallas_call | solution.py:66
  250.9 6.1 %collective-permute-done.29.refs_1_.refs_0_ = bf16[2,512,512]{2,1,0:T(8,128)(2,1)S(1)} collective-permute-done((bf16[2,512,512]{2,1,0:T(8,128)(2,1)}, bf16[2,512,512]{2,1,0:T(8,128)(2,1)S(1)}, u32[]{:S(2)}, u32[]{:S(2)}) %collective-permute-start.29) | collective-permute-done | bytes 1048608 | tf_op jit(solution)/shard_map/ppermute | solution.py:145
  260.5 12.9 %attention.3 = (bf16[512,512]{1,0:T(8,128)(2,1)}, bf16[512,512]{1,0:T(8,128)(2,1)}, bf16[2,512,512]{2,1,0:T(8,128)(2,1)}, bf16[1,2,512,512]{3,2,1,0:T(8,128)(2,1)}) custom-call(s32[3]{0:T(128)} %pad_add_fusion.refs_0_, s32[2,1,512]{2,1,0:T(1,128)} %broadcast_in_dim.64.refs_1_, bf16[2,512,512]{2,1,0:T(8,128)(2,1)} %get-tuple-element.70.refs_2_, ...), custom_call_target="tpu_custom_call" | custom-call | flops 128849016 | bytes 209797 | tf_op jit(solution)/shard_map/attention/pallas_call | solution.py:66
  273.4 10.7 %collective-permute-done.31.refs_1_.refs_7_.refs_3_ = bf16[2,512,512]{2,1,0:T(8,128)(2,1)S(1)} collective-permute-done((bf16[2,512,512]{2,1,0:T(8,128)(2,1)}, bf16[2,512,512]{2,1,0:T(8,128)(2,1)S(1)}, u32[]{:S(2)}, u32[]{:S(2)}) %collective-permute-start.31) | collective-permute-done | bytes 1048608 | tf_op jit(solution)/shard_map/ppermute | solution.py:1260
  287.2 12.2 %project_out.2 = (bf16[512,512]{1,0:T(8,128)(2,1)}, bf16[512,512]{1,0:T(8,128)(2,1)}, bf16[512,512]{1,0:T(8,128)(2,1)}, bf16[512,512]{1,0:T(8,128)(2,1)}) custom-call(s32[3]{0:T(128)} %pad_add_fusion.refs_0_, bf16[512,512]{1,0:T(8,128)(2,1)} %get-tuple-element.80.refs_0_.refs_1_.refs_3_, bf16[2,512,2048]{2,1,0:T(8,128)(2,1)} %get-tuple-element.73.refs_0_.refs_2_.refs_1_, ...), custom_call_target="tpu_custom_call" | custom-call | flops 107374184 | bytes 346030 | tf_op jit(solution)/shard_map/project_out/pallas_call | solution.py:66
  299.4 15.7 %grad_down.1 = (bf16[2,4,512,512]{3,2,1,0:T(8,128)(2,1)}, bf16[2,4,512,512]{3,2,1,0:T(8,128)(2,1)}) custom-call(s32[3]{0:T(128)} %pad_add_fusion.refs_0_, bf16[2,512,2048]{2,1,0:T(8,128)(2,1)} %get-tuple-element.73.refs_0_.refs_2_.refs_1_, bf16[2,512,2048]{2,1,0:T(8,128)(2,1)} %get-tuple-element.87.refs_2_, f32[8,128]{1,0:T(8,128)} %sync.33.refs_3_.refs_2_), custom_call_target="tpu_custom_call" | custom-call | flops 171798688 | bytes 335544 | tf_op jit(solution)/shard_map/grad_down/pallas_call | solution.py:66
  324.6 19.1 %back_in.2 = (bf16[528,512]{1,0:T(8,128)(2,1)}, bf16[528,512]{1,0:T(8,128)(2,1)}, bf16[528,512]{1,0:T(8,128)(2,1)}, bf16[528,512]{1,0:T(8,128)(2,1)}) custom-call(s32[3]{0:T(128)} %pad_add_fusion.refs_0_, bf16[2,512,512]{2,1,0:T(8,128)(2,1)} %refs_19_.1, bf16[2,512,512]{2,1,0:T(8,128)(2,1)} %tie.53.refs_2_, ...), custom_call_target="tpu_custom_call" | custom-call | flops 150323856 | bytes 557793 | tf_op jit(solution)/shard_map/back_in/pallas_call | solution.py:66
  361.4 10.8 %grad_out_query.1 = (bf16[2,2,512,512]{3,2,1,0:T(8,128)(2,1)}, bf16[2,2,512,512]{3,2,1,0:T(8,128)(2,1)}, f32[1,512]{1,0:T(1,128)}) custom-call(s32[3]{0:T(128)} %pad_add_fusion.refs_0_, bf16[2,512,2048]{2,1,0:T(8,128)(2,1)} %get-tuple-element.72.refs_0_.refs_1_, bf16[2,512,2048]{2,1,0:T(8,128)(2,1)} %get-tuple-element.87.refs_2_, ...), custom_call_target="tpu_custom_call" | custom-call | flops 85899344 | bytes 293642 | tf_op jit(solution)/shard_map/grad_out_query/pallas_call | solution.py:66
  372.3 10.0 %grad_key_value.1 = (bf16[2,2,512,512]{3,2,1,0:T(8,128)(2,1)}, bf16[2,2,512,512]{3,2,1,0:T(8,128)(2,1)}, f32[2,1,512]{2,1,0:T(1,128)}) custom-call(s32[3]{0:T(128)} %pad_add_fusion.refs_0_, bf16[2,512,2048]{2,1,0:T(8,128)(2,1)} %get-tuple-element.72.refs_0_.refs_1_, bf16[2,512,512]{2,1,0:T(8,128)(2,1)} %get-tuple-element.92.refs_6_.refs_2_, ...), custom_call_target="tpu_custom_call" | custom-call | flops 85899344 | bytes 251740 | tf_op jit(solution)/shard_map/grad_key_value/pallas_call | solution.py:66
  395.8 12.0 %project_out.3 = (bf16[512,512]{1,0:T(8,128)(2,1)}, bf16[512,512]{1,0:T(8,128)(2,1)}, bf16[512,512]{1,0:T(8,128)(2,1)}, bf16[512,512]{1,0:T(8,128)(2,1)}) custom-call(s32[3]{0:T(128)} %pad_add_fusion.refs_0_, bf16[512,512]{1,0:T(8,128)(2,1)} %get-tuple-element.83.refs_0_.refs_4_.refs_1_, bf16[2,512,2048]{2,1,0:T(8,128)(2,1)} %get-tuple-element.73.refs_0_.refs_2_.refs_1_, ...), custom_call_target="tpu_custom_call" | custom-call | flops 107374184 | bytes 346030 | tf_op jit(solution)/shard_map/project_out/pallas_call | solution.py:66
  407.9 9.9 %collective-permute-done.42.refs_4_.refs_3_ = bf16[512,512]{1,0:T(8,128)(2,1)S(1)} collective-permute-done((bf16[512,512]{1,0:T(8,128)(2,1)}, bf16[512,512]{1,0:T(8,128)(2,1)S(1)}, u32[]{:S(2)}, u32[]{:S(2)}) %collective-permute-start.42) | collective-permute-done | bytes 524320 | tf_op jit(solution)/shard_map/ppermute | solution.py:1082
  429.3 19.1 %back_in.3 = (bf16[528,512]{1,0:T(8,128)(2,1)}, bf16[528,512]{1,0:T(8,128)(2,1)}, bf16[528,512]{1,0:T(8,128)(2,1)}, bf16[528,512]{1,0:T(8,128)(2,1)}) custom-call(s32[3]{0:T(128)} %pad_add_fusion.refs_0_, bf16[2,512,512]{2,1,0:T(8,128)(2,1)} %refs_19_.1, bf16[2,512,512]{2,1,0:T(8,128)(2,1)} %tie.53.refs_2_, ...), custom_call_target="tpu_custom_call" | custom-call | flops 150323856 | bytes 557793 | tf_op jit(solution)/shard_map/back_in/pallas_call | solution.py:66
  465.8 5.9 %finish_blocks.2.refs_4_ = f32[512,2048]{1,0:T(8,128)} custom-call(s32[3]{0:T(128)} %pad_add_fusion.refs_0_, bf16[2,512,512]{2,1,0:T(8,128)(2,1)} %copy-done.33, bf16[2,512,512]{2,1,0:T(8,128)(2,1)} %copy-done.34, bf16[2,512,512]{2,1,0:T(8,128)(2,1)} %fusion.4.refs_3_, bf16[2,512,512]{2,1,0:T(8,128)(2,1)} %copy-done.32, f32[8,128]{1,0:T(8,128)} %sync.39.refs_1_.refs_5_.refs_6_), custom_call_target="tpu_custom_call" | custom-call | bytes 167772 | tf_op jit(solution)/shard_map/finish_blocks/pallas_call | solution.py:66
  471.8 6.1 %finish_blocks.3.refs_5_ = f32[2048,512]{1,0:T(8,128)} custom-call(s32[3]{0:T(128)} %pad_add_fusion.refs_0_, bf16[2,512,512]{2,1,0:T(8,128)(2,1)} %copy-done.35, bf16[2,512,512]{2,1,0:T(8,128)(2,1)} %collective-permute-done.43.refs_1_.refs_2_, bf16[2,512,512]{2,1,0:T(8,128)(2,1)} %fusion.2.refs_3_, ...), custom_call_target="tpu_custom_call" | custom-call | bytes 167772 | tf_op jit(solution)/shard_map/finish_blocks/pallas_call | solution.py:66
  480.2 7.0 %collective-permute-done.53.refs_1_.refs_5_.refs_11_.refs_17_ = bf16[528,512]{1,0:T(8,128)(2,1)S(1)} collective-permute-done((bf16[528,512]{1,0:T(8,128)(2,1)}, bf16[528,512]{1,0:T(8,128)(2,1)S(1)}, u32[]{:S(2)}, u32[]{:S(2)}) %collective-permute-start.53) | collective-permute-done | bytes 540704 | tf_op jit(solution)/shard_map/ppermute | solution.py:1082
  (375 shorter events, 215.3 us)
Async XLA Ops:
  7.0 28.8 %collective-permute-start = (bf16[2,512,512]{2,1,0:T(8,128)(2,1)}, bf16[2,512,512]{2,1,0:T(8,128)(2,1)S(1)}, u32[]{:S(2)}, u32[]{:S(2)}) collective-permute-start(bf16[2,512,512]{2,1,0:T(8,128)(2,1)} %refs_19_.1), channel_id=1, source_target_pairs={{0,1},{1,2},{2,3},{3,0},{4,5},{5,6},{6,7},{7,4},{8,9},{9,10},{10,1... | collective-permute-start | bytes 3145736 | tf_op jit(solution)/shard_map/ppermute | solution.py:1082
  37.7 27.9 %collective-permute-start.10 = (bf16[512,1536]{1,0:T(8,128)(2,1)}, bf16[512,1536]{1,0:T(8,128)(2,1)}, u32[]{:S(2)}, u32[]{:S(2)}) collective-permute-start(bf16[512,1536]{1,0:T(8,128)(2,1)} %tie.52.refs_11_), channel_id=1, source_target_pairs={{0,8},{8,0},{16,24},{24,16},{1,9},{9,1},{17,25},{25,17},{2,10},{10... | collective-permute-start | bytes 4718600 | tf_op jit(solution)/shard_map/ppermute | solution.py:145
  65.7 57.3 %collective-permute-start.16 = (bf16[512,2048]{1,0:T(8,128)(2,1)}, bf16[512,2048]{1,0:T(8,128)(2,1)S(1)}, u32[]{:S(2)}, u32[]{:S(2)}) collective-permute-start(bf16[512,2048]{1,0:T(8,128)(2,1)} %refs_17_.3), channel_id=1, source_target_pairs={{0,8},{8,0},{16,24},{24,16},{1,9},{9,1},{17,25},{25,17},{2,10},{10... | collective-permute-start | bytes 6291464 | tf_op jit(solution)/shard_map/ppermute | solution.py:145
  66.3 31.0 %collective-permute-start.15 = (bf16[2560,256]{1,0:T(8,128)(2,1)}, bf16[2560,256]{1,0:T(8,128)(2,1)S(1)}, u32[]{:S(2)}, u32[]{:S(2)}) collective-permute-start(bf16[2560,256]{1,0:T(8,128)(2,1)} %tie.57), channel_id=1, source_target_pairs={{0,16},{8,24},{16,0},{24,8},{1,17},{9,25},{17,1},{25,9},{2,18},{10... | collective-permute-start | bytes 3932168 | tf_op jit(solution)/shard_map/ppermute | solution.py:145
  67.4 28.2 %collective-permute-start.11 = (bf16[2,512,512]{2,1,0:T(8,128)(2,1)}, bf16[2,512,512]{2,1,0:T(8,128)(2,1)}, u32[]{:S(2)}, u32[]{:S(2)}) collective-permute-start(bf16[2,512,512]{2,1,0:T(8,128)(2,1)} %tie.53.refs_2_), channel_id=1, source_target_pairs={{0,1},{1,2},{2,3},{3,0},{4,5},{5,6},{6,7},{7,4},{8,9},{9,10},{10,1... | collective-permute-start | bytes 3145736 | tf_op jit(solution)/shard_map/ppermute | solution.py:1082
  67.7 27.8 %collective-permute-start.14 = (bf16[256,2048]{1,0:T(8,128)(2,1)}, bf16[256,2048]{1,0:T(8,128)(2,1)}, u32[]{:S(2)}, u32[]{:S(2)}) collective-permute-start(bf16[256,2048]{1,0:T(8,128)(2,1)} %tie.56.refs_0_), channel_id=1, source_target_pairs={{0,4},{4,0},{1,5},{5,1},{2,6},{6,2},{3,7},{7,3},{8,12},{12,8},{9,1... | collective-permute-start | bytes 3145736 | tf_op jit(solution)/shard_map/ppermute | solution.py:145
  76.5 46.4 %collective-permute-start.19 = (bf16[2,512,512]{2,1,0:T(8,128)(2,1)}, bf16[2,512,512]{2,1,0:T(8,128)(2,1)}, u32[]{:S(2)}, u32[]{:S(2)}) collective-permute-start(bf16[2,512,512]{2,1,0:T(8,128)(2,1)} %refs_20_.1), channel_id=1, source_target_pairs={{0,1},{1,2},{2,3},{3,0},{4,5},{5,6},{6,7},{7,4},{8,9},{9,10},{10,1... | collective-permute-start | bytes 3145736 | tf_op jit(solution)/shard_map/ppermute | solution.py:1082
  124.6 50.7 %collective-permute-start.23 = (bf16[2560,512]{1,0:T(8,128)(2,1)}, bf16[2560,512]{1,0:T(8,128)(2,1)S(1)}, u32[]{:S(2)}, u32[]{:S(2)}) collective-permute-start(bf16[2560,512]{1,0:T(8,128)(2,1)} %tie.62.refs_6_.refs_3_), channel_id=1, source_target_pairs={{0,8},{8,0},{16,24},{24,16},{1,9},{9,1},{17,25},{25,17},{2,10},{10... | collective-permute-start | bytes 7864328 | tf_op jit(solution)/shard_map/ppermute | solution.py:145
  124.7 31.4 %collective-permute-start.20 = (bf16[2560,256]{1,0:T(8,128)(2,1)}, bf16[2560,256]{1,0:T(8,128)(2,1)}, u32[]{:S(2)}, u32[]{:S(2)}) collective-permute-start(bf16[2560,256]{1,0:T(8,128)(2,1)} %tie.60.refs_0_), channel_id=1, source_target_pairs={{0,4},{4,0},{1,5},{5,1},{2,6},{6,2},{3,7},{7,3},{8,12},{12,8},{9,1... | collective-permute-start | bytes 3932168 | tf_op jit(solution)/shard_map/ppermute | solution.py:145
  129.1 46.2 %collective-permute-start.22 = (bf16[2,512,512]{2,1,0:T(8,128)(2,1)}, bf16[2,512,512]{2,1,0:T(8,128)(2,1)S(1)}, u32[]{:S(2)}, u32[]{:S(2)}) collective-permute-start(bf16[2,512,512]{2,1,0:T(8,128)(2,1)} %tie.61.refs_2_), channel_id=1, source_target_pairs={{0,1},{1,2},{2,3},{3,0},{4,5},{5,6},{6,7},{7,4},{8,9},{9,10},{10,1... | collective-permute-start | bytes 3145736 | tf_op jit(solution)/shard_map/ppermute | solution.py:1082
  178.3 27.8 %collective-permute-start.24 = (bf16[2,512,512]{2,1,0:T(8,128)(2,1)}, bf16[2,512,512]{2,1,0:T(8,128)(2,1)}, u32[]{:S(2)}, u32[]{:S(2)}) collective-permute-start(bf16[2,512,512]{2,1,0:T(8,128)(2,1)} %tie.63.refs_3_), channel_id=1, source_target_pairs={{0,4},{1,5},{2,6},{3,7},{8,12},{9,13},{10,14},{11,15},{16,20},{17,... | collective-permute-start | bytes 3145736 | tf_op jit(solution)/shard_map/ppermute | solution.py:1240
  285.4 29.6 %collective-permute-start.33 = (bf16[2,512,512]{2,1,0:T(8,128)(2,1)}, bf16[2,512,512]{2,1,0:T(8,128)(2,1)S(1)}, u32[]{:S(2)}, u32[]{:S(2)}) collective-permute-start(bf16[2,512,512]{2,1,0:T(8,128)(2,1)} %tie.72), channel_id=1, source_target_pairs={{4,0},{5,1},{6,2},{7,3},{12,8},{13,9},{14,10},{15,11},{20,16},{21,... | collective-permute-start | bytes 3145736 | tf_op jit(solution)/shard_map/ppermute | solution.py:1260
  316.1 30.5 %collective-permute-start.37 = (bf16[2,4,512,512]{3,2,1,0:T(8,128)(2,1)}, bf16[2,4,512,512]{3,2,1,0:T(8,128)(2,1)}, u32[]{:S(2)}, u32[]{:S(2)}) collective-permute-start(bf16[2,4,512,512]{3,2,1,0:T(8,128)(2,1)} %tie.76), channel_id=1, source_target_pairs={{0,8},{8,0},{16,24},{24,16},{1,9},{9,1},{17,25},{25,17},{2,10},{10... | collective-permute-start | bytes 12582920 | tf_op jit(solution)/shard_map/ppermute | solution.py:145
  319.7 27.0 %collective-permute-start.36 = (bf16[2,512,512]{2,1,0:T(8,128)(2,1)S(1)}, bf16[2,512,512]{2,1,0:T(8,128)(2,1)S(1)}, u32[]{:S(2)}, u32[]{:S(2)}) collective-permute-start(bf16[2,512,512]{2,1,0:T(8,128)(2,1)S(1)} %fusion.5.refs_1_), channel_id=1, source_target_pairs={{0,4},{4,0},{1,5},{5,1},{2,6},{6,2},{3,7},{7,3},{8,12},{12,8},{9,1... | collective-permute-start | bytes 3145736 | tf_op jit(solution)/shard_map/ppermute | solution.py:145
  352.5 30.4 %collective-permute-start.38 = (bf16[2,512,512]{2,1,0:T(8,128)(2,1)}, bf16[2,512,512]{2,1,0:T(8,128)(2,1)S(1)}, u32[]{:S(2)}, u32[]{:S(2)}) collective-permute-start(bf16[2,512,512]{2,1,0:T(8,128)(2,1)} %fusion.4.refs_3_), channel_id=1, source_target_pairs={{0,4},{4,0},{1,5},{5,1},{2,6},{6,2},{3,7},{7,3},{8,12},{12,8},{9,1... | collective-permute-start | bytes 3145736 | tf_op jit(solution)/shard_map/ppermute | solution.py:145
  384.3 33.5 %collective-permute-start.45 = (bf16[2,2,512,512]{3,2,1,0:T(8,128)(2,1)}, bf16[2,2,512,512]{3,2,1,0:T(8,128)(2,1)}, u32[]{:S(2)}, u32[]{:S(2)}) collective-permute-start(bf16[2,2,512,512]{3,2,1,0:T(8,128)(2,1)} %tie.84), channel_id=1, source_target_pairs={{0,8},{8,0},{16,24},{24,16},{1,9},{9,1},{17,25},{25,17},{2,10},{10... | collective-permute-start | bytes 6291464 | tf_op jit(solution)/shard_map/ppermute | solution.py:145
  386.6 31.1 %collective-permute-start.43 = (bf16[2,512,512]{2,1,0:T(8,128)(2,1)S(1)}, bf16[2,512,512]{2,1,0:T(8,128)(2,1)}, u32[]{:S(2)}, u32[]{:S(2)}) collective-permute-start(bf16[2,512,512]{2,1,0:T(8,128)(2,1)S(1)} %fusion.3.refs_1_), channel_id=1, source_target_pairs={{0,4},{4,0},{1,5},{5,1},{2,6},{6,2},{3,7},{7,3},{8,12},{12,8},{9,1... | collective-permute-start | bytes 3145736 | tf_op jit(solution)/shard_map/ppermute | solution.py:145
  388.2 29.6 %collective-permute-start.44 = (bf16[2,512,512]{2,1,0:T(8,128)(2,1)}, bf16[2,512,512]{2,1,0:T(8,128)(2,1)S(1)}, u32[]{:S(2)}, u32[]{:S(2)}) collective-permute-start(bf16[2,512,512]{2,1,0:T(8,128)(2,1)} %tie.83), channel_id=1, source_target_pairs={{0,16},{8,24},{16,0},{24,8},{1,17},{9,25},{17,1},{25,9},{2,18},{10... | collective-permute-start | bytes 3145736 | tf_op jit(solution)/shard_map/ppermute | solution.py:145
  390.4 27.4 %collective-permute-start.46 = (bf16[528,512]{1,0:T(8,128)(2,1)}, bf16[528,512]{1,0:T(8,128)(2,1)S(1)}, u32[]{:S(2)}, u32[]{:S(2)}) collective-permute-start(bf16[528,512]{1,0:T(8,128)(2,1)} %tie.85), channel_id=1, source_target_pairs={{0,1},{1,2},{2,3},{3,0},{4,5},{5,6},{6,7},{7,4},{8,9},{9,10},{10,1... | collective-permute-start | bytes 1622024 | tf_op jit(solution)/shard_map/ppermute | solution.py:1082
  419.1 34.4 %collective-permute-start.51 = (bf16[2,2,512,512]{3,2,1,0:T(8,128)(2,1)}, bf16[2,2,512,512]{3,2,1,0:T(8,128)(2,1)}, u32[]{:S(2)}, u32[]{:S(2)}) collective-permute-start(bf16[2,2,512,512]{3,2,1,0:T(8,128)(2,1)} %tie.90), channel_id=1, source_target_pairs={{0,8},{8,0},{16,24},{24,16},{1,9},{9,1},{17,25},{25,17},{2,10},{10... | collective-permute-start | bytes 6291464 | tf_op jit(solution)/shard_map/ppermute | solution.py:145
  422.5 30.1 %collective-permute-start.49 = (bf16[2,512,512]{2,1,0:T(8,128)(2,1)}, bf16[2,512,512]{2,1,0:T(8,128)(2,1)}, u32[]{:S(2)}, u32[]{:S(2)}) collective-permute-start(bf16[2,512,512]{2,1,0:T(8,128)(2,1)} %fusion.2.refs_3_), channel_id=1, source_target_pairs={{0,4},{4,0},{1,5},{5,1},{2,6},{6,2},{3,7},{7,3},{8,12},{12,8},{9,1... | collective-permute-start | bytes 3145736 | tf_op jit(solution)/shard_map/ppermute | solution.py:145
  425.8 26.9 %collective-permute-start.50 = (bf16[2,512,512]{2,1,0:T(8,128)(2,1)}, bf16[2,512,512]{2,1,0:T(8,128)(2,1)S(1)}, u32[]{:S(2)}, u32[]{:S(2)}) collective-permute-start(bf16[2,512,512]{2,1,0:T(8,128)(2,1)} %tie.89), channel_id=1, source_target_pairs={{0,16},{8,24},{16,0},{24,8},{1,17},{9,25},{17,1},{25,9},{2,18},{10... | collective-permute-start | bytes 3145736 | tf_op jit(solution)/shard_map/ppermute | solution.py:145
  457.5 29.7 %collective-permute-start.54 = (bf16[2,512,512]{2,1,0:T(8,128)(2,1)}, bf16[2,512,512]{2,1,0:T(8,128)(2,1)S(1)}, u32[]{:S(2)}, u32[]{:S(2)}) collective-permute-start(bf16[2,512,512]{2,1,0:T(8,128)(2,1)} %fusion.1.refs_1_), channel_id=1, source_target_pairs={{0,4},{4,0},{1,5},{5,1},{2,6},{6,2},{3,7},{7,3},{8,12},{12,8},{9,1... | collective-permute-start | bytes 3145736 | tf_op jit(solution)/shard_map/ppermute | solution.py:145
  494.0 30.5 %collective-permute-start.58 = (bf16[2,512,512]{2,1,0:T(8,128)(2,1)}, bf16[2,512,512]{2,1,0:T(8,128)(2,1)S(1)}, u32[]{:S(2)}, u32[]{:S(2)}) collective-permute-start(bf16[2,512,512]{2,1,0:T(8,128)(2,1)} %fusion.refs_1_), channel_id=1, source_target_pairs={{0,4},{4,0},{1,5},{5,1},{2,6},{6,2},{3,7},{7,3},{8,12},{12,8},{9,1... | collective-permute-start | bytes 3145736 | tf_op jit(solution)/shard_map/ppermute | solution.py:145
  (96 other events, 885.4 us)

commit v5 on v4

--- a/solution.py
+++ b/solution.py
@@ -16,7 +16,7 @@
 CH = D // N_TP
 EPS = 1e-05
 NEG = -1e30
-VMEM = 56 * 2**20
+VMEM = 127 * 2**19
 COST = 0.02
 
 bf16 = jnp.bfloat16
@@ -42,6 +42,11 @@
 def whole(*block):
     zeros = (0,) * len(block)
     return pl.BlockSpec(block, lambda g, *_: zeros)
+
+
+def once(*block):
+    zeros = (0,) * len(block)
+    return pl.BlockSpec(block, lambda g, *_: zeros, pipeline_mode=pl.Buffered(1))
 
 
 def one_of(s, *block):
@@ -91,6 +96,7 @@
         out_specs=ANYWHERE,
         out_shape=shaped(value.shape, value.dtype),
         input_output_aliases={0: 0},
+        compiler_params=pltpu.CompilerParams(vmem_limit_bytes=VMEM),
         cost_estimate=pl.CostEstimate(flops=0, bytes_accessed=0, transcendentals=0),
         name="tie",
     )(value, *deps)
@@ -135,6 +141,7 @@
                 in_specs=[ANYWHERE] * (len(arrays) + len(self.marks)),
                 out_specs=ANYWHERE,
                 out_shape=shaped((8, 128), f32),
+                compiler_params=pltpu.CompilerParams(vmem_limit_bytes=VMEM),
                 cost_estimate=pl.CostEstimate(flops=0, bytes_accessed=0, transcendentals=0),
                 name="sync",
             )(*arrays, *self.marks),
@@ -663,16 +670,17 @@
     return ((info[2] ^ pl.program_id(0)) + N_TP - info[0]) % N_TP
 
 
-def out_body(layout, info, att, hidden, *refs):
+def out_hidden_body(layout, info, hidden, *refs):
     count = len(layout)
     w, outs = refs[:count], refs[count : count + N_TP]
     held, y, sems = refs[count + N_TP :]
 
     def work(place, window):
-        part = dot_nn(att[...], held[:CH, place]) + dot_nn(hidden[...], held[CH:, place])
-        y[:, window] = part.astype(bf16)
-
-    with_chunk(layout, info, fetch_pieces(layout, [w], [held], sems, 1), work)
+        for s in range(hidden.shape[0]):
+            y[s, :, window] = dot_nn(hidden[s], held[:, place]).astype(bf16)
+
+    lower = [a.at[pl.ds(CH, held.shape[0]), :] for a in w]
+    with_chunk(layout, info, fetch_pieces(layout, [lower], [held], sems, 1), work)
     for r in range(N_TP):
 
         @pl.when(chunk_now(info) == r)
@@ -680,21 +688,60 @@
             outs[r][...] = y[...]
 
 
-def project_out(layout, info, s, att, hidden, w, deps=()):
-    _, rows, units = hidden.shape
+def out_hidden(layout, info, hidden, w, deps=()):
+    seqs, rows, units = hidden.shape
     return call(
-        functools.partial(out_body, layout),
-        "project_out",
+        functools.partial(out_hidden_body, layout),
+        "out_hidden",
         N_TP,
         info,
-        (att, hidden, *w),
-        [whole(rows, CH), one_of(s, rows, units)] + [ANYWHERE] * len(w),
-        (shaped((rows, CH)),) * N_TP,
-        [whole(rows, CH)] * N_TP,
-        2 * rows * D * (CH + units),
+        (hidden, *w),
+        [once(seqs, rows, units)] + [ANYWHERE] * len(w),
+        (shaped((seqs, rows, CH)),) * N_TP,
+        [whole(seqs, rows, CH)] * N_TP,
+        2 * seqs * rows * D * units,
         [
-            pltpu.VMEM((CH + units, D), bf16),
-            pltpu.VMEM((rows, CH), bf16),
+            pltpu.VMEM((units, D), bf16),
+            pltpu.VMEM((seqs, rows, CH), bf16),
+            pltpu.SemaphoreType.DMA((len(w),)),
+        ],
+        deps=deps,
+    )
+
+
+def out_heads_body(layout, info, a0, a1, p0, p1, p2, p3, *refs):
+    count = len(layout)
+    w, outs = refs[:count], refs[count : count + N_TP]
+    held, y, sems = refs[count + N_TP :]
+
+    def work(place, window):
+        for s, att in ((0, a0), (1, a1)):
+            y[s, :, window] = dot_nn(att[...], held[:, place])
+
+    upper = [a.at[pl.ds(0, CH), :] for a in w]
+    with_chunk(layout, info, fetch_pieces(layout, [upper], [held], sems, 1), work)
+    for r, part in enumerate((p0, p1, p2, p3)):
+
+        @pl.when(chunk_now(info) == r)
+        def _(r=r, part=part):
+            outs[r][...] = (y[...] + part[...].astype(f32)).astype(bf16)
+
+
+def out_heads(layout, info, att, parts, w, deps=()):
+    seqs, rows, _ = parts[0].shape
+    return call(
+        functools.partial(out_heads_body, layout),
+        "out_heads",
+        N_TP,
+        info,
+        (*att, *parts, *w),
+        [once(rows, CH)] * 2 + [once(seqs, rows, CH)] * N_TP + [ANYWHERE] * len(w),
+        (shaped((seqs, rows, CH)),) * N_TP,
+        [whole(seqs, rows, CH)] * N_TP,
+        2 * seqs * rows * D * CH,
+        [
+            pltpu.VMEM((CH, D), bf16),
+            pltpu.VMEM((seqs, rows, CH), f32),
             pltpu.SemaphoreType.DMA((len(w),)),
         ],
         deps=deps,
@@ -799,20 +846,20 @@
     sums[...] = sum(jnp.sum(b.astype(f32), axis=0, keepdims=True) for b in rights)
 
 
-def grad_up(info, normed, dup, n, deps=()):
-    rows = dup.shape[1]
-    block = spec((2, rows, CH), lambda j, *_: (0, 0, 2 * n + j))
+def grad_up(info, normed, dup, deps=()):
+    _, rows, units = dup.shape
+    count = units // CH
     message = spec((2, 1, CH, CH), lambda j, *_: (0, j, 0, 0))
     return call(
         grad_up_body,
         "grad_up",
-        2,
+        count,
         info,
         (normed, dup),
-        [whole(2, rows, D), block],
-        (shaped((2, 2, CH, CH)),) * 2 + (shaped((1, 2 * CH), f32),),
+        [whole(2, rows, D), spec((2, rows, CH), lambda j, *_: (0, 0, j))],
+        (shaped((2, count, CH, CH)),) * 2 + (shaped((1, units), f32),),
         [message, message, spec((1, CH), lambda j, *_: (0, j))],
-        8 * rows * D * CH,
+        4 * rows * D * units,
         deps=deps,
     )
 
@@ -925,6 +972,53 @@
         4 * rows * D * 2 * CH,
         deps=deps,
     )
+
+
+def combine_body(counts, info, *refs):
+    ins, outs = refs[: sum(counts)], refs[sum(counts) :]
+    at = 0
+    for count, out in zip(counts, outs):
+        terms = ins[at : at + count]
+        at += count
+
+        def add(terms=terms, out=out):
+            out[...] = sum(a[...].astype(f32) for a in terms).astype(bf16)
+
+        if len(out.shape) == 3:
+            add()
+        else:
+            pl.when(pl.program_id(0) == 0)(add)
+
+
+def combine(info, big, small, deps=()):
+    steps = 2
+    part = 2 * CH // steps
+    ins, in_specs, outs, out_specs = [], [], [], []
+    for job in big:
+        for array, row in job:
+            ins.append(array.reshape(-1, part, CH))
+            in_specs.append(spec((1, part, CH), lambda j, _, at=row // part: (at + j, 0, 0)))
+        outs.append(shaped((steps, part, CH)))
+        out_specs.append(spec((1, part, CH), lambda j, _: (j, 0, 0)))
+    for job in small:
+        ins += job
+        in_specs += [whole(*a.shape) for a in job]
+        outs.append(shaped(job[0].shape))
+        out_specs.append(whole(*job[0].shape))
+    results = call(
+        functools.partial(combine_body, [len(job) for job in (*big, *small)]),
+        "combine",
+        steps,
+        info,
+        ins,
+        in_specs,
+        outs,
+        out_specs,
+        0,
+        deps=deps,
+    )
+    count = len(big)
+    return [a.reshape(2, CH, CH) for a in results[:count]] + list(results[count:])
 
 
 def finish_blocks_body(info, *refs):
@@ -981,25 +1075,21 @@
     )
 
 
-def finish_out_body(info, *refs):
-    *shares, x, shift, out = refs
-    for s in range(2):
-        own, back, near = shares[3 * s : 3 * s + 3]
-        total = own[...].astype(f32) + back[...].astype(f32) + near[...].astype(f32)
-        out[s] = (x[s].astype(f32) + total + shift[...].astype(f32)).astype(bf16)
+def finish_out_body(info, own, back, near, x, shift, out):
+    total = own[...].astype(f32) + back[...].astype(f32) + near[...].astype(f32)
+    out[...] = (x[...].astype(f32) + total + shift[...].astype(f32)).astype(bf16)
 
 
 def finish_out(info, shares, x, shift, deps=()):
     seqs, rows, _ = x.shape
-    part = rows // 2
-    both = spec((seqs, part, CH), lambda j, _: (0, j, 0))
+    both = spec((seqs, rows // 2, CH), lambda j, _: (0, j, 0))
     return call(
         finish_out_body,
         "finish_out",
         2,
         info,
         (*shares, x, shift),
-        [spec((part, CH), lambda j, _: (j, 0))] * 6 + [both, whole(1, CH)],
+        [both] * 4 + [whole(1, CH)],
         shaped(x.shape),
         both,
         0,
@@ -1052,14 +1142,13 @@
 SMALL = 16
 
 
-def small_table_body(info, query, pair, up0, up1, out, last, table):
+def small_table_body(info, query, pair, up, out, last, table):
     table[...] = jnp.zeros(table.shape, f32)
     table[0:1, :] = query[...]
     table[1:2, :] = pair[0]
     table[2:3, :] = pair[1]
-    for n in range(2):
-        table[3 + n : 4 + n, :] = up0[:, CH * n : CH * (n + 1)]
-        table[5 + n : 6 + n, :] = up1[:, CH * n : CH * (n + 1)]
+    for n in range(4):
+        table[3 + n : 4 + n, :] = up[:, CH * n : CH * (n + 1)]
     table[7:8, :] = out[...]
     table[8:10, :] = last[0:2, :]
 
@@ -1104,16 +1193,20 @@
 
 
 class Scatter:
-    def __init__(self, chunks, clock):
-        self.own, self.share, far, self.given = chunks
-        self.far = ring(clock.go(far), 1)
+    def __init__(self, chunks):
+        self.own, self.share, self.first, self.given = chunks
+
+    def forward(self, clock):
+        self.far = ring(clock.go(self.first), 1)
 
     def backward(self, clock):
         self.back = ring(clock.go(self.given), -1)
 
-    def onward(self, clock):
-        both = (self.share.astype(f32) + self.far.astype(f32)).astype(bf16)
-        self.near = ring(clock.go(both), 1)
+    def both(self):
+        return [self.share, self.far]
+
+    def onward(self, both):
+        self.near = ring(both, 1)
 
     def shares(self):
         return self.own, self.back, self.near
@@ -1125,17 +1218,18 @@
         self.got = swap(clock.go(given), "dp", 1, N_DP)
         self.moved, self.here, self.there = {}, {}, {}
 
-    def add(self):
-        total = (self.kept[1].astype(f32) + self.got[1].astype(f32)).astype(bf16)
-        self.across = [total[n : n + 2] for n in range(0, total.shape[0], 2)]
-
-    def over_x(self, n, clock):
-        self.moved[n] = swap(clock.go(self.across[n]), "dp", 2, N_DP)
-
-    def over_y(self, n, clock):
-        at = slice(2 * n, 2 * n + 2)
-        parts = (self.kept[0, at], self.got[0, at], clock.go(self.moved[n]))
-        here = sum(a.astype(f32) for a in parts).astype(bf16)
+    def across(self, n):
+        row = (self.kept.shape[1] + 2 * n) * CH
+        return [(self.kept, row), (self.got, row)]
+
+    def here_sum(self, n):
+        row = 2 * n * CH
+        return [(self.kept, row), (self.got, row), (self.moved[n], 0)]
+
+    def over_x(self, n, across):
+        self.moved[n] = swap(across, "dp", 2, N_DP)
+
+    def over_y(self, n, here):
         self.here[n] = here
         self.there[n] = swap(here, "ctx", 1, 2) if self.two else lax.psum(here, "ctx")
 
@@ -1260,11 +1354,6 @@
             return lax.ppermute(clock.go(sent[0]), "ctx", [(1, 0)])
         return lax.psum_scatter(clock.go(sent), "ctx", scatter_dimension=0, tiled=False)
 
-    def out_step(s):
-        return project_out(
-            layout, info, s, att[s], hidden, shards_o.pieces, deps=clock.marks
-        )
-
     def back_in_step(s):
         return back_in(
             layout,
@@ -1297,111 +1386,124 @@
     shards_o.near_core(clock)
     ct.onward(clock)
     hidden, slope = mlp_up(layout, info, normed, shards_u.pieces, up_shift, deps=clock.marks)
-    clock.sync(hidden, shards_o.second, ct.ahead, ct.far, shards_o.near)
+    clock.sync(hidden, shards_o.second, ct.ahead, shards_o.near)
 
     shards_o.far_core(clock)
     send_keys(0)
     send_keys(1)
     clock.sync(*shards_o.far_near)
+    out_parts = out_hidden(layout, info, hidden, shards_o.pieces, deps=clock.marks)
+    clock.sync(out_parts[0], ct.far)
 
     cf, out_bias_sum, datt, dup = back_out(
         layout, info, ct.parts, shards_o.pieces, slope, deps=clock.marks
     )
-    clock.sync(datt, kvp[0])
-
-    def grad_up_step(n):
-        kept, given, sums = grad_up(info, normed, dup, n, deps=clock.marks)
-        up_sums.append(sums)
-        clock.sync(kept)
-        return Reduction(kept, given, clock, two)
-
-    up, up_sums = [], []
-    up.append(grad_up_step(0))
-    up.append(grad_up_step(1))
-    clock.sync(up[0].got)
-
-    up[0].add()
-    up[0].over_x(0, clock)
+    clock.sync(datt, kvp[0], kvp[1])
+
+    def added(big, small=()):
+        return combine(info, big, list(small), deps=clock.marks)
+
+    up_kept, up_given, up_sum = grad_up(info, normed, dup, deps=clock.marks)
+    clock.sync(up_kept)
+    up = Reduction(up_kept, up_given, clock, two)
     att[0], dq[0], dkv[0], sent[0] = attention_step(0)
-    clock.sync(att[0], up[0].moved[0], up[1].got, kvp[1])
+    clock.sync(att[0], up.got)
 
     sent[0] = returned(sent[0])
-    up[1].add()
-    up[1].over_x(0, clock)
+    across, across_1 = added([up.across(0), up.across(1)])
+    up.over_x(0, across)
+    clock.sync(across)
+    down_kept, down_given = grad_down(info, hidden, cf, deps=clock.marks)
+    clock.sync(down_kept, *clock.marks)
     att[1], dq[1], dkv[1], sent[1] = attention_step(1)
-    clock.sync(att[1], sent[0], up[1].moved[0])
+    clock.sync(att[1], sent[0], up.moved[0])
 
     sent[1] = returned(sent[1])
-    chunks_0 = out_step(0)
-    clock.sync(chunks_0[0], *clock.marks)
-    down_kept, down_given = grad_down(info, hidden, cf, deps=clock.marks)
-    clock.sync(down_kept, sent[1])
-
-    up[0].over_y(0, clock)
+    up.over_x(1, clock.go(across_1))
     down = Reduction(down_kept, down_given, clock, two)
-    out_0 = Scatter(chunks_0, clock)
-    out_0.backward(clock)
-    chunks_0 = back_in_step(0)
-    clock.sync(chunks_0[0], up[0].there[0], down.got, out_0.far, out_0.back)
-
-    up[1].over_y(0, clock)
-    down.add()
-    down.over_x(0, clock)
-    in_0 = Scatter(chunks_0, clock)
-    in_0.backward(clock)
+    (here,) = added([up.here_sum(0)])
+    clock.sync(here)
+    out = Scatter(out_heads(layout, info, att, out_parts, shards_o.pieces, deps=clock.marks))
+    clock.sync(out.own, *clock.marks)
     head_kept, head_given, query_sum = grad_out_query(
         info, normed, cf, att, dq, deps=clock.marks
     )
-    clock.sync(head_kept, *clock.marks)
+    clock.sync(head_kept, down.got)
+    across, across_1 = added([down.across(0), down.across(1)])
+    clock.sync(across, sent[1])
+    clock.sync(up.moved[1])
+
+    out.forward(clock)
+    up.over_y(0, clock.go(here))
+    down.over_x(0, clock.go(across))
+    head = Reduction(head_kept, head_given, clock, two)
+    (here,) = added([up.here_sum(1)])
+    clock.sync(here)
+    back_0 = Scatter(back_in_step(0))
+    clock.sync(back_0.own, out.far)
+    clock.sync(up.there[0])
+    clock.sync(down.moved[0], head.got)
+
+    back_0.forward(clock)
+    back_0.backward(clock)
+    up.over_y(1, clock.go(here))
+    down.over_x(1, clock.go(across_1))
+    here, across, out_both = added([down.here_sum(0), head.across(0)], [out.both()])
+    clock.sync(here)
     pair_kept, pair_given, pair_sum = grad_key_value(info, normed, dkv, sent, deps=clock.marks)
-    clock.sync(pair_kept, up[1].there[0], down.moved[0], in_0.far, in_0.back)
-
-    down.over_y(0, clock)
-    down.over_x(1, clock)
-    head = Reduction(head_kept, head_given, clock, two)
-    out_0.onward(clock)
-    in_0.onward(clock)
-    chunks_1 = out_step(1)
-    clock.sync(chunks_1[0], down.there[0], down.moved[1], head.got, out_0.near, in_0.near)
-
-    down.over_y(1, clock)
-    head.add()
-    head.over_x(0, clock)
+    clock.sync(pair_kept, back_0.far, back_0.back)
+    clock.sync(up.there[1])
+    clock.sync(down.moved[1])
+
+    out.backward(clock)
+    down.over_y(0, clock.go(here))
+    head.over_x(0, clock.go(across))
     pair = Reduction(pair_kept, pair_given, clock, two)
-    out_1 = Scatter(chunks_1, clock)
-    out_1.backward(clock)
-    chunks_1 = back_in_step(1)
-    clock.sync(chunks_1[0], down.there[1], head.moved[0], pair.got, out_1.far, out_1.back)
-
-    in_1 = Scatter(chunks_1, clock)
-    in_1.backward(clock)
-    head.over_y(0, clock)
-    pair.add()
-    pair.over_x(0, clock)
-    up_wg = finish_blocks(info, [up[0].sums(0), up[1].sums(0)], 1, deps=clock.marks)
+    here, both_0 = added([down.here_sum(1)], [back_0.both()])
+    clock.sync(here)
+    back_1 = Scatter(back_in_step(1))
+    clock.sync(back_1.own, out.back)
+    clock.sync(down.there[0])
+    clock.sync(head.moved[0], pair.got)
+
+    back_1.forward(clock)
+    back_1.backward(clock)
+    down.over_y(1, clock.go(here))
+    across, here = added([pair.across(0), head.here_sum(0)])
+    pair.over_x(0, across)
+    clock.sync(across)
+    up_wg = finish_blocks(info, [up.sums(0), up.sums(1)], 1, deps=clock.marks)
+    clock.sync(up_wg, back_1.far, back_1.back)
+    clock.sync(down.there[1])
+    clock.sync(pair.moved[0])
+
+    back_0.onward(clock.go(both_0))
+    head.over_y(0, clock.go(here))
+    here, both_1 = added([pair.here_sum(0)], [back_1.both()])
+    back_1.onward(both_1)
+    clock.sync(here)
     down_wg = finish_blocks(info, [down.sums(0), down.sums(1)], 0, deps=clock.marks)
-    clock.sync(in_1.far, in_1.back, head.there[0], pair.moved[0], up_wg, down_wg)
-
-    in_1.onward(clock)
-    pair.over_y(0, clock)
-    output_wg, query_wg = finish_pair(info, *head.sums(0), deps=clock.marks)
-    clock.sync(in_1.near, output_wg)
-
-    out_1.onward(clock)
+    clock.sync(down_wg, back_0.near, back_1.near)
+    clock.sync(head.there[0])
+
+    out.onward(clock.go(out_both))
+    pair.over_y(0, clock.go(here))
     in_grad, last = finish_in(
         info,
-        (*in_0.shares(), *in_1.shares()),
+        (*back_0.shares(), *back_1.shares()),
         block_in,
         cotangent,
         stats,
         gain_here,
         deps=clock.marks,
     )
-    table = small_table(info, (query_sum, pair_sum, *up_sums, out_bias_sum, last))
+    clock.sync(in_grad)
+    table = small_table(info, (query_sum, pair_sum, up_sum, out_bias_sum, last))
+    output_wg, query_wg = finish_pair(info, *head.sums(0), deps=clock.marks)
     table = table + swap(table, "dp", 1, N_DP)
     table = table + swap(table, "dp", 2, N_DP)
     table = table + swap(table, "ctx", 1, 2) if two else lax.psum(table, "ctx")
-    block_out = finish_out(info, (*out_0.shares(), *out_1.shares()), block_in, output_shift)
+    block_out = finish_out(info, out.shares(), block_in, output_shift)
     key_wg, value_wg = finish_pair(info, *pair.sums(0))
 
     share = CH // N_DP

time: 542 us -> 496 us (0.915)
  other arithmetic: 45.3 us -> 11.9 us
  Pallas kernels: 237 us -> 269 us
  local copies, waits for them, and re-layouts: 44.3 us -> 19.8 us
  waiting for transfers between devices: 137 us -> 121 us
    convert_element_type x15 -> x0, other arithmetic: 33.3 us -> none  [the longest x6 16.9 us: over_y(): here = sum((a.astype(f32) for a in parts)).astype(bf16)]
    pallas_call x21 -> x28, Pallas kernels: 237 us -> 269 us  [call(): pl.pallas_call(without_deps, grid_spec=pltpu.PrefetchScalarGridSpec(num_s...]
    unnamed x135 -> x39, local copies, waits for them, and re-layouts: 33.1 us -> 10.1 us
    ppermute x21 -> x18, waiting for transfers between devices: 101 us -> 78.5 us  [ring(): lax.ppermute(array, 'tp', [(i, (i + step) % N_TP) for i in range(N_TP)])]
    ppermute x21 -> x18, starting transfers between devices: 32 us -> 21.2 us  [ring(): lax.ppermute(array, 'tp', [(i, (i + step) % N_TP) for i in range(N_TP)])]
    ppermute x37 -> x36, waiting for transfers between devices: 21.9 us -> 31.3 us  [swap(): return lax.ppermute(array, axis, [(i, i ^ bit) for i in range(size)])]
    ppermute x37 -> x36, starting transfers between devices: 26.3 us -> 33.6 us  [swap(): return lax.ppermute(array, axis, [(i, i ^ bit) for i in range(size)])]
  transfers between devices with their start and end apart: 62 -> 58, of which waited for: 23 -> 21; matrix products, arithmetic and copies ran while one was open for 10% -> 5% of each run, Pallas kernels for 42% -> 51%
where the time goes in v5:
time: 496 us; the launch traced here: 488 us
  Pallas kernels  269 us (54%)
  waiting for transfers between devices  121 us (24%)
  starting transfers between devices  63.9 us (13%)
  local copies, waits for them, and re-layouts  19.8 us (4%)
  other arithmetic  11.9 us (2%)
    pallas_call x28, Pallas kernels, call(): pl.pallas_call(without_deps, grid_spec=pltpu.PrefetchScalarGridSpec(num_s...  269 us
    ppermute x18, waiting for transfers between devices, ring(): lax.ppermute(array, 'tp', [(i, (i + step) % N_TP) for i in range(N_TP)])  78.5 us
    ppermute x36, starting transfers between devices, swap(): return lax.ppermute(array, axis, [(i, i ^ bit) for i in range(size)])  33.6 us
    ppermute x36, waiting for transfers between devices, swap(): return lax.ppermute(array, axis, [(i, i ^ bit) for i in range(size)])  31.3 us
    ppermute x18, starting transfers between devices, ring(): lax.ppermute(array, 'tp', [(i, (i + step) % N_TP) for i in range(N_TP)])  21.2 us
    ppermute x2, waiting for transfers between devices, returned(): return lax.ppermute(clock.go(sent[0]), 'ctx', [(1, 0)])  11.5 us
    unnamed x39, local copies, waits for them, and re-layouts  10.1 us
  transfers between devices with their start and end apart: 58, of which 21 were waited for; matrix products, arithmetic and copies ran while one was open for 5% of the time, Pallas kernels for 51%

profile of v5, /device:TPU:0, one launch (start us, length us, event | category | flops | bytes accessed | tf_op | source)
XLA Modules:
  0.0 487.5 jit_solution(3974330804979519892)
XLA Ops:
  24.5 8.6 %collective-permute-done.4.refs_2_ = bf16[2,512]{1,0:T(2,128)(2,1)S(1)} collective-permute-done((bf16[2,512]{1,0:T(2,128)(2,1)S(1)}, bf16[2,512]{1,0:T(2,128)(2,1)S(1)}, u32[]{:S(2)}, u32[]{:S(2)}) %collective-permute-start.4) | collective-permute-done | bytes 2080 | tf_op jit(solution)/shard_map/ppermute | solution.py:1171
  46.7 15.7 %collective-permute-done.9.refs_2_.refs_3_ = bf16[2,512,512]{2,1,0:T(8,128)(2,1)} collective-permute-done((bf16[2,512,512]{2,1,0:T(8,128)(2,1)}, bf16[2,512,512]{2,1,0:T(8,128)(2,1)}, u32[]{:S(2)}, u32[]{:S(2)}) %collective-permute-start.9) | collective-permute-done | bytes 1048608 | tf_op jit(solution)/shard_map/ppermute | solution.py:1171
  75.7 15.6 %collective-permute-done.14.refs_3_.refs_0_ = bf16[256,2048]{1,0:T(8,128)(2,1)} collective-permute-done((bf16[256,2048]{1,0:T(8,128)(2,1)}, bf16[256,2048]{1,0:T(8,128)(2,1)}, u32[]{:S(2)}, u32[]{:S(2)}) %collective-permute-start.14) | collective-permute-done | bytes 1048608 | tf_op jit(solution)/shard_map/ppermute | solution.py:152
  97.9 22.5 %norm_qkv.1 = (bf16[2,512,2048]{2,1,0:T(8,128)(2,1)}, f32[2,8,512]{2,1,0:T(8,128)}, bf16[2,512,512]{2,1,0:T(8,128)(2,1)}, bf16[2,512,512]{2,1,0:T(8,128)(2,1)}, bf16[2,512,512]{2,1,0:T(8,128)(2,1)}) custom-call(s32[3]{0:T(128)} %pad_add_fusion.refs_0_, bf16[2,512,512]{2,1,0:T(8,128)(2,1)} %refs_19_.1, bf16[2,512,512]{2,1,0:T(8,128)(2,1)} %tie.46.refs_2_, ...), custom_call_target="tpu_custom_call" | custom-call | flops 128849016 | bytes 388853 | tf_op jit(solution)/shard_map/norm_qkv/pallas_call | solution.py:71
  125.2 19.6 %mlp_up.1 = (bf16[2,512,2048]{2,1,0:T(8,128)(2,1)}, bf16[2,512,2048]{2,1,0:T(8,128)(2,1)}) custom-call(s32[3]{0:T(128)} %pad_add_fusion.refs_0_, bf16[2,512,2048]{2,1,0:T(8,128)(2,1)} %get-tuple-element.82.refs_0_.refs_1_, bf16[1,2048]{1,0:T(2,128)(2,1)} %bitcast.80, bf16[512,2048]{1,0:T(8,128)(2,1)} %refs_17_.3, ...), custom_call_target="tpu_custom_call" | custom-call | flops 171798688 | bytes 419512 | tf_op jit(solution)/shard_map/mlp_up/pallas_call | solution.py:71
  159.3 16.4 %out_hidden.1 = (bf16[2,512,512]{2,1,0:T(8,128)(2,1)}, bf16[2,512,512]{2,1,0:T(8,128)(2,1)}, bf16[2,512,512]{2,1,0:T(8,128)(2,1)}, bf16[2,512,512]{2,1,0:T(8,128)(2,1)}) custom-call(s32[3]{0:T(128)} %pad_add_fusion.refs_0_, bf16[2,512,2048]{2,1,0:T(8,128)(2,1)} %get-tuple-element.83.refs_0_.refs_1_, bf16[2560,512]{1,0:T(8,128)(2,1)} %tie.54.refs_2_.refs_6_.refs_7_, ...), custom_call_target="tpu_custom_call" | custom-call | flops 171798688 | bytes 377487 | tf_op jit(solution)/shard_map/out_hidden/pallas_call | solution.py:71
  179.9 22.1 %back_out.1 = (bf16[2,512,2048]{2,1,0:T(8,128)(2,1)}, f32[1,512]{1,0:T(1,128)}, bf16[2,512,512]{2,1,0:T(8,128)(2,1)}, bf16[2,512,2048]{2,1,0:T(8,128)(2,1)}) custom-call(s32[3]{0:T(128)} %pad_add_fusion.refs_0_, bf16[2,512,512]{2,1,0:T(8,128)(2,1)} %refs_20_.1, bf16[2,512,512]{2,1,0:T(8,128)(2,1)} %tie.56.refs_2_, ...), custom_call_target="tpu_custom_call" | custom-call | flops 214748368 | bytes 566272 | tf_op jit(solution)/shard_map/back_out/pallas_call | solution.py:71
  202.0 14.2 %grad_up.1 = (bf16[2,4,512,512]{3,2,1,0:T(8,128)(2,1)}, bf16[2,4,512,512]{3,2,1,0:T(8,128)(2,1)}, f32[1,2048]{1,0:T(1,128)}) custom-call(s32[3]{0:T(128)} %pad_add_fusion.refs_0_, bf16[2,512,2048]{2,1,0:T(8,128)(2,1)} %get-tuple-element.82.refs_0_.refs_1_, bf16[2,512,2048]{2,1,0:T(8,128)(2,1)} %get-tuple-element.87.refs_2_.refs_8_, ...), custom_call_target="tpu_custom_call" | custom-call | flops 171798688 | bytes 335708 | tf_op jit(solution)/shard_map/grad_up/pallas_call | solution.py:71
  216.8 13.1 %attention.2 = (bf16[512,512]{1,0:T(8,128)(2,1)}, bf16[512,512]{1,0:T(8,128)(2,1)}, bf16[2,512,512]{2,1,0:T(8,128)(2,1)}, bf16[1,2,512,512]{3,2,1,0:T(8,128)(2,1)}) custom-call(s32[3]{0:T(128)} %pad_add_fusion.refs_0_, s32[2,1,512]{2,1,0:T(1,128)} %broadcast_in_dim.64.refs_1_, bf16[2,512,512]{2,1,0:T(8,128)(2,1)} %get-tuple-element.80.refs_2_, ...), custom_call_target="tpu_custom_call" | custom-call | flops 128849016 | bytes 209797 | tf_op jit(solution)/shard_map/attention/pallas_call | solution.py:71
  236.6 15.7 %grad_down.1 = (bf16[2,4,512,512]{3,2,1,0:T(8,128)(2,1)}, bf16[2,4,512,512]{3,2,1,0:T(8,128)(2,1)}) custom-call(s32[3]{0:T(128)} %pad_add_fusion.refs_0_, bf16[2,512,2048]{2,1,0:T(8,128)(2,1)} %get-tuple-element.83.refs_0_.refs_1_, bf16[2,512,2048]{2,1,0:T(8,128)(2,1)} %get-tuple-element.91.refs_2_, f32[8,128]{1,0:T(8,128)} %sync.48.refs_3_.refs_1_.refs_2_), custom_call_target="tpu_custom_call" | custom-call | flops 171798688 | bytes 335544 | tf_op jit(solution)/shard_map/grad_down/pallas_call | solution.py:71
  252.3 13.0 %attention.3 = (bf16[512,512]{1,0:T(8,128)(2,1)}, bf16[512,512]{1,0:T(8,128)(2,1)}, bf16[2,512,512]{2,1,0:T(8,128)(2,1)}, bf16[1,2,512,512]{3,2,1,0:T(8,128)(2,1)}) custom-call(s32[3]{0:T(128)} %pad_add_fusion.refs_0_, s32[2,1,512]{2,1,0:T(1,128)} %broadcast_in_dim.64.refs_1_, bf16[2,512,512]{2,1,0:T(8,128)(2,1)} %get-tuple-element.80.refs_2_, ...), custom_call_target="tpu_custom_call" | custom-call | flops 128849016 | bytes 209797 | tf_op jit(solution)/shard_map/attention/pallas_call | solution.py:71
  271.6 10.2 %out_heads.1 = (bf16[2,512,512]{2,1,0:T(8,128)(2,1)}, bf16[2,512,512]{2,1,0:T(8,128)(2,1)}, bf16[2,512,512]{2,1,0:T(8,128)(2,1)}, bf16[2,512,512]{2,1,0:T(8,128)(2,1)}) custom-call(s32[3]{0:T(128)} %pad_add_fusion.refs_0_, bf16[512,512]{1,0:T(8,128)(2,1)} %get-tuple-element.90.refs_0_.refs_1_.refs_3_, ...), custom_call_target="tpu_custom_call" | custom-call | flops 42949672 | bytes 398458 | tf_op jit(solution)/shard_map/out_heads/pallas_call | solution.py:71
  281.7 10.8 %grad_out_query.1 = (bf16[2,2,512,512]{3,2,1,0:T(8,128)(2,1)}, bf16[2,2,512,512]{3,2,1,0:T(8,128)(2,1)}, f32[1,512]{1,0:T(1,128)}) custom-call(s32[3]{0:T(128)} %pad_add_fusion.refs_0_, bf16[2,512,2048]{2,1,0:T(8,128)(2,1)} %get-tuple-element.82.refs_0_.refs_1_, bf16[2,512,2048]{2,1,0:T(8,128)(2,1)} %get-tuple-element.91.refs_2_, ...), custom_call_target="tpu_custom_call" | custom-call | flops 85899344 | bytes 293642 | tf_op jit(solution)/shard_map/grad_out_query/pallas_call | solution.py:71
  296.5 11.5 %collective-permute-done.33.refs_1_.refs_5_.refs_7_ = bf16[2,512,512]{2,1,0:T(8,128)(2,1)} collective-permute-done((bf16[2,512,512]{2,1,0:T(8,128)(2,1)}, bf16[2,512,512]{2,1,0:T(8,128)(2,1)}, u32[]{:S(2)}, u32[]{:S(2)}) %collective-permute-start.33) | collective-permute-done | bytes 1048608 | tf_op jit(solution)/shard_map/ppermute | solution.py:1354
  308.6 6.4 %collective-permute-start.36 = (bf16[2,512,512]{2,1,0:T(8,128)(2,1)}, bf16[2,512,512]{2,1,0:T(8,128)(2,1)}, u32[]{:S(2)}, u32[]{:S(2)}) collective-permute-start(bf16[2,512,512]{2,1,0:T(8,128)(2,1)} %tie.67.refs_1_), channel_id=1, source_target_pairs={{0,4},{4,0},{1,5},{5,1},{2,6},{6,2},{3,7},{7,3},{8,12},{12,8},{9,1... | collective-permute-start | bytes 3145736 | tf_op jit(solution)/shard_map/ppermute | solution.py:152
  320.5 19.1 %back_in.2 = (bf16[528,512]{1,0:T(8,128)(2,1)}, bf16[528,512]{1,0:T(8,128)(2,1)}, bf16[528,512]{1,0:T(8,128)(2,1)}, bf16[528,512]{1,0:T(8,128)(2,1)}) custom-call(s32[3]{0:T(128)} %pad_add_fusion.refs_0_, bf16[2,512,512]{2,1,0:T(8,128)(2,1)} %refs_19_.1, bf16[2,512,512]{2,1,0:T(8,128)(2,1)} %tie.46.refs_2_, ...), custom_call_target="tpu_custom_call" | custom-call | flops 150323856 | bytes 557793 | tf_op jit(solution)/shard_map/back_in/pallas_call | solution.py:71
  351.4 9.9 %grad_key_value.1 = (bf16[2,2,512,512]{3,2,1,0:T(8,128)(2,1)}, bf16[2,2,512,512]{3,2,1,0:T(8,128)(2,1)}, f32[2,1,512]{2,1,0:T(1,128)}) custom-call(s32[3]{0:T(128)} %pad_add_fusion.refs_0_, bf16[2,512,2048]{2,1,0:T(8,128)(2,1)} %get-tuple-element.82.refs_0_.refs_1_, bf16[2,512,512]{2,1,0:T(8,128)(2,1)} %get-tuple-element.111.refs_6_.refs_2_, ...), custom_call_target="tpu_custom_call" | custom-call | flops 85899344 | bytes 251740 | tf_op jit(solution)/shard_map/grad_key_value/pallas_call | solution.py:71
  361.3 8.7 %collective-permute-done.40.refs_1_.refs_5_ = bf16[528,512]{1,0:T(8,128)(2,1)} collective-permute-done((bf16[528,512]{1,0:T(8,128)(2,1)}, bf16[528,512]{1,0:T(8,128)(2,1)}, u32[]{:S(2)}, u32[]{:S(2)}) %collective-permute-start.40) | collective-permute-done | bytes 540704 | tf_op jit(solution)/shard_map/ppermute | solution.py:1171
  378.2 19.1 %back_in.3 = (bf16[528,512]{1,0:T(8,128)(2,1)}, bf16[528,512]{1,0:T(8,128)(2,1)}, bf16[528,512]{1,0:T(8,128)(2,1)}, bf16[528,512]{1,0:T(8,128)(2,1)}) custom-call(s32[3]{0:T(128)} %pad_add_fusion.refs_0_, bf16[2,512,512]{2,1,0:T(8,128)(2,1)} %refs_19_.1, bf16[2,512,512]{2,1,0:T(8,128)(2,1)} %tie.46.refs_2_, ...), custom_call_target="tpu_custom_call" | custom-call | flops 150323856 | bytes 557793 | tf_op jit(solution)/shard_map/back_in/pallas_call | solution.py:71
  406.2 5.9 %finish_blocks.2.refs_0_ = f32[512,2048]{1,0:T(8,128)} custom-call(s32[3]{0:T(128)} %pad_add_fusion.refs_0_, bf16[2,512,512]{2,1,0:T(8,128)(2,1)} %tie.67.refs_1_, bf16[2,512,512]{2,1,0:T(8,128)(2,1)} %collective-permute-done.36.refs_0_.refs_2_, bf16[2,512,512]{2,1,0:T(8,128)(2,1)} %tie.70.refs_3_, ...), custom_call_target="tpu_custom_call" | custom-call | bytes 167772 | tf_op jit(solution)/shard_map/finish_blocks/pallas_call | solution.py:71
  412.1 6.9 %collective-permute-done.49.refs_2_.refs_5_.refs_11_.refs_17_ = bf16[528,512]{1,0:T(8,128)(2,1)} collective-permute-done((bf16[528,512]{1,0:T(8,128)(2,1)}, bf16[528,512]{1,0:T(8,128)(2,1)}, u32[]{:S(2)}, u32[]{:S(2)}) %collective-permute-start.49) | collective-permute-done | bytes 540704 | tf_op jit(solution)/shard_map/ppermute | solution.py:1171
  419.0 10.4 %collective-permute-done.48.refs_1_.refs_5_ = bf16[528,512]{1,0:T(8,128)(2,1)} collective-permute-done((bf16[528,512]{1,0:T(8,128)(2,1)}, bf16[528,512]{1,0:T(8,128)(2,1)}, u32[]{:S(2)}, u32[]{:S(2)}) %collective-permute-start.48) | collective-permute-done | bytes 540704 | tf_op jit(solution)/shard_map/ppermute | solution.py:1171
  436.3 5.9 %finish_blocks.3.refs_0_ = f32[2048,512]{1,0:T(8,128)} custom-call(s32[3]{0:T(128)} %pad_add_fusion.refs_0_, bf16[2,512,512]{2,1,0:T(8,128)(2,1)} %tie.76.refs_1_, bf16[2,512,512]{2,1,0:T(8,128)(2,1)} %collective-permute-done.45.refs_0_.refs_2_, bf16[2,512,512]{2,1,0:T(8,128)(2,1)} %tie.77.refs_3_, ...), custom_call_target="tpu_custom_call" | custom-call | bytes 167772 | tf_op jit(solution)/shard_map/finish_blocks/pallas_call | solution.py:71
  447.6 8.2 %collective-permute-done.52.refs_2_.refs_6_.refs_12_.refs_18_ = bf16[528,512]{1,0:T(8,128)(2,1)} collective-permute-done((bf16[528,512]{1,0:T(8,128)(2,1)}, bf16[528,512]{1,0:T(8,128)(2,1)}, u32[]{:S(2)}, u32[]{:S(2)}) %collective-permute-start.52) | collective-permute-done | bytes 540704 | tf_op jit(solution)/shard_map/ppermute | solution.py:1171
  (272 shorter events, 176.6 us)
Async XLA Ops:
  7.0 28.9 %collective-permute-start = (bf16[2,512,512]{2,1,0:T(8,128)(2,1)}, bf16[2,512,512]{2,1,0:T(8,128)(2,1)}, u32[]{:S(2)}, u32[]{:S(2)}) collective-permute-start(bf16[2,512,512]{2,1,0:T(8,128)(2,1)} %refs_19_.1), channel_id=1, source_target_pairs={{0,1},{1,2},{2,3},{3,0},{4,5},{5,6},{6,7},{7,4},{8,9},{9,10},{10,1... | collective-permute-start | bytes 3145736 | tf_op jit(solution)/shard_map/ppermute | solution.py:1171
  36.5 27.5 %collective-permute-start.10 = (bf16[512,1536]{1,0:T(8,128)(2,1)}, bf16[512,1536]{1,0:T(8,128)(2,1)}, u32[]{:S(2)}, u32[]{:S(2)}) collective-permute-start(bf16[512,1536]{1,0:T(8,128)(2,1)} %tie.45.refs_11_), channel_id=1, source_target_pairs={{0,8},{8,0},{16,24},{24,16},{1,9},{9,1},{17,25},{25,17},{2,10},{10... | collective-permute-start | bytes 4718600 | tf_op jit(solution)/shard_map/ppermute | solution.py:152
  64.0 56.5 %collective-permute-start.16 = (bf16[512,2048]{1,0:T(8,128)(2,1)}, bf16[512,2048]{1,0:T(8,128)(2,1)}, u32[]{:S(2)}, u32[]{:S(2)}) collective-permute-start(bf16[512,2048]{1,0:T(8,128)(2,1)} %refs_17_.3), channel_id=1, source_target_pairs={{0,8},{8,0},{16,24},{24,16},{1,9},{9,1},{17,25},{25,17},{2,10},{10... | collective-permute-start | bytes 6291464 | tf_op jit(solution)/shard_map/ppermute | solution.py:152
  64.6 31.3 %collective-permute-start.15 = (bf16[2560,256]{1,0:T(8,128)(2,1)}, bf16[2560,256]{1,0:T(8,128)(2,1)}, u32[]{:S(2)}, u32[]{:S(2)}) collective-permute-start(bf16[2560,256]{1,0:T(8,128)(2,1)} %tie.50), channel_id=1, source_target_pairs={{0,16},{8,24},{16,0},{24,8},{1,17},{9,25},{17,1},{25,9},{2,18},{10... | collective-permute-start | bytes 3932168 | tf_op jit(solution)/shard_map/ppermute | solution.py:152
  67.7 28.2 %collective-permute-start.11 = (bf16[2,512,512]{2,1,0:T(8,128)(2,1)}, bf16[2,512,512]{2,1,0:T(8,128)(2,1)}, u32[]{:S(2)}, u32[]{:S(2)}) collective-permute-start(bf16[2,512,512]{2,1,0:T(8,128)(2,1)} %tie.46.refs_2_), channel_id=1, source_target_pairs={{0,1},{1,2},{2,3},{3,0},{4,5},{5,6},{6,7},{7,4},{8,9},{9,10},{10,1... | collective-permute-start | bytes 3145736 | tf_op jit(solution)/shard_map/ppermute | solution.py:1171
  75.2 45.3 %collective-permute-start.19 = (bf16[2,512,512]{2,1,0:T(8,128)(2,1)}, bf16[2,512,512]{2,1,0:T(8,128)(2,1)}, u32[]{:S(2)}, u32[]{:S(2)}) collective-permute-start(bf16[2,512,512]{2,1,0:T(8,128)(2,1)} %refs_20_.1), channel_id=1, source_target_pairs={{0,1},{1,2},{2,3},{3,0},{4,5},{5,6},{6,7},{7,4},{8,9},{9,10},{10,1... | collective-permute-start | bytes 3145736 | tf_op jit(solution)/shard_map/ppermute | solution.py:1171
  120.5 31.6 %collective-permute-start.22 = (bf16[2560,512]{1,0:T(8,128)(2,1)}, bf16[2560,512]{1,0:T(8,128)(2,1)}, u32[]{:S(2)}, u32[]{:S(2)}) collective-permute-start(bf16[2560,512]{1,0:T(8,128)(2,1)} %tie.54.refs_2_.refs_6_.refs_7_), channel_id=1, source_target_pairs={{0,8},{8,0},{16,24},{24,16},{1,9},{9,1},{17,25},{25,17},{2,10},{10... | collective-permute-start | bytes 7864328 | tf_op jit(solution)/shard_map/ppermute | solution.py:152
  120.7 31.4 %collective-permute-start.20 = (bf16[2560,256]{1,0:T(8,128)(2,1)}, bf16[2560,256]{1,0:T(8,128)(2,1)}, u32[]{:S(2)}, u32[]{:S(2)}) collective-permute-start(bf16[2560,256]{1,0:T(8,128)(2,1)} %tie.53.refs_0_), channel_id=1, source_target_pairs={{0,4},{4,0},{1,5},{5,1},{2,6},{6,2},{3,7},{7,3},{8,12},{12,8},{9,1... | collective-permute-start | bytes 3932168 | tf_op jit(solution)/shard_map/ppermute | solution.py:152
  152.6 27.3 %collective-permute-start.24 = (bf16[2,512,512]{2,1,0:T(8,128)(2,1)}, bf16[2,512,512]{2,1,0:T(8,128)(2,1)}, u32[]{:S(2)}, u32[]{:S(2)}) collective-permute-start(bf16[2,512,512]{2,1,0:T(8,128)(2,1)} %tie.56.refs_2_), channel_id=1, source_target_pairs={{0,1},{1,2},{2,3},{3,0},{4,5},{5,6},{6,7},{7,4},{8,9},{9,10},{10,1... | collective-permute-start | bytes 3145736 | tf_op jit(solution)/shard_map/ppermute | solution.py:1171
  152.6 49.3 %collective-permute-start.27 = (bf16[2,512,512]{2,1,0:T(8,128)(2,1)}, bf16[2,512,512]{2,1,0:T(8,128)(2,1)}, u32[]{:S(2)}, u32[]{:S(2)}) collective-permute-start(bf16[2,512,512]{2,1,0:T(8,128)(2,1)} %tie.59.refs_3_), channel_id=1, source_target_pairs={{0,4},{1,5},{2,6},{3,7},{8,12},{9,13},{10,14},{11,15},{16,20},{17,... | collective-permute-start | bytes 3145736 | tf_op jit(solution)/shard_map/ppermute | solution.py:1334
  157.0 45.0 %collective-permute-start.23 = (bf16[2,512,512]{2,1,0:T(8,128)(2,1)}, bf16[2,512,512]{2,1,0:T(8,128)(2,1)}, u32[]{:S(2)}, u32[]{:S(2)}) collective-permute-start(bf16[2,512,512]{2,1,0:T(8,128)(2,1)} %tie.55.refs_3_), channel_id=1, source_target_pairs={{0,4},{1,5},{2,6},{3,7},{8,12},{9,13},{10,14},{11,15},{16,20},{17,... | collective-permute-start | bytes 3145736 | tf_op jit(solution)/shard_map/ppermute | solution.py:1334
  229.9 35.3 %collective-permute-start.30 = (bf16[2,512,512]{2,1,0:T(8,128)(2,1)}, bf16[2,512,512]{2,1,0:T(8,128)(2,1)}, u32[]{:S(2)}, u32[]{:S(2)}) collective-permute-start(bf16[2,512,512]{2,1,0:T(8,128)(2,1)} %tie.61), channel_id=1, source_target_pairs={{4,0},{5,1},{6,2},{7,3},{12,8},{13,9},{14,10},{15,11},{20,16},{21,... | collective-permute-start | bytes 3145736 | tf_op jit(solution)/shard_map/ppermute | solution.py:1354
  235.4 29.8 %collective-permute-start.29 = (bf16[2,512,512]{2,1,0:T(8,128)(2,1)}, bf16[2,512,512]{2,1,0:T(8,128)(2,1)}, u32[]{:S(2)}, u32[]{:S(2)}) collective-permute-start(bf16[2,512,512]{2,1,0:T(8,128)(2,1)} %get-tuple-element.93.refs_0_), channel_id=1, source_target_pairs={{0,16},{8,24},{16,0},{24,8},{1,17},{9,25},{17,1},{25,9},{2,18},{10... | collective-permute-start | bytes 3145736 | tf_op jit(solution)/shard_map/ppermute | solution.py:152
  265.3 27.2 %collective-permute-start.31 = (bf16[2,4,512,512]{3,2,1,0:T(8,128)(2,1)}, bf16[2,4,512,512]{3,2,1,0:T(8,128)(2,1)}, u32[]{:S(2)}, u32[]{:S(2)}) collective-permute-start(bf16[2,4,512,512]{3,2,1,0:T(8,128)(2,1)} %tie.62), channel_id=1, source_target_pairs={{0,8},{8,0},{16,24},{24,16},{1,9},{9,1},{17,25},{25,17},{2,10},{10... | collective-permute-start | bytes 12582920 | tf_op jit(solution)/shard_map/ppermute | solution.py:152
  265.6 42.5 %collective-permute-start.33 = (bf16[2,512,512]{2,1,0:T(8,128)(2,1)}, bf16[2,512,512]{2,1,0:T(8,128)(2,1)}, u32[]{:S(2)}, u32[]{:S(2)}) collective-permute-start(bf16[2,512,512]{2,1,0:T(8,128)(2,1)} %tie.64), channel_id=1, source_target_pairs={{4,0},{5,1},{6,2},{7,3},{12,8},{13,9},{14,10},{15,11},{20,16},{21,... | collective-permute-start | bytes 3145736 | tf_op jit(solution)/shard_map/ppermute | solution.py:1354
  266.9 41.2 %collective-permute-start.32 = (bf16[2,512,512]{2,1,0:T(8,128)(2,1)}, bf16[2,512,512]{2,1,0:T(8,128)(2,1)}, u32[]{:S(2)}, u32[]{:S(2)}) collective-permute-start(bf16[2,512,512]{2,1,0:T(8,128)(2,1)} %tie.63), channel_id=1, source_target_pairs={{0,16},{8,24},{16,0},{24,8},{1,17},{9,25},{17,1},{25,9},{2,18},{10... | collective-permute-start | bytes 3145736 | tf_op jit(solution)/shard_map/ppermute | solution.py:152
  308.0 32.3 %collective-permute-start.35 = (bf16[2,2,512,512]{3,2,1,0:T(8,128)(2,1)}, bf16[2,2,512,512]{3,2,1,0:T(8,128)(2,1)}, u32[]{:S(2)}, u32[]{:S(2)}) collective-permute-start(bf16[2,2,512,512]{3,2,1,0:T(8,128)(2,1)} %tie.66), channel_id=1, source_target_pairs={{0,8},{8,0},{16,24},{24,16},{1,9},{9,1},{17,25},{25,17},{2,10},{10... | collective-permute-start | bytes 6291464 | tf_op jit(solution)/shard_map/ppermute | solution.py:152
  308.1 31.5 %collective-permute-start.37 = (bf16[2,512,512]{2,1,0:T(8,128)(2,1)}, bf16[2,512,512]{2,1,0:T(8,128)(2,1)}, u32[]{:S(2)}, u32[]{:S(2)}) collective-permute-start(bf16[2,512,512]{2,1,0:T(8,128)(2,1)} %tie.68), channel_id=1, source_target_pairs={{0,1},{1,2},{2,3},{3,0},{4,5},{5,6},{6,7},{7,4},{8,9},{9,10},{10,1... | collective-permute-start | bytes 3145736 | tf_op jit(solution)/shard_map/ppermute | solution.py:1171
  308.6 31.0 %collective-permute-start.36 = (bf16[2,512,512]{2,1,0:T(8,128)(2,1)}, bf16[2,512,512]{2,1,0:T(8,128)(2,1)}, u32[]{:S(2)}, u32[]{:S(2)}) collective-permute-start(bf16[2,512,512]{2,1,0:T(8,128)(2,1)} %tie.67.refs_1_), channel_id=1, source_target_pairs={{0,4},{4,0},{1,5},{5,1},{2,6},{6,2},{3,7},{7,3},{8,12},{12,8},{9,1... | collective-permute-start | bytes 3145736 | tf_op jit(solution)/shard_map/ppermute | solution.py:152
  340.3 29.7 %collective-permute-start.39 = (bf16[2,512,512]{2,1,0:T(8,128)(2,1)}, bf16[2,512,512]{2,1,0:T(8,128)(2,1)}, u32[]{:S(2)}, u32[]{:S(2)}) collective-permute-start(bf16[2,512,512]{2,1,0:T(8,128)(2,1)} %tie.70.refs_3_), channel_id=1, source_target_pairs={{0,4},{4,0},{1,5},{5,1},{2,6},{6,2},{3,7},{7,3},{8,12},{12,8},{9,1... | collective-permute-start | bytes 3145736 | tf_op jit(solution)/shard_map/ppermute | solution.py:152
  342.4 27.6 %collective-permute-start.38 = (bf16[2,512,512]{2,1,0:T(8,128)(2,1)}, bf16[2,512,512]{2,1,0:T(8,128)(2,1)}, u32[]{:S(2)}, u32[]{:S(2)}) collective-permute-start(bf16[2,512,512]{2,1,0:T(8,128)(2,1)} %tie.69), channel_id=1, source_target_pairs={{0,16},{8,24},{16,0},{24,8},{1,17},{9,25},{17,1},{25,9},{2,18},{10... | collective-permute-start | bytes 3145736 | tf_op jit(solution)/shard_map/ppermute | solution.py:152
  370.0 28.5 %collective-permute-start.43 = (bf16[2,2,512,512]{3,2,1,0:T(8,128)(2,1)}, bf16[2,2,512,512]{3,2,1,0:T(8,128)(2,1)}, u32[]{:S(2)}, u32[]{:S(2)}) collective-permute-start(bf16[2,2,512,512]{3,2,1,0:T(8,128)(2,1)} %tie.74), channel_id=1, source_target_pairs={{0,8},{8,0},{16,24},{24,16},{1,9},{9,1},{17,25},{25,17},{2,10},{10... | collective-permute-start | bytes 6291464 | tf_op jit(solution)/shard_map/ppermute | solution.py:152
  370.1 27.1 %collective-permute-start.42 = (bf16[2,512,512]{2,1,0:T(8,128)(2,1)}, bf16[2,512,512]{2,1,0:T(8,128)(2,1)}, u32[]{:S(2)}, u32[]{:S(2)}) collective-permute-start(bf16[2,512,512]{2,1,0:T(8,128)(2,1)} %tie.73), channel_id=1, source_target_pairs={{0,3},{1,0},{2,1},{3,2},{4,7},{5,4},{6,5},{7,6},{8,11},{9,8},{10,9... | collective-permute-start | bytes 3145736 | tf_op jit(solution)/shard_map/ppermute | solution.py:1171
  398.6 30.8 %collective-permute-start.47 = (bf16[2,512,512]{2,1,0:T(8,128)(2,1)}, bf16[2,512,512]{2,1,0:T(8,128)(2,1)}, u32[]{:S(2)}, u32[]{:S(2)}) collective-permute-start(bf16[2,512,512]{2,1,0:T(8,128)(2,1)} %tie.77.refs_3_), channel_id=1, source_target_pairs={{0,4},{4,0},{1,5},{5,1},{2,6},{6,2},{3,7},{7,3},{8,12},{12,8},{9,1... | collective-permute-start | bytes 3145736 | tf_op jit(solution)/shard_map/ppermute | solution.py:152
  (44 other events, 642.7 us)

commit v6 on v5

--- a/solution.py
+++ b/solution.py
@@ -360,22 +360,27 @@
 
 
 def back_out_body(layout, info, c0, ca, cc, cb, slope, *refs):
-    *w, cf, bias_grad, datt, dup, held, sems = refs
+    *w, cf, bias_grad, datt, dup, held, sems, cf_sems = refs
     j = pl.program_id(0)
     t = info[0]
     seqs = c0.shape[0]
+    parts = [(c0, t), (ca, (t + 3) % N_TP), (cc, (t + 1) % N_TP), (cb, (t + 2) % N_TP)]
     stream_pieces(layout, info, w, held, sems, 1, held.shape[0] // CH)
+    copies = [
+        pltpu.make_async_copy(part, cf.at[:, :, columns(index)], cf_sems.at[n])
+        for n, (part, index) in enumerate(parts)
+    ]
 
     @pl.when(j == 0)
     def _():
-        for part, step in ((c0, 0), (ca, 3), (cc, 1), (cb, 2)):
-            cf[:, :, columns((t + step) % N_TP)] = part[...]
+        for copy in copies:
+            copy.start()
         bias_grad[...] = sum(
             jnp.sum(c0[s].astype(f32), axis=0, keepdims=True) for s in range(seqs)
         )
 
     for s in range(seqs):
-        y = dot_nt(cf[s], held[columns(j), :])
+        y = sum(dot_nt(part[s], held[columns(j), columns(index)]) for part, index in parts)
 
         @pl.when(j == 0)
         def _(s=s, y=y):
@@ -384,6 +389,11 @@
         @pl.when(j > 0)
         def _(s=s, y=y):
             dup[s] = (y * slope[s].astype(f32)).astype(bf16)
+
+    @pl.when(j == pl.num_programs(0) - 1)
+    def _():
+        for copy in copies:
+            copy.wait()
 
 
 def back_out(layout, info, parts, w, slope, deps=()):
@@ -395,18 +405,19 @@
         1 + units // CH,
         info,
         (*parts, slope, *w),
-        [whole(seqs, rows, CH)] * 4 + [later] + [ANYWHERE] * len(w),
+        [once(seqs, rows, CH)] * 4 + [later] + [ANYWHERE] * len(w),
         (
             shaped((seqs, rows, D)),
             shaped((1, CH), f32),
             shaped((seqs, rows, CH)),
             shaped((seqs, rows, units)),
         ),
-        [whole(seqs, rows, D), whole(1, CH), whole(seqs, rows, CH), later],
+        [ANYWHERE, whole(1, CH), whole(seqs, rows, CH), later],
         2 * seqs * rows * D * (CH + units),
         [
             pltpu.VMEM((CH + units, D), bf16),
             pltpu.SemaphoreType.DMA((1 + units // CH, len(w))),
+            pltpu.SemaphoreType.DMA((len(parts),)),
         ],
         deps=deps,
     )
@@ -530,13 +541,16 @@
                 blocks.append((kvp.at[0], n * part, 0, False))
         for n in range(2):
             blocks.append((kv, n * part, n * part, True))
-        outputs = []
         dk_sum, dv_sum = [0.0] * len(blocks), [0.0] * len(blocks)
+        heads = []
         for head in range(2):
             mine = (lane < HEAD_DIM) if head == 0 else (lane >= HEAD_DIM)
-            half = slice(HEAD_DIM * head, HEAD_DIM * (head + 1))
             qh = jnp.where(mine, q[...] * jnp.asarray(HEAD_DIM**-0.5, bf16), nothing)
             dh = jnp.where(mine, do[...], nothing)
+            heads.append((qh, dh, slice(HEAD_DIM * head, HEAD_DIM * (head + 1))))
+
+        def score(head):
+            qh = heads[head][0]
             scores, peak = [], None
             for ref, row, skip, here in blocks:
                 s = dot_nt(ref[0, row : row + part], qh[skip:])
@@ -547,28 +561,59 @@
                 s = jnp.where(allowed, s, NEG)
                 scores.append(s)
                 peak = merge(peak, jnp.max(s, axis=0, keepdims=True), skip, jnp.maximum)
+            return scores, peak
+
+        def grads(head):
+            dh = heads[head][1]
+            return [
+                dot_nt(ref[1, row : row + part], dh[skip:]) for ref, row, skip, _ in blocks
+            ]
+
+        def soften(scores, peak):
             terms, total = [], None
             for s, (_, _, skip, _) in zip(scores, blocks):
                 e = jnp.exp(s - tail(peak, skip))
                 terms.append(e)
                 total = merge(total, jnp.sum(e, axis=0, keepdims=True), skip, jnp.add)
             scale = 1.0 / total
-            probs, rounded, out_t = [], [], None
-            for e, (ref, row, skip, _) in zip(terms, blocks):
-                p = e * tail(scale, skip)
-                pb = p.astype(bf16)
-                probs.append(p)
-                rounded.append(pb)
-                out_t = merge(out_t, dot_tn(ref[1, row : row + part], pb), skip, jnp.add)
-            delta = jnp.sum(out_t[half] * do_t[half], axis=0, keepdims=True)
+            probs = [e * tail(scale, skip) for e, (_, _, skip, _) in zip(terms, blocks)]
+            return probs, [p.astype(bf16) for p in probs]
+
+        def weigh(head, rounded):
+            out_t = None
+            for n, (ref, row, skip, _) in enumerate(blocks):
+                out_t = merge(
+                    out_t, dot_tn(ref[1, row : row + part], rounded[n]), skip, jnp.add
+                )
+                dv_sum[n] = dv_sum[n] + dot_nn(rounded[n], heads[head][1][skip:])
+            half = heads[head][2]
+            return out_t[half], jnp.sum(out_t[half] * do_t[half], axis=0, keepdims=True)
+
+        def differ(probs, dps, delta):
+            return [
+                (p * (dp - tail(delta, skip))).astype(bf16)
+                for p, dp, (_, _, skip, _) in zip(probs, dps, blocks)
+            ]
+
+        def back(head, dss):
             dq_t = None
             for n, (ref, row, skip, _) in enumerate(blocks):
-                dp = dot_nt(ref[1, row : row + part], dh[skip:])
-                ds = (probs[n] * (dp - tail(delta, skip))).astype(bf16)
-                dv_sum[n] = dv_sum[n] + dot_nn(rounded[n], dh[skip:])
-                dk_sum[n] = dk_sum[n] + dot_nn(ds, qh[skip:])
-                dq_t = merge(dq_t, dot_tn(ref[0, row : row + part], ds), skip, jnp.add)
-            outputs.append((out_t[half], dq_t[half]))
+                dk_sum[n] = dk_sum[n] + dot_nn(dss[n], heads[head][0][skip:])
+                dq_t = merge(dq_t, dot_tn(ref[0, row : row + part], dss[n]), skip, jnp.add)
+            return dq_t[heads[head][2]]
+
+        scores_0 = score(0)
+        scores_1 = score(1)
+        probs_0, rounded_0 = soften(*scores_0)
+        out_0, delta_0 = weigh(0, rounded_0)
+        probs_1, rounded_1 = soften(*scores_1)
+        dss_0 = differ(probs_0, grads(0), delta_0)
+        out_1, delta_1 = weigh(1, rounded_1)
+        dq_0 = back(0, dss_0)
+        dss_1 = differ(probs_1, grads(1), delta_1)
+        dq_1 = back(1, dss_1)
+        outputs = [(out_0, dq_0), (out_1, dq_1)]
+
         att[...] = jnp.concatenate([outputs[0][0], outputs[1][0]], axis=0).T.astype(bf16)
         grad = jnp.concatenate([outputs[0][1], outputs[1][1]], axis=0).T * HEAD_DIM**-0.5
         dq[...] = turn_back(grad, own[...], up[...], down[...]).astype(bf16)
@@ -671,21 +716,14 @@
 
 
 def out_hidden_body(layout, info, hidden, *refs):
-    count = len(layout)
-    w, outs = refs[:count], refs[count : count + N_TP]
-    held, y, sems = refs[count + N_TP :]
+    *w, out, held, sems = refs
 
     def work(place, window):
         for s in range(hidden.shape[0]):
-            y[s, :, window] = dot_nn(hidden[s], held[:, place]).astype(bf16)
+            out[0, s, :, window] = dot_nn(hidden[s], held[:, place]).astype(bf16)
 
     lower = [a.at[pl.ds(CH, held.shape[0]), :] for a in w]
     with_chunk(layout, info, fetch_pieces(layout, [lower], [held], sems, 1), work)
-    for r in range(N_TP):
-
-        @pl.when(chunk_now(info) == r)
-        def _(r=r):
-            outs[r][...] = y[...]
 
 
 def out_hidden(layout, info, hidden, w, deps=()):
@@ -693,56 +731,62 @@
     return call(
         functools.partial(out_hidden_body, layout),
         "out_hidden",
-        N_TP,
+        N_DP,
         info,
         (hidden, *w),
         [once(seqs, rows, units)] + [ANYWHERE] * len(w),
-        (shaped((seqs, rows, CH)),) * N_TP,
-        [whole(seqs, rows, CH)] * N_TP,
+        shaped((N_DP, seqs, rows, CH)),
+        spec((1, seqs, rows, CH), lambda j, *_: (j, 0, 0, 0)),
         2 * seqs * rows * D * units,
-        [
-            pltpu.VMEM((units, D), bf16),
-            pltpu.VMEM((seqs, rows, CH), bf16),
-            pltpu.SemaphoreType.DMA((len(w),)),
-        ],
+        [pltpu.VMEM((units, D), bf16), pltpu.SemaphoreType.DMA((len(w),))],
         deps=deps,
     )
 
 
-def out_heads_body(layout, info, a0, a1, p0, p1, p2, p3, *refs):
+def out_heads_body(layout, info, a0, a1, part, *refs):
     count = len(layout)
     w, outs = refs[:count], refs[count : count + N_TP]
-    held, y, sems = refs[count + N_TP :]
+    held, y, sems, out_sems = refs[count + N_TP :]
+    j = pl.program_id(0)
 
     def work(place, window):
         for s, att in ((0, a0), (1, a1)):
-            y[s, :, window] = dot_nn(att[...], held[:, place])
+            total = dot_nn(att[...], held[:, place]) + part[0, s, :, window].astype(f32)
+            y[j, s, :, window] = total.astype(bf16)
 
     upper = [a.at[pl.ds(0, CH), :] for a in w]
     with_chunk(layout, info, fetch_pieces(layout, [upper], [held], sems, 1), work)
-    for r, part in enumerate((p0, p1, p2, p3)):
+    for r in range(N_TP):
 
         @pl.when(chunk_now(info) == r)
-        def _(r=r, part=part):
-            outs[r][...] = (y[...] + part[...].astype(f32)).astype(bf16)
+        def _(r=r):
+            pltpu.make_async_copy(y.at[j], outs[r], out_sems.at[r]).start()
+
+    @pl.when(j == N_TP - 1)
+    def _():
+        for r in range(N_TP):
+            pltpu.make_async_copy(y.at[r], outs[r], out_sems.at[r]).wait()
 
 
 def out_heads(layout, info, att, parts, w, deps=()):
-    seqs, rows, _ = parts[0].shape
+    _, seqs, rows, _ = parts.shape
     return call(
         functools.partial(out_heads_body, layout),
         "out_heads",
         N_TP,
         info,
-        (*att, *parts, *w),
-        [once(rows, CH)] * 2 + [once(seqs, rows, CH)] * N_TP + [ANYWHERE] * len(w),
+        (*att, parts, *w),
+        [once(rows, CH)] * 2
+        + [spec((1, seqs, rows, CH), lambda j, *_: (j, 0, 0, 0))]
+        + [ANYWHERE] * len(w),
         (shaped((seqs, rows, CH)),) * N_TP,
-        [whole(seqs, rows, CH)] * N_TP,
+        [ANYWHERE] * N_TP,
         2 * seqs * rows * D * CH,
         [
             pltpu.VMEM((CH, D), bf16),
-            pltpu.VMEM((seqs, rows, CH), f32),
+            pltpu.VMEM((N_TP, seqs, rows, CH), bf16),
             pltpu.SemaphoreType.DMA((len(w),)),
+            pltpu.SemaphoreType.DMA((N_TP,)),
         ],
         deps=deps,
     )
@@ -865,41 +909,27 @@
 
 
 def grad_down_body(info, hidden, ct, kept, given):
-    j = pl.program_id(0)
-    y = (dot_tn(hidden[0], ct[0]) + dot_tn(hidden[1], ct[1])).astype(bf16)
-
-    def store(target):
-        for n in range(target.shape[1]):
-            target[0, n] = y[CH * n : CH * (n + 1), :]
-
-    @pl.when(j < 2)
-    def _():
-        store(given)
-
-    @pl.when(j >= 2)
-    def _():
-        store(kept)
+    d = info[2]
+    for target, which in ((given, GIVEN), (kept, KEPT)):
+        for r, at in which:
+            window = columns(d ^ r)
+            y = dot_tn(hidden[0], ct[0, :, window]) + dot_tn(hidden[1], ct[1, :, window])
+            target[at, 0] = y.astype(bf16)
 
 
 def grad_down(info, hidden, ct, deps=()):
     _, rows, units = hidden.shape
     count = units // CH
-    block = spec(
-        (2, rows, CH),
-        lambda j, info: (0, 0, info[2] ^ jnp.where(j < 2, 2 * j + 1, 2 * j - 4)),
-    )
+    message = spec((2, 1, CH, CH), lambda j, *_: (0, j, 0, 0))
     return call(
         grad_down_body,
         "grad_down",
-        N_DP,
+        count,
         info,
         (hidden, ct),
-        [whole(2, rows, units), block],
+        [spec((2, rows, CH), lambda j, *_: (0, 0, j)), once(2, rows, D)],
         (shaped((2, count, CH, CH)),) * 2,
-        [
-            spec((1, count, CH, CH), lambda j, *_: (jnp.maximum(j - 2, 0), 0, 0, 0)),
-            spec((1, count, CH, CH), lambda j, *_: (jnp.minimum(j, 1), 0, 0, 0)),
-        ],
+        [message, message],
         4 * rows * D * units,
         deps=deps,
     )
@@ -1075,23 +1105,26 @@
     )
 
 
-def finish_out_body(info, own, back, near, x, shift, out):
+def finish_last_body(info, own, back, near, x, shift, here, there, out, first, second):
     total = own[...].astype(f32) + back[...].astype(f32) + near[...].astype(f32)
     out[...] = (x[...].astype(f32) + total + shift[...].astype(f32)).astype(bf16)
-
-
-def finish_out(info, shares, x, shift, deps=()):
+    finish_pair_body(info, here, there, first, second)
+
+
+def finish_last(info, shares, x, shift, here, there, deps=()):
     seqs, rows, _ = x.shape
     both = spec((seqs, rows // 2, CH), lambda j, _: (0, j, 0))
+    pair = spec((2, CH // 2, CH), lambda j, _: (0, j, 0))
+    half = spec((CH // 2, CH), lambda j, _: (j, 0))
     return call(
-        finish_out_body,
-        "finish_out",
+        finish_last_body,
+        "finish_last",
         2,
         info,
-        (*shares, x, shift),
-        [both] * 4 + [whole(1, CH)],
-        shaped(x.shape),
-        both,
+        (*shares, x, shift, here, there),
+        [both] * 4 + [whole(1, CH), pair, pair],
+        (shaped(x.shape), shaped((CH, CH), f32), shaped((CH, CH), f32)),
+        [both, half, half],
         0,
         deps=deps,
     )
@@ -1381,30 +1414,29 @@
     normed, stats, q, *kv = norm_qkv(
         layout, info, x.parts, gain, shift, shards_q.pieces, qkv_bias, tables, deps=clock.marks
     )
-    clock.sync(normed, *shards_u.far_near, shards_u.near, ct.behind)
+    clock.sync(normed, *shards_u.far_near, shards_u.near, ct.behind, shards_o.second)
 
     shards_o.near_core(clock)
+    shards_o.far_core(clock)
     ct.onward(clock)
     hidden, slope = mlp_up(layout, info, normed, shards_u.pieces, up_shift, deps=clock.marks)
-    clock.sync(hidden, shards_o.second, ct.ahead, shards_o.near)
-
-    shards_o.far_core(clock)
+    clock.sync(hidden, shards_o.near, *shards_o.far_near)
+
     send_keys(0)
     send_keys(1)
-    clock.sync(*shards_o.far_near)
     out_parts = out_hidden(layout, info, hidden, shards_o.pieces, deps=clock.marks)
-    clock.sync(out_parts[0], ct.far)
+    clock.sync(out_parts, ct.ahead, ct.far)
 
     cf, out_bias_sum, datt, dup = back_out(
         layout, info, ct.parts, shards_o.pieces, slope, deps=clock.marks
     )
-    clock.sync(datt, kvp[0], kvp[1])
+    clock.sync(datt, kvp[0])
 
     def added(big, small=()):
         return combine(info, big, list(small), deps=clock.marks)
 
     up_kept, up_given, up_sum = grad_up(info, normed, dup, deps=clock.marks)
-    clock.sync(up_kept)
+    clock.sync(up_kept, kvp[1])
     up = Reduction(up_kept, up_given, clock, two)
     att[0], dq[0], dkv[0], sent[0] = attention_step(0)
     clock.sync(att[0], up.got)
@@ -1421,73 +1453,79 @@
     sent[1] = returned(sent[1])
     up.over_x(1, clock.go(across_1))
     down = Reduction(down_kept, down_given, clock, two)
-    (here,) = added([up.here_sum(0)])
-    clock.sync(here)
     out = Scatter(out_heads(layout, info, att, out_parts, shards_o.pieces, deps=clock.marks))
     clock.sync(out.own, *clock.marks)
     head_kept, head_given, query_sum = grad_out_query(
         info, normed, cf, att, dq, deps=clock.marks
     )
     clock.sync(head_kept, down.got)
-    across, across_1 = added([down.across(0), down.across(1)])
+    across, across_1, here = added([down.across(0), down.across(1), up.here_sum(0)])
     clock.sync(across, sent[1])
+
+    up.over_y(0, clock.go(here))
+    out.forward(clock)
     clock.sync(up.moved[1])
-
-    out.forward(clock)
-    up.over_y(0, clock.go(here))
     down.over_x(0, clock.go(across))
     head = Reduction(head_kept, head_given, clock, two)
     (here,) = added([up.here_sum(1)])
     clock.sync(here)
     back_0 = Scatter(back_in_step(0))
-    clock.sync(back_0.own, out.far)
+    clock.sync(back_0.own)
     clock.sync(up.there[0])
-    clock.sync(down.moved[0], head.got)
-
+
+    up.over_y(1, clock.go(here))
+    clock.sync(out.far)
     back_0.forward(clock)
     back_0.backward(clock)
-    up.over_y(1, clock.go(here))
+    clock.sync(down.moved[0], head.got)
     down.over_x(1, clock.go(across_1))
     here, across, out_both = added([down.here_sum(0), head.across(0)], [out.both()])
     clock.sync(here)
     pair_kept, pair_given, pair_sum = grad_key_value(info, normed, dkv, sent, deps=clock.marks)
-    clock.sync(pair_kept, back_0.far, back_0.back)
+    clock.sync(pair_kept)
     clock.sync(up.there[1])
+
+    down.over_y(0, clock.go(here))
+    clock.sync(back_0.far, back_0.back)
+    out.backward(clock)
     clock.sync(down.moved[1])
-
-    out.backward(clock)
-    down.over_y(0, clock.go(here))
     head.over_x(0, clock.go(across))
     pair = Reduction(pair_kept, pair_given, clock, two)
     here, both_0 = added([down.here_sum(1)], [back_0.both()])
     clock.sync(here)
     back_1 = Scatter(back_in_step(1))
-    clock.sync(back_1.own, out.back)
+    clock.sync(back_1.own)
     clock.sync(down.there[0])
-    clock.sync(head.moved[0], pair.got)
-
+
+    down.over_y(1, clock.go(here))
+    clock.sync(out.back)
     back_1.forward(clock)
     back_1.backward(clock)
-    down.over_y(1, clock.go(here))
-    across, here = added([pair.across(0), head.here_sum(0)])
+    clock.sync(head.moved[0], pair.got)
+    (across,) = added([pair.across(0)])
     pair.over_x(0, across)
     clock.sync(across)
+    (here,) = added([head.here_sum(0)])
+    clock.sync(here)
     up_wg = finish_blocks(info, [up.sums(0), up.sums(1)], 1, deps=clock.marks)
-    clock.sync(up_wg, back_1.far, back_1.back)
+    clock.sync(up_wg)
     clock.sync(down.there[1])
+
+    head.over_y(0, clock.go(here))
+    back_0.onward(clock.go(both_0))
+    clock.sync(back_1.far, back_1.back)
+    (both_1,) = added([], [back_1.both()])
+    back_1.onward(both_1)
     clock.sync(pair.moved[0])
-
-    back_0.onward(clock.go(both_0))
-    head.over_y(0, clock.go(here))
-    here, both_1 = added([pair.here_sum(0)], [back_1.both()])
-    back_1.onward(both_1)
+    (here,) = added([pair.here_sum(0)])
     clock.sync(here)
     down_wg = finish_blocks(info, [down.sums(0), down.sums(1)], 0, deps=clock.marks)
-    clock.sync(down_wg, back_0.near, back_1.near)
+    clock.sync(down_wg)
     clock.sync(head.there[0])
 
+    pair.over_y(0, clock.go(here))
+    clock.sync(back_0.near, back_1.near)
     out.onward(clock.go(out_both))
-    pair.over_y(0, clock.go(here))
     in_grad, last = finish_in(
         info,
         (*back_0.shares(), *back_1.shares()),
@@ -1503,8 +1541,9 @@
     table = table + swap(table, "dp", 1, N_DP)
     table = table + swap(table, "dp", 2, N_DP)
     table = table + swap(table, "ctx", 1, 2) if two else lax.psum(table, "ctx")
-    block_out = finish_out(info, out.shares(), block_in, output_shift)
-    key_wg, value_wg = finish_pair(info, *pair.sums(0))
+    block_out, key_wg, value_wg = finish_last(
+        info, out.shares(), block_in, output_shift, *pair.sums(0)
+    )
 
     share = CH // N_DP
     mine = lax.dynamic_slice_in_dim(table, d * share, share, 1)

time: 496 us -> 476 us (0.960)
  Pallas kernels: 269 us -> 260 us
  waiting for transfers between devices: 121 us -> 115 us
  starting transfers between devices: 63.9 us -> 58.9 us
    ppermute x18, waiting for transfers between devices: 78.5 us -> 51.6 us  [ring(): lax.ppermute(array, 'tp', [(i, (i + step) % N_TP) for i in range(N_TP)])]
    ppermute x36, waiting for transfers between devices: 31.3 us -> 48.5 us  [swap(): return lax.ppermute(array, axis, [(i, i ^ bit) for i in range(size)])]
    pallas_call x28, Pallas kernels: 269 us -> 260 us  [call(): pl.pallas_call(without_deps, grid_spec=pltpu.PrefetchScalarGridSpec(num_s...]
    ppermute x36, starting transfers between devices: 33.6 us -> 27.7 us  [swap(): return lax.ppermute(array, axis, [(i, i ^ bit) for i in range(size)])]
  transfers between devices with their start and end apart: 58 -> 58, of which waited for: 21 -> 23; matrix products, arithmetic and copies ran while one was open for 5% -> 5% of each run, Pallas kernels for 51% -> 55%
where the time goes in v6:
time: 476 us; the launch traced here: 467 us
  Pallas kernels  260 us (55%)
  waiting for transfers between devices  115 us (24%)
  starting transfers between devices  58.9 us (12%)
  local copies, waits for them, and re-layouts  19.8 us (4%)
  other arithmetic  11.9 us (2%)
    pallas_call x28, Pallas kernels, call(): pl.pallas_call(without_deps, grid_spec=pltpu.PrefetchScalarGridSpec(num_s...  260 us
    ppermute x18, waiting for transfers between devices, ring(): lax.ppermute(array, 'tp', [(i, (i + step) % N_TP) for i in range(N_TP)])  51.6 us
    ppermute x36, waiting for transfers between devices, swap(): return lax.ppermute(array, axis, [(i, i ^ bit) for i in range(size)])  48.5 us
    ppermute x36, starting transfers between devices, swap(): return lax.ppermute(array, axis, [(i, i ^ bit) for i in range(size)])  27.7 us
    ppermute x18, starting transfers between devices, ring(): lax.ppermute(array, 'tp', [(i, (i + step) % N_TP) for i in range(N_TP)])  21.9 us
    ppermute x2, waiting for transfers between devices, returned(): return lax.ppermute(clock.go(sent[0]), 'ctx', [(1, 0)])  14.8 us
    unnamed x39, local copies, waits for them, and re-layouts  10.1 us
  transfers between devices with their start and end apart: 58, of which 23 were waited for; matrix products, arithmetic and copies ran while one was open for 5% of the time, Pallas kernels for 55%

profile of v6, /device:TPU:0, one launch (start us, length us, event | category | flops | bytes accessed | tf_op | source)
XLA Modules:
  0.0 467.5 jit_solution(983040384627823955)
XLA Ops:
  24.5 8.6 %collective-permute-done.4.refs_2_ = bf16[2,512]{1,0:T(2,128)(2,1)S(1)} collective-permute-done((bf16[2,512]{1,0:T(2,128)(2,1)S(1)}, bf16[2,512]{1,0:T(2,128)(2,1)S(1)}, u32[]{:S(2)}, u32[]{:S(2)}) %collective-permute-start.4) | collective-permute-done | bytes 2080 | tf_op jit(solution)/shard_map/ppermute | solution.py:1204
  46.7 15.7 %collective-permute-done.9.refs_2_.refs_3_ = bf16[2,512,512]{2,1,0:T(8,128)(2,1)} collective-permute-done((bf16[2,512,512]{2,1,0:T(8,128)(2,1)}, bf16[2,512,512]{2,1,0:T(8,128)(2,1)}, u32[]{:S(2)}, u32[]{:S(2)}) %collective-permute-start.9) | collective-permute-done | bytes 1048608 | tf_op jit(solution)/shard_map/ppermute | solution.py:1204
  75.6 15.6 %collective-permute-done.14.refs_3_.refs_0_ = bf16[256,2048]{1,0:T(8,128)(2,1)} collective-permute-done((bf16[256,2048]{1,0:T(8,128)(2,1)}, bf16[256,2048]{1,0:T(8,128)(2,1)}, u32[]{:S(2)}, u32[]{:S(2)}) %collective-permute-start.14) | collective-permute-done | bytes 1048608 | tf_op jit(solution)/shard_map/ppermute | solution.py:152
  99.1 22.5 %norm_qkv.1 = (bf16[2,512,2048]{2,1,0:T(8,128)(2,1)}, f32[2,8,512]{2,1,0:T(8,128)}, bf16[2,512,512]{2,1,0:T(8,128)(2,1)}, bf16[2,512,512]{2,1,0:T(8,128)(2,1)}, bf16[2,512,512]{2,1,0:T(8,128)(2,1)}) custom-call(s32[3]{0:T(128)} %pad_add_fusion.refs_0_, bf16[2,512,512]{2,1,0:T(8,128)(2,1)} %refs_19_.1, bf16[2,512,512]{2,1,0:T(8,128)(2,1)} %tie.46.refs_2_, ...), custom_call_target="tpu_custom_call" | custom-call | flops 128849016 | bytes 388853 | tf_op jit(solution)/shard_map/norm_qkv/pallas_call | solution.py:71
  130.1 19.5 %mlp_up.1 = (bf16[2,512,2048]{2,1,0:T(8,128)(2,1)}, bf16[2,512,2048]{2,1,0:T(8,128)(2,1)}) custom-call(s32[3]{0:T(128)} %pad_add_fusion.refs_0_, bf16[2,512,2048]{2,1,0:T(8,128)(2,1)} %get-tuple-element.76.refs_0_.refs_1_, bf16[1,2048]{1,0:T(2,128)(2,1)} %bitcast.80, bf16[512,2048]{1,0:T(8,128)(2,1)} %refs_17_.3, ...), custom_call_target="tpu_custom_call" | custom-call | flops 171798688 | bytes 419512 | tf_op jit(solution)/shard_map/mlp_up/pallas_call | solution.py:71
  156.4 15.0 %out_hidden.1.refs_0_.refs_3_ = bf16[4,2,512,512]{3,2,1,0:T(8,128)(2,1)} custom-call(s32[3]{0:T(128)} %pad_add_fusion.refs_0_, bf16[2,512,2048]{2,1,0:T(8,128)(2,1)} %get-tuple-element.77.refs_0_.refs_1_, bf16[2560,512]{1,0:T(8,128)(2,1)} %tie.54.refs_2_.refs_6_.refs_4_, bf16[2560,512]{1,0:T(8,128)(2,1)} %collective-permute-done.21.refs_1_.refs_3_.refs_7_.refs_5_, ...), custom_call_target="tpu_custom_call" | custom-call | flops 171798688 | bytes 377487 | tf_op jit(solution)/shard_map/out_hidden/pallas_call | solution.py:71
  175.6 20.5 %back_out.1 = (bf16[2,512,2048]{2,1,0:T(8,128)(2,1)}, f32[1,512]{1,0:T(1,128)}, bf16[2,512,512]{2,1,0:T(8,128)(2,1)}, bf16[2,512,2048]{2,1,0:T(8,128)(2,1)}) custom-call(s32[3]{0:T(128)} %pad_add_fusion.refs_0_, bf16[2,512,512]{2,1,0:T(8,128)(2,1)} %refs_20_.1, bf16[2,512,512]{2,1,0:T(8,128)(2,1)} %tie.58.refs_2_, ...), custom_call_target="tpu_custom_call" | custom-call | flops 214748368 | bytes 566272 | tf_op jit(solution)/shard_map/back_out/pallas_call | solution.py:71
  196.0 14.2 %grad_up.1 = (bf16[2,4,512,512]{3,2,1,0:T(8,128)(2,1)}, bf16[2,4,512,512]{3,2,1,0:T(8,128)(2,1)}, f32[1,2048]{1,0:T(1,128)}) custom-call(s32[3]{0:T(128)} %pad_add_fusion.refs_0_, bf16[2,512,2048]{2,1,0:T(8,128)(2,1)} %get-tuple-element.76.refs_0_.refs_1_, bf16[2,512,2048]{2,1,0:T(8,128)(2,1)} %get-tuple-element.80.refs_2_.refs_8_, ...), custom_call_target="tpu_custom_call" | custom-call | flops 171798688 | bytes 335708 | tf_op jit(solution)/shard_map/grad_up/pallas_call | solution.py:71
  210.9 11.9 %attention.2 = (bf16[512,512]{1,0:T(8,128)(2,1)}, bf16[512,512]{1,0:T(8,128)(2,1)}, bf16[2,512,512]{2,1,0:T(8,128)(2,1)}, bf16[1,2,512,512]{3,2,1,0:T(8,128)(2,1)}) custom-call(s32[3]{0:T(128)} %pad_add_fusion.refs_0_, s32[2,1,512]{2,1,0:T(1,128)} %broadcast_in_dim.64.refs_1_, bf16[2,512,512]{2,1,0:T(8,128)(2,1)} %get-tuple-element.74.refs_2_, ...), custom_call_target="tpu_custom_call" | custom-call | flops 128849016 | bytes 209797 | tf_op jit(solution)/shard_map/attention/pallas_call | solution.py:71
  229.7 14.1 %grad_down.1 = (bf16[2,4,512,512]{3,2,1,0:T(8,128)(2,1)}, bf16[2,4,512,512]{3,2,1,0:T(8,128)(2,1)}) custom-call(s32[3]{0:T(128)} %pad_add_fusion.refs_0_, bf16[2,512,2048]{2,1,0:T(8,128)(2,1)} %get-tuple-element.77.refs_0_.refs_1_, bf16[2,512,2048]{2,1,0:T(8,128)(2,1)} %get-tuple-element.84.refs_2_, f32[8,128]{1,0:T(8,128)} %sync.51.refs_3_.refs_1_.refs_2_), custom_call_target="tpu_custom_call" | custom-call | flops 171798688 | bytes 335544 | tf_op jit(solution)/shard_map/grad_down/pallas_call | solution.py:71
  243.8 11.8 %attention.3 = (bf16[512,512]{1,0:T(8,128)(2,1)}, bf16[512,512]{1,0:T(8,128)(2,1)}, bf16[2,512,512]{2,1,0:T(8,128)(2,1)}, bf16[1,2,512,512]{3,2,1,0:T(8,128)(2,1)}) custom-call(s32[3]{0:T(128)} %pad_add_fusion.refs_0_, s32[2,1,512]{2,1,0:T(1,128)} %broadcast_in_dim.64.refs_1_, bf16[2,512,512]{2,1,0:T(8,128)(2,1)} %get-tuple-element.74.refs_2_, ...), custom_call_target="tpu_custom_call" | custom-call | flops 128849016 | bytes 209797 | tf_op jit(solution)/shard_map/attention/pallas_call | solution.py:71
  259.5 8.5 %out_heads.1 = (bf16[2,512,512]{2,1,0:T(8,128)(2,1)}, bf16[2,512,512]{2,1,0:T(8,128)(2,1)}, bf16[2,512,512]{2,1,0:T(8,128)(2,1)}, bf16[2,512,512]{2,1,0:T(8,128)(2,1)}) custom-call(s32[3]{0:T(128)} %pad_add_fusion.refs_0_, bf16[512,512]{1,0:T(8,128)(2,1)} %get-tuple-element.83.refs_0_.refs_1_.refs_3_, ...), custom_call_target="tpu_custom_call" | custom-call | flops 42949672 | bytes 398458 | tf_op jit(solution)/shard_map/out_heads/pallas_call | solution.py:71
  268.1 10.8 %grad_out_query.1 = (bf16[2,2,512,512]{3,2,1,0:T(8,128)(2,1)}, bf16[2,2,512,512]{3,2,1,0:T(8,128)(2,1)}, f32[1,512]{1,0:T(1,128)}) custom-call(s32[3]{0:T(128)} %pad_add_fusion.refs_0_, bf16[2,512,2048]{2,1,0:T(8,128)(2,1)} %get-tuple-element.76.refs_0_.refs_1_, bf16[2,512,2048]{2,1,0:T(8,128)(2,1)} %get-tuple-element.84.refs_2_, ...), custom_call_target="tpu_custom_call" | custom-call | flops 85899344 | bytes 293642 | tf_op jit(solution)/shard_map/grad_out_query/pallas_call | solution.py:71
  278.9 5.2 %combine.10 = (bf16[2,512,512]{2,1,0:T(8,128)(2,1)}, bf16[2,512,512]{2,1,0:T(8,128)(2,1)}, bf16[2,512,512]{2,1,0:T(8,128)(2,1)}) custom-call(s32[3]{0:T(128)} %pad_add_fusion.refs_0_, bf16[8,512,512]{2,1,0:T(8,128)(2,1)} %bitcast.66, bf16[8,512,512]{2,1,0:T(8,128)(2,1)} %bitcast.9.refs_2_.refs_4_, bf16[8,512,512]{2,1,0:T(8,128)(2,1)} %bitcast.67, ...), custom_call_target="tpu_custom_call" | custom-call | bytes 587202 | tf_op jit(solution)/shard_map/combine/pallas_call | solution.py:71
  284.1 13.6 %collective-permute-done.33.refs_1_.refs_5_.refs_7_ = bf16[2,512,512]{2,1,0:T(8,128)(2,1)} collective-permute-done((bf16[2,512,512]{2,1,0:T(8,128)(2,1)}, bf16[2,512,512]{2,1,0:T(8,128)(2,1)}, u32[]{:S(2)}, u32[]{:S(2)}) %collective-permute-start.33) | collective-permute-done | bytes 1048608 | tf_op jit(solution)/shard_map/ppermute | solution.py:1387
  307.3 19.2 %back_in.2 = (bf16[528,512]{1,0:T(8,128)(2,1)}, bf16[528,512]{1,0:T(8,128)(2,1)}, bf16[528,512]{1,0:T(8,128)(2,1)}, bf16[528,512]{1,0:T(8,128)(2,1)}) custom-call(s32[3]{0:T(128)} %pad_add_fusion.refs_0_, bf16[2,512,512]{2,1,0:T(8,128)(2,1)} %refs_19_.1, bf16[2,512,512]{2,1,0:T(8,128)(2,1)} %tie.46.refs_2_, ...), custom_call_target="tpu_custom_call" | custom-call | flops 150323856 | bytes 557793 | tf_op jit(solution)/shard_map/back_in/pallas_call | solution.py:71
  331.0 5.6 %combine.12 = (bf16[2,512,512]{2,1,0:T(8,128)(2,1)}, bf16[2,512,512]{2,1,0:T(8,128)(2,1)}, bf16[2,512,512]{2,1,0:T(8,128)(2,1)}) custom-call(s32[3]{0:T(128)} %pad_add_fusion.refs_0_, bf16[8,512,512]{2,1,0:T(8,128)(2,1)} %bitcast.68, bf16[8,512,512]{2,1,0:T(8,128)(2,1)} %bitcast.9.refs_2_.refs_4_, ...), custom_call_target="tpu_custom_call" | custom-call | bytes 377487 | tf_op jit(solution)/shard_map/combine/pallas_call | solution.py:71
  336.6 9.9 %grad_key_value.1 = (bf16[2,2,512,512]{3,2,1,0:T(8,128)(2,1)}, bf16[2,2,512,512]{3,2,1,0:T(8,128)(2,1)}, f32[2,1,512]{2,1,0:T(1,128)}) custom-call(s32[3]{0:T(128)} %pad_add_fusion.refs_0_, bf16[2,512,2048]{2,1,0:T(8,128)(2,1)} %get-tuple-element.76.refs_0_.refs_1_, bf16[2,512,512]{2,1,0:T(8,128)(2,1)} %get-tuple-element.93.refs_6_.refs_2_, ...), custom_call_target="tpu_custom_call" | custom-call | flops 85899344 | bytes 251740 | tf_op jit(solution)/shard_map/grad_key_value/pallas_call | solution.py:71
  362.4 19.1 %back_in.3 = (bf16[528,512]{1,0:T(8,128)(2,1)}, bf16[528,512]{1,0:T(8,128)(2,1)}, bf16[528,512]{1,0:T(8,128)(2,1)}, bf16[528,512]{1,0:T(8,128)(2,1)}) custom-call(s32[3]{0:T(128)} %pad_add_fusion.refs_0_, bf16[2,512,512]{2,1,0:T(8,128)(2,1)} %refs_19_.1, bf16[2,512,512]{2,1,0:T(8,128)(2,1)} %tie.46.refs_2_, ...), custom_call_target="tpu_custom_call" | custom-call | flops 150323856 | bytes 557793 | tf_op jit(solution)/shard_map/back_in/pallas_call | solution.py:71
  394.2 5.9 %finish_blocks.2.refs_0_ = f32[512,2048]{1,0:T(8,128)} custom-call(s32[3]{0:T(128)} %pad_add_fusion.refs_0_, bf16[2,512,512]{2,1,0:T(8,128)(2,1)} %tie.66.refs_1_, bf16[2,512,512]{2,1,0:T(8,128)(2,1)} %collective-permute-done.35.refs_0_.refs_2_, bf16[2,512,512]{2,1,0:T(8,128)(2,1)} %tie.69.refs_3_, ...), custom_call_target="tpu_custom_call" | custom-call | bytes 167772 | tf_op jit(solution)/shard_map/finish_blocks/pallas_call | solution.py:71
  400.2 6.4 %collective-permute-done.44.refs_0_.refs_4_ = bf16[2,512,512]{2,1,0:T(8,128)(2,1)} collective-permute-done((bf16[2,512,512]{2,1,0:T(8,128)(2,1)}, bf16[2,512,512]{2,1,0:T(8,128)(2,1)}, u32[]{:S(2)}, u32[]{:S(2)}) %collective-permute-start.44) | collective-permute-done | bytes 1048608 | tf_op jit(solution)/shard_map/ppermute | solution.py:152
  417.6 5.9 %finish_blocks.3.refs_0_ = f32[2048,512]{1,0:T(8,128)} custom-call(s32[3]{0:T(128)} %pad_add_fusion.refs_0_, bf16[2,512,512]{2,1,0:T(8,128)(2,1)} %tie.74.refs_1_, bf16[2,512,512]{2,1,0:T(8,128)(2,1)} %collective-permute-done.43.refs_0_.refs_2_, bf16[2,512,512]{2,1,0:T(8,128)(2,1)} %tie.75.refs_3_, ...), custom_call_target="tpu_custom_call" | custom-call | bytes 167772 | tf_op jit(solution)/shard_map/finish_blocks/pallas_call | solution.py:71
  423.5 7.2 %collective-permute-done.51.refs_0_.refs_2_ = bf16[2,512,512]{2,1,0:T(8,128)(2,1)} collective-permute-done((bf16[2,512,512]{2,1,0:T(8,128)(2,1)}, bf16[2,512,512]{2,1,0:T(8,128)(2,1)}, u32[]{:S(2)}, u32[]{:S(2)}) %collective-permute-start.51) | collective-permute-done | bytes 1048608 | tf_op jit(solution)/shard_map/ppermute | solution.py:152
  431.3 6.3 %collective-permute-done.47.refs_0_.refs_3_.refs_9_.refs_15_ = bf16[528,512]{1,0:T(8,128)(2,1)} collective-permute-done((bf16[528,512]{1,0:T(8,128)(2,1)}, bf16[528,512]{1,0:T(8,128)(2,1)}, u32[]{:S(2)}, u32[]{:S(2)}) %collective-permute-start.47) | collective-permute-done | bytes 540704 | tf_op jit(solution)/shard_map/ppermute | solution.py:1204
  (276 shorter events, 172.9 us)
Async XLA Ops:
  7.0 28.9 %collective-permute-start = (bf16[2,512,512]{2,1,0:T(8,128)(2,1)}, bf16[2,512,512]{2,1,0:T(8,128)(2,1)}, u32[]{:S(2)}, u32[]{:S(2)}) collective-permute-start(bf16[2,512,512]{2,1,0:T(8,128)(2,1)} %refs_19_.1), channel_id=1, source_target_pairs={{0,1},{1,2},{2,3},{3,0},{4,5},{5,6},{6,7},{7,4},{8,9},{9,10},{10,1... | collective-permute-start | bytes 3145736 | tf_op jit(solution)/shard_map/ppermute | solution.py:1204
  36.5 27.5 %collective-permute-start.10 = (bf16[512,1536]{1,0:T(8,128)(2,1)}, bf16[512,1536]{1,0:T(8,128)(2,1)}, u32[]{:S(2)}, u32[]{:S(2)}) collective-permute-start(bf16[512,1536]{1,0:T(8,128)(2,1)} %tie.45.refs_11_), channel_id=1, source_target_pairs={{0,8},{8,0},{16,24},{24,16},{1,9},{9,1},{17,25},{25,17},{2,10},{10... | collective-permute-start | bytes 4718600 | tf_op jit(solution)/shard_map/ppermute | solution.py:152
  36.5 25.9 %collective-permute-start.9 = (bf16[2,512,512]{2,1,0:T(8,128)(2,1)}, bf16[2,512,512]{2,1,0:T(8,128)(2,1)}, u32[]{:S(2)}, u32[]{:S(2)}) collective-permute-start(bf16[2,512,512]{2,1,0:T(8,128)(2,1)} %refs_19_.1), channel_id=1, source_target_pairs={{0,3},{1,0},{2,1},{3,2},{4,7},{5,4},{6,5},{7,6},{8,11},{9,8},{10,9... | collective-permute-start | bytes 3145736 | tf_op jit(solution)/shard_map/ppermute | solution.py:1204
  64.0 31.5 %collective-permute-start.15 = (bf16[2560,256]{1,0:T(8,128)(2,1)}, bf16[2560,256]{1,0:T(8,128)(2,1)}, u32[]{:S(2)}, u32[]{:S(2)}) collective-permute-start(bf16[2560,256]{1,0:T(8,128)(2,1)} %tie.50), channel_id=1, source_target_pairs={{0,16},{8,24},{16,0},{24,8},{1,17},{9,25},{17,1},{25,9},{2,18},{10... | collective-permute-start | bytes 3932168 | tf_op jit(solution)/shard_map/ppermute | solution.py:152
  67.1 28.1 %collective-permute-start.11 = (bf16[2,512,512]{2,1,0:T(8,128)(2,1)}, bf16[2,512,512]{2,1,0:T(8,128)(2,1)}, u32[]{:S(2)}, u32[]{:S(2)}) collective-permute-start(bf16[2,512,512]{2,1,0:T(8,128)(2,1)} %tie.46.refs_2_), channel_id=1, source_target_pairs={{0,1},{1,2},{2,3},{3,0},{4,5},{5,6},{6,7},{7,4},{8,9},{9,10},{10,1... | collective-permute-start | bytes 3145736 | tf_op jit(solution)/shard_map/ppermute | solution.py:1204
  67.5 54.1 %collective-permute-start.16 = (bf16[512,2048]{1,0:T(8,128)(2,1)}, bf16[512,2048]{1,0:T(8,128)(2,1)}, u32[]{:S(2)}, u32[]{:S(2)}) collective-permute-start(bf16[512,2048]{1,0:T(8,128)(2,1)} %refs_17_.3), channel_id=1, source_target_pairs={{0,8},{8,0},{16,24},{24,16},{1,9},{9,1},{17,25},{25,17},{2,10},{10... | collective-permute-start | bytes 6291464 | tf_op jit(solution)/shard_map/ppermute | solution.py:152
  75.1 46.5 %collective-permute-start.19 = (bf16[2,512,512]{2,1,0:T(8,128)(2,1)}, bf16[2,512,512]{2,1,0:T(8,128)(2,1)}, u32[]{:S(2)}, u32[]{:S(2)}) collective-permute-start(bf16[2,512,512]{2,1,0:T(8,128)(2,1)} %refs_20_.1), channel_id=1, source_target_pairs={{0,1},{1,2},{2,3},{3,0},{4,5},{5,6},{6,7},{7,4},{8,9},{9,10},{10,1... | collective-permute-start | bytes 3145736 | tf_op jit(solution)/shard_map/ppermute | solution.py:1204
  95.5 30.7 %collective-permute-start.20 = (bf16[2560,256]{1,0:T(8,128)(2,1)}, bf16[2560,256]{1,0:T(8,128)(2,1)}, u32[]{:S(2)}, u32[]{:S(2)}) collective-permute-start(bf16[2560,256]{1,0:T(8,128)(2,1)} %tie.53.refs_0_), channel_id=1, source_target_pairs={{0,4},{4,0},{1,5},{5,1},{2,6},{6,2},{3,7},{7,3},{8,12},{12,8},{9,1... | collective-permute-start | bytes 3932168 | tf_op jit(solution)/shard_map/ppermute | solution.py:152
  126.8 44.5 %collective-permute-start.25 = (bf16[2,512,512]{2,1,0:T(8,128)(2,1)}, bf16[2,512,512]{2,1,0:T(8,128)(2,1)}, u32[]{:S(2)}, u32[]{:S(2)}) collective-permute-start(bf16[2,512,512]{2,1,0:T(8,128)(2,1)} %refs_20_.1), channel_id=1, source_target_pairs={{0,3},{1,0},{2,1},{3,2},{4,7},{5,4},{6,5},{7,6},{8,11},{9,8},{10,9... | collective-permute-start | bytes 3145736 | tf_op jit(solution)/shard_map/ppermute | solution.py:1204
  129.0 46.6 %collective-permute-start.26 = (bf16[2,512,512]{2,1,0:T(8,128)(2,1)}, bf16[2,512,512]{2,1,0:T(8,128)(2,1)}, u32[]{:S(2)}, u32[]{:S(2)}) collective-permute-start(bf16[2,512,512]{2,1,0:T(8,128)(2,1)} %tie.58.refs_2_), channel_id=1, source_target_pairs={{0,1},{1,2},{2,3},{3,0},{4,5},{5,6},{6,7},{7,4},{8,9},{9,10},{10,1... | collective-permute-start | bytes 3145736 | tf_op jit(solution)/shard_map/ppermute | solution.py:1204
  149.7 46.4 %collective-permute-start.24 = (bf16[2,512,512]{2,1,0:T(8,128)(2,1)}, bf16[2,512,512]{2,1,0:T(8,128)(2,1)}, u32[]{:S(2)}, u32[]{:S(2)}) collective-permute-start(bf16[2,512,512]{2,1,0:T(8,128)(2,1)} %tie.57.refs_3_), channel_id=1, source_target_pairs={{0,4},{1,5},{2,6},{3,7},{8,12},{9,13},{10,14},{11,15},{16,20},{17,... | collective-permute-start | bytes 3145736 | tf_op jit(solution)/shard_map/ppermute | solution.py:1367
  154.1 56.1 %collective-permute-start.27 = (bf16[2,512,512]{2,1,0:T(8,128)(2,1)}, bf16[2,512,512]{2,1,0:T(8,128)(2,1)}, u32[]{:S(2)}, u32[]{:S(2)}) collective-permute-start(bf16[2,512,512]{2,1,0:T(8,128)(2,1)} %tie.59.refs_3_), channel_id=1, source_target_pairs={{0,4},{1,5},{2,6},{3,7},{8,12},{9,13},{10,14},{11,15},{16,20},{17,... | collective-permute-start | bytes 3145736 | tf_op jit(solution)/shard_map/ppermute | solution.py:1367
  222.8 34.0 %collective-permute-start.29 = (bf16[2,512,512]{2,1,0:T(8,128)(2,1)}, bf16[2,512,512]{2,1,0:T(8,128)(2,1)}, u32[]{:S(2)}, u32[]{:S(2)}) collective-permute-start(bf16[2,512,512]{2,1,0:T(8,128)(2,1)} %tie.61), channel_id=1, source_target_pairs={{4,0},{5,1},{6,2},{7,3},{12,8},{13,9},{14,10},{15,11},{20,16},{21,... | collective-permute-start | bytes 3145736 | tf_op jit(solution)/shard_map/ppermute | solution.py:1387
  228.3 28.5 %collective-permute-start.30 = (bf16[2,512,512]{2,1,0:T(8,128)(2,1)}, bf16[2,512,512]{2,1,0:T(8,128)(2,1)}, u32[]{:S(2)}, u32[]{:S(2)}) collective-permute-start(bf16[2,512,512]{2,1,0:T(8,128)(2,1)} %get-tuple-element.86.refs_0_), channel_id=1, source_target_pairs={{0,16},{8,24},{16,0},{24,8},{1,17},{9,25},{17,1},{25,9},{2,18},{10... | collective-permute-start | bytes 3145736 | tf_op jit(solution)/shard_map/ppermute | solution.py:152
  256.8 40.8 %collective-permute-start.33 = (bf16[2,512,512]{2,1,0:T(8,128)(2,1)}, bf16[2,512,512]{2,1,0:T(8,128)(2,1)}, u32[]{:S(2)}, u32[]{:S(2)}) collective-permute-start(bf16[2,512,512]{2,1,0:T(8,128)(2,1)} %tie.64), channel_id=1, source_target_pairs={{4,0},{5,1},{6,2},{7,3},{12,8},{13,9},{14,10},{15,11},{20,16},{21,... | collective-permute-start | bytes 3145736 | tf_op jit(solution)/shard_map/ppermute | solution.py:1387
  258.1 39.5 %collective-permute-start.31 = (bf16[2,512,512]{2,1,0:T(8,128)(2,1)}, bf16[2,512,512]{2,1,0:T(8,128)(2,1)}, u32[]{:S(2)}, u32[]{:S(2)}) collective-permute-start(bf16[2,512,512]{2,1,0:T(8,128)(2,1)} %tie.62), channel_id=1, source_target_pairs={{0,16},{8,24},{16,0},{24,8},{1,17},{9,25},{17,1},{25,9},{2,18},{10... | collective-permute-start | bytes 3145736 | tf_op jit(solution)/shard_map/ppermute | solution.py:152
  297.7 30.2 %collective-permute-start.40 = (bf16[2,2,512,512]{3,2,1,0:T(8,128)(2,1)}, bf16[2,2,512,512]{3,2,1,0:T(8,128)(2,1)}, u32[]{:S(2)}, u32[]{:S(2)}) collective-permute-start(bf16[2,2,512,512]{3,2,1,0:T(8,128)(2,1)} %tie.71), channel_id=1, source_target_pairs={{0,8},{8,0},{16,24},{24,16},{1,9},{9,1},{17,25},{25,17},{2,10},{10... | collective-permute-start | bytes 6291464 | tf_op jit(solution)/shard_map/ppermute | solution.py:152
  297.7 28.8 %collective-permute-start.35 = (bf16[2,512,512]{2,1,0:T(8,128)(2,1)}, bf16[2,512,512]{2,1,0:T(8,128)(2,1)}, u32[]{:S(2)}, u32[]{:S(2)}) collective-permute-start(bf16[2,512,512]{2,1,0:T(8,128)(2,1)} %tie.66.refs_1_), channel_id=1, source_target_pairs={{0,4},{4,0},{1,5},{5,1},{2,6},{6,2},{3,7},{7,3},{8,12},{12,8},{9,1... | collective-permute-start | bytes 3145736 | tf_op jit(solution)/shard_map/ppermute | solution.py:152
  300.4 27.4 %collective-permute-start.34 = (bf16[2,512,512]{2,1,0:T(8,128)(2,1)}, bf16[2,512,512]{2,1,0:T(8,128)(2,1)}, u32[]{:S(2)}, u32[]{:S(2)}) collective-permute-start(bf16[2,512,512]{2,1,0:T(8,128)(2,1)} %tie.65), channel_id=1, source_target_pairs={{0,1},{1,2},{2,3},{3,0},{4,5},{5,6},{6,7},{7,4},{8,9},{9,10},{10,1... | collective-permute-start | bytes 3145736 | tf_op jit(solution)/shard_map/ppermute | solution.py:1204
  327.8 26.2 %collective-permute-start.42 = (bf16[2,512,512]{2,1,0:T(8,128)(2,1)}, bf16[2,512,512]{2,1,0:T(8,128)(2,1)}, u32[]{:S(2)}, u32[]{:S(2)}) collective-permute-start(bf16[2,512,512]{2,1,0:T(8,128)(2,1)} %tie.73), channel_id=1, source_target_pairs={{0,16},{8,24},{16,0},{24,8},{1,17},{9,25},{17,1},{25,9},{2,18},{10... | collective-permute-start | bytes 3145736 | tf_op jit(solution)/shard_map/ppermute | solution.py:152
  354.1 32.5 %collective-permute-start.46 = (bf16[2,2,512,512]{3,2,1,0:T(8,128)(2,1)}, bf16[2,2,512,512]{3,2,1,0:T(8,128)(2,1)}, u32[]{:S(2)}, u32[]{:S(2)}) collective-permute-start(bf16[2,2,512,512]{3,2,1,0:T(8,128)(2,1)} %tie.77), channel_id=1, source_target_pairs={{0,8},{8,0},{16,24},{24,16},{1,9},{9,1},{17,25},{25,17},{2,10},{10... | collective-permute-start | bytes 6291464 | tf_op jit(solution)/shard_map/ppermute | solution.py:152
  354.2 27.3 %collective-permute-start.43 = (bf16[2,512,512]{2,1,0:T(8,128)(2,1)}, bf16[2,512,512]{2,1,0:T(8,128)(2,1)}, u32[]{:S(2)}, u32[]{:S(2)}) collective-permute-start(bf16[2,512,512]{2,1,0:T(8,128)(2,1)} %tie.74.refs_1_), channel_id=1, source_target_pairs={{0,4},{4,0},{1,5},{5,1},{2,6},{6,2},{3,7},{7,3},{8,12},{12,8},{9,1... | collective-permute-start | bytes 3145736 | tf_op jit(solution)/shard_map/ppermute | solution.py:152
  355.3 27.0 %collective-permute-start.41 = (bf16[2,512,512]{2,1,0:T(8,128)(2,1)}, bf16[2,512,512]{2,1,0:T(8,128)(2,1)}, u32[]{:S(2)}, u32[]{:S(2)}) collective-permute-start(bf16[2,512,512]{2,1,0:T(8,128)(2,1)} %tie.72), channel_id=1, source_target_pairs={{0,3},{1,0},{2,1},{3,2},{4,7},{5,4},{6,5},{7,6},{8,11},{9,8},{10,9... | collective-permute-start | bytes 3145736 | tf_op jit(solution)/shard_map/ppermute | solution.py:1204
  430.7 26.5 %collective-permute-start.54 = (bf16[2,512,512]{2,1,0:T(8,128)(2,1)}, bf16[2,512,512]{2,1,0:T(8,128)(2,1)}, u32[]{:S(2)}, u32[]{:S(2)}) collective-permute-start(bf16[2,512,512]{2,1,0:T(8,128)(2,1)} %tie.83.refs_6_), channel_id=1, source_target_pairs={{0,4},{4,0},{1,5},{5,1},{2,6},{6,2},{3,7},{7,3},{8,12},{12,8},{9,1... | collective-permute-start | bytes 3145736 | tf_op jit(solution)/shard_map/ppermute | solution.py:152
  (44 other events, 684.8 us)

commit v7 on v6

--- a/solution.py
+++ b/solution.py
@@ -61,7 +61,9 @@
 ANYWHERE = pl.BlockSpec(memory_space=pl.ANY)
 
 
-def call(body, name, grid, info, ins, in_specs, outs, out_specs, flops, scratch=(), deps=()):
+def call(
+    body, name, grid, info, ins, in_specs, outs, out_specs, flops, scratch=(), deps=(), aliases=()
+):
     moved = sum(math.prod(a.shape) * a.dtype.itemsize for a in (*ins, *jax.tree.leaves(outs)))
     first, last = 1 + len(ins), 1 + len(ins) + len(deps)
 
@@ -78,6 +80,7 @@
             scratch_shapes=list(scratch),
         ),
         out_shape=outs,
+        input_output_aliases={1 + n: m for n, m in aliases},
         compiler_params=pltpu.CompilerParams(vmem_limit_bytes=VMEM),
         cost_estimate=pl.CostEstimate(
             flops=int(flops * COST), bytes_accessed=int(moved * COST), transcendentals=0
@@ -606,10 +609,10 @@
         scores_1 = score(1)
         probs_0, rounded_0 = soften(*scores_0)
         out_0, delta_0 = weigh(0, rounded_0)
+        dss_0 = differ(probs_0, grads(0), delta_0)
         probs_1, rounded_1 = soften(*scores_1)
-        dss_0 = differ(probs_0, grads(0), delta_0)
+        dq_0 = back(0, dss_0)
         out_1, delta_1 = weigh(1, rounded_1)
-        dq_0 = back(0, dss_0)
         dss_1 = differ(probs_1, grads(1), delta_1)
         dq_1 = back(1, dss_1)
         outputs = [(out_0, dq_0), (out_1, dq_1)]
@@ -908,30 +911,49 @@
     )
 
 
-def grad_down_body(info, hidden, ct, kept, given):
-    d = info[2]
-    for target, which in ((given, GIVEN), (kept, KEPT)):
-        for r, at in which:
-            window = columns(d ^ r)
-            y = dot_tn(hidden[0], ct[0, :, window]) + dot_tn(hidden[1], ct[1, :, window])
-            target[at, 0] = y.astype(bf16)
-
-
-def grad_down(info, hidden, ct, deps=()):
+def grad_down_body(offsets, info, hidden, *refs):
+    parts = refs[: len(offsets)]
+    kept, given, tiles, sems = refs[-4:]
+    n = pl.program_id(0)
+    for i, (part, offset) in enumerate(zip(parts, offsets)):
+        tiles[n, i] = (dot_tn(hidden[0], part[0]) + dot_tn(hidden[1], part[1])).astype(bf16)
+        r = ((info[0] + offset) % N_TP) ^ info[2]
+        for odd, target in ((0, kept), (1, given)):
+
+            @pl.when(r % 2 == odd)
+            def _(i=i, r=r, target=target):
+                place = target.at[r // 2, n]
+                pltpu.make_async_copy(tiles.at[n, i], place, sems.at[n, i]).start()
+
+    @pl.when(n == tiles.shape[0] - 1)
+    def _():
+        for m in range(tiles.shape[0]):
+            for i in range(len(offsets)):
+                pltpu.make_async_copy(tiles.at[m, i], kept.at[0, 0], sems.at[m, i]).wait()
+
+
+def grad_down(info, hidden, parts, offsets, begun=(), deps=()):
     _, rows, units = hidden.shape
     count = units // CH
-    message = spec((2, 1, CH, CH), lambda j, *_: (0, j, 0, 0))
+    at = 1 + len(parts)
     return call(
-        grad_down_body,
+        functools.partial(grad_down_body, offsets),
         "grad_down",
         count,
         info,
-        (hidden, ct),
-        [spec((2, rows, CH), lambda j, *_: (0, 0, j)), once(2, rows, D)],
+        (hidden, *parts, *begun),
+        [spec((2, rows, CH), lambda j, *_: (0, 0, j))]
+        + [once(2, rows, CH)] * len(parts)
+        + [ANYWHERE] * len(begun),
         (shaped((2, count, CH, CH)),) * 2,
-        [message, message],
-        4 * rows * D * units,
+        [ANYWHERE] * 2,
+        4 * rows * CH * units * len(parts),
+        [
+            pltpu.VMEM((count, len(parts), CH, CH), bf16),
+            pltpu.SemaphoreType.DMA((count, len(parts))),
+        ],
         deps=deps,
+        aliases=[(at + n, n) for n in range(len(begun))],
     )
 
 
@@ -1425,7 +1447,11 @@
     send_keys(0)
     send_keys(1)
     out_parts = out_hidden(layout, info, hidden, shards_o.pieces, deps=clock.marks)
-    clock.sync(out_parts, ct.ahead, ct.far)
+    clock.sync(out_parts, ct.ahead)
+    down_begun = grad_down(
+        info, hidden, (ct.own, ct.behind, ct.ahead), (0, 3, 1), deps=clock.marks
+    )
+    clock.sync(down_begun[0], ct.far)
 
     cf, out_bias_sum, datt, dup = back_out(
         layout, info, ct.parts, shards_o.pieces, slope, deps=clock.marks
@@ -1445,7 +1471,9 @@
     across, across_1 = added([up.across(0), up.across(1)])
     up.over_x(0, across)
     clock.sync(across)
-    down_kept, down_given = grad_down(info, hidden, cf, deps=clock.marks)
+    down_kept, down_given = grad_down(
+        info, hidden, (ct.far,), (2,), down_begun, deps=clock.marks
+    )
     clock.sync(down_kept, *clock.marks)
     att[1], dq[1], dkv[1], sent[1] = attention_step(1)
     clock.sync(att[1], sent[0], up.moved[0])

time: 476 us -> 472 us (level)
  waiting for transfers between devices: 115 us -> 106 us
  Pallas kernels: 260 us -> 265 us
    ppermute x2, waiting for transfers between devices: 14.8 us -> 7.93 us  [returned(): return lax.ppermute(clock.go(sent[0]), 'ctx', [(1, 0)])]
    pallas_call x28 -> x29, Pallas kernels: 260 us -> 264 us  [call(): pl.pallas_call(without_deps, grid_spec=pltpu.PrefetchScalarGridSpec(num_s...]
    unnamed x39 -> x41, local copies, waits for them, and re-layouts: 10.1 us -> 10.2 us
  transfers between devices with their start and end apart: 58 -> 58, of which waited for: 23 -> 24; matrix products, arithmetic and copies ran while one was open for 5% -> 5% of each run, Pallas kernels for 55% -> 56%
where the time goes in v7:
time: 472 us; the launch traced here: 464 us
  Pallas kernels  265 us (56%)
  waiting for transfers between devices  106 us (22%)
  starting transfers between devices  58.8 us (12%)
  local copies, waits for them, and re-layouts  19.9 us (4%)
  other arithmetic  12.4 us (3%)
    pallas_call x29, Pallas kernels, call(): pl.pallas_call(without_deps, grid_spec=pltpu.PrefetchScalarGridSpec(num_s...  264 us
    ppermute x18, waiting for transfers between devices, ring(): lax.ppermute(array, 'tp', [(i, (i + step) % N_TP) for i in range(N_TP)])  49.3 us
    ppermute x36, waiting for transfers between devices, swap(): return lax.ppermute(array, axis, [(i, i ^ bit) for i in range(size)])  48.9 us
    ppermute x36, starting transfers between devices, swap(): return lax.ppermute(array, axis, [(i, i ^ bit) for i in range(size)])  29.4 us
    ppermute x18, starting transfers between devices, ring(): lax.ppermute(array, 'tp', [(i, (i + step) % N_TP) for i in range(N_TP)])  20.1 us
    unnamed x41, local copies, waits for them, and re-layouts  10.2 us
  transfers between devices with their start and end apart: 58, of which 24 were waited for; matrix products, arithmetic and copies ran while one was open for 5% of the time, Pallas kernels for 56%

profile of v7, /device:TPU:0, one launch (start us, length us, event | category | flops | bytes accessed | tf_op | source)
XLA Modules:
  0.0 463.6 jit_solution(1415468990471184976)
XLA Ops:
  25.0 8.0 %collective-permute-done.4.refs_2_ = bf16[2,512]{1,0:T(2,128)(2,1)S(1)} collective-permute-done((bf16[2,512]{1,0:T(2,128)(2,1)S(1)}, bf16[2,512]{1,0:T(2,128)(2,1)S(1)}, u32[]{:S(2)}, u32[]{:S(2)}) %collective-permute-start.4) | collective-permute-done | bytes 2080 | tf_op jit(solution)/shard_map/ppermute | solution.py:1226
  46.8 15.6 %collective-permute-done.9.refs_2_.refs_3_ = bf16[2,512,512]{2,1,0:T(8,128)(2,1)} collective-permute-done((bf16[2,512,512]{2,1,0:T(8,128)(2,1)}, bf16[2,512,512]{2,1,0:T(8,128)(2,1)}, u32[]{:S(2)}, u32[]{:S(2)}) %collective-permute-start.9) | collective-permute-done | bytes 1048608 | tf_op jit(solution)/shard_map/ppermute | solution.py:1226
  75.6 15.6 %collective-permute-done.14.refs_3_.refs_0_ = bf16[256,2048]{1,0:T(8,128)(2,1)} collective-permute-done((bf16[256,2048]{1,0:T(8,128)(2,1)}, bf16[256,2048]{1,0:T(8,128)(2,1)}, u32[]{:S(2)}, u32[]{:S(2)}) %collective-permute-start.14) | collective-permute-done | bytes 1048608 | tf_op jit(solution)/shard_map/ppermute | solution.py:155
  99.2 22.5 %norm_qkv.1 = (bf16[2,512,2048]{2,1,0:T(8,128)(2,1)}, f32[2,8,512]{2,1,0:T(8,128)}, bf16[2,512,512]{2,1,0:T(8,128)(2,1)}, bf16[2,512,512]{2,1,0:T(8,128)(2,1)}, bf16[2,512,512]{2,1,0:T(8,128)(2,1)}) custom-call(s32[3]{0:T(128)} %pad_add_fusion.refs_0_, bf16[2,512,512]{2,1,0:T(8,128)(2,1)} %refs_19_.1, bf16[2,512,512]{2,1,0:T(8,128)(2,1)} %tie.46.refs_2_, ...), custom_call_target="tpu_custom_call" | custom-call | flops 128849016 | bytes 388853 | tf_op jit(solution)/shard_map/norm_qkv/pallas_call | solution.py:73
  129.9 19.6 %mlp_up.1 = (bf16[2,512,2048]{2,1,0:T(8,128)(2,1)}, bf16[2,512,2048]{2,1,0:T(8,128)(2,1)}) custom-call(s32[3]{0:T(128)} %pad_add_fusion.refs_0_, bf16[2,512,2048]{2,1,0:T(8,128)(2,1)} %get-tuple-element.78.refs_0_.refs_1_, bf16[1,2048]{1,0:T(2,128)(2,1)} %bitcast.80, bf16[512,2048]{1,0:T(8,128)(2,1)} %refs_17_.3, ...), custom_call_target="tpu_custom_call" | custom-call | flops 171798688 | bytes 419512 | tf_op jit(solution)/shard_map/mlp_up/pallas_call | solution.py:73
  156.2 14.9 %out_hidden.1.refs_0_.refs_3_ = bf16[4,2,512,512]{3,2,1,0:T(8,128)(2,1)} custom-call(s32[3]{0:T(128)} %pad_add_fusion.refs_0_, bf16[2,512,2048]{2,1,0:T(8,128)(2,1)} %get-tuple-element.79.refs_0_.refs_1_, bf16[2560,512]{1,0:T(8,128)(2,1)} %tie.54.refs_2_.refs_6_.refs_4_, bf16[2560,512]{1,0:T(8,128)(2,1)} %collective-permute-done.21.refs_1_.refs_3_.refs_7_.refs_5_, ...), custom_call_target="tpu_custom_call" | custom-call | flops 171798688 | bytes 377487 | tf_op jit(solution)/shard_map/out_hidden/pallas_call | solution.py:73
  171.1 11.1 %grad_down.2 = (bf16[2,4,512,512]{3,2,1,0:T(8,128)(2,1)}, bf16[2,4,512,512]{3,2,1,0:T(8,128)(2,1)}) custom-call(s32[3]{0:T(128)} %pad_add_fusion.refs_0_, bf16[2,512,2048]{2,1,0:T(8,128)(2,1)} %get-tuple-element.79.refs_0_.refs_1_, bf16[2,512,512]{2,1,0:T(8,128)(2,1)} %refs_20_.1, bf16[2,512,512]{2,1,0:T(8,128)(2,1)} %tie.58.refs_3_.refs_2_, ...), custom_call_target="tpu_custom_call" | custom-call | flops 128849016 | bytes 314572 | tf_op jit(solution)/shard_map/grad_down/pallas_call | solution.py:73
  182.3 20.5 %back_out.1 = (bf16[2,512,2048]{2,1,0:T(8,128)(2,1)}, f32[1,512]{1,0:T(1,128)}, bf16[2,512,512]{2,1,0:T(8,128)(2,1)}, bf16[2,512,2048]{2,1,0:T(8,128)(2,1)}) custom-call(s32[3]{0:T(128)} %pad_add_fusion.refs_0_, bf16[2,512,512]{2,1,0:T(8,128)(2,1)} %refs_20_.1, bf16[2,512,512]{2,1,0:T(8,128)(2,1)} %tie.58.refs_3_.refs_2_, ...), custom_call_target="tpu_custom_call" | custom-call | flops 214748368 | bytes 566272 | tf_op jit(solution)/shard_map/back_out/pallas_call | solution.py:73
  202.8 14.2 %grad_up.1 = (bf16[2,4,512,512]{3,2,1,0:T(8,128)(2,1)}, bf16[2,4,512,512]{3,2,1,0:T(8,128)(2,1)}, f32[1,2048]{1,0:T(1,128)}) custom-call(s32[3]{0:T(128)} %pad_add_fusion.refs_0_, bf16[2,512,2048]{2,1,0:T(8,128)(2,1)} %get-tuple-element.78.refs_0_.refs_1_, bf16[2,512,2048]{2,1,0:T(8,128)(2,1)} %get-tuple-element.83.refs_2_.refs_8_, ...), custom_call_target="tpu_custom_call" | custom-call | flops 171798688 | bytes 335708 | tf_op jit(solution)/shard_map/grad_up/pallas_call | solution.py:73
  217.7 12.2 %attention.2 = (bf16[512,512]{1,0:T(8,128)(2,1)}, bf16[512,512]{1,0:T(8,128)(2,1)}, bf16[2,512,512]{2,1,0:T(8,128)(2,1)}, bf16[1,2,512,512]{3,2,1,0:T(8,128)(2,1)}) custom-call(s32[3]{0:T(128)} %pad_add_fusion.refs_0_, s32[2,1,512]{2,1,0:T(1,128)} %broadcast_in_dim.64.refs_1_, bf16[2,512,512]{2,1,0:T(8,128)(2,1)} %get-tuple-element.76.refs_2_, ...), custom_call_target="tpu_custom_call" | custom-call | flops 128849016 | bytes 209797 | tf_op jit(solution)/shard_map/attention/pallas_call | solution.py:73
  236.7 6.8 %grad_down.3 = (bf16[2,4,512,512]{3,2,1,0:T(8,128)(2,1)}, bf16[2,4,512,512]{3,2,1,0:T(8,128)(2,1)}) custom-call(s32[3]{0:T(128)} %pad_add_fusion.refs_0_, bf16[2,512,2048]{2,1,0:T(8,128)(2,1)} %get-tuple-element.79.refs_0_.refs_1_, ...), custom_call_target="tpu_custom_call", output_to_operand_aliasing={{0}: (3, {}), {1}: (4, {})} | custom-call | flops 42949672 | bytes 440401 | tf_op jit(solution)/shard_map/grad_down/pallas_call | solution.py:73
  243.5 11.9 %attention.3 = (bf16[512,512]{1,0:T(8,128)(2,1)}, bf16[512,512]{1,0:T(8,128)(2,1)}, bf16[2,512,512]{2,1,0:T(8,128)(2,1)}, bf16[1,2,512,512]{3,2,1,0:T(8,128)(2,1)}) custom-call(s32[3]{0:T(128)} %pad_add_fusion.refs_0_, s32[2,1,512]{2,1,0:T(1,128)} %broadcast_in_dim.64.refs_1_, bf16[2,512,512]{2,1,0:T(8,128)(2,1)} %get-tuple-element.76.refs_2_, ...), custom_call_target="tpu_custom_call" | custom-call | flops 128849016 | bytes 209797 | tf_op jit(solution)/shard_map/attention/pallas_call | solution.py:73
  264.0 8.5 %out_heads.1 = (bf16[2,512,512]{2,1,0:T(8,128)(2,1)}, bf16[2,512,512]{2,1,0:T(8,128)(2,1)}, bf16[2,512,512]{2,1,0:T(8,128)(2,1)}, bf16[2,512,512]{2,1,0:T(8,128)(2,1)}) custom-call(s32[3]{0:T(128)} %pad_add_fusion.refs_0_, bf16[512,512]{1,0:T(8,128)(2,1)} %get-tuple-element.86.refs_0_.refs_1_.refs_3_, ...), custom_call_target="tpu_custom_call" | custom-call | flops 42949672 | bytes 398458 | tf_op jit(solution)/shard_map/out_heads/pallas_call | solution.py:73
  272.5 10.8 %grad_out_query.1 = (bf16[2,2,512,512]{3,2,1,0:T(8,128)(2,1)}, bf16[2,2,512,512]{3,2,1,0:T(8,128)(2,1)}, f32[1,512]{1,0:T(1,128)}) custom-call(s32[3]{0:T(128)} %pad_add_fusion.refs_0_, bf16[2,512,2048]{2,1,0:T(8,128)(2,1)} %get-tuple-element.78.refs_0_.refs_1_, bf16[2,512,2048]{2,1,0:T(8,128)(2,1)} %get-tuple-element.100.refs_2_, ...), custom_call_target="tpu_custom_call" | custom-call | flops 85899344 | bytes 293642 | tf_op jit(solution)/shard_map/grad_out_query/pallas_call | solution.py:73
  300.1 19.1 %back_in.2 = (bf16[528,512]{1,0:T(8,128)(2,1)}, bf16[528,512]{1,0:T(8,128)(2,1)}, bf16[528,512]{1,0:T(8,128)(2,1)}, bf16[528,512]{1,0:T(8,128)(2,1)}) custom-call(s32[3]{0:T(128)} %pad_add_fusion.refs_0_, bf16[2,512,512]{2,1,0:T(8,128)(2,1)} %refs_19_.1, bf16[2,512,512]{2,1,0:T(8,128)(2,1)} %tie.46.refs_2_, ...), custom_call_target="tpu_custom_call" | custom-call | flops 150323856 | bytes 557793 | tf_op jit(solution)/shard_map/back_in/pallas_call | solution.py:73
  325.9 5.7 %combine.12 = (bf16[2,512,512]{2,1,0:T(8,128)(2,1)}, bf16[2,512,512]{2,1,0:T(8,128)(2,1)}, bf16[2,512,512]{2,1,0:T(8,128)(2,1)}) custom-call(s32[3]{0:T(128)} %pad_add_fusion.refs_0_, bf16[8,512,512]{2,1,0:T(8,128)(2,1)} %bitcast.68, bf16[8,512,512]{2,1,0:T(8,128)(2,1)} %bitcast.9.refs_2_.refs_4_, ...), custom_call_target="tpu_custom_call" | custom-call | bytes 377487 | tf_op jit(solution)/shard_map/combine/pallas_call | solution.py:73
  331.6 9.9 %grad_key_value.1 = (bf16[2,2,512,512]{3,2,1,0:T(8,128)(2,1)}, bf16[2,2,512,512]{3,2,1,0:T(8,128)(2,1)}, f32[2,1,512]{2,1,0:T(1,128)}) custom-call(s32[3]{0:T(128)} %pad_add_fusion.refs_0_, bf16[2,512,2048]{2,1,0:T(8,128)(2,1)} %get-tuple-element.78.refs_0_.refs_1_, bf16[2,512,512]{2,1,0:T(8,128)(2,1)} %get-tuple-element.96.refs_6_.refs_2_, ...), custom_call_target="tpu_custom_call" | custom-call | flops 85899344 | bytes 251740 | tf_op jit(solution)/shard_map/grad_key_value/pallas_call | solution.py:73
  358.5 19.1 %back_in.3 = (bf16[528,512]{1,0:T(8,128)(2,1)}, bf16[528,512]{1,0:T(8,128)(2,1)}, bf16[528,512]{1,0:T(8,128)(2,1)}, bf16[528,512]{1,0:T(8,128)(2,1)}) custom-call(s32[3]{0:T(128)} %pad_add_fusion.refs_0_, bf16[2,512,512]{2,1,0:T(8,128)(2,1)} %refs_19_.1, bf16[2,512,512]{2,1,0:T(8,128)(2,1)} %tie.46.refs_2_, ...), custom_call_target="tpu_custom_call" | custom-call | flops 150323856 | bytes 557793 | tf_op jit(solution)/shard_map/back_in/pallas_call | solution.py:73
  390.4 5.9 %finish_blocks.2.refs_0_ = f32[512,2048]{1,0:T(8,128)} custom-call(s32[3]{0:T(128)} %pad_add_fusion.refs_0_, bf16[2,512,512]{2,1,0:T(8,128)(2,1)} %tie.66.refs_1_, bf16[2,512,512]{2,1,0:T(8,128)(2,1)} %collective-permute-done.35.refs_0_.refs_2_, bf16[2,512,512]{2,1,0:T(8,128)(2,1)} %tie.69.refs_3_, ...), custom_call_target="tpu_custom_call" | custom-call | bytes 167772 | tf_op jit(solution)/shard_map/finish_blocks/pallas_call | solution.py:73
  396.3 6.4 %collective-permute-done.44.refs_0_.refs_4_ = bf16[2,512,512]{2,1,0:T(8,128)(2,1)} collective-permute-done((bf16[2,512,512]{2,1,0:T(8,128)(2,1)}, bf16[2,512,512]{2,1,0:T(8,128)(2,1)}, u32[]{:S(2)}, u32[]{:S(2)}) %collective-permute-start.44) | collective-permute-done | bytes 1048608 | tf_op jit(solution)/shard_map/ppermute | solution.py:155
  413.8 5.9 %finish_blocks.3.refs_0_ = f32[2048,512]{1,0:T(8,128)} custom-call(s32[3]{0:T(128)} %pad_add_fusion.refs_0_, bf16[2,512,512]{2,1,0:T(8,128)(2,1)} %tie.74.refs_1_, bf16[2,512,512]{2,1,0:T(8,128)(2,1)} %collective-permute-done.43.refs_0_.refs_2_, bf16[2,512,512]{2,1,0:T(8,128)(2,1)} %tie.75.refs_3_, ...), custom_call_target="tpu_custom_call" | custom-call | bytes 167772 | tf_op jit(solution)/shard_map/finish_blocks/pallas_call | solution.py:73
  419.7 7.1 %collective-permute-done.51.refs_0_.refs_2_ = bf16[2,512,512]{2,1,0:T(8,128)(2,1)} collective-permute-done((bf16[2,512,512]{2,1,0:T(8,128)(2,1)}, bf16[2,512,512]{2,1,0:T(8,128)(2,1)}, u32[]{:S(2)}, u32[]{:S(2)}) %collective-permute-start.51) | collective-permute-done | bytes 1048608 | tf_op jit(solution)/shard_map/ppermute | solution.py:155
  427.7 5.7 %collective-permute-done.47.refs_0_.refs_3_.refs_9_.refs_15_ = bf16[528,512]{1,0:T(8,128)(2,1)} collective-permute-done((bf16[528,512]{1,0:T(8,128)(2,1)}, bf16[528,512]{1,0:T(8,128)(2,1)}, u32[]{:S(2)}, u32[]{:S(2)}) %collective-permute-start.47) | collective-permute-done | bytes 540704 | tf_op jit(solution)/shard_map/ppermute | solution.py:1226
  452.5 5.6 %collective-permute-done.53.refs_3_ = bf16[2,512,512]{2,1,0:T(8,128)(2,1)} collective-permute-done((bf16[2,512,512]{2,1,0:T(8,128)(2,1)}, bf16[2,512,512]{2,1,0:T(8,128)(2,1)}, u32[]{:S(2)}, u32[]{:S(2)}) %collective-permute-start.53) | collective-permute-done | bytes 1048608 | tf_op jit(solution)/shard_map/ppermute | solution.py:1226
  (280 shorter events, 179.0 us)
Async XLA Ops:
  7.0 28.9 %collective-permute-start = (bf16[2,512,512]{2,1,0:T(8,128)(2,1)}, bf16[2,512,512]{2,1,0:T(8,128)(2,1)}, u32[]{:S(2)}, u32[]{:S(2)}) collective-permute-start(bf16[2,512,512]{2,1,0:T(8,128)(2,1)} %refs_19_.1), channel_id=1, source_target_pairs={{0,1},{1,2},{2,3},{3,0},{4,5},{5,6},{6,7},{7,4},{8,9},{9,10},{10,1... | collective-permute-start | bytes 3145736 | tf_op jit(solution)/shard_map/ppermute | solution.py:1226
  36.5 27.5 %collective-permute-start.10 = (bf16[512,1536]{1,0:T(8,128)(2,1)}, bf16[512,1536]{1,0:T(8,128)(2,1)}, u32[]{:S(2)}, u32[]{:S(2)}) collective-permute-start(bf16[512,1536]{1,0:T(8,128)(2,1)} %tie.45.refs_11_), channel_id=1, source_target_pairs={{0,8},{8,0},{16,24},{24,16},{1,9},{9,1},{17,25},{25,17},{2,10},{10... | collective-permute-start | bytes 4718600 | tf_op jit(solution)/shard_map/ppermute | solution.py:155
  36.5 25.9 %collective-permute-start.9 = (bf16[2,512,512]{2,1,0:T(8,128)(2,1)}, bf16[2,512,512]{2,1,0:T(8,128)(2,1)}, u32[]{:S(2)}, u32[]{:S(2)}) collective-permute-start(bf16[2,512,512]{2,1,0:T(8,128)(2,1)} %refs_19_.1), channel_id=1, source_target_pairs={{0,3},{1,0},{2,1},{3,2},{4,7},{5,4},{6,5},{7,6},{8,11},{9,8},{10,9... | collective-permute-start | bytes 3145736 | tf_op jit(solution)/shard_map/ppermute | solution.py:1226
  64.1 31.5 %collective-permute-start.15 = (bf16[2560,256]{1,0:T(8,128)(2,1)}, bf16[2560,256]{1,0:T(8,128)(2,1)}, u32[]{:S(2)}, u32[]{:S(2)}) collective-permute-start(bf16[2560,256]{1,0:T(8,128)(2,1)} %tie.50), channel_id=1, source_target_pairs={{0,16},{8,24},{16,0},{24,8},{1,17},{9,25},{17,1},{25,9},{2,18},{10... | collective-permute-start | bytes 3932168 | tf_op jit(solution)/shard_map/ppermute | solution.py:155
  67.1 28.1 %collective-permute-start.11 = (bf16[2,512,512]{2,1,0:T(8,128)(2,1)}, bf16[2,512,512]{2,1,0:T(8,128)(2,1)}, u32[]{:S(2)}, u32[]{:S(2)}) collective-permute-start(bf16[2,512,512]{2,1,0:T(8,128)(2,1)} %tie.46.refs_2_), channel_id=1, source_target_pairs={{0,1},{1,2},{2,3},{3,0},{4,5},{5,6},{6,7},{7,4},{8,9},{9,10},{10,1... | collective-permute-start | bytes 3145736 | tf_op jit(solution)/shard_map/ppermute | solution.py:1226
  67.5 54.2 %collective-permute-start.16 = (bf16[512,2048]{1,0:T(8,128)(2,1)}, bf16[512,2048]{1,0:T(8,128)(2,1)}, u32[]{:S(2)}, u32[]{:S(2)}) collective-permute-start(bf16[512,2048]{1,0:T(8,128)(2,1)} %refs_17_.3), channel_id=1, source_target_pairs={{0,8},{8,0},{16,24},{24,16},{1,9},{9,1},{17,25},{25,17},{2,10},{10... | collective-permute-start | bytes 6291464 | tf_op jit(solution)/shard_map/ppermute | solution.py:155
  75.1 46.6 %collective-permute-start.19 = (bf16[2,512,512]{2,1,0:T(8,128)(2,1)}, bf16[2,512,512]{2,1,0:T(8,128)(2,1)}, u32[]{:S(2)}, u32[]{:S(2)}) collective-permute-start(bf16[2,512,512]{2,1,0:T(8,128)(2,1)} %refs_20_.1), channel_id=1, source_target_pairs={{0,1},{1,2},{2,3},{3,0},{4,5},{5,6},{6,7},{7,4},{8,9},{9,10},{10,1... | collective-permute-start | bytes 3145736 | tf_op jit(solution)/shard_map/ppermute | solution.py:1226
  95.6 30.7 %collective-permute-start.20 = (bf16[2560,256]{1,0:T(8,128)(2,1)}, bf16[2560,256]{1,0:T(8,128)(2,1)}, u32[]{:S(2)}, u32[]{:S(2)}) collective-permute-start(bf16[2560,256]{1,0:T(8,128)(2,1)} %tie.53.refs_0_), channel_id=1, source_target_pairs={{0,4},{4,0},{1,5},{5,1},{2,6},{6,2},{3,7},{7,3},{8,12},{12,8},{9,1... | collective-permute-start | bytes 3932168 | tf_op jit(solution)/shard_map/ppermute | solution.py:155
  126.9 44.2 %collective-permute-start.25 = (bf16[2,512,512]{2,1,0:T(8,128)(2,1)}, bf16[2,512,512]{2,1,0:T(8,128)(2,1)}, u32[]{:S(2)}, u32[]{:S(2)}) collective-permute-start(bf16[2,512,512]{2,1,0:T(8,128)(2,1)} %refs_20_.1), channel_id=1, source_target_pairs={{0,3},{1,0},{2,1},{3,2},{4,7},{5,4},{6,5},{7,6},{8,11},{9,8},{10,9... | collective-permute-start | bytes 3145736 | tf_op jit(solution)/shard_map/ppermute | solution.py:1226
  129.0 53.2 %collective-permute-start.26 = (bf16[2,512,512]{2,1,0:T(8,128)(2,1)}, bf16[2,512,512]{2,1,0:T(8,128)(2,1)}, u32[]{:S(2)}, u32[]{:S(2)}) collective-permute-start(bf16[2,512,512]{2,1,0:T(8,128)(2,1)} %tie.58.refs_3_.refs_2_), channel_id=1, source_target_pairs={{0,1},{1,2},{2,3},{3,0},{4,5},{5,6},{6,7},{7,4},{8,9},{9,10},{10,1... | collective-permute-start | bytes 3145736 | tf_op jit(solution)/shard_map/ppermute | solution.py:1226
  149.5 53.3 %collective-permute-start.24 = (bf16[2,512,512]{2,1,0:T(8,128)(2,1)}, bf16[2,512,512]{2,1,0:T(8,128)(2,1)}, u32[]{:S(2)}, u32[]{:S(2)}) collective-permute-start(bf16[2,512,512]{2,1,0:T(8,128)(2,1)} %tie.57.refs_3_), channel_id=1, source_target_pairs={{0,4},{1,5},{2,6},{3,7},{8,12},{9,13},{10,14},{11,15},{16,20},{17,... | collective-permute-start | bytes 3145736 | tf_op jit(solution)/shard_map/ppermute | solution.py:1389
  153.9 63.1 %collective-permute-start.27 = (bf16[2,512,512]{2,1,0:T(8,128)(2,1)}, bf16[2,512,512]{2,1,0:T(8,128)(2,1)}, u32[]{:S(2)}, u32[]{:S(2)}) collective-permute-start(bf16[2,512,512]{2,1,0:T(8,128)(2,1)} %tie.59.refs_3_), channel_id=1, source_target_pairs={{0,4},{1,5},{2,6},{3,7},{8,12},{9,13},{10,14},{11,15},{16,20},{17,... | collective-permute-start | bytes 3145736 | tf_op jit(solution)/shard_map/ppermute | solution.py:1389
  230.0 29.3 %collective-permute-start.29 = (bf16[2,512,512]{2,1,0:T(8,128)(2,1)}, bf16[2,512,512]{2,1,0:T(8,128)(2,1)}, u32[]{:S(2)}, u32[]{:S(2)}) collective-permute-start(bf16[2,512,512]{2,1,0:T(8,128)(2,1)} %tie.61), channel_id=1, source_target_pairs={{4,0},{5,1},{6,2},{7,3},{12,8},{13,9},{14,10},{15,11},{20,16},{21,... | collective-permute-start | bytes 3145736 | tf_op jit(solution)/shard_map/ppermute | solution.py:1409
  235.4 25.9 %collective-permute-start.30 = (bf16[2,512,512]{2,1,0:T(8,128)(2,1)}, bf16[2,512,512]{2,1,0:T(8,128)(2,1)}, u32[]{:S(2)}, u32[]{:S(2)}) collective-permute-start(bf16[2,512,512]{2,1,0:T(8,128)(2,1)} %get-tuple-element.89.refs_0_), channel_id=1, source_target_pairs={{0,16},{8,24},{16,0},{24,8},{1,17},{9,25},{17,1},{25,9},{2,18},{10... | collective-permute-start | bytes 3145736 | tf_op jit(solution)/shard_map/ppermute | solution.py:155
  261.3 31.3 %collective-permute-start.33 = (bf16[2,512,512]{2,1,0:T(8,128)(2,1)}, bf16[2,512,512]{2,1,0:T(8,128)(2,1)}, u32[]{:S(2)}, u32[]{:S(2)}) collective-permute-start(bf16[2,512,512]{2,1,0:T(8,128)(2,1)} %tie.64), channel_id=1, source_target_pairs={{4,0},{5,1},{6,2},{7,3},{12,8},{13,9},{14,10},{15,11},{20,16},{21,... | collective-permute-start | bytes 3145736 | tf_op jit(solution)/shard_map/ppermute | solution.py:1409
  262.6 30.0 %collective-permute-start.31 = (bf16[2,512,512]{2,1,0:T(8,128)(2,1)}, bf16[2,512,512]{2,1,0:T(8,128)(2,1)}, u32[]{:S(2)}, u32[]{:S(2)}) collective-permute-start(bf16[2,512,512]{2,1,0:T(8,128)(2,1)} %tie.62), channel_id=1, source_target_pairs={{0,16},{8,24},{16,0},{24,8},{1,17},{9,25},{17,1},{25,9},{2,18},{10... | collective-permute-start | bytes 3145736 | tf_op jit(solution)/shard_map/ppermute | solution.py:155
  292.6 30.2 %collective-permute-start.40 = (bf16[2,2,512,512]{3,2,1,0:T(8,128)(2,1)}, bf16[2,2,512,512]{3,2,1,0:T(8,128)(2,1)}, u32[]{:S(2)}, u32[]{:S(2)}) collective-permute-start(bf16[2,2,512,512]{3,2,1,0:T(8,128)(2,1)} %tie.71), channel_id=1, source_target_pairs={{0,8},{8,0},{16,24},{24,16},{1,9},{9,1},{17,25},{25,17},{2,10},{10... | collective-permute-start | bytes 6291464 | tf_op jit(solution)/shard_map/ppermute | solution.py:155
  292.6 26.9 %collective-permute-start.35 = (bf16[2,512,512]{2,1,0:T(8,128)(2,1)}, bf16[2,512,512]{2,1,0:T(8,128)(2,1)}, u32[]{:S(2)}, u32[]{:S(2)}) collective-permute-start(bf16[2,512,512]{2,1,0:T(8,128)(2,1)} %tie.66.refs_1_), channel_id=1, source_target_pairs={{0,4},{4,0},{1,5},{5,1},{2,6},{6,2},{3,7},{7,3},{8,12},{12,8},{9,1... | collective-permute-start | bytes 3145736 | tf_op jit(solution)/shard_map/ppermute | solution.py:155
  295.3 27.5 %collective-permute-start.34 = (bf16[2,512,512]{2,1,0:T(8,128)(2,1)}, bf16[2,512,512]{2,1,0:T(8,128)(2,1)}, u32[]{:S(2)}, u32[]{:S(2)}) collective-permute-start(bf16[2,512,512]{2,1,0:T(8,128)(2,1)} %tie.65), channel_id=1, source_target_pairs={{0,1},{1,2},{2,3},{3,0},{4,5},{5,6},{6,7},{7,4},{8,9},{9,10},{10,1... | collective-permute-start | bytes 3145736 | tf_op jit(solution)/shard_map/ppermute | solution.py:1226
  295.3 27.5 %collective-permute-start.39 = (bf16[2,512,512]{2,1,0:T(8,128)(2,1)}, bf16[2,512,512]{2,1,0:T(8,128)(2,1)}, u32[]{:S(2)}, u32[]{:S(2)}) collective-permute-start(bf16[2,512,512]{2,1,0:T(8,128)(2,1)} %tie.70), channel_id=1, source_target_pairs={{0,16},{8,24},{16,0},{24,8},{1,17},{9,25},{17,1},{25,9},{2,18},{10... | collective-permute-start | bytes 3145736 | tf_op jit(solution)/shard_map/ppermute | solution.py:155
  322.8 27.3 %collective-permute-start.42 = (bf16[2,512,512]{2,1,0:T(8,128)(2,1)}, bf16[2,512,512]{2,1,0:T(8,128)(2,1)}, u32[]{:S(2)}, u32[]{:S(2)}) collective-permute-start(bf16[2,512,512]{2,1,0:T(8,128)(2,1)} %tie.73), channel_id=1, source_target_pairs={{0,16},{8,24},{16,0},{24,8},{1,17},{9,25},{17,1},{25,9},{2,18},{10... | collective-permute-start | bytes 3145736 | tf_op jit(solution)/shard_map/ppermute | solution.py:155
  350.1 32.7 %collective-permute-start.46 = (bf16[2,2,512,512]{3,2,1,0:T(8,128)(2,1)}, bf16[2,2,512,512]{3,2,1,0:T(8,128)(2,1)}, u32[]{:S(2)}, u32[]{:S(2)}) collective-permute-start(bf16[2,2,512,512]{3,2,1,0:T(8,128)(2,1)} %tie.77), channel_id=1, source_target_pairs={{0,8},{8,0},{16,24},{24,16},{1,9},{9,1},{17,25},{25,17},{2,10},{10... | collective-permute-start | bytes 6291464 | tf_op jit(solution)/shard_map/ppermute | solution.py:155
  350.1 27.5 %collective-permute-start.43 = (bf16[2,512,512]{2,1,0:T(8,128)(2,1)}, bf16[2,512,512]{2,1,0:T(8,128)(2,1)}, u32[]{:S(2)}, u32[]{:S(2)}) collective-permute-start(bf16[2,512,512]{2,1,0:T(8,128)(2,1)} %tie.74.refs_1_), channel_id=1, source_target_pairs={{0,4},{4,0},{1,5},{5,1},{2,6},{6,2},{3,7},{7,3},{8,12},{12,8},{9,1... | collective-permute-start | bytes 3145736 | tf_op jit(solution)/shard_map/ppermute | solution.py:155
  351.4 27.3 %collective-permute-start.41 = (bf16[2,512,512]{2,1,0:T(8,128)(2,1)}, bf16[2,512,512]{2,1,0:T(8,128)(2,1)}, u32[]{:S(2)}, u32[]{:S(2)}) collective-permute-start(bf16[2,512,512]{2,1,0:T(8,128)(2,1)} %tie.72), channel_id=1, source_target_pairs={{0,3},{1,0},{2,1},{3,2},{4,7},{5,4},{6,5},{7,6},{8,11},{9,8},{10,9... | collective-permute-start | bytes 3145736 | tf_op jit(solution)/shard_map/ppermute | solution.py:1226
  (45 other events, 692.5 us)

commit v8 on v7

--- a/solution.py
+++ b/solution.py
@@ -333,14 +333,18 @@
     j = pl.program_id(0)
     stream_pieces(layout, info, w, held, sems, 0, held.shape[1] // CH)
     root = math.sqrt(2.0 / math.pi)
+    part = 512
     for s in range(normed.shape[0]):
-        u = dot_nn(normed[s], held[:, columns(j)]) + bias[...].astype(f32)
-        square = u * u
-        t = jnp.tanh(u * (root + (root * 0.044715) * square))
-        half = 0.5 + 0.5 * t
-        hidden[s] = (u * half).astype(bf16)
-        slope = root + (3 * 0.044715 * root) * square
-        grad[s] = (half + (0.5 * u) * (1.0 - t * t) * slope).astype(bf16)
+        for row in range(0, normed.shape[1], part):
+            window = slice(row, row + part)
+            u = dot_nn(normed[s, window], held[:, columns(j)]) + bias[...].astype(f32)
+            square = u * u
+            t = jnp.tanh(u * (root + (root * 0.044715) * square))
+            half = 0.5 + 0.5 * t
+            value = u * half
+            hidden[s, window] = value.astype(bf16)
+            slope = 2 * root + (6 * 0.044715 * root) * square
+            grad[s, window] = (half + value * (1.0 - half) * slope).astype(bf16)
 
 
 def mlp_up(layout, info, normed, w, bias, deps=()):
@@ -1386,7 +1390,7 @@
     def send_keys(s):
         kv[s] = clock.go(kv[s])
         if two:
-            kvp[s] = lax.ppermute(kv[s], "ctx", [(0, 1)])[None]
+            kvp[s] = swap(kv[s], "ctx", 1, 2)[None]
         else:
             kvp[s] = lax.all_gather(kv[s], "ctx", axis=0, tiled=False)
 
@@ -1406,7 +1410,7 @@
 
     def returned(sent):
         if two:
-            return lax.ppermute(clock.go(sent[0]), "ctx", [(1, 0)])
+            return swap(clock.go(sent[0]), "ctx", 1, 2)
         return lax.psum_scatter(clock.go(sent), "ctx", scatter_dimension=0, tiled=False)
 
     def back_in_step(s):
@@ -1546,13 +1550,13 @@
     back_1.onward(both_1)
     clock.sync(pair.moved[0])
     (here,) = added([pair.here_sum(0)])
-    clock.sync(here)
+    clock.sync(here, back_0.near)
     down_wg = finish_blocks(info, [down.sums(0), down.sums(1)], 0, deps=clock.marks)
     clock.sync(down_wg)
     clock.sync(head.there[0])
 
     pair.over_y(0, clock.go(here))
-    clock.sync(back_0.near, back_1.near)
+    clock.sync(back_1.near)
     out.onward(clock.go(out_both))
     in_grad, last = finish_in(
         info,

time: 472 us -> 464 us (0.983)
  waiting for transfers between devices: 106 us -> 98 us
    ppermute x4 -> x0, starting transfers between devices: 9.27 us -> none  [the longest x2 6.7 us: send_keys(): kvp[s] = lax.ppermute(kv[s], 'ctx', [(0, 1)])[None]]
    ppermute x36 -> x40, starting transfers between devices: 29.4 us -> 38.3 us  [swap(): return lax.ppermute(array, axis, [(i, i ^ bit) for i in range(size)])]
    ppermute x4 -> x0, waiting for transfers between devices: 7.93 us -> none  [the longest x2 7.93 us: returned(): return lax.ppermute(clock.go(sent[0]), 'ctx', [(1, 0)])]
    ppermute x36 -> x40, waiting for transfers between devices: 48.9 us -> 47.1 us  [swap(): return lax.ppermute(array, axis, [(i, i ^ bit) for i in range(size)])]
  transfers between devices with their start and end apart: 58 -> 58, of which waited for: 24 -> 22; matrix products, arithmetic and copies ran while one was open for 5% -> 5% of each run, Pallas kernels for 56% -> 57%
where the time goes in v8:
time: 464 us; the launch traced here: 455 us
  Pallas kernels  264 us (57%)
  waiting for transfers between devices  98 us (21%)
  starting transfers between devices  59.6 us (13%)
  local copies, waits for them, and re-layouts  19.9 us (4%)
  other arithmetic  12.5 us (3%)
    pallas_call x29, Pallas kernels, call(): pl.pallas_call(without_deps, grid_spec=pltpu.PrefetchScalarGridSpec(num_s...  263 us
    ppermute x18, waiting for transfers between devices, ring(): lax.ppermute(array, 'tp', [(i, (i + step) % N_TP) for i in range(N_TP)])  50.9 us
    ppermute x40, waiting for transfers between devices, swap(): return lax.ppermute(array, axis, [(i, i ^ bit) for i in range(size)])  47.1 us
    ppermute x40, starting transfers between devices, swap(): return lax.ppermute(array, axis, [(i, i ^ bit) for i in range(size)])  38.3 us
    ppermute x18, starting transfers between devices, ring(): lax.ppermute(array, 'tp', [(i, (i + step) % N_TP) for i in range(N_TP)])  21.2 us
    unnamed x41, local copies, waits for them, and re-layouts  10.2 us
  transfers between devices with their start and end apart: 58, of which 22 were waited for; matrix products, arithmetic and copies ran while one was open for 5% of the time, Pallas kernels for 57%

profile of v8, /device:TPU:0, one launch (start us, length us, event | category | flops | bytes accessed | tf_op | source)
XLA Modules:
  0.0 455.2 jit_solution(17626737292606474076)
XLA Ops:
  25.0 8.0 %collective-permute-done.4.refs_2_ = bf16[2,512]{1,0:T(2,128)(2,1)S(1)} collective-permute-done((bf16[2,512]{1,0:T(2,128)(2,1)S(1)}, bf16[2,512]{1,0:T(2,128)(2,1)S(1)}, u32[]{:S(2)}, u32[]{:S(2)}) %collective-permute-start.4) | collective-permute-done | bytes 2080 | tf_op jit(solution)/shard_map/ppermute | solution.py:1230
  46.8 15.6 %collective-permute-done.9.refs_2_.refs_3_ = bf16[2,512,512]{2,1,0:T(8,128)(2,1)} collective-permute-done((bf16[2,512,512]{2,1,0:T(8,128)(2,1)}, bf16[2,512,512]{2,1,0:T(8,128)(2,1)}, u32[]{:S(2)}, u32[]{:S(2)}) %collective-permute-start.9) | collective-permute-done | bytes 1048608 | tf_op jit(solution)/shard_map/ppermute | solution.py:1230
  75.6 15.5 %collective-permute-done.14.refs_3_.refs_0_ = bf16[256,2048]{1,0:T(8,128)(2,1)} collective-permute-done((bf16[256,2048]{1,0:T(8,128)(2,1)}, bf16[256,2048]{1,0:T(8,128)(2,1)}, u32[]{:S(2)}, u32[]{:S(2)}) %collective-permute-start.14) | collective-permute-done | bytes 1048608 | tf_op jit(solution)/shard_map/ppermute | solution.py:155
  99.2 22.5 %norm_qkv.1 = (bf16[2,512,2048]{2,1,0:T(8,128)(2,1)}, f32[2,8,512]{2,1,0:T(8,128)}, bf16[2,512,512]{2,1,0:T(8,128)(2,1)}, bf16[2,512,512]{2,1,0:T(8,128)(2,1)}, bf16[2,512,512]{2,1,0:T(8,128)(2,1)}) custom-call(s32[3]{0:T(128)} %pad_add_fusion.refs_0_, bf16[2,512,512]{2,1,0:T(8,128)(2,1)} %refs_19_.1, bf16[2,512,512]{2,1,0:T(8,128)(2,1)} %tie.46.refs_2_, ...), custom_call_target="tpu_custom_call" | custom-call | flops 128849016 | bytes 388853 | tf_op jit(solution)/shard_map/norm_qkv/pallas_call | solution.py:73
  129.9 18.9 %mlp_up.1 = (bf16[2,512,2048]{2,1,0:T(8,128)(2,1)}, bf16[2,512,2048]{2,1,0:T(8,128)(2,1)}) custom-call(s32[3]{0:T(128)} %pad_add_fusion.refs_0_, bf16[2,512,2048]{2,1,0:T(8,128)(2,1)} %get-tuple-element.78.refs_0_.refs_1_, bf16[1,2048]{1,0:T(2,128)(2,1)} %bitcast.80, bf16[512,2048]{1,0:T(8,128)(2,1)} %refs_17_.3, ...), custom_call_target="tpu_custom_call" | custom-call | flops 171798688 | bytes 419512 | tf_op jit(solution)/shard_map/mlp_up/pallas_call | solution.py:73
  151.0 15.0 %out_hidden.1.refs_0_.refs_3_ = bf16[4,2,512,512]{3,2,1,0:T(8,128)(2,1)} custom-call(s32[3]{0:T(128)} %pad_add_fusion.refs_0_, bf16[2,512,2048]{2,1,0:T(8,128)(2,1)} %get-tuple-element.79.refs_0_.refs_1_, bf16[2560,512]{1,0:T(8,128)(2,1)} %tie.54.refs_2_.refs_6_.refs_4_, bf16[2560,512]{1,0:T(8,128)(2,1)} %collective-permute-done.21.refs_1_.refs_3_.refs_7_.refs_5_, ...), custom_call_target="tpu_custom_call" | custom-call | flops 171798688 | bytes 377487 | tf_op jit(solution)/shard_map/out_hidden/pallas_call | solution.py:73
  166.0 11.1 %grad_down.2 = (bf16[2,4,512,512]{3,2,1,0:T(8,128)(2,1)}, bf16[2,4,512,512]{3,2,1,0:T(8,128)(2,1)}) custom-call(s32[3]{0:T(128)} %pad_add_fusion.refs_0_, bf16[2,512,2048]{2,1,0:T(8,128)(2,1)} %get-tuple-element.79.refs_0_.refs_1_, bf16[2,512,512]{2,1,0:T(8,128)(2,1)} %refs_20_.1, bf16[2,512,512]{2,1,0:T(8,128)(2,1)} %tie.58.refs_3_.refs_2_, ...), custom_call_target="tpu_custom_call" | custom-call | flops 128849016 | bytes 314572 | tf_op jit(solution)/shard_map/grad_down/pallas_call | solution.py:73
  177.1 20.9 %back_out.1 = (bf16[2,512,2048]{2,1,0:T(8,128)(2,1)}, f32[1,512]{1,0:T(1,128)}, bf16[2,512,512]{2,1,0:T(8,128)(2,1)}, bf16[2,512,2048]{2,1,0:T(8,128)(2,1)}) custom-call(s32[3]{0:T(128)} %pad_add_fusion.refs_0_, bf16[2,512,512]{2,1,0:T(8,128)(2,1)} %refs_20_.1, bf16[2,512,512]{2,1,0:T(8,128)(2,1)} %tie.58.refs_3_.refs_2_, ...), custom_call_target="tpu_custom_call" | custom-call | flops 214748368 | bytes 566272 | tf_op jit(solution)/shard_map/back_out/pallas_call | solution.py:73
  198.0 14.2 %grad_up.1 = (bf16[2,4,512,512]{3,2,1,0:T(8,128)(2,1)}, bf16[2,4,512,512]{3,2,1,0:T(8,128)(2,1)}, f32[1,2048]{1,0:T(1,128)}) custom-call(s32[3]{0:T(128)} %pad_add_fusion.refs_0_, bf16[2,512,2048]{2,1,0:T(8,128)(2,1)} %get-tuple-element.78.refs_0_.refs_1_, bf16[2,512,2048]{2,1,0:T(8,128)(2,1)} %get-tuple-element.83.refs_2_.refs_8_, ...), custom_call_target="tpu_custom_call" | custom-call | flops 171798688 | bytes 335708 | tf_op jit(solution)/shard_map/grad_up/pallas_call | solution.py:73
  213.0 11.8 %attention.2 = (bf16[512,512]{1,0:T(8,128)(2,1)}, bf16[512,512]{1,0:T(8,128)(2,1)}, bf16[2,512,512]{2,1,0:T(8,128)(2,1)}, bf16[1,2,512,512]{3,2,1,0:T(8,128)(2,1)}) custom-call(s32[3]{0:T(128)} %pad_add_fusion.refs_0_, s32[2,1,512]{2,1,0:T(1,128)} %broadcast_in_dim.64.refs_1_, bf16[2,512,512]{2,1,0:T(8,128)(2,1)} %get-tuple-element.76.refs_2_, ...), custom_call_target="tpu_custom_call" | custom-call | flops 128849016 | bytes 209797 | tf_op jit(solution)/shard_map/attention/pallas_call | solution.py:73
  224.8 8.1 %collective-permute-start.29 = (bf16[2,512,512]{2,1,0:T(8,128)(2,1)}, bf16[2,512,512]{2,1,0:T(8,128)(2,1)}, u32[]{:S(2)}, u32[]{:S(2)}) collective-permute-start(bf16[2,512,512]{2,1,0:T(8,128)(2,1)} %tie.61), channel_id=1, source_target_pairs={{0,4},{4,0},{1,5},{5,1},{2,6},{6,2},{3,7},{7,3},{8,12},{12,8},{9,1... | collective-permute-start | bytes 3145736 | tf_op jit(solution)/shard_map/ppermute | solution.py:155
  238.2 6.8 %grad_down.3 = (bf16[2,4,512,512]{3,2,1,0:T(8,128)(2,1)}, bf16[2,4,512,512]{3,2,1,0:T(8,128)(2,1)}) custom-call(s32[3]{0:T(128)} %pad_add_fusion.refs_0_, bf16[2,512,2048]{2,1,0:T(8,128)(2,1)} %get-tuple-element.79.refs_0_.refs_1_, ...), custom_call_target="tpu_custom_call", output_to_operand_aliasing={{0}: (3, {}), {1}: (4, {})} | custom-call | flops 42949672 | bytes 440401 | tf_op jit(solution)/shard_map/grad_down/pallas_call | solution.py:73
  245.0 12.1 %attention.3 = (bf16[512,512]{1,0:T(8,128)(2,1)}, bf16[512,512]{1,0:T(8,128)(2,1)}, bf16[2,512,512]{2,1,0:T(8,128)(2,1)}, bf16[1,2,512,512]{3,2,1,0:T(8,128)(2,1)}) custom-call(s32[3]{0:T(128)} %pad_add_fusion.refs_0_, s32[2,1,512]{2,1,0:T(1,128)} %broadcast_in_dim.64.refs_1_, bf16[2,512,512]{2,1,0:T(8,128)(2,1)} %get-tuple-element.76.refs_2_, ...), custom_call_target="tpu_custom_call" | custom-call | flops 128849016 | bytes 209797 | tf_op jit(solution)/shard_map/attention/pallas_call | solution.py:73
  257.1 5.4 %collective-permute-done.30.refs_2_.refs_7_ = bf16[2,512,512]{2,1,0:T(8,128)(2,1)} collective-permute-done((bf16[2,512,512]{2,1,0:T(8,128)(2,1)}, bf16[2,512,512]{2,1,0:T(8,128)(2,1)}, u32[]{:S(2)}, u32[]{:S(2)}) %collective-permute-start.30) | collective-permute-done | bytes 1048608 | tf_op jit(solution)/shard_map/ppermute | solution.py:155
  264.7 8.3 %out_heads.1 = (bf16[2,512,512]{2,1,0:T(8,128)(2,1)}, bf16[2,512,512]{2,1,0:T(8,128)(2,1)}, bf16[2,512,512]{2,1,0:T(8,128)(2,1)}, bf16[2,512,512]{2,1,0:T(8,128)(2,1)}) custom-call(s32[3]{0:T(128)} %pad_add_fusion.refs_0_, bf16[512,512]{1,0:T(8,128)(2,1)} %get-tuple-element.86.refs_0_.refs_1_.refs_3_, ...), custom_call_target="tpu_custom_call" | custom-call | flops 42949672 | bytes 398458 | tf_op jit(solution)/shard_map/out_heads/pallas_call | solution.py:73
  273.0 10.8 %grad_out_query.1 = (bf16[2,2,512,512]{3,2,1,0:T(8,128)(2,1)}, bf16[2,2,512,512]{3,2,1,0:T(8,128)(2,1)}, f32[1,512]{1,0:T(1,128)}) custom-call(s32[3]{0:T(128)} %pad_add_fusion.refs_0_, bf16[2,512,2048]{2,1,0:T(8,128)(2,1)} %get-tuple-element.78.refs_0_.refs_1_, bf16[2,512,2048]{2,1,0:T(8,128)(2,1)} %get-tuple-element.100.refs_2_, ...), custom_call_target="tpu_custom_call" | custom-call | flops 85899344 | bytes 293642 | tf_op jit(solution)/shard_map/grad_out_query/pallas_call | solution.py:73
  295.2 19.1 %back_in.2 = (bf16[528,512]{1,0:T(8,128)(2,1)}, bf16[528,512]{1,0:T(8,128)(2,1)}, bf16[528,512]{1,0:T(8,128)(2,1)}, bf16[528,512]{1,0:T(8,128)(2,1)}) custom-call(s32[3]{0:T(128)} %pad_add_fusion.refs_0_, bf16[2,512,512]{2,1,0:T(8,128)(2,1)} %refs_19_.1, bf16[2,512,512]{2,1,0:T(8,128)(2,1)} %tie.46.refs_2_, ...), custom_call_target="tpu_custom_call" | custom-call | flops 150323856 | bytes 557793 | tf_op jit(solution)/shard_map/back_in/pallas_call | solution.py:73
  321.2 5.6 %combine.12 = (bf16[2,512,512]{2,1,0:T(8,128)(2,1)}, bf16[2,512,512]{2,1,0:T(8,128)(2,1)}, bf16[2,512,512]{2,1,0:T(8,128)(2,1)}) custom-call(s32[3]{0:T(128)} %pad_add_fusion.refs_0_, bf16[8,512,512]{2,1,0:T(8,128)(2,1)} %bitcast.68, bf16[8,512,512]{2,1,0:T(8,128)(2,1)} %bitcast.9.refs_2_.refs_4_, ...), custom_call_target="tpu_custom_call" | custom-call | bytes 377487 | tf_op jit(solution)/shard_map/combine/pallas_call | solution.py:73
  326.9 9.9 %grad_key_value.1 = (bf16[2,2,512,512]{3,2,1,0:T(8,128)(2,1)}, bf16[2,2,512,512]{3,2,1,0:T(8,128)(2,1)}, f32[2,1,512]{2,1,0:T(1,128)}) custom-call(s32[3]{0:T(128)} %pad_add_fusion.refs_0_, bf16[2,512,2048]{2,1,0:T(8,128)(2,1)} %get-tuple-element.78.refs_0_.refs_1_, bf16[2,512,512]{2,1,0:T(8,128)(2,1)} %get-tuple-element.96.refs_6_.refs_2_, ...), custom_call_target="tpu_custom_call" | custom-call | flops 85899344 | bytes 251740 | tf_op jit(solution)/shard_map/grad_key_value/pallas_call | solution.py:73
  353.5 19.1 %back_in.3 = (bf16[528,512]{1,0:T(8,128)(2,1)}, bf16[528,512]{1,0:T(8,128)(2,1)}, bf16[528,512]{1,0:T(8,128)(2,1)}, bf16[528,512]{1,0:T(8,128)(2,1)}) custom-call(s32[3]{0:T(128)} %pad_add_fusion.refs_0_, bf16[2,512,512]{2,1,0:T(8,128)(2,1)} %refs_19_.1, bf16[2,512,512]{2,1,0:T(8,128)(2,1)} %tie.46.refs_2_, ...), custom_call_target="tpu_custom_call" | custom-call | flops 150323856 | bytes 557793 | tf_op jit(solution)/shard_map/back_in/pallas_call | solution.py:73
  383.5 5.9 %finish_blocks.2.refs_0_ = f32[512,2048]{1,0:T(8,128)} custom-call(s32[3]{0:T(128)} %pad_add_fusion.refs_0_, bf16[2,512,512]{2,1,0:T(8,128)(2,1)} %tie.66.refs_1_, bf16[2,512,512]{2,1,0:T(8,128)(2,1)} %collective-permute-done.35.refs_0_.refs_2_, bf16[2,512,512]{2,1,0:T(8,128)(2,1)} %tie.69.refs_3_, ...), custom_call_target="tpu_custom_call" | custom-call | bytes 167772 | tf_op jit(solution)/shard_map/finish_blocks/pallas_call | solution.py:73
  389.5 8.2 %collective-permute-done.46.refs_0_.refs_4_ = bf16[2,512,512]{2,1,0:T(8,128)(2,1)} collective-permute-done((bf16[2,512,512]{2,1,0:T(8,128)(2,1)}, bf16[2,512,512]{2,1,0:T(8,128)(2,1)}, u32[]{:S(2)}, u32[]{:S(2)}) %collective-permute-start.46) | collective-permute-done | bytes 1048608 | tf_op jit(solution)/shard_map/ppermute | solution.py:155
  408.2 7.9 %collective-permute-done.52.refs_1_.refs_3_.refs_9_.refs_15_ = bf16[528,512]{1,0:T(8,128)(2,1)} collective-permute-done((bf16[528,512]{1,0:T(8,128)(2,1)}, bf16[528,512]{1,0:T(8,128)(2,1)}, u32[]{:S(2)}, u32[]{:S(2)}) %collective-permute-start.52) | collective-permute-done | bytes 540704 | tf_op jit(solution)/shard_map/ppermute | solution.py:1230
  416.1 5.9 %finish_blocks.3.refs_0_ = f32[2048,512]{1,0:T(8,128)} custom-call(s32[3]{0:T(128)} %pad_add_fusion.refs_0_, bf16[2,512,512]{2,1,0:T(8,128)(2,1)} %tie.74.refs_1_, bf16[2,512,512]{2,1,0:T(8,128)(2,1)} %collective-permute-done.43.refs_0_.refs_2_, bf16[2,512,512]{2,1,0:T(8,128)(2,1)} %tie.77.refs_3_, ...), custom_call_target="tpu_custom_call" | custom-call | bytes 167772 | tf_op jit(solution)/shard_map/finish_blocks/pallas_call | solution.py:73
  (280 shorter events, 166.7 us)
Async XLA Ops:
  7.0 28.9 %collective-permute-start = (bf16[2,512,512]{2,1,0:T(8,128)(2,1)}, bf16[2,512,512]{2,1,0:T(8,128)(2,1)}, u32[]{:S(2)}, u32[]{:S(2)}) collective-permute-start(bf16[2,512,512]{2,1,0:T(8,128)(2,1)} %refs_19_.1), channel_id=1, source_target_pairs={{0,1},{1,2},{2,3},{3,0},{4,5},{5,6},{6,7},{7,4},{8,9},{9,10},{10,1... | collective-permute-start | bytes 3145736 | tf_op jit(solution)/shard_map/ppermute | solution.py:1230
  36.5 27.5 %collective-permute-start.10 = (bf16[512,1536]{1,0:T(8,128)(2,1)}, bf16[512,1536]{1,0:T(8,128)(2,1)}, u32[]{:S(2)}, u32[]{:S(2)}) collective-permute-start(bf16[512,1536]{1,0:T(8,128)(2,1)} %tie.45.refs_11_), channel_id=1, source_target_pairs={{0,8},{8,0},{16,24},{24,16},{1,9},{9,1},{17,25},{25,17},{2,10},{10... | collective-permute-start | bytes 4718600 | tf_op jit(solution)/shard_map/ppermute | solution.py:155
  36.5 25.9 %collective-permute-start.9 = (bf16[2,512,512]{2,1,0:T(8,128)(2,1)}, bf16[2,512,512]{2,1,0:T(8,128)(2,1)}, u32[]{:S(2)}, u32[]{:S(2)}) collective-permute-start(bf16[2,512,512]{2,1,0:T(8,128)(2,1)} %refs_19_.1), channel_id=1, source_target_pairs={{0,3},{1,0},{2,1},{3,2},{4,7},{5,4},{6,5},{7,6},{8,11},{9,8},{10,9... | collective-permute-start | bytes 3145736 | tf_op jit(solution)/shard_map/ppermute | solution.py:1230
  64.1 31.5 %collective-permute-start.15 = (bf16[2560,256]{1,0:T(8,128)(2,1)}, bf16[2560,256]{1,0:T(8,128)(2,1)}, u32[]{:S(2)}, u32[]{:S(2)}) collective-permute-start(bf16[2560,256]{1,0:T(8,128)(2,1)} %tie.50), channel_id=1, source_target_pairs={{0,16},{8,24},{16,0},{24,8},{1,17},{9,25},{17,1},{25,9},{2,18},{10... | collective-permute-start | bytes 3932168 | tf_op jit(solution)/shard_map/ppermute | solution.py:155
  67.1 28.1 %collective-permute-start.11 = (bf16[2,512,512]{2,1,0:T(8,128)(2,1)}, bf16[2,512,512]{2,1,0:T(8,128)(2,1)}, u32[]{:S(2)}, u32[]{:S(2)}) collective-permute-start(bf16[2,512,512]{2,1,0:T(8,128)(2,1)} %tie.46.refs_2_), channel_id=1, source_target_pairs={{0,1},{1,2},{2,3},{3,0},{4,5},{5,6},{6,7},{7,4},{8,9},{9,10},{10,1... | collective-permute-start | bytes 3145736 | tf_op jit(solution)/shard_map/ppermute | solution.py:1230
  67.5 54.2 %collective-permute-start.16 = (bf16[512,2048]{1,0:T(8,128)(2,1)}, bf16[512,2048]{1,0:T(8,128)(2,1)}, u32[]{:S(2)}, u32[]{:S(2)}) collective-permute-start(bf16[512,2048]{1,0:T(8,128)(2,1)} %refs_17_.3), channel_id=1, source_target_pairs={{0,8},{8,0},{16,24},{24,16},{1,9},{9,1},{17,25},{25,17},{2,10},{10... | collective-permute-start | bytes 6291464 | tf_op jit(solution)/shard_map/ppermute | solution.py:155
  75.1 46.6 %collective-permute-start.19 = (bf16[2,512,512]{2,1,0:T(8,128)(2,1)}, bf16[2,512,512]{2,1,0:T(8,128)(2,1)}, u32[]{:S(2)}, u32[]{:S(2)}) collective-permute-start(bf16[2,512,512]{2,1,0:T(8,128)(2,1)} %refs_20_.1), channel_id=1, source_target_pairs={{0,1},{1,2},{2,3},{3,0},{4,5},{5,6},{6,7},{7,4},{8,9},{9,10},{10,1... | collective-permute-start | bytes 3145736 | tf_op jit(solution)/shard_map/ppermute | solution.py:1230
  95.6 30.7 %collective-permute-start.20 = (bf16[2560,256]{1,0:T(8,128)(2,1)}, bf16[2560,256]{1,0:T(8,128)(2,1)}, u32[]{:S(2)}, u32[]{:S(2)}) collective-permute-start(bf16[2560,256]{1,0:T(8,128)(2,1)} %tie.53.refs_0_), channel_id=1, source_target_pairs={{0,4},{4,0},{1,5},{5,1},{2,6},{6,2},{3,7},{7,3},{8,12},{12,8},{9,1... | collective-permute-start | bytes 3932168 | tf_op jit(solution)/shard_map/ppermute | solution.py:155
  126.9 39.1 %collective-permute-start.25 = (bf16[2,512,512]{2,1,0:T(8,128)(2,1)}, bf16[2,512,512]{2,1,0:T(8,128)(2,1)}, u32[]{:S(2)}, u32[]{:S(2)}) collective-permute-start(bf16[2,512,512]{2,1,0:T(8,128)(2,1)} %refs_20_.1), channel_id=1, source_target_pairs={{0,3},{1,0},{2,1},{3,2},{4,7},{5,4},{6,5},{7,6},{8,11},{9,8},{10,9... | collective-permute-start | bytes 3145736 | tf_op jit(solution)/shard_map/ppermute | solution.py:1230
  129.0 48.1 %collective-permute-start.26 = (bf16[2,512,512]{2,1,0:T(8,128)(2,1)}, bf16[2,512,512]{2,1,0:T(8,128)(2,1)}, u32[]{:S(2)}, u32[]{:S(2)}) collective-permute-start(bf16[2,512,512]{2,1,0:T(8,128)(2,1)} %tie.58.refs_3_.refs_2_), channel_id=1, source_target_pairs={{0,1},{1,2},{2,3},{3,0},{4,5},{5,6},{6,7},{7,4},{8,9},{9,10},{10,1... | collective-permute-start | bytes 3145736 | tf_op jit(solution)/shard_map/ppermute | solution.py:1230
  148.9 49.1 %collective-permute-start.24 = (bf16[2,512,512]{2,1,0:T(8,128)(2,1)}, bf16[2,512,512]{2,1,0:T(8,128)(2,1)}, u32[]{:S(2)}, u32[]{:S(2)}) collective-permute-start(bf16[2,512,512]{2,1,0:T(8,128)(2,1)} %tie.57.refs_3_), channel_id=1, source_target_pairs={{0,4},{4,0},{1,5},{5,1},{2,6},{6,2},{3,7},{7,3},{8,12},{12,8},{9,1... | collective-permute-start | bytes 3145736 | tf_op jit(solution)/shard_map/ppermute | solution.py:155
  150.5 61.8 %collective-permute-start.27 = (bf16[2,512,512]{2,1,0:T(8,128)(2,1)}, bf16[2,512,512]{2,1,0:T(8,128)(2,1)}, u32[]{:S(2)}, u32[]{:S(2)}) collective-permute-start(bf16[2,512,512]{2,1,0:T(8,128)(2,1)} %tie.59.refs_3_), channel_id=1, source_target_pairs={{0,4},{4,0},{1,5},{5,1},{2,6},{6,2},{3,7},{7,3},{8,12},{12,8},{9,1... | collective-permute-start | bytes 3145736 | tf_op jit(solution)/shard_map/ppermute | solution.py:155
  224.8 32.3 %collective-permute-start.29 = (bf16[2,512,512]{2,1,0:T(8,128)(2,1)}, bf16[2,512,512]{2,1,0:T(8,128)(2,1)}, u32[]{:S(2)}, u32[]{:S(2)}) collective-permute-start(bf16[2,512,512]{2,1,0:T(8,128)(2,1)} %tie.61), channel_id=1, source_target_pairs={{0,4},{4,0},{1,5},{5,1},{2,6},{6,2},{3,7},{7,3},{8,12},{12,8},{9,1... | collective-permute-start | bytes 3145736 | tf_op jit(solution)/shard_map/ppermute | solution.py:155
  262.5 26.6 %collective-permute-start.33 = (bf16[2,512,512]{2,1,0:T(8,128)(2,1)}, bf16[2,512,512]{2,1,0:T(8,128)(2,1)}, u32[]{:S(2)}, u32[]{:S(2)}) collective-permute-start(bf16[2,512,512]{2,1,0:T(8,128)(2,1)} %tie.64), channel_id=1, source_target_pairs={{0,4},{4,0},{1,5},{5,1},{2,6},{6,2},{3,7},{7,3},{8,12},{12,8},{9,1... | collective-permute-start | bytes 3145736 | tf_op jit(solution)/shard_map/ppermute | solution.py:155
  289.3 28.8 %collective-permute-start.40 = (bf16[2,2,512,512]{3,2,1,0:T(8,128)(2,1)}, bf16[2,2,512,512]{3,2,1,0:T(8,128)(2,1)}, u32[]{:S(2)}, u32[]{:S(2)}) collective-permute-start(bf16[2,2,512,512]{3,2,1,0:T(8,128)(2,1)} %tie.71), channel_id=1, source_target_pairs={{0,8},{8,0},{16,24},{24,16},{1,9},{9,1},{17,25},{25,17},{2,10},{10... | collective-permute-start | bytes 6291464 | tf_op jit(solution)/shard_map/ppermute | solution.py:155
  289.3 25.9 %collective-permute-start.35 = (bf16[2,512,512]{2,1,0:T(8,128)(2,1)}, bf16[2,512,512]{2,1,0:T(8,128)(2,1)}, u32[]{:S(2)}, u32[]{:S(2)}) collective-permute-start(bf16[2,512,512]{2,1,0:T(8,128)(2,1)} %tie.66.refs_1_), channel_id=1, source_target_pairs={{0,4},{4,0},{1,5},{5,1},{2,6},{6,2},{3,7},{7,3},{8,12},{12,8},{9,1... | collective-permute-start | bytes 3145736 | tf_op jit(solution)/shard_map/ppermute | solution.py:155
  290.6 27.6 %collective-permute-start.34 = (bf16[2,512,512]{2,1,0:T(8,128)(2,1)}, bf16[2,512,512]{2,1,0:T(8,128)(2,1)}, u32[]{:S(2)}, u32[]{:S(2)}) collective-permute-start(bf16[2,512,512]{2,1,0:T(8,128)(2,1)} %tie.65), channel_id=1, source_target_pairs={{0,1},{1,2},{2,3},{3,0},{4,5},{5,6},{6,7},{7,4},{8,9},{9,10},{10,1... | collective-permute-start | bytes 3145736 | tf_op jit(solution)/shard_map/ppermute | solution.py:1230
  290.8 27.3 %collective-permute-start.39 = (bf16[2,512,512]{2,1,0:T(8,128)(2,1)}, bf16[2,512,512]{2,1,0:T(8,128)(2,1)}, u32[]{:S(2)}, u32[]{:S(2)}) collective-permute-start(bf16[2,512,512]{2,1,0:T(8,128)(2,1)} %tie.70), channel_id=1, source_target_pairs={{0,16},{8,24},{16,0},{24,8},{1,17},{9,25},{17,1},{25,9},{2,18},{10... | collective-permute-start | bytes 3145736 | tf_op jit(solution)/shard_map/ppermute | solution.py:155
  318.2 27.3 %collective-permute-start.42 = (bf16[2,512,512]{2,1,0:T(8,128)(2,1)}, bf16[2,512,512]{2,1,0:T(8,128)(2,1)}, u32[]{:S(2)}, u32[]{:S(2)}) collective-permute-start(bf16[2,512,512]{2,1,0:T(8,128)(2,1)} %tie.73), channel_id=1, source_target_pairs={{0,16},{8,24},{16,0},{24,8},{1,17},{9,25},{17,1},{25,9},{2,18},{10... | collective-permute-start | bytes 3145736 | tf_op jit(solution)/shard_map/ppermute | solution.py:155
  345.5 30.4 %collective-permute-start.48 = (bf16[2,2,512,512]{3,2,1,0:T(8,128)(2,1)}, bf16[2,2,512,512]{3,2,1,0:T(8,128)(2,1)}, u32[]{:S(2)}, u32[]{:S(2)}) collective-permute-start(bf16[2,2,512,512]{3,2,1,0:T(8,128)(2,1)} %tie.79), channel_id=1, source_target_pairs={{0,8},{8,0},{16,24},{24,16},{1,9},{9,1},{17,25},{25,17},{2,10},{10... | collective-permute-start | bytes 6291464 | tf_op jit(solution)/shard_map/ppermute | solution.py:155
  345.5 27.1 %collective-permute-start.43 = (bf16[2,512,512]{2,1,0:T(8,128)(2,1)}, bf16[2,512,512]{2,1,0:T(8,128)(2,1)}, u32[]{:S(2)}, u32[]{:S(2)}) collective-permute-start(bf16[2,512,512]{2,1,0:T(8,128)(2,1)} %tie.74.refs_1_), channel_id=1, source_target_pairs={{0,4},{4,0},{1,5},{5,1},{2,6},{6,2},{3,7},{7,3},{8,12},{12,8},{9,1... | collective-permute-start | bytes 3145736 | tf_op jit(solution)/shard_map/ppermute | solution.py:155
  346.6 27.2 %collective-permute-start.41 = (bf16[2,512,512]{2,1,0:T(8,128)(2,1)}, bf16[2,512,512]{2,1,0:T(8,128)(2,1)}, u32[]{:S(2)}, u32[]{:S(2)}) collective-permute-start(bf16[2,512,512]{2,1,0:T(8,128)(2,1)} %tie.72), channel_id=1, source_target_pairs={{0,3},{1,0},{2,1},{3,2},{4,7},{5,4},{6,5},{7,6},{8,11},{9,8},{10,9... | collective-permute-start | bytes 3145736 | tf_op jit(solution)/shard_map/ppermute | solution.py:1230
  348.4 27.5 %collective-permute-start.47 = (bf16[2,512,512]{2,1,0:T(8,128)(2,1)}, bf16[2,512,512]{2,1,0:T(8,128)(2,1)}, u32[]{:S(2)}, u32[]{:S(2)}) collective-permute-start(bf16[2,512,512]{2,1,0:T(8,128)(2,1)} %tie.78), channel_id=1, source_target_pairs={{0,16},{8,24},{16,0},{24,8},{1,17},{9,25},{17,1},{25,9},{2,18},{10... | collective-permute-start | bytes 3145736 | tf_op jit(solution)/shard_map/ppermute | solution.py:155
  379.0 25.7 %collective-permute-start.51 = (bf16[2,512,512]{2,1,0:T(8,128)(2,1)}, bf16[2,512,512]{2,1,0:T(8,128)(2,1)}, u32[]{:S(2)}, u32[]{:S(2)}) collective-permute-start(bf16[2,512,512]{2,1,0:T(8,128)(2,1)} %combine.14.refs_0_), channel_id=1, source_target_pairs={{0,16},{8,24},{16,0},{24,8},{1,17},{9,25},{17,1},{25,9},{2,18},{10... | collective-permute-start | bytes 3145736 | tf_op jit(solution)/shard_map/ppermute | solution.py:155
  (45 other events, 687.7 us)

commit v9 on v8

--- a/solution.py
+++ b/solution.py
@@ -915,21 +915,24 @@
     )
 
 
-def grad_down_body(offsets, info, hidden, *refs):
+def grad_down_body(offsets, group, info, hidden, *refs):
     parts = refs[: len(offsets)]
     kept, given, tiles, sems = refs[-4:]
-    n = pl.program_id(0)
-    for i, (part, offset) in enumerate(zip(parts, offsets)):
-        tiles[n, i] = (dot_tn(hidden[0], part[0]) + dot_tn(hidden[1], part[1])).astype(bf16)
-        r = ((info[0] + offset) % N_TP) ^ info[2]
-        for odd, target in ((0, kept), (1, given)):
-
-            @pl.when(r % 2 == odd)
-            def _(i=i, r=r, target=target):
-                place = target.at[r // 2, n]
-                pltpu.make_async_copy(tiles.at[n, i], place, sems.at[n, i]).start()
-
-    @pl.when(n == tiles.shape[0] - 1)
+    for k in range(group):
+        n = pl.program_id(0) * group + k
+        units = slice(CH * k, CH * (k + 1))
+        for i, (part, offset) in enumerate(zip(parts, offsets)):
+            y = dot_tn(hidden[0, :, units], part[0]) + dot_tn(hidden[1, :, units], part[1])
+            tiles[n, i] = y.astype(bf16)
+            r = ((info[0] + offset) % N_TP) ^ info[2]
+            for odd, target in ((0, kept), (1, given)):
+
+                @pl.when(r % 2 == odd)
+                def _(i=i, n=n, r=r, target=target):
+                    place = target.at[r // 2, n]
+                    pltpu.make_async_copy(tiles.at[n, i], place, sems.at[n, i]).start()
+
+    @pl.when(pl.program_id(0) == tiles.shape[0] // group - 1)
     def _():
         for m in range(tiles.shape[0]):
             for i in range(len(offsets)):
@@ -939,14 +942,15 @@
 def grad_down(info, hidden, parts, offsets, begun=(), deps=()):
     _, rows, units = hidden.shape
     count = units // CH
+    group = 2 if len(parts) == 1 else 1
     at = 1 + len(parts)
     return call(
-        functools.partial(grad_down_body, offsets),
+        functools.partial(grad_down_body, offsets, group),
         "grad_down",
-        count,
+        count // group,
         info,
         (hidden, *parts, *begun),
-        [spec((2, rows, CH), lambda j, *_: (0, 0, j))]
+        [spec((2, rows, group * CH), lambda j, *_: (0, 0, j))]
         + [once(2, rows, CH)] * len(parts)
         + [ANYWHERE] * len(begun),
         (shaped((2, count, CH, CH)),) * 2,
@@ -971,36 +975,45 @@
 
 def grad_out_query_body(info, normed, ct, a0, a1, q0, q1, kept, given, sums):
     j = pl.program_id(0)
-    d = info[2]
+    out = dot_tn(a0[...], ct[0]) + dot_tn(a1[...], ct[1])
+    query = dot_tn(normed[0], q0[...]) + dot_tn(normed[1], q1[...])
+
+    def store(target):
+        target[0, 0] = out.astype(bf16)
+        target[0, 1] = query.astype(bf16)
+
+    @pl.when(j < 2)
+    def _():
+        store(given)
+
+    @pl.when(j >= 2)
+    def _():
+        store(kept)
 
     @pl.when(j == 0)
     def _():
-        lefts = (a0[...], a1[...])
-        for target, which in ((given, GIVEN), (kept, KEPT)):
-            for r, at in which:
-                window = columns(d ^ r)
-                y = sum(dot_tn(a, ct[s, :, window]) for s, a in enumerate(lefts))
-                target[at, 0] = y.astype(bf16)
-
-    @pl.when(j == 1)
-    def _():
-        rights = (q0[...], q1[...])
-        store_by_rows(d, normed, rights, kept, given)
-        sums[...] = sum(jnp.sum(b.astype(f32), axis=0, keepdims=True) for b in rights)
+        sums[...] = sum(jnp.sum(b[...].astype(f32), axis=0, keepdims=True) for b in (q0, q1))
 
 
 def grad_out_query(info, normed, ct, att, dq, deps=()):
     rows = normed.shape[1]
-    message = spec((2, 1, CH, CH), lambda j, *_: (0, j, 0, 0))
+
+    def of_step(j, info):
+        return 0, 0, info[2] ^ jnp.where(j < 2, 2 * j + 1, 2 * j - 4)
+
     return call(
         grad_out_query_body,
         "grad_out_query",
-        2,
+        N_DP,
         info,
         (normed, ct, *att, *dq),
-        [whole(2, rows, D)] * 2 + [whole(rows, CH)] * 4,
+        [spec((2, rows, CH), of_step)] * 2 + [once(rows, CH)] * 4,
         (shaped((2, 2, CH, CH)),) * 2 + (shaped((1, CH), f32),),
-        [message, message, whole(1, CH)],
+        [
+            spec((1, 2, CH, CH), lambda j, *_: (jnp.maximum(j - 2, 0), 0, 0, 0)),
+            spec((1, 2, CH, CH), lambda j, *_: (jnp.minimum(j, 1), 0, 0, 0)),
+            whole(1, CH),
+        ],
         4 * rows * D * 2 * CH,
         deps=deps,
     )

time: 464 us -> 464 us (level)
  transfers between devices with their start and end apart: 58 -> 58, of which waited for: 22 -> 24; matrix products, arithmetic and copies ran while one was open for 5% -> 5% of each run, Pallas kernels for 57% -> 57%
where the time goes in v9:
time: 464 us; the launch traced here: 455 us
  Pallas kernels  262 us (56%)
  waiting for transfers between devices  97.5 us (21%)
  starting transfers between devices  60.9 us (13%)
  local copies, waits for them, and re-layouts  19.9 us (4%)
  other arithmetic  12.5 us (3%)
    pallas_call x29, Pallas kernels, call(): pl.pallas_call(without_deps, grid_spec=pltpu.PrefetchScalarGridSpec(num_s...  262 us
    ppermute x18, waiting for transfers between devices, ring(): lax.ppermute(array, 'tp', [(i, (i + step) % N_TP) for i in range(N_TP)])  50.9 us
    ppermute x40, waiting for transfers between devices, swap(): return lax.ppermute(array, axis, [(i, i ^ bit) for i in range(size)])  46.6 us
    ppermute x40, starting transfers between devices, swap(): return lax.ppermute(array, axis, [(i, i ^ bit) for i in range(size)])  39.9 us
    ppermute x18, starting transfers between devices, ring(): lax.ppermute(array, 'tp', [(i, (i + step) % N_TP) for i in range(N_TP)])  20.9 us
    unnamed x41, local copies, waits for them, and re-layouts  10.2 us
  transfers between devices with their start and end apart: 58, of which 24 were waited for; matrix products, arithmetic and copies ran while one was open for 5% of the time, Pallas kernels for 57%

profile of v9, /device:TPU:0, one launch (start us, length us, event | category | flops | bytes accessed | tf_op | source)
XLA Modules:
  0.0 455.0 jit_solution(7105211312338010834)
XLA Ops:
  25.0 8.0 %collective-permute-done.4.refs_2_ = bf16[2,512]{1,0:T(2,128)(2,1)S(1)} collective-permute-done((bf16[2,512]{1,0:T(2,128)(2,1)S(1)}, bf16[2,512]{1,0:T(2,128)(2,1)S(1)}, u32[]{:S(2)}, u32[]{:S(2)}) %collective-permute-start.4) | collective-permute-done | bytes 2080 | tf_op jit(solution)/shard_map/ppermute | solution.py:1243
  46.8 15.6 %collective-permute-done.9.refs_2_.refs_3_ = bf16[2,512,512]{2,1,0:T(8,128)(2,1)} collective-permute-done((bf16[2,512,512]{2,1,0:T(8,128)(2,1)}, bf16[2,512,512]{2,1,0:T(8,128)(2,1)}, u32[]{:S(2)}, u32[]{:S(2)}) %collective-permute-start.9) | collective-permute-done | bytes 1048608 | tf_op jit(solution)/shard_map/ppermute | solution.py:1243
  75.6 15.5 %collective-permute-done.14.refs_3_.refs_0_ = bf16[256,2048]{1,0:T(8,128)(2,1)} collective-permute-done((bf16[256,2048]{1,0:T(8,128)(2,1)}, bf16[256,2048]{1,0:T(8,128)(2,1)}, u32[]{:S(2)}, u32[]{:S(2)}) %collective-permute-start.14) | collective-permute-done | bytes 1048608 | tf_op jit(solution)/shard_map/ppermute | solution.py:155
  99.2 22.5 %norm_qkv.1 = (bf16[2,512,2048]{2,1,0:T(8,128)(2,1)}, f32[2,8,512]{2,1,0:T(8,128)}, bf16[2,512,512]{2,1,0:T(8,128)(2,1)}, bf16[2,512,512]{2,1,0:T(8,128)(2,1)}, bf16[2,512,512]{2,1,0:T(8,128)(2,1)}) custom-call(s32[3]{0:T(128)} %pad_add_fusion.refs_0_, bf16[2,512,512]{2,1,0:T(8,128)(2,1)} %refs_19_.1, bf16[2,512,512]{2,1,0:T(8,128)(2,1)} %tie.46.refs_2_, ...), custom_call_target="tpu_custom_call" | custom-call | flops 128849016 | bytes 388853 | tf_op jit(solution)/shard_map/norm_qkv/pallas_call | solution.py:73
  129.9 18.9 %mlp_up.1 = (bf16[2,512,2048]{2,1,0:T(8,128)(2,1)}, bf16[2,512,2048]{2,1,0:T(8,128)(2,1)}) custom-call(s32[3]{0:T(128)} %pad_add_fusion.refs_0_, bf16[2,512,2048]{2,1,0:T(8,128)(2,1)} %get-tuple-element.78.refs_0_.refs_1_, bf16[1,2048]{1,0:T(2,128)(2,1)} %bitcast.80, bf16[512,2048]{1,0:T(8,128)(2,1)} %refs_17_.3, ...), custom_call_target="tpu_custom_call" | custom-call | flops 171798688 | bytes 419512 | tf_op jit(solution)/shard_map/mlp_up/pallas_call | solution.py:73
  151.0 15.0 %out_hidden.1.refs_0_.refs_3_ = bf16[4,2,512,512]{3,2,1,0:T(8,128)(2,1)} custom-call(s32[3]{0:T(128)} %pad_add_fusion.refs_0_, bf16[2,512,2048]{2,1,0:T(8,128)(2,1)} %get-tuple-element.79.refs_0_.refs_1_, bf16[2560,512]{1,0:T(8,128)(2,1)} %tie.54.refs_2_.refs_6_.refs_4_, bf16[2560,512]{1,0:T(8,128)(2,1)} %collective-permute-done.21.refs_1_.refs_3_.refs_7_.refs_5_, ...), custom_call_target="tpu_custom_call" | custom-call | flops 171798688 | bytes 377487 | tf_op jit(solution)/shard_map/out_hidden/pallas_call | solution.py:73
  166.0 11.1 %grad_down.2 = (bf16[2,4,512,512]{3,2,1,0:T(8,128)(2,1)}, bf16[2,4,512,512]{3,2,1,0:T(8,128)(2,1)}) custom-call(s32[3]{0:T(128)} %pad_add_fusion.refs_0_, bf16[2,512,2048]{2,1,0:T(8,128)(2,1)} %get-tuple-element.79.refs_0_.refs_1_, bf16[2,512,512]{2,1,0:T(8,128)(2,1)} %refs_20_.1, bf16[2,512,512]{2,1,0:T(8,128)(2,1)} %tie.58.refs_3_.refs_2_, ...), custom_call_target="tpu_custom_call" | custom-call | flops 128849016 | bytes 314572 | tf_op jit(solution)/shard_map/grad_down/pallas_call | solution.py:73
  177.1 20.9 %back_out.1 = (bf16[2,512,2048]{2,1,0:T(8,128)(2,1)}, f32[1,512]{1,0:T(1,128)}, bf16[2,512,512]{2,1,0:T(8,128)(2,1)}, bf16[2,512,2048]{2,1,0:T(8,128)(2,1)}) custom-call(s32[3]{0:T(128)} %pad_add_fusion.refs_0_, bf16[2,512,512]{2,1,0:T(8,128)(2,1)} %refs_20_.1, bf16[2,512,512]{2,1,0:T(8,128)(2,1)} %tie.58.refs_3_.refs_2_, ...), custom_call_target="tpu_custom_call" | custom-call | flops 214748368 | bytes 566272 | tf_op jit(solution)/shard_map/back_out/pallas_call | solution.py:73
  198.0 14.2 %grad_up.1 = (bf16[2,4,512,512]{3,2,1,0:T(8,128)(2,1)}, bf16[2,4,512,512]{3,2,1,0:T(8,128)(2,1)}, f32[1,2048]{1,0:T(1,128)}) custom-call(s32[3]{0:T(128)} %pad_add_fusion.refs_0_, bf16[2,512,2048]{2,1,0:T(8,128)(2,1)} %get-tuple-element.78.refs_0_.refs_1_, bf16[2,512,2048]{2,1,0:T(8,128)(2,1)} %get-tuple-element.83.refs_2_.refs_8_, ...), custom_call_target="tpu_custom_call" | custom-call | flops 171798688 | bytes 335708 | tf_op jit(solution)/shard_map/grad_up/pallas_call | solution.py:73
  213.0 11.8 %attention.2 = (bf16[512,512]{1,0:T(8,128)(2,1)}, bf16[512,512]{1,0:T(8,128)(2,1)}, bf16[2,512,512]{2,1,0:T(8,128)(2,1)}, bf16[1,2,512,512]{3,2,1,0:T(8,128)(2,1)}) custom-call(s32[3]{0:T(128)} %pad_add_fusion.refs_0_, s32[2,1,512]{2,1,0:T(1,128)} %broadcast_in_dim.64.refs_1_, bf16[2,512,512]{2,1,0:T(8,128)(2,1)} %get-tuple-element.76.refs_2_, ...), custom_call_target="tpu_custom_call" | custom-call | flops 128849016 | bytes 209797 | tf_op jit(solution)/shard_map/attention/pallas_call | solution.py:73
  224.8 8.1 %collective-permute-start.29 = (bf16[2,512,512]{2,1,0:T(8,128)(2,1)}, bf16[2,512,512]{2,1,0:T(8,128)(2,1)}, u32[]{:S(2)}, u32[]{:S(2)}) collective-permute-start(bf16[2,512,512]{2,1,0:T(8,128)(2,1)} %tie.61), channel_id=1, source_target_pairs={{0,4},{4,0},{1,5},{5,1},{2,6},{6,2},{3,7},{7,3},{8,12},{12,8},{9,1... | collective-permute-start | bytes 3145736 | tf_op jit(solution)/shard_map/ppermute | solution.py:155
  238.2 5.9 %grad_down.3 = (bf16[2,4,512,512]{3,2,1,0:T(8,128)(2,1)}, bf16[2,4,512,512]{3,2,1,0:T(8,128)(2,1)}) custom-call(s32[3]{0:T(128)} %pad_add_fusion.refs_0_, bf16[2,512,2048]{2,1,0:T(8,128)(2,1)} %get-tuple-element.79.refs_0_.refs_1_, ...), custom_call_target="tpu_custom_call", output_to_operand_aliasing={{0}: (3, {}), {1}: (4, {})} | custom-call | flops 42949672 | bytes 440401 | tf_op jit(solution)/shard_map/grad_down/pallas_call | solution.py:73
  244.2 12.1 %attention.3 = (bf16[512,512]{1,0:T(8,128)(2,1)}, bf16[512,512]{1,0:T(8,128)(2,1)}, bf16[2,512,512]{2,1,0:T(8,128)(2,1)}, bf16[1,2,512,512]{3,2,1,0:T(8,128)(2,1)}) custom-call(s32[3]{0:T(128)} %pad_add_fusion.refs_0_, s32[2,1,512]{2,1,0:T(1,128)} %broadcast_in_dim.64.refs_1_, bf16[2,512,512]{2,1,0:T(8,128)(2,1)} %get-tuple-element.76.refs_2_, ...), custom_call_target="tpu_custom_call" | custom-call | flops 128849016 | bytes 209797 | tf_op jit(solution)/shard_map/attention/pallas_call | solution.py:73
  264.1 8.3 %out_heads.1 = (bf16[2,512,512]{2,1,0:T(8,128)(2,1)}, bf16[2,512,512]{2,1,0:T(8,128)(2,1)}, bf16[2,512,512]{2,1,0:T(8,128)(2,1)}, bf16[2,512,512]{2,1,0:T(8,128)(2,1)}) custom-call(s32[3]{0:T(128)} %pad_add_fusion.refs_0_, bf16[512,512]{1,0:T(8,128)(2,1)} %get-tuple-element.86.refs_0_.refs_1_.refs_3_, ...), custom_call_target="tpu_custom_call" | custom-call | flops 42949672 | bytes 398458 | tf_op jit(solution)/shard_map/out_heads/pallas_call | solution.py:73
  272.4 10.5 %grad_out_query.1 = (bf16[2,2,512,512]{3,2,1,0:T(8,128)(2,1)}, bf16[2,2,512,512]{3,2,1,0:T(8,128)(2,1)}, f32[1,512]{1,0:T(1,128)}) custom-call(s32[3]{0:T(128)} %pad_add_fusion.refs_0_, bf16[2,512,2048]{2,1,0:T(8,128)(2,1)} %get-tuple-element.78.refs_0_.refs_1_, bf16[2,512,2048]{2,1,0:T(8,128)(2,1)} %get-tuple-element.100.refs_2_, ...), custom_call_target="tpu_custom_call" | custom-call | flops 85899344 | bytes 293642 | tf_op jit(solution)/shard_map/grad_out_query/pallas_call | solution.py:73
  295.4 19.1 %back_in.2 = (bf16[528,512]{1,0:T(8,128)(2,1)}, bf16[528,512]{1,0:T(8,128)(2,1)}, bf16[528,512]{1,0:T(8,128)(2,1)}, bf16[528,512]{1,0:T(8,128)(2,1)}) custom-call(s32[3]{0:T(128)} %pad_add_fusion.refs_0_, bf16[2,512,512]{2,1,0:T(8,128)(2,1)} %refs_19_.1, bf16[2,512,512]{2,1,0:T(8,128)(2,1)} %tie.46.refs_2_, ...), custom_call_target="tpu_custom_call" | custom-call | flops 150323856 | bytes 557793 | tf_op jit(solution)/shard_map/back_in/pallas_call | solution.py:73
  321.2 5.6 %combine.12 = (bf16[2,512,512]{2,1,0:T(8,128)(2,1)}, bf16[2,512,512]{2,1,0:T(8,128)(2,1)}, bf16[2,512,512]{2,1,0:T(8,128)(2,1)}) custom-call(s32[3]{0:T(128)} %pad_add_fusion.refs_0_, bf16[8,512,512]{2,1,0:T(8,128)(2,1)} %bitcast.68, bf16[8,512,512]{2,1,0:T(8,128)(2,1)} %bitcast.9.refs_2_.refs_4_, ...), custom_call_target="tpu_custom_call" | custom-call | bytes 377487 | tf_op jit(solution)/shard_map/combine/pallas_call | solution.py:73
  326.9 9.9 %grad_key_value.1 = (bf16[2,2,512,512]{3,2,1,0:T(8,128)(2,1)}, bf16[2,2,512,512]{3,2,1,0:T(8,128)(2,1)}, f32[2,1,512]{2,1,0:T(1,128)}) custom-call(s32[3]{0:T(128)} %pad_add_fusion.refs_0_, bf16[2,512,2048]{2,1,0:T(8,128)(2,1)} %get-tuple-element.78.refs_0_.refs_1_, bf16[2,512,512]{2,1,0:T(8,128)(2,1)} %get-tuple-element.96.refs_6_.refs_2_, ...), custom_call_target="tpu_custom_call" | custom-call | flops 85899344 | bytes 251740 | tf_op jit(solution)/shard_map/grad_key_value/pallas_call | solution.py:73
  339.7 5.8 %collective-permute-done.36.refs_0_.refs_5_ = bf16[528,512]{1,0:T(8,128)(2,1)} collective-permute-done((bf16[528,512]{1,0:T(8,128)(2,1)}, bf16[528,512]{1,0:T(8,128)(2,1)}, u32[]{:S(2)}, u32[]{:S(2)}) %collective-permute-start.36) | collective-permute-done | bytes 540704 | tf_op jit(solution)/shard_map/ppermute | solution.py:1243
  353.6 19.1 %back_in.3 = (bf16[528,512]{1,0:T(8,128)(2,1)}, bf16[528,512]{1,0:T(8,128)(2,1)}, bf16[528,512]{1,0:T(8,128)(2,1)}, bf16[528,512]{1,0:T(8,128)(2,1)}) custom-call(s32[3]{0:T(128)} %pad_add_fusion.refs_0_, bf16[2,512,512]{2,1,0:T(8,128)(2,1)} %refs_19_.1, bf16[2,512,512]{2,1,0:T(8,128)(2,1)} %tie.46.refs_2_, ...), custom_call_target="tpu_custom_call" | custom-call | flops 150323856 | bytes 557793 | tf_op jit(solution)/shard_map/back_in/pallas_call | solution.py:73
  383.5 5.9 %finish_blocks.2.refs_0_ = f32[512,2048]{1,0:T(8,128)} custom-call(s32[3]{0:T(128)} %pad_add_fusion.refs_0_, bf16[2,512,512]{2,1,0:T(8,128)(2,1)} %tie.66.refs_1_, bf16[2,512,512]{2,1,0:T(8,128)(2,1)} %collective-permute-done.35.refs_0_.refs_2_, bf16[2,512,512]{2,1,0:T(8,128)(2,1)} %tie.69.refs_3_, ...), custom_call_target="tpu_custom_call" | custom-call | bytes 167772 | tf_op jit(solution)/shard_map/finish_blocks/pallas_call | solution.py:73
  389.5 8.4 %collective-permute-done.46.refs_0_.refs_4_ = bf16[2,512,512]{2,1,0:T(8,128)(2,1)} collective-permute-done((bf16[2,512,512]{2,1,0:T(8,128)(2,1)}, bf16[2,512,512]{2,1,0:T(8,128)(2,1)}, u32[]{:S(2)}, u32[]{:S(2)}) %collective-permute-start.46) | collective-permute-done | bytes 1048608 | tf_op jit(solution)/shard_map/ppermute | solution.py:155
  407.7 8.1 %collective-permute-done.52.refs_1_.refs_3_.refs_9_.refs_15_ = bf16[528,512]{1,0:T(8,128)(2,1)} collective-permute-done((bf16[528,512]{1,0:T(8,128)(2,1)}, bf16[528,512]{1,0:T(8,128)(2,1)}, u32[]{:S(2)}, u32[]{:S(2)}) %collective-permute-start.52) | collective-permute-done | bytes 540704 | tf_op jit(solution)/shard_map/ppermute | solution.py:1243
  415.9 5.9 %finish_blocks.3.refs_0_ = f32[2048,512]{1,0:T(8,128)} custom-call(s32[3]{0:T(128)} %pad_add_fusion.refs_0_, bf16[2,512,512]{2,1,0:T(8,128)(2,1)} %tie.74.refs_1_, bf16[2,512,512]{2,1,0:T(8,128)(2,1)} %collective-permute-done.43.refs_0_.refs_2_, bf16[2,512,512]{2,1,0:T(8,128)(2,1)} %tie.77.refs_3_, ...), custom_call_target="tpu_custom_call" | custom-call | bytes 167772 | tf_op jit(solution)/shard_map/finish_blocks/pallas_call | solution.py:73
  (280 shorter events, 166.8 us)
Async XLA Ops:
  7.0 28.9 %collective-permute-start = (bf16[2,512,512]{2,1,0:T(8,128)(2,1)}, bf16[2,512,512]{2,1,0:T(8,128)(2,1)}, u32[]{:S(2)}, u32[]{:S(2)}) collective-permute-start(bf16[2,512,512]{2,1,0:T(8,128)(2,1)} %refs_19_.1), channel_id=1, source_target_pairs={{0,1},{1,2},{2,3},{3,0},{4,5},{5,6},{6,7},{7,4},{8,9},{9,10},{10,1... | collective-permute-start | bytes 3145736 | tf_op jit(solution)/shard_map/ppermute | solution.py:1243
  36.5 27.5 %collective-permute-start.10 = (bf16[512,1536]{1,0:T(8,128)(2,1)}, bf16[512,1536]{1,0:T(8,128)(2,1)}, u32[]{:S(2)}, u32[]{:S(2)}) collective-permute-start(bf16[512,1536]{1,0:T(8,128)(2,1)} %tie.45.refs_11_), channel_id=1, source_target_pairs={{0,8},{8,0},{16,24},{24,16},{1,9},{9,1},{17,25},{25,17},{2,10},{10... | collective-permute-start | bytes 4718600 | tf_op jit(solution)/shard_map/ppermute | solution.py:155
  36.5 25.9 %collective-permute-start.9 = (bf16[2,512,512]{2,1,0:T(8,128)(2,1)}, bf16[2,512,512]{2,1,0:T(8,128)(2,1)}, u32[]{:S(2)}, u32[]{:S(2)}) collective-permute-start(bf16[2,512,512]{2,1,0:T(8,128)(2,1)} %refs_19_.1), channel_id=1, source_target_pairs={{0,3},{1,0},{2,1},{3,2},{4,7},{5,4},{6,5},{7,6},{8,11},{9,8},{10,9... | collective-permute-start | bytes 3145736 | tf_op jit(solution)/shard_map/ppermute | solution.py:1243
  64.1 31.5 %collective-permute-start.15 = (bf16[2560,256]{1,0:T(8,128)(2,1)}, bf16[2560,256]{1,0:T(8,128)(2,1)}, u32[]{:S(2)}, u32[]{:S(2)}) collective-permute-start(bf16[2560,256]{1,0:T(8,128)(2,1)} %tie.50), channel_id=1, source_target_pairs={{0,16},{8,24},{16,0},{24,8},{1,17},{9,25},{17,1},{25,9},{2,18},{10... | collective-permute-start | bytes 3932168 | tf_op jit(solution)/shard_map/ppermute | solution.py:155
  65.5 25.7 %collective-permute-start.14 = (bf16[256,2048]{1,0:T(8,128)(2,1)}, bf16[256,2048]{1,0:T(8,128)(2,1)}, u32[]{:S(2)}, u32[]{:S(2)}) collective-permute-start(bf16[256,2048]{1,0:T(8,128)(2,1)} %tie.49.refs_0_), channel_id=1, source_target_pairs={{0,4},{4,0},{1,5},{5,1},{2,6},{6,2},{3,7},{7,3},{8,12},{12,8},{9,1... | collective-permute-start | bytes 3145736 | tf_op jit(solution)/shard_map/ppermute | solution.py:155
  67.1 28.1 %collective-permute-start.11 = (bf16[2,512,512]{2,1,0:T(8,128)(2,1)}, bf16[2,512,512]{2,1,0:T(8,128)(2,1)}, u32[]{:S(2)}, u32[]{:S(2)}) collective-permute-start(bf16[2,512,512]{2,1,0:T(8,128)(2,1)} %tie.46.refs_2_), channel_id=1, source_target_pairs={{0,1},{1,2},{2,3},{3,0},{4,5},{5,6},{6,7},{7,4},{8,9},{9,10},{10,1... | collective-permute-start | bytes 3145736 | tf_op jit(solution)/shard_map/ppermute | solution.py:1243
  67.5 54.2 %collective-permute-start.16 = (bf16[512,2048]{1,0:T(8,128)(2,1)}, bf16[512,2048]{1,0:T(8,128)(2,1)}, u32[]{:S(2)}, u32[]{:S(2)}) collective-permute-start(bf16[512,2048]{1,0:T(8,128)(2,1)} %refs_17_.3), channel_id=1, source_target_pairs={{0,8},{8,0},{16,24},{24,16},{1,9},{9,1},{17,25},{25,17},{2,10},{10... | collective-permute-start | bytes 6291464 | tf_op jit(solution)/shard_map/ppermute | solution.py:155
  75.1 46.6 %collective-permute-start.19 = (bf16[2,512,512]{2,1,0:T(8,128)(2,1)}, bf16[2,512,512]{2,1,0:T(8,128)(2,1)}, u32[]{:S(2)}, u32[]{:S(2)}) collective-permute-start(bf16[2,512,512]{2,1,0:T(8,128)(2,1)} %refs_20_.1), channel_id=1, source_target_pairs={{0,1},{1,2},{2,3},{3,0},{4,5},{5,6},{6,7},{7,4},{8,9},{9,10},{10,1... | collective-permute-start | bytes 3145736 | tf_op jit(solution)/shard_map/ppermute | solution.py:1243
  95.6 30.7 %collective-permute-start.20 = (bf16[2560,256]{1,0:T(8,128)(2,1)}, bf16[2560,256]{1,0:T(8,128)(2,1)}, u32[]{:S(2)}, u32[]{:S(2)}) collective-permute-start(bf16[2560,256]{1,0:T(8,128)(2,1)} %tie.53.refs_0_), channel_id=1, source_target_pairs={{0,4},{4,0},{1,5},{5,1},{2,6},{6,2},{3,7},{7,3},{8,12},{12,8},{9,1... | collective-permute-start | bytes 3932168 | tf_op jit(solution)/shard_map/ppermute | solution.py:155
  126.9 39.1 %collective-permute-start.25 = (bf16[2,512,512]{2,1,0:T(8,128)(2,1)}, bf16[2,512,512]{2,1,0:T(8,128)(2,1)}, u32[]{:S(2)}, u32[]{:S(2)}) collective-permute-start(bf16[2,512,512]{2,1,0:T(8,128)(2,1)} %refs_20_.1), channel_id=1, source_target_pairs={{0,3},{1,0},{2,1},{3,2},{4,7},{5,4},{6,5},{7,6},{8,11},{9,8},{10,9... | collective-permute-start | bytes 3145736 | tf_op jit(solution)/shard_map/ppermute | solution.py:1243
  129.0 48.1 %collective-permute-start.26 = (bf16[2,512,512]{2,1,0:T(8,128)(2,1)}, bf16[2,512,512]{2,1,0:T(8,128)(2,1)}, u32[]{:S(2)}, u32[]{:S(2)}) collective-permute-start(bf16[2,512,512]{2,1,0:T(8,128)(2,1)} %tie.58.refs_3_.refs_2_), channel_id=1, source_target_pairs={{0,1},{1,2},{2,3},{3,0},{4,5},{5,6},{6,7},{7,4},{8,9},{9,10},{10,1... | collective-permute-start | bytes 3145736 | tf_op jit(solution)/shard_map/ppermute | solution.py:1243
  148.9 49.1 %collective-permute-start.24 = (bf16[2,512,512]{2,1,0:T(8,128)(2,1)}, bf16[2,512,512]{2,1,0:T(8,128)(2,1)}, u32[]{:S(2)}, u32[]{:S(2)}) collective-permute-start(bf16[2,512,512]{2,1,0:T(8,128)(2,1)} %tie.57.refs_3_), channel_id=1, source_target_pairs={{0,4},{4,0},{1,5},{5,1},{2,6},{6,2},{3,7},{7,3},{8,12},{12,8},{9,1... | collective-permute-start | bytes 3145736 | tf_op jit(solution)/shard_map/ppermute | solution.py:155
  150.5 61.8 %collective-permute-start.27 = (bf16[2,512,512]{2,1,0:T(8,128)(2,1)}, bf16[2,512,512]{2,1,0:T(8,128)(2,1)}, u32[]{:S(2)}, u32[]{:S(2)}) collective-permute-start(bf16[2,512,512]{2,1,0:T(8,128)(2,1)} %tie.59.refs_3_), channel_id=1, source_target_pairs={{0,4},{4,0},{1,5},{5,1},{2,6},{6,2},{3,7},{7,3},{8,12},{12,8},{9,1... | collective-permute-start | bytes 3145736 | tf_op jit(solution)/shard_map/ppermute | solution.py:155
  224.8 32.2 %collective-permute-start.29 = (bf16[2,512,512]{2,1,0:T(8,128)(2,1)}, bf16[2,512,512]{2,1,0:T(8,128)(2,1)}, u32[]{:S(2)}, u32[]{:S(2)}) collective-permute-start(bf16[2,512,512]{2,1,0:T(8,128)(2,1)} %tie.61), channel_id=1, source_target_pairs={{0,4},{4,0},{1,5},{5,1},{2,6},{6,2},{3,7},{7,3},{8,12},{12,8},{9,1... | collective-permute-start | bytes 3145736 | tf_op jit(solution)/shard_map/ppermute | solution.py:155
  262.5 25.9 %collective-permute-start.33 = (bf16[2,512,512]{2,1,0:T(8,128)(2,1)}, bf16[2,512,512]{2,1,0:T(8,128)(2,1)}, u32[]{:S(2)}, u32[]{:S(2)}) collective-permute-start(bf16[2,512,512]{2,1,0:T(8,128)(2,1)} %tie.64), channel_id=1, source_target_pairs={{0,4},{4,0},{1,5},{5,1},{2,6},{6,2},{3,7},{7,3},{8,12},{12,8},{9,1... | collective-permute-start | bytes 3145736 | tf_op jit(solution)/shard_map/ppermute | solution.py:155
  288.5 29.3 %collective-permute-start.40 = (bf16[2,2,512,512]{3,2,1,0:T(8,128)(2,1)}, bf16[2,2,512,512]{3,2,1,0:T(8,128)(2,1)}, u32[]{:S(2)}, u32[]{:S(2)}) collective-permute-start(bf16[2,2,512,512]{3,2,1,0:T(8,128)(2,1)} %tie.71), channel_id=1, source_target_pairs={{0,8},{8,0},{16,24},{24,16},{1,9},{9,1},{17,25},{25,17},{2,10},{10... | collective-permute-start | bytes 6291464 | tf_op jit(solution)/shard_map/ppermute | solution.py:155
  288.5 26.0 %collective-permute-start.35 = (bf16[2,512,512]{2,1,0:T(8,128)(2,1)}, bf16[2,512,512]{2,1,0:T(8,128)(2,1)}, u32[]{:S(2)}, u32[]{:S(2)}) collective-permute-start(bf16[2,512,512]{2,1,0:T(8,128)(2,1)} %tie.66.refs_1_), channel_id=1, source_target_pairs={{0,4},{4,0},{1,5},{5,1},{2,6},{6,2},{3,7},{7,3},{8,12},{12,8},{9,1... | collective-permute-start | bytes 3145736 | tf_op jit(solution)/shard_map/ppermute | solution.py:155
  290.2 27.6 %collective-permute-start.34 = (bf16[2,512,512]{2,1,0:T(8,128)(2,1)}, bf16[2,512,512]{2,1,0:T(8,128)(2,1)}, u32[]{:S(2)}, u32[]{:S(2)}) collective-permute-start(bf16[2,512,512]{2,1,0:T(8,128)(2,1)} %tie.65), channel_id=1, source_target_pairs={{0,1},{1,2},{2,3},{3,0},{4,5},{5,6},{6,7},{7,4},{8,9},{9,10},{10,1... | collective-permute-start | bytes 3145736 | tf_op jit(solution)/shard_map/ppermute | solution.py:1243
  290.4 27.4 %collective-permute-start.39 = (bf16[2,512,512]{2,1,0:T(8,128)(2,1)}, bf16[2,512,512]{2,1,0:T(8,128)(2,1)}, u32[]{:S(2)}, u32[]{:S(2)}) collective-permute-start(bf16[2,512,512]{2,1,0:T(8,128)(2,1)} %tie.70), channel_id=1, source_target_pairs={{0,16},{8,24},{16,0},{24,8},{1,17},{9,25},{17,1},{25,9},{2,18},{10... | collective-permute-start | bytes 3145736 | tf_op jit(solution)/shard_map/ppermute | solution.py:155
  317.8 27.7 %collective-permute-start.42 = (bf16[2,512,512]{2,1,0:T(8,128)(2,1)}, bf16[2,512,512]{2,1,0:T(8,128)(2,1)}, u32[]{:S(2)}, u32[]{:S(2)}) collective-permute-start(bf16[2,512,512]{2,1,0:T(8,128)(2,1)} %tie.73), channel_id=1, source_target_pairs={{0,16},{8,24},{16,0},{24,8},{1,17},{9,25},{17,1},{25,9},{2,18},{10... | collective-permute-start | bytes 3145736 | tf_op jit(solution)/shard_map/ppermute | solution.py:155
  345.5 30.1 %collective-permute-start.48 = (bf16[2,2,512,512]{3,2,1,0:T(8,128)(2,1)}, bf16[2,2,512,512]{3,2,1,0:T(8,128)(2,1)}, u32[]{:S(2)}, u32[]{:S(2)}) collective-permute-start(bf16[2,2,512,512]{3,2,1,0:T(8,128)(2,1)} %tie.79), channel_id=1, source_target_pairs={{0,8},{8,0},{16,24},{24,16},{1,9},{9,1},{17,25},{25,17},{2,10},{10... | collective-permute-start | bytes 6291464 | tf_op jit(solution)/shard_map/ppermute | solution.py:155
  345.5 27.2 %collective-permute-start.43 = (bf16[2,512,512]{2,1,0:T(8,128)(2,1)}, bf16[2,512,512]{2,1,0:T(8,128)(2,1)}, u32[]{:S(2)}, u32[]{:S(2)}) collective-permute-start(bf16[2,512,512]{2,1,0:T(8,128)(2,1)} %tie.74.refs_1_), channel_id=1, source_target_pairs={{0,4},{4,0},{1,5},{5,1},{2,6},{6,2},{3,7},{7,3},{8,12},{12,8},{9,1... | collective-permute-start | bytes 3145736 | tf_op jit(solution)/shard_map/ppermute | solution.py:155
  346.3 27.3 %collective-permute-start.41 = (bf16[2,512,512]{2,1,0:T(8,128)(2,1)}, bf16[2,512,512]{2,1,0:T(8,128)(2,1)}, u32[]{:S(2)}, u32[]{:S(2)}) collective-permute-start(bf16[2,512,512]{2,1,0:T(8,128)(2,1)} %tie.72), channel_id=1, source_target_pairs={{0,3},{1,0},{2,1},{3,2},{4,7},{5,4},{6,5},{7,6},{8,11},{9,8},{10,9... | collective-permute-start | bytes 3145736 | tf_op jit(solution)/shard_map/ppermute | solution.py:1243
  348.0 27.6 %collective-permute-start.47 = (bf16[2,512,512]{2,1,0:T(8,128)(2,1)}, bf16[2,512,512]{2,1,0:T(8,128)(2,1)}, u32[]{:S(2)}, u32[]{:S(2)}) collective-permute-start(bf16[2,512,512]{2,1,0:T(8,128)(2,1)} %tie.78), channel_id=1, source_target_pairs={{0,16},{8,24},{16,0},{24,8},{1,17},{9,25},{17,1},{25,9},{2,18},{10... | collective-permute-start | bytes 3145736 | tf_op jit(solution)/shard_map/ppermute | solution.py:155
  (45 other events, 687.1 us)
